TPU v7x, 32 devices: a whole 2x2x4 slice. The times are simulated.
32 devices in a mesh: span: 2 (over y), stream: 16 (over z, x, core).
Axes of the slice: x: 2, y: 2, z: 4, core: 2. Of those that a mesh axis runs over, the one named last changes fastest.
Arguments:
- velocity: float32 [3, 8, 128, 256], P(None, 'span', 'stream'), may hold values from -32 to 32
- strain: float32 [6, 8, 128, 256], P(None, 'span', 'stream'), may hold values from -4 to 4
- row_bins: int32 [128], P('stream'), may hold values from 0 to 63, never falling along the last dimension, each value on 1 to 4 neighbouring positions
- cotangent: float32 [6, 8, 128, 256], P(None, 'span', 'stream'), may hold values from -6 to 6
Outputs:
- model_residual: float32 [6, 8, 128, 256], P(None, 'span', 'stream')
- velocity_grad: float32 [3, 8, 128, 256], P(None, 'span', 'stream')
Inputs may be any that keep to these rules, and one draw needn't show every extreme that they name: `row_bins`: bins never fall along the rows, and every bin holds 1 to 4 rows.
All inputs are finite; a program needn't handle non-finite values.
Results may differ from a plain program's by a relative error of at most 0.0003.
Values sent between devices are 32-bit elements; how exact they have to be, the bound alone decides.
No kernel may reach another device: no remote copies, remote signals or barrier semaphores. Data moves between devices by JAX's collectives and lax.ppermute only.
A program may use at most 64 MiB of HBM per device.

v0:
```python
import jax
import jax.numpy as jnp
import numpy as np
from jax import lax
from jax.sharding import PartitionSpec as P

NBINS = 64


FILTER_ALPHA = 0.45
CENTER_WEIGHT = 0.95
SIDE_WEIGHT = 0.475
STRAIN_FLOOR = 0.25
EPSILON = 1e-06
INDEX_PAIRS = ((0, 0), (0, 1), (0, 2), (1, 1), (1, 2), (2, 2))
PAIR_WEIGHTS = (1.0, 2.0, 2.0, 1.0, 2.0, 1.0)
HIGHEST = lax.Precision.HIGHEST


def extended(array, sides, width):
    for axis, dim in sides:
        peers, length = (lax.axis_size(axis), array.shape[dim])
        up = [(i, (i + 1) % peers) for i in range(peers)]
        down = [(j, i) for i, j in up]
        last = lax.slice_in_dim(array, length - width, length, axis=dim)
        first = lax.slice_in_dim(array, 0, width, axis=dim)
        before = lax.ppermute(last, axis, up)
        after = lax.ppermute(first, axis, down)
        array = jnp.concatenate([before, array, after], axis=dim)
    return array


def invert_table(matrix):
    extent = matrix.shape[0]
    augmented = np.concatenate([np.array(matrix), np.eye(extent)], axis=1)
    for column in range(extent):
        pivot_row = column + int(np.argmax(np.abs(augmented[column:, column])))
        swapped = augmented[[pivot_row, column]]
        augmented[[column, pivot_row]] = swapped
        augmented[column] = augmented[column] / augmented[column, column]
        for row_index in range(extent):
            if row_index != column:
                augmented[row_index] = (
                    augmented[row_index] - augmented[row_index, column] * augmented[column]
                )
    return augmented[:, extent:]


def loop_tables(cell_count, devices):
    local_system = np.eye(cell_count) + FILTER_ALPHA * (
        np.eye(cell_count, k=1) + np.eye(cell_count, k=-1)
    )
    local_inverse = invert_table(local_system)
    first_column = local_inverse[:, 0]
    last_column = local_inverse[:, cell_count - 1]
    unknowns = 2 * devices
    coupling = np.eye(unknowns)
    for device in range(devices):
        previous = (device - 1) % devices
        following = (device + 1) % devices
        for which_end, cell_index in ((0, 0), (1, cell_count - 1)):
            target = 2 * device + which_end
            coupling[target, 2 * previous + 1] += FILTER_ALPHA * first_column[cell_index]
            coupling[target, 2 * following] += FILTER_ALPHA * last_column[cell_index]
    reduced = invert_table(coupling)
    selectors = np.stack(
        [
            reduced[[2 * ((device - 1) % devices) + 1, 2 * ((device + 1) % devices)], :]
            for device in range(devices)
        ]
    )
    return (
        jnp.asarray(local_inverse, jnp.float32),
        jnp.asarray(first_column, jnp.float32),
        jnp.asarray(last_column, jnp.float32),
        jnp.asarray(selectors, jnp.float32),
    )


def rim_side(values):
    padded = extended(values, (("span", 1),), 1)
    return CENTER_WEIGHT * values + SIDE_WEIGHT * (padded[:, 2:] + padded[:, :-2])


def solve_loop(values, tables, own_index):
    local_inverse, first_column, last_column, selectors = tables
    particular = jnp.einsum("ij,fjyx->fiyx", local_inverse, values, precision=HIGHEST)
    end_values = jnp.stack([particular[:, 0], particular[:, -1]], axis=0)
    selector = lax.dynamic_index_in_dim(selectors, own_index, 0, keepdims=False)
    gathered_piece = lax.all_gather(end_values, "span", axis=0, tiled=True)
    columns = lax.slice_in_dim(selector, 0, gathered_piece.shape[0], axis=1)
    neighbours = jnp.zeros_like(end_values) + jnp.einsum(
        "ae,efyx->afyx", columns, gathered_piece, precision=HIGHEST
    )
    previous = neighbours[0]
    following = neighbours[1]
    solved = particular - FILTER_ALPHA * (
        first_column[None, :, None, None] * previous[:, None]
        + last_column[None, :, None, None] * following[:, None]
    )
    return (solved, previous, following)


def solve_back(values, tables, own_index):
    local_inverse, first_column, last_column, selectors = tables
    selector = lax.dynamic_index_in_dim(selectors, own_index, 0, keepdims=False)
    near_bar = -FILTER_ALPHA * jnp.stack(
        [
            jnp.einsum("i,fiyx->fyx", first_column, values, precision=HIGHEST),
            jnp.einsum("i,fiyx->fyx", last_column, values, precision=HIGHEST),
        ],
        axis=0,
    )
    columns = lax.slice_in_dim(selector, 0, 2 * lax.axis_size("span"), axis=1)
    end_bar = lax.psum_scatter(
        jnp.einsum("ae,afyx->efyx", columns, near_bar, precision=HIGHEST),
        "span",
        scatter_dimension=0,
        tiled=True,
    )
    particular_bar = values.at[:, 0].add(end_bar[0]).at[:, -1].add(end_bar[1])
    return jnp.einsum("ji,fjyx->fiyx", local_inverse, particular_bar, precision=HIGHEST)


def smooth(values, tables, own_index):
    return solve_loop(rim_side(values), tables, own_index)[0]


def unsmooth(values, tables, own_index):
    return rim_side(solve_back(values, tables, own_index))


def on_device(velocity, strain, row_bins, cotangent):
    tables = loop_tables(velocity.shape[1], lax.axis_size("span"))
    own_index = lax.axis_index("span")
    weights = jnp.asarray(PAIR_WEIGHTS, jnp.float32)[:, None, None, None]
    products = jnp.stack([velocity[former] * velocity[latter] for former, latter in INDEX_PAIRS])
    size_field = jnp.sqrt(
        jnp.maximum(2.0 * jnp.sum(weights * strain * strain, axis=0), STRAIN_FLOOR)
    )
    fields = jnp.concatenate([velocity, products, size_field[None]], axis=0)
    filtered = smooth(fields, tables, own_index)
    coarse = jnp.stack([filtered[former] * filtered[latter] for former, latter in INDEX_PAIRS])
    leonard = filtered[3:9] - coarse
    model_term = products - coarse + 2.0 * (4.0 * filtered[9] - size_field)[None] * strain
    onehot = (row_bins[:, None] == jnp.arange(NBINS, dtype=jnp.int32)[None, :]).astype(jnp.float32)
    cross_local = jnp.dot(
        jnp.sum(weights * leonard * model_term, axis=(0, 1, 3)), onehot, precision=HIGHEST
    )
    square_local = jnp.dot(
        jnp.sum(weights * model_term * model_term, axis=(0, 1, 3)), onehot, precision=HIGHEST
    )
    blame_local = jnp.dot(
        jnp.sum(cotangent * model_term, axis=(0, 1, 3)), onehot, precision=HIGHEST
    )
    cross_bins, square_bins, blame_bins = lax.psum(
        (cross_local, square_local, blame_local), ("span", "stream")
    )
    denominator = square_bins + EPSILON
    coefficient = cross_bins / denominator
    row_coefficient = jnp.dot(onehot, coefficient, precision=HIGHEST)[None, None, :, None]
    residual = leonard - row_coefficient * model_term
    coefficient_bar = -blame_bins
    cross_bar = coefficient_bar / denominator
    square_bar = -coefficient_bar * coefficient / denominator
    row_cross = jnp.dot(onehot, cross_bar, precision=HIGHEST)[None, None, :, None]
    row_square = jnp.dot(onehot, square_bar, precision=HIGHEST)[None, None, :, None]
    leonard_bar = cotangent + row_cross * weights * model_term
    model_bar = (
        -row_coefficient * cotangent
        + row_cross * weights * leonard
        + 2.0 * row_square * weights * model_term
    )
    zero_field = jnp.zeros_like(velocity[0])
    coarse_bar = [zero_field, zero_field, zero_field]
    for position, (former, latter) in enumerate(INDEX_PAIRS):
        combined = leonard_bar[position] + model_bar[position]
        coarse_bar[former] = coarse_bar[former] - combined * filtered[latter]
        coarse_bar[latter] = coarse_bar[latter] - combined * filtered[former]
    pulled = unsmooth(
        jnp.concatenate([jnp.stack(coarse_bar), leonard_bar], axis=0), tables, own_index
    )
    gradient_parts = [pulled[0], pulled[1], pulled[2]]
    for position, (former, latter) in enumerate(INDEX_PAIRS):
        through = pulled[3 + position] + model_bar[position]
        gradient_parts[former] = gradient_parts[former] + through * velocity[latter]
        gradient_parts[latter] = gradient_parts[latter] + through * velocity[former]
    return (residual, jnp.stack(gradient_parts))


def solution(mesh):
    return jax.shard_map(
        on_device,
        mesh=mesh,
        in_specs=(
            P(None, "span", "stream", None),
            P(None, "span", "stream", None),
            P("stream"),
            P(None, "span", "stream", None),
        ),
        out_specs=(P(None, "span", "stream", None), P(None, "span", "stream", None)),
        check_vma=False,
    )
```

profile of v0, /device:TPU:0, one launch (start us, length us, event | category | flops | bytes accessed | tf_op | source)
XLA Modules:
  0.0 106.5 jit_solution(10292901475350277093)
XLA Ops:
  7.2 0.9 fusion.61
  8.1 0.6 copy-done.4
  8.8 0.1 fusion.10
  9.3 3.0 %collective-permute-start = (f32[10,1,8,256]{3,2,1,0:T(8,128)S(1)}, f32[10,1,8,256]{3,2,1,0:T(8,128)S(1)}, u32[]{:S(2)}, u32[]{:S(2)}) collective-permute-start(f32[10,1,8,256]{3,2,1,0:T(8,128)S(1)} %get-tuple-element.54), channel_id=1, source_target_pairs={{16,0},{0,16},{17,1},{1,17},{18,2},{2,18},{19,3},{3,19},{20,4},{4,... | collective-permute-start | bytes 245768 | tf_op jit(solution)/shard_map/ppermute | solution.py:28
  12.3 0.1 collective-permute-start.1
  12.4 2.7 %collective-permute-done = f32[10,1,8,256]{3,2,1,0:T(8,128)S(1)} collective-permute-done((f32[10,1,8,256]{3,2,1,0:T(8,128)S(1)}, f32[10,1,8,256]{3,2,1,0:T(8,128)S(1)}, u32[]{:S(2)}, u32[]{:S(2)}) %collective-permute-start) | collective-permute-done | bytes 81952 | tf_op jit(solution)/shard_map/ppermute | solution.py:28
  15.1 1.7 %collective-permute-done.1 = f32[10,1,8,256]{3,2,1,0:T(8,128)S(1)} collective-permute-done((f32[10,1,8,256]{3,2,1,0:T(8,128)S(1)}, f32[10,1,8,256]{3,2,1,0:T(8,128)S(1)}, u32[]{:S(2)}, u32[]{:S(2)}) %collective-permute-start.1) | collective-permute-done | bytes 81952 | tf_op jit(solution)/shard_map/ppermute | solution.py:27
  16.8 0.7 convolution_bitcast_fusion
  17.5 0.1 slice_bitcast_fusion.1
  17.7 0.2 pad_maximum_fusion.5
  17.9 6.0 %all_gather.3 = f32[4,10,8,256]{3,2,1,0:T(8,128)S(1)} all-gather(f32[2,10,8,256]{3,2,1,0:T(8,128)S(1)} %copy.44), channel_id=1, replica_groups=mesh['span'=2,'stream'=16] {'span'}, dimensions={0}, use_global_device_ids=true | all-gather | bytes 491520 | tf_op jit(solution)/shard_map/all_gather | solution.py:90
  23.9 0.8 fusion.4
  24.7 0.1 fusion.59
  24.9 0.6 copy-done.8
  25.5 0.2 multiply_subtract_fusion
  25.9 0.8 copy-done
  26.7 0.4 fusion.11
  27.1 0.7 copy-done.10
  27.8 0.2 convolution_bitcast_fusion.6
  28.0 0.2 convolution_bitcast_fusion.7
  28.1 0.2 convolution_bitcast_fusion.4
  28.3 40.5 %all-reduce = (f32[64]{0:T(128)S(1)}, f32[64]{0:T(128)S(1)}, f32[64]{0:T(128)S(1)}) all-reduce(f32[64]{0:T(128)S(1)} %convolution_bitcast_fusion.7, f32[64]{0:T(128)S(1)} %convolution_bitcast_fusion.6, f32[64]{0:T(128)S(1)} %convolution_bitcast_fusion.4), channel_id=1, replica_groups=mesh['span'=2,'stream'=16] {'span','stream'}, use_global_device_ids=true, to_apply=%region_2.3 | all-reduce | flops 192 | bytes 1536 | tf_op jit(solution)/shard_map/psum | solution.py:156
  68.9 0.2 convolution_bitcast_fusion.3
  69.0 0.2 fusion
  69.2 0.2 fusion.62
  69.5 0.2 multiply_add_fusion
  70.0 0.6 copy-done.7
  70.5 0.6 fusion.64
  71.2 0.6 copy-done.6
  71.8 0.6 fusion.63
  72.5 0.8 fusion.12
  73.4 0.8 copy.50
  74.1 12.3 %reduce-scatter.2.cloned.1.call-done = f32[2,9,8,256]{3,2,1,0:T(8,128)} async-done(((f32[4,9,8,256]{3,2,1,0:T(8,128)}), f32[2,9,8,256]{3,2,1,0:T(8,128)}) %reduce-scatter.2.cloned.1.call-update) | async-done | bytes 147472 | tf_op jit(solution)/shard_map/reduce_scatter | solution.py:115
  86.5 0.9 fusion.60
  87.4 0.1 slice_add_fusion.1
  87.5 2.2 %scatter-add.6 = f32[9,4,8,256]{3,1,2,0:T(4,128)S(1)} dynamic-update-slice(f32[9,4,8,256]{3,1,2,0:T(4,128)S(1)} %pad_maximum_fusion.4, f32[9,1,8,256]{3,1,2,0:T(1,128)S(1)} %slice_add_fusion.1, s32[]{:T(128)} %constant.94.clone.1, s32[]{:T(128)} %constant.94.clone.1, s32[]{:T(128)} %constant.94.clone.1, s32[]{:T(128)} %constant.94.clone.1) | dynamic-update-slice | bytes 147460 | tf_op jit(solution)/shard_map/scatter-add | solution.py:121
  89.7 0.1 slice_add_fusion
  89.8 2.2 %scatter-add.9 = f32[9,4,8,256]{3,1,2,0:T(4,128)S(1)} dynamic-update-slice(f32[9,4,8,256]{3,1,2,0:T(4,128)S(1)} %scatter-add.6, f32[9,1,8,256]{3,1,2,0:T(1,128)S(1)} %slice_add_fusion, s32[]{:T(128)} %constant.94.clone.1, s32[]{:T(128)} %constant.100.clone.1, s32[]{:T(128)} %constant.94.clone.1, s32[]{:T(128)} %constant.94.clone.1) | dynamic-update-slice | bytes 147460 | tf_op jit(solution)/shard_map/scatter-add | solution.py:121
  92.0 0.7 convolution_bitcast_fusion.1
  92.7 0.1 fusion.58
  92.8 0.4 collective-permute-start.2
  93.2 1.7 %collective-permute-start.3 = (f32[9,1,8,256]{3,1,2,0:T(1,128)S(1)}, f32[9,1,8,256]{3,1,2,0:T(1,128)S(1)}, u32[]{:S(2)}, u32[]{:S(2)}) collective-permute-start(f32[9,1,8,256]{3,1,2,0:T(1,128)S(1)} %get-tuple-element.57), channel_id=1, source_target_pairs={{0,16},{16,0},{1,17},{17,1},{2,18},{18,2},{3,19},{19,3},{4,20},{20... | collective-permute-start | bytes 221192 | tf_op jit(solution)/shard_map/ppermute | solution.py:27
  94.9 0.7 copy.54
  95.6 2.0 %collective-permute-done.2 = f32[9,1,8,256]{3,1,2,0:T(1,128)S(1)} collective-permute-done((f32[9,1,8,256]{3,1,2,0:T(1,128)S(1)}, f32[9,1,8,256]{3,1,2,0:T(1,128)S(1)}, u32[]{:S(2)}, u32[]{:S(2)}) %collective-permute-start.2) | collective-permute-done | bytes 73760 | tf_op jit(solution)/shard_map/ppermute | solution.py:28
  97.7 0.8 collective-permute-done.3
  98.5 0.3 fusion.9
  98.8 0.1 fusion.20
  99.0 0.7 copy.55
  (54 shorter events, 1.1 us)
Async XLA Ops:
  7.2 0.9 copy-start.2
  7.2 1.0 copy-start.1
  7.2 79.3 %reduce-scatter.2.cloned.1.call-start = ((), (), s32[]{:S(2)}) async-start(), calls=%async_computation.1 | async-start | bytes 442368 | tf_op jit(solution)/shard_map/reduce_scatter | solution.py:115
  8.1 0.7 copy-start.4
  9.3 5.8 %collective-permute-start = (f32[10,1,8,256]{3,2,1,0:T(8,128)S(1)}, f32[10,1,8,256]{3,2,1,0:T(8,128)S(1)}, u32[]{:S(2)}, u32[]{:S(2)}) collective-permute-start(f32[10,1,8,256]{3,2,1,0:T(8,128)S(1)} %get-tuple-element.54), channel_id=1, source_target_pairs={{16,0},{0,16},{17,1},{1,17},{18,2},{2,18},{19,3},{3,19},{20,4},{4,... | collective-permute-start | bytes 245768 | tf_op jit(solution)/shard_map/ppermute | solution.py:28
  12.3 4.4 %collective-permute-start.1 = (f32[10,1,8,256]{3,2,1,0:T(8,128)S(1)}, f32[10,1,8,256]{3,2,1,0:T(8,128)S(1)}, u32[]{:S(2)}, u32[]{:S(2)}) collective-permute-start(f32[10,1,8,256]{3,2,1,0:T(8,128)S(1)} %get-tuple-element.55), channel_id=1, source_target_pairs={{0,16},{16,0},{1,17},{17,1},{2,18},{18,2},{3,19},{19,3},{4,20},{20... | collective-permute-start | bytes 245768 | tf_op jit(solution)/shard_map/ppermute | solution.py:27
  12.4 4.4 %copy-start.3 = (f32[4,4,1,1]{1,0,3,2:T(4,128)S(1)}, f32[4,4,1,1]{1,0,3,2:T(4,128)}, u32[]{:S(2)}) copy-start(f32[4,4,1,1]{1,0,3,2:T(4,128)} %constant.110) | copy-start | bytes 196
  17.9 6.0 %copy-start.5 = (f32[2,2,4]{2,1,0:T(2,128)S(1)}, f32[2,2,4]{2,1,0:T(2,128)}, u32[]{:S(2)}) copy-start(f32[2,2,4]{2,1,0:T(2,128)} %constant.104.clone) | copy-start | bytes 196
  24.9 0.7 copy-start.8
  24.9 0.7 copy-start.9
  25.8 0.9 copy-start
  27.1 0.7 copy-start.10
  69.9 0.7 copy-start.7
  71.2 0.7 copy-start.6
  92.8 4.9 %collective-permute-start.2 = (f32[9,1,8,256]{3,1,2,0:T(1,128)S(1)}, f32[9,1,8,256]{3,1,2,0:T(1,128)S(1)}, u32[]{:S(2)}, u32[]{:S(2)}) collective-permute-start(f32[9,1,8,256]{3,1,2,0:T(1,128)S(1)} %get-tuple-element.56), channel_id=1, source_target_pairs={{16,0},{0,16},{17,1},{1,17},{18,2},{2,18},{19,3},{3,19},{20,4},{4,... | collective-permute-start | bytes 221192 | tf_op jit(solution)/shard_map/ppermute | solution.py:28
  93.2 5.3 %collective-permute-start.3 = (f32[9,1,8,256]{3,1,2,0:T(1,128)S(1)}, f32[9,1,8,256]{3,1,2,0:T(1,128)S(1)}, u32[]{:S(2)}, u32[]{:S(2)}) collective-permute-start(f32[9,1,8,256]{3,1,2,0:T(1,128)S(1)} %get-tuple-element.57), channel_id=1, source_target_pairs={{0,16},{16,0},{1,17},{17,1},{2,18},{18,2},{3,19},{19,3},{4,20},{20... | collective-permute-start | bytes 221192 | tf_op jit(solution)/shard_map/ppermute | solution.py:27
Sparse Core Ops, SparseCore 0:
  74.3 12.1 reduce-scatter.1
where the time goes:
time: 107 us; the launch traced here: 106 us
  blocking collectives  46.5 us (43%)
  waiting for transfers between devices  19.6 us (18%)
  between operations  14.5 us (14%)
  local copies, waits for them, and re-layouts  12.8 us (12%)
  matrix products  5.4 us (5%)
  starting transfers between devices  5.24 us (5%)
  other arithmetic  2.49 us (2%)
    psum x1, blocking collectives, on_device(): lax.psum((cross_local, square_local, blame_local), ('span', 'stream'))  40.5 us
    reduce_scatter x1, waiting for transfers between devices, solve_back(): lax.psum_scatter(jnp.einsum('ae,afyx->efyx', columns, near_bar, precision...  12.3 us
    all_gather x1, blocking collectives, solve_loop(): gathered_piece = lax.all_gather(end_values, 'span', axis=0, tiled=True)  6 us
    unnamed x32, local copies, waits for them, and re-layouts  5.38 us
    ppermute x2, waiting for transfers between devices, extended(): after = lax.ppermute(first, axis, down)  4.76 us
    scatter-add x2, local copies, waits for them, and re-layouts, solve_back(): particular_bar = values.at[:, 0].add(end_bar[0]).at[:, -1].add(end_bar[1])  4.34 us
    ppermute x2, starting transfers between devices, extended(): after = lax.ppermute(first, axis, down)  3.41 us
    ppermute x2, waiting for transfers between devices, extended(): before = lax.ppermute(last, axis, up)  2.44 us
  transfers between devices with their start and end apart: 5, of which 5 were waited for; matrix products, arithmetic and copies ran while one was open for 1% of the time, Pallas kernels for 0%

commit v1 on v0

v1 whole, which is shorter than its diff:
```python
import functools

import jax
import jax.numpy as jnp
import numpy as np
from jax import lax
from jax.experimental import pallas as pl
from jax.experimental.pallas import tpu as pltpu
from jax.sharding import PartitionSpec as P

NBINS = 64
FILTER_ALPHA = 0.45
CENTER_WEIGHT = 0.95
SIDE_WEIGHT = 0.475
STRAIN_FLOOR = 0.25
EPSILON = 1e-06
INDEX_PAIRS = ((0, 0), (0, 1), (0, 2), (1, 1), (1, 2), (2, 2))
PAIR_WEIGHTS = (1.0, 2.0, 2.0, 1.0, 2.0, 1.0)
PAIR_OF = ((0, 1, 2), (1, 3, 4), (2, 4, 5))
LANES = 128


def filter_row(extent):
    eye = np.eye(extent)
    ring = np.roll(eye, 1, axis=1) + np.roll(eye, -1, axis=1)
    system = eye + FILTER_ALPHA * ring
    side = CENTER_WEIGHT * eye + SIDE_WEIGHT * ring
    return np.linalg.solve(system, side)[0]


def end_weights(cells):
    weights = np.zeros((2, cells))
    weights[0, 0] = 1.0
    weights[1, cells - 1] = 1.0
    inner = cells - 2
    if inner > 0:
        system = np.eye(inner) + FILTER_ALPHA * (np.eye(inner, k=1) + np.eye(inner, k=-1))
        right = np.zeros((inner, 2))
        right[0, 0] = -FILTER_ALPHA
        right[inner - 1, 1] = -FILTER_ALPHA
        weights[:, 1:-1] = np.linalg.solve(system, right).T
    return weights


class Tables:
    def __init__(self, cells, devices):
        row = filter_row(cells * devices)
        extent = cells * devices
        self.cells = cells
        self.devices = devices
        self.own = [[float(row[(z - w) % extent]) for w in range(cells)] for z in range(cells)]
        self.ends = [[float(x) for x in line] for line in end_weights(cells)]
        self.couple = [
            [[float(row[(z - shift * cells - w) % extent]) for w in (0, cells - 1)] for z in range(cells)]
            for shift in range(devices)
        ]

    def project(self, values):
        return [weighted(line, values) for line in self.ends]

    def inside(self, values):
        return [weighted(line, values) for line in self.own]

    def outside(self, shift, ends):
        return [weighted(line, ends) for line in self.couple[shift]]


def weighted(weights, values):
    total = None
    for weight, value in zip(weights, values):
        if weight == 0.0:
            continue
        term = value if weight == 1.0 else value * weight
        total = term if total is None else total + term
    return total


def add_lists(left, right):
    return [x + y for x, y in zip(left, right)]


def halves(width):
    return [pl.ds(start, LANES) for start in range(0, width, LANES)]


def prepare_kernel(tables, strain_ref, cot_ref, size_ref, size_ends_ref, cot_ends_ref):
    cells = tables.cells
    for lanes in halves(strain_ref.shape[-1]):
        size = []
        for z in range(cells):
            total = None
            for k, weight in enumerate(PAIR_WEIGHTS):
                value = strain_ref[k, z, :, lanes]
                term = weight * (value * value)
                total = term if total is None else total + term
            size.append(jnp.sqrt(jnp.maximum(2.0 * total, STRAIN_FLOOR)))
            size_ref[z, :, lanes] = size[z]
        for end, value in enumerate(tables.project(size)):
            size_ends_ref[end, :, lanes] = value
        for k in range(6):
            cells_of = [cot_ref[k, z, :, lanes] for z in range(cells)]
            for end, value in enumerate(tables.project(cells_of)):
                cot_ends_ref[2 * k + end, :, lanes] = value


def forward_kernel(tables, *refs):
    peers = tables.devices - 1
    cells = tables.cells
    v_ref, strain_ref, cot_ref, size_ref, bins_ref = refs[:5]
    far_v_refs = refs[5 : 5 + peers]
    far_size_refs = refs[5 + peers : 5 + 2 * peers]
    leonard_ref, model_ref, duals_ref, message_ref, sums_ref = refs[5 + 2 * peers :]
    cross = square = blame = None
    for lanes in halves(v_ref.shape[-1]):
        v = [[v_ref[a, z, :, lanes] for z in range(cells)] for a in range(3)]
        size = [size_ref[z, :, lanes] for z in range(cells)]
        products = [[v[a][z] * v[b][z] for z in range(cells)] for a, b in INDEX_PAIRS]
        filtered = [tables.inside(field) for field in v + products + [size]]
        for shift in range(1, tables.devices):
            far_v_ref = far_v_refs[shift - 1]
            far = [[far_v_ref[a, z, :, lanes] for z in range(cells)] for a in range(3)]
            far_products = [[far[a][z] * far[b][z] for z in range(cells)] for a, b in INDEX_PAIRS]
            ends = [tables.project(field) for field in far + far_products]
            ends.append([far_size_refs[shift - 1][end, :, lanes] for end in range(2)])
            filtered = [add_lists(near, tables.outside(shift, pair)) for near, pair in zip(filtered, ends)]
        smooth_v = filtered[:3]
        factor = [2.0 * (4.0 * filtered[9][z] - size[z]) for z in range(cells)]
        model, leonard = [], []
        for k, (a, b) in enumerate(INDEX_PAIRS):
            model.append([])
            leonard.append([])
            for z in range(cells):
                coarse = smooth_v[a][z] * smooth_v[b][z]
                big = filtered[3 + k][z] - coarse
                term = products[k][z] - coarse + factor[z] * strain_ref[k, z, :, lanes]
                leonard[k].append(big)
                model[k].append(term)
                leonard_ref[k, z, :, lanes] = big
                model_ref[k, z, :, lanes] = term
                scaled = PAIR_WEIGHTS[k] * term
                parts = (scaled * big, scaled * term, term * cot_ref[k, z, :, lanes])
                if cross is None:
                    cross, square, blame = parts
                else:
                    cross, square, blame = cross + parts[0], square + parts[1], blame + parts[2]
            for end, value in enumerate(tables.project(model[k])):
                message_ref[2 * k + end, :, lanes] = value
        for a in range(3):
            of_cot, of_both, of_model = [], [], []
            for z in range(cells):
                first = second = third = None
                for b in range(3):
                    k = PAIR_OF[a][b]
                    value = cot_ref[k, z, :, lanes] * smooth_v[b][z]
                    if a == b:
                        value = 2.0 * value
                    other = model[k][z] * smooth_v[b][z]
                    both = leonard[k][z] * smooth_v[b][z] + other
                    first = value if first is None else first + value
                    second = both if second is None else second + both
                    third = other if third is None else third + other
                of_cot.append(first)
                of_both.append(2.0 * second)
                of_model.append(2.0 * third)
            for kind, dual in enumerate((of_cot, of_both, of_model)):
                place = 3 * kind + a
                for z in range(cells):
                    duals_ref[place, z, :, lanes] = dual[z]
                for end, value in enumerate(tables.project(dual)):
                    message_ref[12 + 2 * place + end, :, lanes] = value
    rows = cross.shape[0]
    lane = lax.broadcasted_iota(jnp.int32, (rows, LANES), 1)
    mine = bins_ref[...] == lane
    place = lax.broadcasted_iota(jnp.int32, (8, LANES), 0)
    table = jnp.zeros((8, LANES), jnp.float32)
    for index, sums in enumerate((cross, square, blame)):
        per_row = jnp.sum(sums, axis=1, keepdims=True)
        per_bin = jnp.sum(jnp.where(mine, per_row, 0.0), axis=0, keepdims=True)
        table = jnp.where(place == index, per_bin, table)
    sums_ref[...] = table


def local_kernel(tables, v_ref, cot_ref, leonard_ref, model_ref, duals_ref, parts_ref):
    cells = tables.cells
    for lanes in halves(v_ref.shape[-1]):
        v = [[v_ref[a, z, :, lanes] for z in range(cells)] for a in range(3)]
        cot = [[cot_ref[k, z, :, lanes] for z in range(cells)] for k in range(6)]
        model = [[model_ref[k, z, :, lanes] for z in range(cells)] for k in range(6)]
        smooth_cot = [tables.inside(field) for field in cot]
        inner = [
            add_lists(tables.inside(model[k]), [leonard_ref[k, z, :, lanes] for z in range(cells)]) for k in range(6)
        ]
        for a in range(3):
            smooth_duals = [
                tables.inside([duals_ref[3 * kind + a, z, :, lanes] for z in range(cells)]) for kind in range(3)
            ]
            for z in range(cells):
                first = second = third = fourth = None
                for b in range(3):
                    k = PAIR_OF[a][b]
                    twice = 2.0 * v[b][z]
                    single = twice if a == b else v[b][z]
                    terms = (
                        smooth_cot[k][z] * single,
                        cot[k][z] * single,
                        inner[k][z] * twice,
                        model[k][z] * twice,
                    )
                    if first is None:
                        first, second, third, fourth = terms
                    else:
                        first, second = first + terms[0], second + terms[1]
                        third, fourth = third + terms[2], fourth + terms[3]
                parts_ref[a, z, :, lanes] = first - smooth_duals[0][z]
                parts_ref[3 + a, z, :, lanes] = smooth_duals[0][z] - second
                parts_ref[6 + a, z, :, lanes] = third - smooth_duals[1][z]
                parts_ref[9 + a, z, :, lanes] = 2.0 * (smooth_duals[2][z] - fourth)


def finish_kernel(tables, count, *refs):
    peers = tables.devices - 1
    cells = tables.cells
    v_ref, leonard_ref, model_ref, parts_ref, bins_ref = refs[:5]
    sums_refs = refs[5 : 5 + count]
    far_cot_refs = refs[5 + count : 5 + count + peers]
    far_message_refs = refs[5 + count + peers : 5 + count + 2 * peers]
    residual_ref, grad_ref = refs[5 + count + 2 * peers :]
    total = sums_refs[0][...]
    for ref in sums_refs[1:]:
        total = total + ref[...]
    inverse = 1.0 / (total[1:2] + EPSILON)
    rows = v_ref.shape[2]
    lane = lax.broadcasted_iota(jnp.int32, (rows, LANES), 1)
    mine = bins_ref[...] == lane

    def of_rows(per_bin):
        column = jnp.sum(jnp.where(mine, per_bin, 0.0), axis=1, keepdims=True)
        return jnp.broadcast_to(column, (rows, LANES))

    coefficient = of_rows(total[0:1] * inverse)
    pull = of_rows(-(total[2:3] * inverse))
    both = pull * coefficient
    for lanes in halves(v_ref.shape[-1]):
        for k in range(6):
            for z in range(cells):
                residual_ref[k, z, :, lanes] = (
                    leonard_ref[k, z, :, lanes] - coefficient * model_ref[k, z, :, lanes]
                )
        v = [[v_ref[a, z, :, lanes] for z in range(cells)] for a in range(3)]
        from_products = [None] * 6
        from_velocity = [None] * 3
        for shift in range(1, tables.devices):
            cot_ends = far_cot_refs[shift - 1]
            ends = far_message_refs[shift - 1]
            for k in range(6):
                pair = [
                    cot_ends[2 * k + end, :, lanes] + (PAIR_WEIGHTS[k] * pull) * ends[2 * k + end, :, lanes]
                    for end in range(2)
                ]
                far = tables.outside(shift, pair)
                from_products[k] = far if from_products[k] is None else add_lists(from_products[k], far)
            for a in range(3):
                pair = [
                    (coefficient - 1.0) * ends[12 + 2 * a + end, :, lanes]
                    - pull * ends[18 + 2 * a + end, :, lanes]
                    + (2.0 * both) * ends[24 + 2 * a + end, :, lanes]
                    for end in range(2)
                ]
                far = tables.outside(shift, pair)
                from_velocity[a] = far if from_velocity[a] is None else add_lists(from_velocity[a], far)
        for a in range(3):
            for z in range(cells):
                value = (
                    parts_ref[a, z, :, lanes]
                    + coefficient * parts_ref[3 + a, z, :, lanes]
                    + pull * parts_ref[6 + a, z, :, lanes]
                    + both * parts_ref[9 + a, z, :, lanes]
                )
                if peers:
                    value = value + from_velocity[a][z]
                    for b in range(3):
                        term = from_products[PAIR_OF[a][b]][z] * v[b][z]
                        value = value + (2.0 * term if a == b else term)
                grad_ref[a, z, :, lanes] = value


def call(kernel, outs, operations, *operands):
    nbytes = sum(4 * int(np.prod(x.shape)) for x in (*operands, *outs))
    whole = pl.BlockSpec(memory_space=pltpu.VMEM)
    return pl.pallas_call(
        kernel,
        out_shape=outs,
        in_specs=[whole] * len(operands),
        out_specs=[whole] * len(outs),
        compiler_params=pltpu.CompilerParams(vmem_limit_bytes=32 * 1024 * 1024),
        cost_estimate=pl.CostEstimate(flops=operations, bytes_accessed=nbytes, transcendentals=0),
    )(*operands)


def from_ahead(values, shift):
    peers = lax.axis_size("span")
    return lax.ppermute(values, "span", [((i + shift) % peers, i) for i in range(peers)])


def from_place(values, span_shift, stream_shift):
    span, stream = lax.axis_size("span"), lax.axis_size("stream")
    pairs = []
    for i in range(span):
        for j in range(stream):
            source = ((i + span_shift) % span) * stream + (j + stream_shift) % stream
            pairs.append((source, i * stream + j))
    return lax.ppermute(values, ("span", "stream"), pairs)


def on_device(velocity, strain, row_bins, cotangent):
    span, stream = lax.axis_size("span"), lax.axis_size("stream")
    cells, rows, width = velocity.shape[1:]
    tables = Tables(cells, span)
    slab = (rows, width)

    def shaped(*leading):
        return jax.ShapeDtypeStruct(leading + slab, jnp.float32)

    bins = jnp.broadcast_to(row_bins[:, None], (rows, LANES))
    far_v = [from_ahead(velocity, shift) for shift in range(1, span)]
    work = cells * rows * width
    size, size_ends, cot_ends = call(
        functools.partial(prepare_kernel, tables),
        [shaped(cells), shaped(2), shaped(12)],
        60 * work,
        strain,
        cotangent,
    )
    far_size = [from_ahead(size_ends, shift) for shift in range(1, span)]
    far_cot = [from_ahead(cot_ends, shift) for shift in range(1, span)]
    leonard, model, duals, message, sums = call(
        functools.partial(forward_kernel, tables),
        [shaped(6, cells), shaped(6, cells), shaped(9, cells), shaped(30), jax.ShapeDtypeStruct((8, LANES), jnp.float32)],
        400 * work,
        velocity,
        strain,
        cotangent,
        size,
        bins,
        *far_v,
        *far_size,
    )
    most_rows = 2 * rows * stream // NBINS
    reach = min(-(-(most_rows - 1) // rows), (stream - 1) // 2)
    all_sums = [sums]
    for span_shift in range(span):
        for stream_shift in range(-reach, reach + 1):
            if span_shift or stream_shift:
                all_sums.append(from_place(sums, span_shift, stream_shift))
    far_message = [from_ahead(message, shift) for shift in range(1, span)]
    (parts,) = call(
        functools.partial(local_kernel, tables), [shaped(12, cells)], 300 * work, velocity, cotangent, leonard, model, duals
    )
    return tuple(
        call(
            functools.partial(finish_kernel, tables, len(all_sums)),
            [shaped(6, cells), shaped(3, cells)],
            200 * work,
            velocity,
            leonard,
            model,
            parts,
            bins,
            *all_sums,
            *far_cot,
            *far_message,
        )
    )


def solution(mesh):
    fields = P(None, "span", "stream", None)
    return jax.shard_map(
        on_device,
        mesh=mesh,
        in_specs=(fields, fields, P("stream"), fields),
        out_specs=(fields, fields),
        check_vma=False,
    )
```

time: 107 us -> 27 us (0.25)
  blocking collectives: 46.5 us -> 0 us
  between operations: 14.5 us -> 0.67 us
  local copies, waits for them, and re-layouts: 12.8 us -> 1.94 us
  waiting for transfers between devices: 19.6 us -> 12.2 us
  matrix products: 5.4 us -> 0 us
  starting transfers between devices: 5.24 us -> 10.5 us
  other arithmetic: 2.49 us -> 0 us
  Pallas kernels: 0 us -> 1.57 us
    psum x1 -> x0, blocking collectives: 40.5 us -> none  [on_device(): lax.psum((cross_local, square_local, blame_local), ('span', 'stream'))]
    reduce_scatter x1 -> x0, waiting for transfers between devices: 12.3 us -> none  [solve_back(): lax.psum_scatter(jnp.einsum('ae,afyx->efyx', columns, near_bar, precision...]
    all_gather x1 -> x0, blocking collectives: 6 us -> none  [solve_loop(): gathered_piece = lax.all_gather(end_values, 'span', axis=0, tiled=True)]
    dot_general x12 -> x0, matrix products: 5.4 us -> none  [the longest x1 0.83 us: solve_back(): jnp.einsum('ae,afyx->efyx', columns, near_bar, precision=HIGHEST)]
    ppermute x4 -> x9, starting transfers between devices: 5.2 us -> 10.5 us  [the longest x5 5.25 us: from_place(): return lax.ppermute(values, ('span', 'stream'), pairs)]
    ppermute x4 -> x9, waiting for transfers between devices: 7.2 us -> 12.2 us  [the longest x4 6.76 us: from_ahead(): lax.ppermute(values, 'span', [((i + shift) % peers, i) for i in range(pee...]
    scatter-add x2 -> x0, local copies, waits for them, and re-layouts: 4.34 us -> none  [solve_back(): particular_bar = values.at[:, 0].add(end_bar[0]).at[:, -1].add(end_bar[1])]
    unnamed x32 -> x10, local copies, waits for them, and re-layouts: 5.38 us -> 1.87 us
  transfers between devices with their start and end apart: 5 -> 9, of which waited for: 5 -> 4; matrix products, arithmetic and copies ran while one was open for 1% -> 0% of each run, Pallas kernels for 0% -> 1%
where the time goes in v1:
time: 27 us; the launch traced here: 26.8 us
  waiting for transfers between devices  12.2 us (45%)
  starting transfers between devices  10.5 us (39%)
  local copies, waits for them, and re-layouts  1.94 us (7%)
  Pallas kernels  1.57 us (6%)
  between operations  0.67 us (2%)
    ppermute x4, waiting for transfers between devices, from_ahead(): lax.ppermute(values, 'span', [((i + shift) % peers, i) for i in range(pee...  6.76 us
    ppermute x5, waiting for transfers between devices, from_place(): return lax.ppermute(values, ('span', 'stream'), pairs)  5.43 us
    ppermute x5, starting transfers between devices, from_place(): return lax.ppermute(values, ('span', 'stream'), pairs)  5.25 us
    ppermute x4, starting transfers between devices, from_ahead(): lax.ppermute(values, 'span', [((i + shift) % peers, i) for i in range(pee...  5.2 us
    unnamed x10, local copies, waits for them, and re-layouts  1.87 us
    pallas_call x4, Pallas kernels, call(): pl.pallas_call(kernel, out_shape=outs, in_specs=[whole] * len(operands),...  1.57 us
  transfers between devices with their start and end apart: 9, of which 4 were waited for; matrix products, arithmetic and copies ran while one was open for 0% of the time, Pallas kernels for 1%

profile of v1, /device:TPU:0, one launch (start us, length us, event | category | flops | bytes accessed | tf_op | source)
XLA Modules:
  0.0 26.8 jit_solution(4710071493032537300)
XLA Ops:
  0.6 3.0 %collective-permute-start = (f32[3,4,8,256]{3,2,1,0:T(8,128)}, f32[3,4,8,256]{3,2,1,0:T(8,128)S(1)}, u32[]{:S(2)}, u32[]{:S(2)}) collective-permute-start(f32[3,4,8,256]{3,2,1,0:T(8,128)} %refs_0_.3), channel_id=1, source_target_pairs={{16,0},{0,16},{17,1},{1,17},{18,2},{2,18},{19,3},{3,19},{20,4},{4,... | collective-permute-start | bytes 294920 | tf_op jit(solution)/shard_map/ppermute | solution.py:302
  3.7 0.0 copy-start
  3.7 0.9 %copy-done = f32[6,4,8,256]{3,2,1,0:T(8,128)S(1)} copy-done((f32[6,4,8,256]{3,2,1,0:T(8,128)S(1)}, f32[6,4,8,256]{3,2,1,0:T(8,128)}, u32[]{:S(2)}) %copy-start) | copy-done | bytes 196632
  4.6 0.0 copy-start.3
  4.6 0.9 %copy-done.3 = f32[6,4,8,256]{3,2,1,0:T(8,128)S(1)} copy-done((f32[6,4,8,256]{3,2,1,0:T(8,128)S(1)}, f32[6,4,8,256]{3,2,1,0:T(8,128)}, u32[]{:S(2)}) %copy-start.3) | copy-done | bytes 196632
  5.5 0.0 copy-start.2
  5.6 0.0 copy-start.4
  5.6 0.1 collective-permute-start.1
  5.7 3.7 %collective-permute-done.1.refs_6_ = f32[2,8,256]{2,1,0:T(8,128)S(1)} collective-permute-done((f32[2,8,256]{2,1,0:T(8,128)S(1)}, f32[2,8,256]{2,1,0:T(8,128)S(1)}, u32[]{:S(2)}, u32[]{:S(2)}) %collective-permute-start.1) | collective-permute-done | bytes 16416 | tf_op jit(solution)/shard_map/ppermute | solution.py:302
  9.4 0.0 collective-permute-done.refs_5_
  9.4 0.0 copy-done.4
  9.4 0.1 broadcast_in_dim.2.refs_4_
  9.5 0.0 copy-done.2
  9.5 0.0 copy-start.1
  9.5 0.4 %shard_map.60 = (f32[6,4,8,256]{3,2,1,0:T(8,128)S(1)}, f32[6,4,8,256]{3,2,1,0:T(8,128)S(1)}, f32[9,4,8,256]{3,2,1,0:T(8,128)S(1)}, f32[30,8,256]{2,1,0:T(8,128)S(1)}, f32[8,128]{1,0:T(8,128)S(1)}) custom-call(f32[3,4,8,256]{3,2,1,0:T(8,128)S(1)} %copy-done.2, f32[6,4,8,256]{3,2,1,0:T(8,128)S(1)} %copy-done.3, f32[6,4,8,256]{3,2,1,0:T(8,128)S(1)} %copy-done, ...), custom_call_target="tpu_custom_call" | custom-call | flops 3276800 | bytes 1581056 | tf_op jit(solution)/shard_map/pallas_call | solution.py:290
  9.9 0.1 collective-permute-start.8
  9.9 2.0 %collective-permute-start.7 = (f32[12,8,256]{2,1,0:T(8,128)S(1)}, f32[12,8,256]{2,1,0:T(8,128)S(1)}, u32[]{:S(2)}, u32[]{:S(2)}) collective-permute-start(f32[12,8,256]{2,1,0:T(8,128)S(1)} %get-tuple-element.16), channel_id=1, source_target_pairs={{16,0},{0,16},{17,1},{1,17},{18,2},{2,18},{19,3},{3,19},{20,4},{4,... | collective-permute-start | bytes 294920 | tf_op jit(solution)/shard_map/ppermute | solution.py:302
  11.9 2.4 %collective-permute-start.6 = (f32[8,128]{1,0:T(8,128)S(1)}, f32[8,128]{1,0:T(8,128)S(1)}, u32[]{:S(2)}, u32[]{:S(2)}) collective-permute-start(f32[8,128]{1,0:T(8,128)S(1)} %get-tuple-element.15.refs_5_), channel_id=1, source_target_pairs={{17,0},{18,1},{19,2},{20,3},{21,4},{22,5},{23,6},{24,7},{25,8},{26... | collective-permute-start | bytes 12296 | tf_op jit(solution)/shard_map/ppermute | solution.py:312
  14.3 1.1 %collective-permute-start.5 = (f32[8,128]{1,0:T(8,128)S(1)}, f32[8,128]{1,0:T(8,128)S(1)}, u32[]{:S(2)}, u32[]{:S(2)}) collective-permute-start(f32[8,128]{1,0:T(8,128)S(1)} %get-tuple-element.15.refs_5_), channel_id=1, source_target_pairs={{16,0},{17,1},{18,2},{19,3},{20,4},{21,5},{22,6},{23,7},{24,8},{25... | collective-permute-start | bytes 12296 | tf_op jit(solution)/shard_map/ppermute | solution.py:312
  15.4 0.0 collective-permute-start.4
  15.4 3.0 %collective-permute-done.7.refs_11_ = f32[12,8,256]{2,1,0:T(8,128)S(1)} collective-permute-done((f32[12,8,256]{2,1,0:T(8,128)S(1)}, f32[12,8,256]{2,1,0:T(8,128)S(1)}, u32[]{:S(2)}, u32[]{:S(2)}) %collective-permute-start.7) | collective-permute-done | bytes 98336 | tf_op jit(solution)/shard_map/ppermute | solution.py:302
  18.4 1.8 %collective-permute-start.3 = (f32[8,128]{1,0:T(8,128)S(1)}, f32[8,128]{1,0:T(8,128)S(1)}, u32[]{:S(2)}, u32[]{:S(2)}) collective-permute-start(f32[8,128]{1,0:T(8,128)S(1)} %get-tuple-element.15.refs_5_), channel_id=1, source_target_pairs={{1,0},{2,1},{3,2},{4,3},{5,4},{6,5},{7,6},{8,7},{9,8},{10,9},{11,1... | collective-permute-start | bytes 12296 | tf_op jit(solution)/shard_map/ppermute | solution.py:312
  20.2 0.0 collective-permute-done.6.refs_10_
  20.2 0.0 collective-permute-start.2
  20.2 0.0 copy-done.1
  20.2 0.3 %shard_map.61.refs_3_ = f32[12,4,8,256]{3,2,1,0:T(8,128)S(1)} custom-call(f32[3,4,8,256]{3,2,1,0:T(8,128)S(1)} %copy-done.2, f32[6,4,8,256]{3,2,1,0:T(8,128)S(1)} %copy-done.1, f32[6,4,8,256]{3,2,1,0:T(8,128)S(1)} %get-tuple-element.12.leonard_ref.refs_1_, f32[6,4,8,256]{3,2,1,0:T(8,128)S(1)} %get-tuple-element.13.model_ref.refs_2_, ...), custom_call_target="tpu_custom_call" | custom-call | flops 2457600 | bytes 1376256 | tf_op jit(solution)/shard_map/pallas_call | solution.py:290
  20.5 0.0 collective-permute-done.5.refs_9_
  20.5 1.5 %collective-permute-done.4.refs_8_ = f32[8,128]{1,0:T(8,128)S(1)} collective-permute-done((f32[8,128]{1,0:T(8,128)S(1)}, f32[8,128]{1,0:T(8,128)S(1)}, u32[]{:S(2)}, u32[]{:S(2)}) %collective-permute-start.4) | collective-permute-done | bytes 4128 | tf_op jit(solution)/shard_map/ppermute | solution.py:312
  22.0 0.0 collective-permute-done.3.refs_7_
  22.0 3.9 %collective-permute-done.2.refs_6_ = f32[8,128]{1,0:T(8,128)S(1)} collective-permute-done((f32[8,128]{1,0:T(8,128)S(1)}, f32[8,128]{1,0:T(8,128)S(1)}, u32[]{:S(2)}, u32[]{:S(2)}) %collective-permute-start.2) | collective-permute-done | bytes 4128 | tf_op jit(solution)/shard_map/ppermute | solution.py:312
  26.0 0.0 collective-permute-done.8.refs_12_
  26.0 0.9 %shard_map.62 = (f32[6,4,8,256]{3,2,1,0:T(8,128)}, f32[3,4,8,256]{3,2,1,0:T(8,128)}) custom-call(f32[3,4,8,256]{3,2,1,0:T(8,128)S(1)} %copy-done.2, f32[6,4,8,256]{3,2,1,0:T(8,128)S(1)} %get-tuple-element.12.leonard_ref.refs_1_, f32[6,4,8,256]{3,2,1,0:T(8,128)S(1)} %get-tuple-element.13.model_ref.refs_2_, f32[12,4,8,256]{3,2,1,0:T(8,128)S(1)} %shard_map.61.refs_3_, ...), custom_call_target="tpu_custom_call" | custom-call | flops 1638400 | bytes 1552384 | tf_op jit(solution)/shard_map/pallas_call | solution.py:290
  (1 shorter events, 0.0 us)
Async XLA Ops:
  0.6 8.8 %collective-permute-start = (f32[3,4,8,256]{3,2,1,0:T(8,128)}, f32[3,4,8,256]{3,2,1,0:T(8,128)S(1)}, u32[]{:S(2)}, u32[]{:S(2)}) collective-permute-start(f32[3,4,8,256]{3,2,1,0:T(8,128)} %refs_0_.3), channel_id=1, source_target_pairs={{16,0},{0,16},{17,1},{1,17},{18,2},{2,18},{19,3},{3,19},{20,4},{4,... | collective-permute-start | bytes 294920 | tf_op jit(solution)/shard_map/ppermute | solution.py:302
  3.7 0.9 %copy-start = (f32[6,4,8,256]{3,2,1,0:T(8,128)S(1)}, f32[6,4,8,256]{3,2,1,0:T(8,128)}, u32[]{:S(2)}) copy-start(f32[6,4,8,256]{3,2,1,0:T(8,128)} %cot_ref.3) | copy-start | bytes 589828
  4.6 0.9 %copy-start.3 = (f32[6,4,8,256]{3,2,1,0:T(8,128)S(1)}, f32[6,4,8,256]{3,2,1,0:T(8,128)}, u32[]{:S(2)}) copy-start(f32[6,4,8,256]{3,2,1,0:T(8,128)} %refs_1_.1) | copy-start | bytes 589828
  5.5 3.9 %copy-start.2 = (f32[3,4,8,256]{3,2,1,0:T(8,128)S(1)}, f32[3,4,8,256]{3,2,1,0:T(8,128)}, u32[]{:S(2)}) copy-start(f32[3,4,8,256]{3,2,1,0:T(8,128)} %refs_0_.3) | copy-start | bytes 294916
  5.6 3.8 %copy-start.4 = (s32[8]{0:T(128)S(1)}, s32[8]{0:T(128)}, u32[]{:S(2)}) copy-start(s32[8]{0:T(128)} %param.6) | copy-start | bytes 100
  5.6 3.8 %collective-permute-start.1 = (f32[2,8,256]{2,1,0:T(8,128)S(1)}, f32[2,8,256]{2,1,0:T(8,128)S(1)}, u32[]{:S(2)}, u32[]{:S(2)}) collective-permute-start(f32[2,8,256]{2,1,0:T(8,128)S(1)} %get-tuple-element.11), channel_id=1, source_target_pairs={{16,0},{0,16},{17,1},{1,17},{18,2},{2,18},{19,3},{3,19},{20,4},{4,... | collective-permute-start | bytes 49160 | tf_op jit(solution)/shard_map/ppermute | solution.py:302
  9.5 10.8 %copy-start.1 = (f32[6,4,8,256]{3,2,1,0:T(8,128)S(1)}, f32[6,4,8,256]{3,2,1,0:T(8,128)}, u32[]{:S(2)}) copy-start(f32[6,4,8,256]{3,2,1,0:T(8,128)} %cot_ref.3) | copy-start | bytes 589828
  9.9 16.1 %collective-permute-start.8 = (f32[30,8,256]{2,1,0:T(8,128)S(1)}, f32[30,8,256]{2,1,0:T(8,128)S(1)}, u32[]{:S(2)}, u32[]{:S(2)}) collective-permute-start(f32[30,8,256]{2,1,0:T(8,128)S(1)} %get-tuple-element.17), channel_id=1, source_target_pairs={{16,0},{0,16},{17,1},{1,17},{18,2},{2,18},{19,3},{3,19},{20,4},{4,... | collective-permute-start | bytes 737288 | tf_op jit(solution)/shard_map/ppermute | solution.py:302
  9.9 8.5 %collective-permute-start.7 = (f32[12,8,256]{2,1,0:T(8,128)S(1)}, f32[12,8,256]{2,1,0:T(8,128)S(1)}, u32[]{:S(2)}, u32[]{:S(2)}) collective-permute-start(f32[12,8,256]{2,1,0:T(8,128)S(1)} %get-tuple-element.16), channel_id=1, source_target_pairs={{16,0},{0,16},{17,1},{1,17},{18,2},{2,18},{19,3},{3,19},{20,4},{4,... | collective-permute-start | bytes 294920 | tf_op jit(solution)/shard_map/ppermute | solution.py:302
  11.9 8.3 %collective-permute-start.6 = (f32[8,128]{1,0:T(8,128)S(1)}, f32[8,128]{1,0:T(8,128)S(1)}, u32[]{:S(2)}, u32[]{:S(2)}) collective-permute-start(f32[8,128]{1,0:T(8,128)S(1)} %get-tuple-element.15.refs_5_), channel_id=1, source_target_pairs={{17,0},{18,1},{19,2},{20,3},{21,4},{22,5},{23,6},{24,7},{25,8},{26... | collective-permute-start | bytes 12296 | tf_op jit(solution)/shard_map/ppermute | solution.py:312
  14.3 6.2 %collective-permute-start.5 = (f32[8,128]{1,0:T(8,128)S(1)}, f32[8,128]{1,0:T(8,128)S(1)}, u32[]{:S(2)}, u32[]{:S(2)}) collective-permute-start(f32[8,128]{1,0:T(8,128)S(1)} %get-tuple-element.15.refs_5_), channel_id=1, source_target_pairs={{16,0},{17,1},{18,2},{19,3},{20,4},{21,5},{22,6},{23,7},{24,8},{25... | collective-permute-start | bytes 12296 | tf_op jit(solution)/shard_map/ppermute | solution.py:312
  15.4 6.6 %collective-permute-start.4 = (f32[8,128]{1,0:T(8,128)S(1)}, f32[8,128]{1,0:T(8,128)S(1)}, u32[]{:S(2)}, u32[]{:S(2)}) collective-permute-start(f32[8,128]{1,0:T(8,128)S(1)} %get-tuple-element.15.refs_5_), channel_id=1, source_target_pairs={{31,0},{16,1},{17,2},{18,3},{19,4},{20,5},{21,6},{22,7},{23,8},{24... | collective-permute-start | bytes 12296 | tf_op jit(solution)/shard_map/ppermute | solution.py:312
  18.4 3.6 %collective-permute-start.3 = (f32[8,128]{1,0:T(8,128)S(1)}, f32[8,128]{1,0:T(8,128)S(1)}, u32[]{:S(2)}, u32[]{:S(2)}) collective-permute-start(f32[8,128]{1,0:T(8,128)S(1)} %get-tuple-element.15.refs_5_), channel_id=1, source_target_pairs={{1,0},{2,1},{3,2},{4,3},{5,4},{6,5},{7,6},{8,7},{9,8},{10,9},{11,1... | collective-permute-start | bytes 12296 | tf_op jit(solution)/shard_map/ppermute | solution.py:312
  20.2 5.7 %collective-permute-start.2 = (f32[8,128]{1,0:T(8,128)S(1)}, f32[8,128]{1,0:T(8,128)S(1)}, u32[]{:S(2)}, u32[]{:S(2)}) collective-permute-start(f32[8,128]{1,0:T(8,128)S(1)} %get-tuple-element.15.refs_5_), channel_id=1, source_target_pairs={{15,0},{0,1},{1,2},{2,3},{3,4},{4,5},{5,6},{6,7},{7,8},{8,9},{9,10... | collective-permute-start | bytes 12296 | tf_op jit(solution)/shard_map/ppermute | solution.py:312

commit v2 on v1

v2 whole, which is shorter than its diff:
```python
import functools

import jax
import jax.numpy as jnp
import numpy as np
from jax import lax
from jax.experimental import pallas as pl
from jax.experimental.pallas import tpu as pltpu
from jax.sharding import PartitionSpec as P

NBINS = 64
FILTER_ALPHA = 0.45
CENTER_WEIGHT = 0.95
SIDE_WEIGHT = 0.475
STRAIN_FLOOR = 0.25
EPSILON = 1e-06
INDEX_PAIRS = ((0, 0), (0, 1), (0, 2), (1, 1), (1, 2), (2, 2))
PAIR_WEIGHTS = (1.0, 2.0, 2.0, 1.0, 2.0, 1.0)
PAIR_OF = ((0, 1, 2), (1, 3, 4), (2, 4, 5))
LANES = 128


def filter_row(extent):
    eye = np.eye(extent)
    ring = np.roll(eye, 1, axis=1) + np.roll(eye, -1, axis=1)
    system = eye + FILTER_ALPHA * ring
    side = CENTER_WEIGHT * eye + SIDE_WEIGHT * ring
    return np.linalg.solve(system, side)[0]


def end_weights(cells):
    weights = np.zeros((2, cells))
    weights[0, 0] = 1.0
    weights[1, cells - 1] = 1.0
    inner = cells - 2
    if inner > 0:
        system = np.eye(inner) + FILTER_ALPHA * (np.eye(inner, k=1) + np.eye(inner, k=-1))
        right = np.zeros((inner, 2))
        right[0, 0] = -FILTER_ALPHA
        right[inner - 1, 1] = -FILTER_ALPHA
        weights[:, 1:-1] = np.linalg.solve(system, right).T
    return weights


class Tables:
    def __init__(self, cells, devices):
        row = filter_row(cells * devices)
        extent = cells * devices
        self.cells = cells
        self.devices = devices
        self.own = [[float(row[(z - w) % extent]) for w in range(cells)] for z in range(cells)]
        self.ends = [[float(x) for x in line] for line in end_weights(cells)]
        self.couple = [
            [[float(row[(z - shift * cells - w) % extent]) for w in (0, cells - 1)] for z in range(cells)]
            for shift in range(devices)
        ]

    def project(self, values):
        return [weighted(line, values) for line in self.ends]

    def inside(self, values):
        return [weighted(line, values) for line in self.own]

    def outside(self, shift, ends):
        return [weighted(line, ends) for line in self.couple[shift]]


def weighted(weights, values):
    total = None
    for weight, value in zip(weights, values):
        if weight == 0.0:
            continue
        term = value if weight == 1.0 else value * weight
        total = term if total is None else total + term
    return total


def add_lists(left, right):
    return [x + y for x, y in zip(left, right)]


def halves(width):
    return [pl.ds(start, LANES) for start in range(0, width, LANES)]


def sum_up(terms):
    total = terms[0]
    for term in terms[1:]:
        total = total + term
    return total


def prepare_kernel(tables, strain_ref, size_ref, size_ends_ref):
    cells = tables.cells
    for lanes in halves(strain_ref.shape[-1]):
        size = []
        for z in range(cells):
            values = [strain_ref[k, z, :, lanes] for k in range(6)]
            total = sum_up([weight * (value * value) for weight, value in zip(PAIR_WEIGHTS, values)])
            size.append(jnp.sqrt(jnp.maximum(2.0 * total, STRAIN_FLOOR)))
            size_ref[z, :, lanes] = size[z]
        for end, value in enumerate(tables.project(size)):
            size_ends_ref[end, :, lanes] = value


def products_of(v):
    return [[x * y for x, y in zip(v[a], v[b])] for a, b in INDEX_PAIRS]


def filtered_block(tables, place, fields, ends):
    filtered = [tables.inside(field) for field in fields]
    for other in range(tables.devices):
        if other != place:
            shift = (other - place) % tables.devices
            filtered = [add_lists(near, tables.outside(shift, far)) for near, far in zip(filtered, ends[other])]
    return filtered


def plain_dual(tensor, vector, a, cells):
    return [sum_up([tensor[PAIR_OF[a][b]][z] * vector[b][z] for b in range(3)]) for z in range(cells)]


def weighted_dual(tensor, vector, a, cells):
    plain = plain_dual(tensor, vector, a, cells)
    return [plain[z] + tensor[PAIR_OF[a][a]][z] * vector[a][z] for z in range(cells)]


def forward_kernel(tables, *refs):
    peers = tables.devices - 1
    cells = tables.cells
    v_ref, strain_ref, cot_ref, size_ref, bins_ref = refs[:5]
    far_v_refs = refs[5 : 5 + peers]
    far_size_refs = refs[5 + peers : 5 + 2 * peers]
    smooth_ref, leonard_ref, model_ref, dual_ref, message_ref, sums_ref = refs[5 + 2 * peers :]
    cross, square, blame = [], [], []
    for lanes in halves(v_ref.shape[-1]):
        v = [[v_ref[a, z, :, lanes] for z in range(cells)] for a in range(3)]
        size = [size_ref[z, :, lanes] for z in range(cells)]
        products = products_of(v)
        ends = [None]
        for far_v_ref, far_size_ref in zip(far_v_refs, far_size_refs):
            far = [[far_v_ref[a, z, :, lanes] for z in range(cells)] for a in range(3)]
            ends.append([tables.project(field) for field in far + products_of(far)])
            ends[-1].append([far_size_ref[end, :, lanes] for end in range(2)])
        filtered = filtered_block(tables, 0, v + products + [size], ends)
        smooth_v = filtered[:3]
        factor = [2.0 * (4.0 * filtered[9][z] - size[z]) for z in range(cells)]
        model = []
        for k, (a, b) in enumerate(INDEX_PAIRS):
            model.append([])
            for z in range(cells):
                coarse = smooth_v[a][z] * smooth_v[b][z]
                leonard = filtered[3 + k][z] - coarse
                term = products[k][z] - coarse + factor[z] * strain_ref[k, z, :, lanes]
                model[k].append(term)
                leonard_ref[k, z, :, lanes] = leonard
                model_ref[k, z, :, lanes] = term
                scaled = PAIR_WEIGHTS[k] * term
                cross.append(scaled * leonard)
                square.append(scaled * term)
                blame.append(term * cot_ref[k, z, :, lanes])
            cross, square, blame = [sum_up(cross)], [sum_up(square)], [sum_up(blame)]
            for end, value in enumerate(tables.project(model[k])):
                message_ref[2 * k + end, :, lanes] = value
        for a in range(3):
            dual = [2.0 * x for x in plain_dual(model, smooth_v, a, cells)]
            for z in range(cells):
                smooth_ref[a, z, :, lanes] = smooth_v[a][z]
                dual_ref[a, z, :, lanes] = dual[z]
            for end, value in enumerate(tables.project(dual)):
                message_ref[12 + 2 * a + end, :, lanes] = value
    lane = lax.broadcasted_iota(jnp.int32, bins_ref.shape, 1)
    mine = bins_ref[...] == lane
    place = lax.broadcasted_iota(jnp.int32, (8, LANES), 0)
    table = jnp.zeros((8, LANES), jnp.float32)
    for index, sums in enumerate((cross, square, blame)):
        per_row = jnp.sum(sums[0], axis=1, keepdims=True)
        per_bin = jnp.sum(jnp.where(mine, per_row, 0.0), axis=0, keepdims=True)
        table = jnp.where(place == index, per_bin, table)
    sums_ref[...] = table
    message_ref[18, 0:8, 0:LANES] = table


def local_kernel(tables, *refs):
    peers = tables.devices - 1
    cells = tables.cells
    v_ref, cot_ref, smooth_ref, leonard_ref, model_ref, dual_ref = refs[:6]
    far_v_refs = refs[6 : 6 + peers]
    far_cot_refs = refs[6 + peers : 6 + 2 * peers]
    parts_ref = refs[-1]
    for lanes in halves(v_ref.shape[-1]):

        def load(ref, count):
            return [[ref[f, z, :, lanes] for z in range(cells)] for f in range(count)]

        fields, ends = [], []
        for ref in (v_ref, *far_v_refs):
            v = load(ref, 3)
            fields.append(v + products_of(v))
            ends.append([tables.project(field) for field in fields[-1]])
        v = fields[0][:3]
        cot, model, leonard, smooth_v = load(cot_ref, 6), load(model_ref, 6), load(leonard_ref, 6), load(smooth_ref, 3)
        smooth_cot = [tables.inside(field) for field in cot]
        duals = [weighted_dual(cot, smooth_v, a, cells) for a in range(3)]
        others = [plain_dual(leonard, smooth_v, a, cells) for a in range(3)]
        smooth_duals = [tables.inside(field) for field in duals]
        smooth_others = [tables.inside(field) for field in others]
        for place in range(1, tables.devices):
            far_cot = load(far_cot_refs[place - 1], 6)
            filtered = filtered_block(tables, place, fields[place], ends)
            far_smooth = filtered[:3]
            far_leonard = [
                [filtered[3 + k][z] - far_smooth[a][z] * far_smooth[b][z] for z in range(cells)]
                for k, (a, b) in enumerate(INDEX_PAIRS)
            ]
            for k in range(6):
                far = tables.outside(place, tables.project(far_cot[k]))
                smooth_cot[k] = add_lists(smooth_cot[k], far)
            for a in range(3):
                far = tables.outside(place, tables.project(weighted_dual(far_cot, far_smooth, a, cells)))
                smooth_duals[a] = add_lists(smooth_duals[a], far)
                far = tables.outside(place, tables.project(plain_dual(far_leonard, far_smooth, a, cells)))
                smooth_others[a] = add_lists(smooth_others[a], far)
        inner = [add_lists(tables.inside(model[k]), leonard[k]) for k in range(6)]
        for a in range(3):
            first = weighted_dual(smooth_cot, v, a, cells)
            second = weighted_dual(cot, v, a, cells)
            dual = tables.inside([dual_ref[a, z, :, lanes] for z in range(cells)])
            third = plain_dual(inner, v, a, cells)
            fourth = plain_dual(model, v, a, cells)
            for z in range(cells):
                parts_ref[a, z, :, lanes] = first[z] - smooth_duals[a][z]
                parts_ref[3 + a, z, :, lanes] = smooth_duals[a][z] - second[z]
                parts_ref[6 + a, z, :, lanes] = 2.0 * (third[z] - smooth_others[a][z]) - dual[z]
                parts_ref[9 + a, z, :, lanes] = 2.0 * dual[z] - 4.0 * fourth[z]


def finish_kernel(tables, count, *refs):
    peers = tables.devices - 1
    cells = tables.cells
    v_ref, leonard_ref, model_ref, parts_ref, bins_ref = refs[:5]
    sums_refs = refs[5 : 5 + count]
    far_message_refs = refs[5 + count : 5 + count + peers]
    residual_hbm, grad_hbm, residual_ref, grad_ref, left = refs[5 + count + peers :]
    total = sum_up([ref[...] for ref in sums_refs] + [ref[18, 0:8, 0:LANES] for ref in far_message_refs])
    inverse = 1.0 / (total[1:2] + EPSILON)
    rows = v_ref.shape[2]
    lane = lax.broadcasted_iota(jnp.int32, bins_ref.shape, 1)
    mine = bins_ref[...] == lane

    def of_rows(per_bin):
        column = jnp.sum(jnp.where(mine, per_bin, 0.0), axis=1, keepdims=True)
        return jnp.broadcast_to(column, (rows, LANES))

    coefficient = of_rows(total[0:1] * inverse)
    pull = of_rows(-(total[2:3] * inverse))
    copies = []
    for k in range(6):
        for lanes in halves(v_ref.shape[-1]):
            for z in range(cells):
                residual_ref[k, z, :, lanes] = (
                    leonard_ref[k, z, :, lanes] - coefficient * model_ref[k, z, :, lanes]
                )
        copies.append(pltpu.make_async_copy(residual_ref.at[k], residual_hbm.at[k], left.at[k]))
        copies[k].start()
    for lanes in halves(v_ref.shape[-1]):
        v = [[v_ref[a, z, :, lanes] for z in range(cells)] for a in range(3)]
        from_model = [[] for _ in range(6)]
        from_dual = [[] for _ in range(3)]
        for place, ends in enumerate(far_message_refs, start=1):
            for k in range(6):
                from_model[k].append(tables.outside(place, [2.0 * ends[2 * k + end, :, lanes] for end in range(2)]))
            for a in range(3):
                pair = [(2.0 * coefficient - 1.0) * ends[12 + 2 * a + end, :, lanes] for end in range(2)]
                from_dual[a].append(tables.outside(place, pair))
        from_model = [functools.reduce(add_lists, lists) if lists else None for lists in from_model]
        from_dual = [functools.reduce(add_lists, lists) if lists else None for lists in from_dual]
        for a in range(3):
            for z in range(cells):
                pulled = parts_ref[6 + a, z, :, lanes] + coefficient * parts_ref[9 + a, z, :, lanes]
                if peers:
                    terms = [from_model[PAIR_OF[a][b]][z] * v[b][z] for b in range(3)]
                    pulled = pulled + from_dual[a][z] + sum_up(terms)
                grad_ref[a, z, :, lanes] = (
                    parts_ref[a, z, :, lanes] + coefficient * parts_ref[3 + a, z, :, lanes] + pull * pulled
                )
    for a in range(3):
        copies.append(pltpu.make_async_copy(grad_ref.at[a], grad_hbm.at[a], left.at[6 + a]))
        copies[6 + a].start()
    for copy in copies:
        copy.wait()


WHOLE = pl.BlockSpec(memory_space=pltpu.VMEM)
REMAIN = pl.BlockSpec(memory_space=pltpu.HBM)


def call(kernel, outs, operations, *operands, in_specs=None, out_specs=None, scratch=()):
    nbytes = sum(4 * int(np.prod(x.shape)) for x in (*operands, *outs))
    return pl.pallas_call(
        kernel,
        out_shape=outs,
        in_specs=in_specs or [WHOLE] * len(operands),
        out_specs=out_specs or [WHOLE] * len(outs),
        scratch_shapes=list(scratch),
        compiler_params=pltpu.CompilerParams(vmem_limit_bytes=32 * 1024 * 1024),
        cost_estimate=pl.CostEstimate(flops=operations, bytes_accessed=nbytes, transcendentals=0),
    )(*operands)


def from_ahead(values, shift):
    peers = lax.axis_size("span")
    return lax.ppermute(values, "span", [((i + shift) % peers, i) for i in range(peers)])


def swapped(values, span_shift, distance, parity):
    span, stream = lax.axis_size("span"), lax.axis_size("stream")
    pairs = []
    for i in range(span):
        row = ((i + span_shift) % span) * stream
        for j in range(stream - distance):
            if (j // distance) % 2 == parity:
                pairs.append((row + j, i * stream + j + distance))
                pairs.append((row + j + distance, i * stream + j))
    return lax.ppermute(values, ("span", "stream"), pairs)


def on_device(velocity, strain, row_bins, cotangent):
    span, stream = lax.axis_size("span"), lax.axis_size("stream")
    cells, rows, width = velocity.shape[1:]
    tables = Tables(cells, span)
    slab = (rows, width)

    def shaped(*leading):
        return jax.ShapeDtypeStruct(leading + slab, jnp.float32)

    bins = jnp.broadcast_to(row_bins[:, None], (rows, LANES))
    far_v = [from_ahead(velocity, shift) for shift in range(1, span)]
    far_cot = [from_ahead(cotangent, shift) for shift in range(1, span)]
    work = cells * rows * width
    size, size_ends = call(functools.partial(prepare_kernel, tables), [shaped(cells), shaped(2)], 40 * work, strain)
    far_size = [from_ahead(size_ends, shift) for shift in range(1, span)]
    smooth, leonard, model, dual, message, sums = call(
        functools.partial(forward_kernel, tables),
        [
            shaped(3, cells),
            shaped(6, cells),
            shaped(6, cells),
            shaped(3, cells),
            shaped(19),
            jax.ShapeDtypeStruct((8, LANES), jnp.float32),
        ],
        300 * work,
        velocity,
        strain,
        cotangent,
        size,
        bins,
        *far_v,
        *far_size,
    )
    far_message = [from_ahead(message, shift) for shift in range(1, span)]
    most_rows = 2 * rows * stream // NBINS
    reach = min(-(-(most_rows - 1) // rows), stream - 1)
    all_sums = [sums]
    for span_shift in range(span):
        for distance in range(1, reach + 1):
            for parity in range(2):
                all_sums.append(swapped(sums, span_shift, distance, parity))
    (parts,) = call(
        functools.partial(local_kernel, tables),
        [shaped(12, cells)],
        500 * work,
        velocity,
        cotangent,
        smooth,
        leonard,
        model,
        dual,
        *far_v,
        *far_cot,
    )
    outs = [shaped(6, cells), shaped(3, cells)]
    return tuple(
        call(
            functools.partial(finish_kernel, tables, len(all_sums)),
            outs,
            200 * work,
            velocity,
            leonard,
            model,
            parts,
            bins,
            *all_sums,
            *far_message,
            out_specs=[REMAIN] * 2,
            scratch=[pltpu.VMEM(x.shape, x.dtype) for x in outs] + [pltpu.SemaphoreType.DMA((9,))],
        )
    )


def solution(mesh):
    fields = P(None, "span", "stream", None)
    return jax.shard_map(
        on_device,
        mesh=mesh,
        in_specs=(fields, fields, P("stream"), fields),
        out_specs=(fields, fields),
        check_vma=False,
    )
```

time: 27 us -> 24.6 us (0.911)
  waiting for transfers between devices: 12.2 us -> 4.74 us
  starting transfers between devices: 10.5 us -> 15.2 us
    ppermute x5 -> x4, waiting for transfers between devices: 5.43 us -> 0.24 us  [swapped(): return lax.ppermute(values, ('span', 'stream'), pairs)]
    ppermute x5 -> x4, starting transfers between devices: 5.25 us -> 8.26 us  [swapped(): return lax.ppermute(values, ('span', 'stream'), pairs)]
    ppermute x4, waiting for transfers between devices: 6.76 us -> 4.51 us  [from_ahead(): lax.ppermute(values, 'span', [((i + shift) % peers, i) for i in range(pee...]
    ppermute x4, starting transfers between devices: 5.2 us -> 6.91 us  [from_ahead(): lax.ppermute(values, 'span', [((i + shift) % peers, i) for i in range(pee...]
  transfers between devices with their start and end apart: 9 -> 8, of which waited for: 4 -> 2; matrix products, arithmetic and copies ran while one was open for 0% -> 0% of each run, Pallas kernels for 1% -> 4%
where the time goes in v2:
time: 24.6 us; the launch traced here: 24.4 us
  starting transfers between devices  15.2 us (62%)
  waiting for transfers between devices  4.74 us (19%)
  local copies, waits for them, and re-layouts  1.94 us (8%)
  Pallas kernels  1.82 us (7%)
  between operations  0.71 us (3%)
    ppermute x4, starting transfers between devices, swapped(): return lax.ppermute(values, ('span', 'stream'), pairs)  8.26 us
    ppermute x4, starting transfers between devices, from_ahead(): lax.ppermute(values, 'span', [((i + shift) % peers, i) for i in range(pee...  6.91 us
    ppermute x4, waiting for transfers between devices, from_ahead(): lax.ppermute(values, 'span', [((i + shift) % peers, i) for i in range(pee...  4.51 us
    unnamed x10, local copies, waits for them, and re-layouts  1.87 us
    pallas_call x4, Pallas kernels, call(): pl.pallas_call(kernel, out_shape=outs, in_specs=in_specs or [WHOLE] * len...  1.82 us
  transfers between devices with their start and end apart: 8, of which 2 were waited for; matrix products, arithmetic and copies ran while one was open for 0% of the time, Pallas kernels for 4%

profile of v2, /device:TPU:0, one launch (start us, length us, event | category | flops | bytes accessed | tf_op | source)
XLA Modules:
  0.0 24.4 jit_solution(10759112512707553204)
XLA Ops:
  0.6 0.0 copy-start
  0.6 3.0 %collective-permute-start = (f32[3,4,8,256]{3,2,1,0:T(8,128)}, f32[3,4,8,256]{3,2,1,0:T(8,128)S(1)}, u32[]{:S(2)}, u32[]{:S(2)}) collective-permute-start(f32[3,4,8,256]{3,2,1,0:T(8,128)} %refs_0_.5), channel_id=1, source_target_pairs={{16,0},{0,16},{17,1},{1,17},{18,2},{2,18},{19,3},{3,19},{20,4},{4,... | collective-permute-start | bytes 294920 | tf_op jit(solution)/shard_map/ppermute | solution.py:313
  3.7 0.1 collective-permute-start.2
  3.8 0.0 copy-start.3
  3.8 0.9 %copy-done.3 = f32[6,4,8,256]{3,2,1,0:T(8,128)S(1)} copy-done((f32[6,4,8,256]{3,2,1,0:T(8,128)S(1)}, f32[6,4,8,256]{3,2,1,0:T(8,128)}, u32[]{:S(2)}) %copy-start.3) | copy-done | bytes 196632
  4.7 0.0 copy-start.4
  4.7 2.0 %collective-permute-start.1 = (f32[2,8,256]{2,1,0:T(8,128)S(1)}, f32[2,8,256]{2,1,0:T(8,128)S(1)}, u32[]{:S(2)}, u32[]{:S(2)}) collective-permute-start(f32[2,8,256]{2,1,0:T(8,128)S(1)} %get-tuple-element.11), channel_id=1, source_target_pairs={{16,0},{0,16},{17,1},{1,17},{18,2},{2,18},{19,3},{3,19},{20,4},{4,... | collective-permute-start | bytes 49160 | tf_op jit(solution)/shard_map/ppermute | solution.py:313
  6.7 4.5 %collective-permute-done.1.refs_6_ = f32[2,8,256]{2,1,0:T(8,128)S(1)} collective-permute-done((f32[2,8,256]{2,1,0:T(8,128)S(1)}, f32[2,8,256]{2,1,0:T(8,128)S(1)}, u32[]{:S(2)}, u32[]{:S(2)}) %collective-permute-start.1) | collective-permute-done | bytes 16416 | tf_op jit(solution)/shard_map/ppermute | solution.py:313
  11.2 0.0 collective-permute-done.refs_5_.refs_6_
  11.2 0.0 copy-done.4
  11.2 0.1 broadcast_in_dim.2.refs_4_
  11.3 0.0 copy-done
  11.3 0.0 copy-start.1
  11.3 0.9 %copy-done.1 = f32[6,4,8,256]{3,2,1,0:T(8,128)S(1)} copy-done((f32[6,4,8,256]{3,2,1,0:T(8,128)S(1)}, f32[6,4,8,256]{3,2,1,0:T(8,128)}, u32[]{:S(2)}) %copy-start.1) | copy-done | bytes 196632
  12.2 0.0 copy-start.2
  12.3 0.3 %shard_map.60 = (f32[3,4,8,256]{3,2,1,0:T(8,128)S(1)}, f32[6,4,8,256]{3,2,1,0:T(8,128)S(1)}, f32[6,4,8,256]{3,2,1,0:T(8,128)S(1)}, f32[3,4,8,256]{3,2,1,0:T(8,12...) custom-call(f32[3,4,8,256]{3,2,1,0:T(8,128)S(1)} %copy-done, f32[6,4,8,256]{3,2,1,0:T(8,128)S(1)} %copy-done.3, ...), custom_call_target="tpu_custom_call" | custom-call | flops 2457600 | bytes 1392640 | tf_op jit(solution)/shard_map/pallas_call | solution.py:300
  12.6 1.8 %collective-permute-start.7 = (f32[19,8,256]{2,1,0:T(8,128)S(1)}, f32[19,8,256]{2,1,0:T(8,128)S(1)}, u32[]{:S(2)}, u32[]{:S(2)}) collective-permute-start(f32[19,8,256]{2,1,0:T(8,128)S(1)} %get-tuple-element.17), channel_id=1, source_target_pairs={{16,0},{0,16},{17,1},{1,17},{18,2},{2,18},{19,3},{3,19},{20,4},{4,... | collective-permute-start | bytes 466952 | tf_op jit(solution)/shard_map/ppermute | solution.py:313
  14.4 0.6 %collective-permute-start.6 = (f32[8,128]{1,0:T(8,128)S(1)}, f32[8,128]{1,0:T(8,128)S(1)}, u32[]{:S(2)}, u32[]{:S(2)}) collective-permute-start(f32[8,128]{1,0:T(8,128)S(1)} %get-tuple-element.16.refs_5_), channel_id=1, source_target_pairs={{17,2},{18,1},{19,4},{20,3},{21,6},{22,5},{23,8},{24,7},{25,10},{2... | collective-permute-start | bytes 12296 | tf_op jit(solution)/shard_map/ppermute | solution.py:325
  15.0 4.0 %collective-permute-start.5 = (f32[8,128]{1,0:T(8,128)S(1)}, f32[8,128]{1,0:T(8,128)S(1)}, u32[]{:S(2)}, u32[]{:S(2)}) collective-permute-start(f32[8,128]{1,0:T(8,128)S(1)} %get-tuple-element.16.refs_5_), channel_id=1, source_target_pairs={{16,1},{17,0},{18,3},{19,2},{20,5},{21,4},{22,7},{23,6},{24,9},{25... | collective-permute-start | bytes 12296 | tf_op jit(solution)/shard_map/ppermute | solution.py:325
  19.0 0.6 %collective-permute-start.4 = (f32[8,128]{1,0:T(8,128)S(1)}, f32[8,128]{1,0:T(8,128)S(1)}, u32[]{:S(2)}, u32[]{:S(2)}) collective-permute-start(f32[8,128]{1,0:T(8,128)S(1)} %get-tuple-element.16.refs_5_), channel_id=1, source_target_pairs={{1,2},{2,1},{3,4},{4,3},{5,6},{6,5},{7,8},{8,7},{9,10},{10,9},{11,... | collective-permute-start | bytes 12296 | tf_op jit(solution)/shard_map/ppermute | solution.py:325
  19.7 0.0 collective-permute-done.2.refs_7_
  19.7 3.0 %collective-permute-start.3 = (f32[8,128]{1,0:T(8,128)S(1)}, f32[8,128]{1,0:T(8,128)S(1)}, u32[]{:S(2)}, u32[]{:S(2)}) collective-permute-start(f32[8,128]{1,0:T(8,128)S(1)} %get-tuple-element.16.refs_5_), channel_id=1, source_target_pairs={{0,1},{1,0},{2,3},{3,2},{4,5},{5,4},{6,7},{7,6},{8,9},{9,8},{10,11... | collective-permute-start | bytes 12296 | tf_op jit(solution)/shard_map/ppermute | solution.py:325
  22.7 0.0 copy-done.2
  22.7 0.6 %shard_map.61.refs_3_ = f32[12,4,8,256]{3,2,1,0:T(8,128)S(1)} custom-call(f32[3,4,8,256]{3,2,1,0:T(8,128)S(1)} %copy-done, f32[6,4,8,256]{3,2,1,0:T(8,128)S(1)} %copy-done.2, f32[3,4,8,256]{3,2,1,0:T(8,128)S(1)} %get-tuple-element.14.refs_2_, f32[6,4,8,256]{3,2,1,0:T(8,128)S(1)} %get-tuple-element.12.refs_3_.refs_1_, ...), custom_call_target="tpu_custom_call" | custom-call | flops 4096000 | bytes 1572864 | tf_op jit(solution)/shard_map/pallas_call | solution.py:300
  23.2 0.0 collective-permute-done.6.refs_9_
  23.2 0.0 collective-permute-done.5.refs_8_
  23.3 0.0 collective-permute-done.4.refs_7_
  23.3 0.2 collective-permute-done.3.refs_6_
  23.5 0.0 collective-permute-done.7.refs_10_
  23.5 0.9 %shard_map.62 = (f32[6,4,8,256]{3,2,1,0:T(8,128)}, f32[3,4,8,256]{3,2,1,0:T(8,128)}) custom-call(f32[3,4,8,256]{3,2,1,0:T(8,128)S(1)} %copy-done, f32[6,4,8,256]{3,2,1,0:T(8,128)S(1)} %get-tuple-element.12.refs_3_.refs_1_, f32[6,4,8,256]{3,2,1,0:T(8,128)S(1)} %get-tuple-element.13.refs_4_.refs_2_, f32[12,4,8,256]{3,2,1,0:T(8,128)S(1)} %shard_map.61.refs_3_, ...), custom_call_target="tpu_custom_call" | custom-call | flops 1638400 | bytes 1359872 | tf_op jit(solution)/shard_map/pallas_call | solution.py:300
  (1 shorter events, 0.0 us)
Async XLA Ops:
  0.6 10.7 %copy-start = (f32[3,4,8,256]{3,2,1,0:T(8,128)S(1)}, f32[3,4,8,256]{3,2,1,0:T(8,128)}, u32[]{:S(2)}) copy-start(f32[3,4,8,256]{3,2,1,0:T(8,128)} %refs_0_.5) | copy-start | bytes 294916
  0.6 10.6 %collective-permute-start = (f32[3,4,8,256]{3,2,1,0:T(8,128)}, f32[3,4,8,256]{3,2,1,0:T(8,128)S(1)}, u32[]{:S(2)}, u32[]{:S(2)}) collective-permute-start(f32[3,4,8,256]{3,2,1,0:T(8,128)} %refs_0_.5), channel_id=1, source_target_pairs={{16,0},{0,16},{17,1},{1,17},{18,2},{2,18},{19,3},{3,19},{20,4},{4,... | collective-permute-start | bytes 294920 | tf_op jit(solution)/shard_map/ppermute | solution.py:313
  3.7 16.0 %collective-permute-start.2 = (f32[6,4,8,256]{3,2,1,0:T(8,128)}, f32[6,4,8,256]{3,2,1,0:T(8,128)S(1)}, u32[]{:S(2)}, u32[]{:S(2)}) collective-permute-start(f32[6,4,8,256]{3,2,1,0:T(8,128)} %refs_1_.3), channel_id=1, source_target_pairs={{16,0},{0,16},{17,1},{1,17},{18,2},{2,18},{19,3},{3,19},{20,4},{4,... | collective-permute-start | bytes 589832 | tf_op jit(solution)/shard_map/ppermute | solution.py:313
  3.8 0.9 %copy-start.3 = (f32[6,4,8,256]{3,2,1,0:T(8,128)S(1)}, f32[6,4,8,256]{3,2,1,0:T(8,128)}, u32[]{:S(2)}) copy-start(f32[6,4,8,256]{3,2,1,0:T(8,128)} %refs_1_.2) | copy-start | bytes 589828
  4.7 6.5 %copy-start.4 = (s32[8]{0:T(128)S(1)}, s32[8]{0:T(128)}, u32[]{:S(2)}) copy-start(s32[8]{0:T(128)} %param.6) | copy-start | bytes 100
  4.7 6.5 %collective-permute-start.1 = (f32[2,8,256]{2,1,0:T(8,128)S(1)}, f32[2,8,256]{2,1,0:T(8,128)S(1)}, u32[]{:S(2)}, u32[]{:S(2)}) collective-permute-start(f32[2,8,256]{2,1,0:T(8,128)S(1)} %get-tuple-element.11), channel_id=1, source_target_pairs={{16,0},{0,16},{17,1},{1,17},{18,2},{2,18},{19,3},{3,19},{20,4},{4,... | collective-permute-start | bytes 49160 | tf_op jit(solution)/shard_map/ppermute | solution.py:313
  11.3 0.9 %copy-start.1 = (f32[6,4,8,256]{3,2,1,0:T(8,128)S(1)}, f32[6,4,8,256]{3,2,1,0:T(8,128)}, u32[]{:S(2)}) copy-start(f32[6,4,8,256]{3,2,1,0:T(8,128)} %refs_1_.3) | copy-start | bytes 589828
  12.2 10.4 %copy-start.2 = (f32[6,4,8,256]{3,2,1,0:T(8,128)S(1)}, f32[6,4,8,256]{3,2,1,0:T(8,128)}, u32[]{:S(2)}) copy-start(f32[6,4,8,256]{3,2,1,0:T(8,128)} %refs_1_.3) | copy-start | bytes 589828
  12.6 10.9 %collective-permute-start.7 = (f32[19,8,256]{2,1,0:T(8,128)S(1)}, f32[19,8,256]{2,1,0:T(8,128)S(1)}, u32[]{:S(2)}, u32[]{:S(2)}) collective-permute-start(f32[19,8,256]{2,1,0:T(8,128)S(1)} %get-tuple-element.17), channel_id=1, source_target_pairs={{16,0},{0,16},{17,1},{1,17},{18,2},{2,18},{19,3},{3,19},{20,4},{4,... | collective-permute-start | bytes 466952 | tf_op jit(solution)/shard_map/ppermute | solution.py:313
  14.4 8.9 %collective-permute-start.6 = (f32[8,128]{1,0:T(8,128)S(1)}, f32[8,128]{1,0:T(8,128)S(1)}, u32[]{:S(2)}, u32[]{:S(2)}) collective-permute-start(f32[8,128]{1,0:T(8,128)S(1)} %get-tuple-element.16.refs_5_), channel_id=1, source_target_pairs={{17,2},{18,1},{19,4},{20,3},{21,6},{22,5},{23,8},{24,7},{25,10},{2... | collective-permute-start | bytes 12296 | tf_op jit(solution)/shard_map/ppermute | solution.py:325
  15.0 8.2 %collective-permute-start.5 = (f32[8,128]{1,0:T(8,128)S(1)}, f32[8,128]{1,0:T(8,128)S(1)}, u32[]{:S(2)}, u32[]{:S(2)}) collective-permute-start(f32[8,128]{1,0:T(8,128)S(1)} %get-tuple-element.16.refs_5_), channel_id=1, source_target_pairs={{16,1},{17,0},{18,3},{19,2},{20,5},{21,4},{22,7},{23,6},{24,9},{25... | collective-permute-start | bytes 12296 | tf_op jit(solution)/shard_map/ppermute | solution.py:325
  19.0 4.2 %collective-permute-start.4 = (f32[8,128]{1,0:T(8,128)S(1)}, f32[8,128]{1,0:T(8,128)S(1)}, u32[]{:S(2)}, u32[]{:S(2)}) collective-permute-start(f32[8,128]{1,0:T(8,128)S(1)} %get-tuple-element.16.refs_5_), channel_id=1, source_target_pairs={{1,2},{2,1},{3,4},{4,3},{5,6},{6,5},{7,8},{8,7},{9,10},{10,9},{11,... | collective-permute-start | bytes 12296 | tf_op jit(solution)/shard_map/ppermute | solution.py:325
  19.7 3.8 %collective-permute-start.3 = (f32[8,128]{1,0:T(8,128)S(1)}, f32[8,128]{1,0:T(8,128)S(1)}, u32[]{:S(2)}, u32[]{:S(2)}) collective-permute-start(f32[8,128]{1,0:T(8,128)S(1)} %get-tuple-element.16.refs_5_), channel_id=1, source_target_pairs={{0,1},{1,0},{2,3},{3,2},{4,5},{5,4},{6,7},{7,6},{8,9},{9,8},{10,11... | collective-permute-start | bytes 12296 | tf_op jit(solution)/shard_map/ppermute | solution.py:325

commit v3 on v2

--- a/solution.py
+++ b/solution.py
@@ -90,8 +90,17 @@
     return total
 
 
-def prepare_kernel(tables, strain_ref, size_ref, size_ends_ref):
+def fetch(source, target, arrived):
+    copies = [pltpu.make_async_copy(source.at[k], target.at[k], arrived.at[k]) for k in range(source.shape[0])]
+    for copy in copies:
+        copy.start()
+    return copies
+
+
+def prepare_kernel(tables, strain_hbm, strain_ref, size_ref, size_ends_ref, arrived):
     cells = tables.cells
+    for copy in fetch(strain_hbm, strain_ref, arrived):
+        copy.wait()
     for lanes in halves(strain_ref.shape[-1]):
         size = []
         for z in range(cells):
@@ -101,6 +110,11 @@
             size_ref[z, :, lanes] = size[z]
         for end, value in enumerate(tables.project(size)):
             size_ends_ref[end, :, lanes] = value
+
+
+def fetch_kernel(cot_hbm, cot_ref, arrived):
+    for copy in fetch(cot_hbm, cot_ref, arrived):
+        copy.wait()
 
 
 def products_of(v):
@@ -177,8 +191,8 @@
         per_row = jnp.sum(sums[0], axis=1, keepdims=True)
         per_bin = jnp.sum(jnp.where(mine, per_row, 0.0), axis=0, keepdims=True)
         table = jnp.where(place == index, per_bin, table)
-    sums_ref[...] = table
-    message_ref[18, 0:8, 0:LANES] = table
+    for index in range(sums_ref.shape[0]):
+        sums_ref[index] = table
 
 
 def local_kernel(tables, *refs):
@@ -235,14 +249,14 @@
                 parts_ref[9 + a, z, :, lanes] = 2.0 * dual[z] - 4.0 * fourth[z]
 
 
-def finish_kernel(tables, count, *refs):
+def finish_kernel(tables, *refs):
     peers = tables.devices - 1
     cells = tables.cells
     v_ref, leonard_ref, model_ref, parts_ref, bins_ref = refs[:5]
-    sums_refs = refs[5 : 5 + count]
-    far_message_refs = refs[5 + count : 5 + count + peers]
-    residual_hbm, grad_hbm, residual_ref, grad_ref, left = refs[5 + count + peers :]
-    total = sum_up([ref[...] for ref in sums_refs] + [ref[18, 0:8, 0:LANES] for ref in far_message_refs])
+    sums_ref = refs[5]
+    far_message_refs = refs[6 : 6 + peers]
+    residual_hbm, grad_hbm, residual_ref, grad_ref, left = refs[6 + peers :]
+    total = jnp.sum(sums_ref[...], axis=0)
     inverse = 1.0 / (total[1:2] + EPSILON)
     rows = v_ref.shape[2]
     lane = lax.broadcasted_iota(jnp.int32, bins_ref.shape, 1)
@@ -313,18 +327,6 @@
     return lax.ppermute(values, "span", [((i + shift) % peers, i) for i in range(peers)])
 
 
-def swapped(values, span_shift, distance, parity):
-    span, stream = lax.axis_size("span"), lax.axis_size("stream")
-    pairs = []
-    for i in range(span):
-        row = ((i + span_shift) % span) * stream
-        for j in range(stream - distance):
-            if (j // distance) % 2 == parity:
-                pairs.append((row + j, i * stream + j + distance))
-                pairs.append((row + j + distance, i * stream + j))
-    return lax.ppermute(values, ("span", "stream"), pairs)
-
-
 def on_device(velocity, strain, row_bins, cotangent):
     span, stream = lax.axis_size("span"), lax.axis_size("stream")
     cells, rows, width = velocity.shape[1:]
@@ -332,14 +334,30 @@
     slab = (rows, width)
 
     def shaped(*leading):
-        return jax.ShapeDtypeStruct(leading + slab, jnp.float32)
+        return pltpu.VMEM(leading + slab, jnp.float32)
 
     bins = jnp.broadcast_to(row_bins[:, None], (rows, LANES))
     far_v = [from_ahead(velocity, shift) for shift in range(1, span)]
-    far_cot = [from_ahead(cotangent, shift) for shift in range(1, span)]
     work = cells * rows * width
-    size, size_ends = call(functools.partial(prepare_kernel, tables), [shaped(cells), shaped(2)], 40 * work, strain)
+    near_strain, size, size_ends = call(
+        functools.partial(prepare_kernel, tables),
+        [shaped(6, cells), shaped(cells), shaped(2)],
+        40 * work,
+        pltpu.with_memory_space_constraint(strain, pltpu.HBM),
+        in_specs=[REMAIN],
+        scratch=[pltpu.SemaphoreType.DMA((6,))],
+    )
+    size_ends, sent_cot = lax.optimization_barrier((size_ends, cotangent))
     far_size = [from_ahead(size_ends, shift) for shift in range(1, span)]
+    far_cot = [from_ahead(sent_cot, shift) for shift in range(1, span)]
+    (near_cot,) = call(
+        fetch_kernel,
+        [shaped(6, cells)],
+        work,
+        pltpu.with_memory_space_constraint(cotangent, pltpu.HBM),
+        in_specs=[REMAIN],
+        scratch=[pltpu.SemaphoreType.DMA((6,))],
+    )
     smooth, leonard, model, dual, message, sums = call(
         functools.partial(forward_kernel, tables),
         [
@@ -347,32 +365,26 @@
             shaped(6, cells),
             shaped(6, cells),
             shaped(3, cells),
-            shaped(19),
-            jax.ShapeDtypeStruct((8, LANES), jnp.float32),
+            shaped(18),
+            pltpu.VMEM((span * stream, 8, LANES), jnp.float32),
         ],
         300 * work,
         velocity,
-        strain,
-        cotangent,
+        near_strain,
+        near_cot,
         size,
         bins,
         *far_v,
         *far_size,
     )
     far_message = [from_ahead(message, shift) for shift in range(1, span)]
-    most_rows = 2 * rows * stream // NBINS
-    reach = min(-(-(most_rows - 1) // rows), stream - 1)
-    all_sums = [sums]
-    for span_shift in range(span):
-        for distance in range(1, reach + 1):
-            for parity in range(2):
-                all_sums.append(swapped(sums, span_shift, distance, parity))
+    all_sums = lax.all_to_all(sums, ("span", "stream"), 0, 0, tiled=True)
     (parts,) = call(
         functools.partial(local_kernel, tables),
         [shaped(12, cells)],
         500 * work,
         velocity,
-        cotangent,
+        near_cot,
         smooth,
         leonard,
         model,
@@ -380,10 +392,10 @@
         *far_v,
         *far_cot,
     )
-    outs = [shaped(6, cells), shaped(3, cells)]
+    outs = [jax.ShapeDtypeStruct((n, cells) + slab, jnp.float32) for n in (6, 3)]
     return tuple(
         call(
-            functools.partial(finish_kernel, tables, len(all_sums)),
+            functools.partial(finish_kernel, tables),
             outs,
             200 * work,
             velocity,
@@ -391,7 +403,7 @@
             model,
             parts,
             bins,
-            *all_sums,
+            all_sums,
             *far_message,
             out_specs=[REMAIN] * 2,
             scratch=[pltpu.VMEM(x.shape, x.dtype) for x in outs] + [pltpu.SemaphoreType.DMA((9,))],

time: 24.6 us -> 27.3 us (1.11)
  waiting for transfers between devices: 4.74 us -> 11.9 us
  starting transfers between devices: 15.2 us -> 10.1 us
  Pallas kernels: 1.82 us -> 4.28 us
  local copies, waits for them, and re-layouts: 1.94 us -> 0.09 us
    ppermute x4 -> x0, starting transfers between devices: 8.26 us -> none  [swapped(): return lax.ppermute(values, ('span', 'stream'), pairs)]
    ppermute x4, waiting for transfers between devices: 4.51 us -> 11.9 us  [from_ahead(): lax.ppermute(values, 'span', [((i + shift) % peers, i) for i in range(pee...]
    all_to_all x0 -> x1, starting transfers between devices: none -> 4.89 us  [on_device(): all_sums = lax.all_to_all(sums, ('span', 'stream'), 0, 0, tiled=True)]
    pallas_call x4 -> x5, Pallas kernels: 1.82 us -> 4.28 us  [call(): pl.pallas_call(kernel, out_shape=outs, in_specs=in_specs or [WHOLE] * len...]
    unnamed x10 -> x6, local copies, waits for them, and re-layouts: 1.87 us -> 0.02 us
    ppermute x4, starting transfers between devices: 6.91 us -> 5.21 us  [from_ahead(): lax.ppermute(values, 'span', [((i + shift) % peers, i) for i in range(pee...]
  transfers between devices with their start and end apart: 8 -> 5, of which waited for: 2 -> 3; matrix products, arithmetic and copies ran while one was open for 0% -> 0% of each run, Pallas kernels for 4% -> 9%
where the time goes in v3:
time: 27.3 us; the launch traced here: 27 us
  waiting for transfers between devices  11.9 us (44%)
  starting transfers between devices  10.1 us (37%)
  Pallas kernels  4.28 us (16%)
  between operations  0.69 us (3%)
    ppermute x4, waiting for transfers between devices, from_ahead(): lax.ppermute(values, 'span', [((i + shift) % peers, i) for i in range(pee...  11.9 us
    ppermute x4, starting transfers between devices, from_ahead(): lax.ppermute(values, 'span', [((i + shift) % peers, i) for i in range(pee...  5.21 us
    all_to_all x1, starting transfers between devices, on_device(): all_sums = lax.all_to_all(sums, ('span', 'stream'), 0, 0, tiled=True)  4.89 us
    pallas_call x5, Pallas kernels, call(): pl.pallas_call(kernel, out_shape=outs, in_specs=in_specs or [WHOLE] * len...  4.28 us
  transfers between devices with their start and end apart: 5, of which 3 were waited for; matrix products, arithmetic and copies ran while one was open for 0% of the time, Pallas kernels for 9%

profile of v3, /device:TPU:0, one launch (start us, length us, event | category | flops | bytes accessed | tf_op | source)
XLA Modules:
  0.0 27.0 jit_solution(4410421494935219539)
XLA Ops:
  0.6 3.0 %collective-permute-start = (f32[3,4,8,256]{3,2,1,0:T(8,128)}, f32[3,4,8,256]{3,2,1,0:T(8,128)S(1)}, u32[]{:S(2)}, u32[]{:S(2)}) collective-permute-start(f32[3,4,8,256]{3,2,1,0:T(8,128)} %refs_0_.5), channel_id=1, source_target_pairs={{16,0},{0,16},{17,1},{1,17},{18,2},{2,18},{19,3},{3,19},{20,4},{4,... | collective-permute-start | bytes 294920 | tf_op jit(solution)/shard_map/ppermute | solution.py:327
  3.7 0.9 %shard_map.59 = (f32[6,4,8,256]{3,2,1,0:T(8,128)S(1)}, f32[4,8,256]{2,1,0:T(8,128)S(1)}, f32[2,8,256]{2,1,0:T(8,128)S(1)}) custom-call(f32[6,4,8,256]{3,2,1,0:T(8,128)} %strain_hbm.1), custom_call_target="tpu_custom_call" | custom-call | flops 327680 | bytes 442368 | tf_op jit(solution)/shard_map/pallas_call | solution.py:314
  4.6 0.0 copy-start.2
  4.6 0.0 copy-start
  4.6 0.1 collective-permute-start.1
  4.7 0.9 %shard_map.60.refs_2_.refs_1_ = f32[6,4,8,256]{3,2,1,0:T(8,128)S(1)} custom-call(f32[6,4,8,256]{3,2,1,0:T(8,128)} %cot_hbm.1), custom_call_target="tpu_custom_call" | custom-call | flops 8192 | bytes 393216 | tf_op jit(solution)/shard_map/pallas_call | solution.py:314
  5.6 2.8 %collective-permute-done.1.refs_6_ = f32[2,8,256]{2,1,0:T(8,128)S(1)} collective-permute-done((f32[2,8,256]{2,1,0:T(8,128)S(1)}, f32[2,8,256]{2,1,0:T(8,128)S(1)}, u32[]{:S(2)}, u32[]{:S(2)}) %collective-permute-start.1) | collective-permute-done | bytes 16416 | tf_op jit(solution)/shard_map/ppermute | solution.py:327
  8.4 0.0 collective-permute-done.refs_5_.refs_6_
  8.4 0.0 copy-done.2
  8.4 0.1 broadcast_in_dim.2.refs_4_
  8.5 0.0 copy-done
  8.5 1.0 %shard_map.61 = (f32[3,4,8,256]{3,2,1,0:T(8,128)S(1)}, f32[6,4,8,256]{3,2,1,0:T(8,128)S(1)}, f32[6,4,8,256]{3,2,1,0:T(8,128)S(1)}, f32[3,4,8,256]{3,2,1,0:T(8,12...) custom-call(f32[3,4,8,256]{3,2,1,0:T(8,128)S(1)} %copy-done, f32[6,4,8,256]{3,2,1,0:T(8,128)S(1)} %get-tuple-element.13.refs_1_, ...), custom_call_target="tpu_custom_call" | custom-call | flops 2457600 | bytes 1511424 | tf_op jit(solution)/shard_map/pallas_call | solution.py:314
  9.5 0.0 copy-start.1
  9.5 4.9 %all-to-all-start = ((f32[32,8,128]{2,1,0:T(8,128)}), f32[32,8,128]{2,1,0:T(8,128)S(1)}, u32[]{:S(2)}, u32[]{:S(2)}) async-start(f32[32,8,128]{2,1,0:T(8,128)} %get-tuple-element.22), calls=%async_computation | async-start | bytes 262144 | tf_op jit(solution)/shard_map/all_to_all | solution.py:381
  14.4 0.0 copy-done.1
  14.4 1.8 %collective-permute-start.2 = (f32[6,4,8,256]{3,2,1,0:T(8,128)S(1)}, f32[6,4,8,256]{3,2,1,0:T(8,128)S(1)}, u32[]{:S(2)}, u32[]{:S(2)}) collective-permute-start(f32[6,4,8,256]{3,2,1,0:T(8,128)S(1)} %copy-done.1), channel_id=1, source_target_pairs={{16,0},{0,16},{17,1},{1,17},{18,2},{2,18},{19,3},{3,19},{20,4},{4,... | collective-permute-start | bytes 589832 | tf_op jit(solution)/shard_map/ppermute | solution.py:327
  16.3 0.3 collective-permute-start.3
  16.5 6.9 %collective-permute-done.2.refs_7_ = f32[6,4,8,256]{3,2,1,0:T(8,128)S(1)} collective-permute-done((f32[6,4,8,256]{3,2,1,0:T(8,128)S(1)}, f32[6,4,8,256]{3,2,1,0:T(8,128)S(1)}, u32[]{:S(2)}, u32[]{:S(2)}) %collective-permute-start.2) | collective-permute-done | bytes 196640 | tf_op jit(solution)/shard_map/ppermute | solution.py:327
  23.4 0.6 %shard_map.62.refs_3_ = f32[12,4,8,256]{3,2,1,0:T(8,128)S(1)} custom-call(f32[3,4,8,256]{3,2,1,0:T(8,128)S(1)} %copy-done, f32[6,4,8,256]{3,2,1,0:T(8,128)S(1)} %shard_map.60.refs_2_.refs_1_, f32[3,4,8,256]{3,2,1,0:T(8,128)S(1)} %get-tuple-element.19.refs_2_, f32[6,4,8,256]{3,2,1,0:T(8,128)S(1)} %get-tuple-element.17.refs_3_.refs_1_, ...), custom_call_target="tpu_custom_call" | custom-call | flops 4096000 | bytes 1572864 | tf_op jit(solution)/shard_map/pallas_call | solution.py:314
  24.0 2.1 %collective-permute-done.3.refs_6_ = f32[18,8,256]{2,1,0:T(8,128)S(1)} collective-permute-done((f32[18,8,256]{2,1,0:T(8,128)S(1)}, f32[18,8,256]{2,1,0:T(8,128)S(1)}, u32[]{:S(2)}, u32[]{:S(2)}) %collective-permute-start.3) | collective-permute-done | bytes 147488 | tf_op jit(solution)/shard_map/ppermute | solution.py:327
  26.1 0.0 all-to-all-done.refs_5_
  26.1 0.9 %shard_map.63 = (f32[6,4,8,256]{3,2,1,0:T(8,128)}, f32[3,4,8,256]{3,2,1,0:T(8,128)}) custom-call(f32[3,4,8,256]{3,2,1,0:T(8,128)S(1)} %copy-done, f32[6,4,8,256]{3,2,1,0:T(8,128)S(1)} %get-tuple-element.17.refs_3_.refs_1_, f32[6,4,8,256]{3,2,1,0:T(8,128)S(1)} %get-tuple-element.18.refs_4_.refs_2_, f32[12,4,8,256]{3,2,1,0:T(8,128)S(1)} %shard_map.62.refs_3_, ...), custom_call_target="tpu_custom_call" | custom-call | flops 1638400 | bytes 1462272 | tf_op jit(solution)/shard_map/pallas_call | solution.py:314
Async XLA Ops:
  0.6 7.8 %collective-permute-start = (f32[3,4,8,256]{3,2,1,0:T(8,128)}, f32[3,4,8,256]{3,2,1,0:T(8,128)S(1)}, u32[]{:S(2)}, u32[]{:S(2)}) collective-permute-start(f32[3,4,8,256]{3,2,1,0:T(8,128)} %refs_0_.5), channel_id=1, source_target_pairs={{16,0},{0,16},{17,1},{1,17},{18,2},{2,18},{19,3},{3,19},{20,4},{4,... | collective-permute-start | bytes 294920 | tf_op jit(solution)/shard_map/ppermute | solution.py:327
  4.6 3.8 %copy-start.2 = (s32[8]{0:T(128)S(1)}, s32[8]{0:T(128)}, u32[]{:S(2)}) copy-start(s32[8]{0:T(128)} %param.6) | copy-start | bytes 100
  4.6 3.9 %copy-start = (f32[3,4,8,256]{3,2,1,0:T(8,128)S(1)}, f32[3,4,8,256]{3,2,1,0:T(8,128)}, u32[]{:S(2)}) copy-start(f32[3,4,8,256]{3,2,1,0:T(8,128)} %refs_0_.5) | copy-start | bytes 294916
  4.6 3.8 %collective-permute-start.1 = (f32[2,8,256]{2,1,0:T(8,128)S(1)}, f32[2,8,256]{2,1,0:T(8,128)S(1)}, u32[]{:S(2)}, u32[]{:S(2)}) collective-permute-start(f32[2,8,256]{2,1,0:T(8,128)S(1)} %get-tuple-element.16), channel_id=1, source_target_pairs={{16,0},{0,16},{17,1},{1,17},{18,2},{2,18},{19,3},{3,19},{20,4},{4,... | collective-permute-start | bytes 49160 | tf_op jit(solution)/shard_map/ppermute | solution.py:327
  9.5 4.9 %copy-start.1 = (f32[6,4,8,256]{3,2,1,0:T(8,128)S(1)}, f32[6,4,8,256]{3,2,1,0:T(8,128)}, u32[]{:S(2)}) copy-start(f32[6,4,8,256]{3,2,1,0:T(8,128)} %cot_hbm.1) | copy-start | bytes 589828
  9.5 16.6 %all-to-all-start = ((f32[32,8,128]{2,1,0:T(8,128)}), f32[32,8,128]{2,1,0:T(8,128)S(1)}, u32[]{:S(2)}, u32[]{:S(2)}) async-start(f32[32,8,128]{2,1,0:T(8,128)} %get-tuple-element.22), calls=%async_computation | async-start | bytes 262144 | tf_op jit(solution)/shard_map/all_to_all | solution.py:381
  14.4 9.0 %collective-permute-start.2 = (f32[6,4,8,256]{3,2,1,0:T(8,128)S(1)}, f32[6,4,8,256]{3,2,1,0:T(8,128)S(1)}, u32[]{:S(2)}, u32[]{:S(2)}) collective-permute-start(f32[6,4,8,256]{3,2,1,0:T(8,128)S(1)} %copy-done.1), channel_id=1, source_target_pairs={{16,0},{0,16},{17,1},{1,17},{18,2},{2,18},{19,3},{3,19},{20,4},{4,... | collective-permute-start | bytes 589832 | tf_op jit(solution)/shard_map/ppermute | solution.py:327
  16.3 9.9 %collective-permute-start.3 = (f32[18,8,256]{2,1,0:T(8,128)S(1)}, f32[18,8,256]{2,1,0:T(8,128)S(1)}, u32[]{:S(2)}, u32[]{:S(2)}) collective-permute-start(f32[18,8,256]{2,1,0:T(8,128)S(1)} %get-tuple-element.23), channel_id=1, source_target_pairs={{16,0},{0,16},{17,1},{1,17},{18,2},{2,18},{19,3},{3,19},{20,4},{4,... | collective-permute-start | bytes 442376 | tf_op jit(solution)/shard_map/ppermute | solution.py:327

commit v4 on v3

--- a/solution.py
+++ b/solution.py
@@ -112,7 +112,7 @@
             size_ends_ref[end, :, lanes] = value
 
 
-def fetch_kernel(cot_hbm, cot_ref, arrived):
+def fetch_kernel(cot_hbm, size_ends_ref, cot_ref, arrived):
     for copy in fetch(cot_hbm, cot_ref, arrived):
         copy.wait()
 
@@ -145,7 +145,7 @@
     v_ref, strain_ref, cot_ref, size_ref, bins_ref = refs[:5]
     far_v_refs = refs[5 : 5 + peers]
     far_size_refs = refs[5 + peers : 5 + 2 * peers]
-    smooth_ref, leonard_ref, model_ref, dual_ref, message_ref, sums_ref = refs[5 + 2 * peers :]
+    smooth_ref, leonard_ref, model_ref, sums_ref = refs[5 + 2 * peers :]
     cross, square, blame = [], [], []
     for lanes in halves(v_ref.shape[-1]):
         v = [[v_ref[a, z, :, lanes] for z in range(cells)] for a in range(3)]
@@ -159,14 +159,11 @@
         filtered = filtered_block(tables, 0, v + products + [size], ends)
         smooth_v = filtered[:3]
         factor = [2.0 * (4.0 * filtered[9][z] - size[z]) for z in range(cells)]
-        model = []
         for k, (a, b) in enumerate(INDEX_PAIRS):
-            model.append([])
             for z in range(cells):
                 coarse = smooth_v[a][z] * smooth_v[b][z]
                 leonard = filtered[3 + k][z] - coarse
                 term = products[k][z] - coarse + factor[z] * strain_ref[k, z, :, lanes]
-                model[k].append(term)
                 leonard_ref[k, z, :, lanes] = leonard
                 model_ref[k, z, :, lanes] = term
                 scaled = PAIR_WEIGHTS[k] * term
@@ -174,15 +171,9 @@
                 square.append(scaled * term)
                 blame.append(term * cot_ref[k, z, :, lanes])
             cross, square, blame = [sum_up(cross)], [sum_up(square)], [sum_up(blame)]
-            for end, value in enumerate(tables.project(model[k])):
-                message_ref[2 * k + end, :, lanes] = value
         for a in range(3):
-            dual = [2.0 * x for x in plain_dual(model, smooth_v, a, cells)]
             for z in range(cells):
                 smooth_ref[a, z, :, lanes] = smooth_v[a][z]
-                dual_ref[a, z, :, lanes] = dual[z]
-            for end, value in enumerate(tables.project(dual)):
-                message_ref[12 + 2 * a + end, :, lanes] = value
     lane = lax.broadcasted_iota(jnp.int32, bins_ref.shape, 1)
     mine = bins_ref[...] == lane
     place = lax.broadcasted_iota(jnp.int32, (8, LANES), 0)
@@ -191,8 +182,26 @@
         per_row = jnp.sum(sums[0], axis=1, keepdims=True)
         per_bin = jnp.sum(jnp.where(mine, per_row, 0.0), axis=0, keepdims=True)
         table = jnp.where(place == index, per_bin, table)
-    for index in range(sums_ref.shape[0]):
-        sums_ref[index] = table
+    sums_ref[...] = table
+
+
+def message_kernel(tables, smooth_ref, model_ref, sums_ref, other_sums_ref, dual_ref, message_ref, pair_ref):
+    cells = tables.cells
+    pair_sums = sums_ref[...] + other_sums_ref[...]
+    pair_ref[...] = pair_sums
+    message_ref[18, 0:8, 0:LANES] = pair_sums
+    for lanes in halves(model_ref.shape[-1]):
+        model = [[model_ref[k, z, :, lanes] for z in range(cells)] for k in range(6)]
+        smooth_v = [[smooth_ref[a, z, :, lanes] for z in range(cells)] for a in range(3)]
+        for k in range(6):
+            for end, value in enumerate(tables.project(model[k])):
+                message_ref[2 * k + end, :, lanes] = value
+        for a in range(3):
+            dual = [2.0 * x for x in plain_dual(model, smooth_v, a, cells)]
+            for z in range(cells):
+                dual_ref[a, z, :, lanes] = dual[z]
+            for end, value in enumerate(tables.project(dual)):
+                message_ref[12 + 2 * a + end, :, lanes] = value
 
 
 def local_kernel(tables, *refs):
@@ -249,14 +258,21 @@
                 parts_ref[9 + a, z, :, lanes] = 2.0 * dual[z] - 4.0 * fourth[z]
 
 
-def finish_kernel(tables, *refs):
+def finish_kernel(tables, count, turning, *refs):
     peers = tables.devices - 1
     cells = tables.cells
     v_ref, leonard_ref, model_ref, parts_ref, bins_ref = refs[:5]
-    sums_ref = refs[5]
-    far_message_refs = refs[6 : 6 + peers]
-    residual_hbm, grad_hbm, residual_ref, grad_ref, left = refs[6 + peers :]
-    total = jnp.sum(sums_ref[...], axis=0)
+    pair_ref = refs[5]
+    near_refs = refs[6 : 6 + count]
+    far_message_refs = refs[6 + count : 6 + count + peers]
+    residual_hbm, grad_hbm, residual_ref, grad_ref, left = refs[6 + count + peers :]
+    total = sum_up([pair_ref[...]] + [ref[18, 0:8, 0:LANES] for ref in far_message_refs])
+    near = sum_up([ref[...] for ref in near_refs])
+    if turning:
+        place = lax.axis_index("stream")
+        inner = jnp.logical_and(place > 0, place < lax.axis_size("stream") - 1)
+        near = jnp.where(inner, near, 0.0)
+    total = total + near
     inverse = 1.0 / (total[1:2] + EPSILON)
     rows = v_ref.shape[2]
     lane = lax.broadcasted_iota(jnp.int32, bins_ref.shape, 1)
@@ -327,6 +343,25 @@
     return lax.ppermute(values, "span", [((i + shift) % peers, i) for i in range(peers)])
 
 
+def from_source(values, span_shift, source):
+    span, stream = lax.axis_size("span"), lax.axis_size("stream")
+    pairs = [
+        (((i + span_shift) % span) * stream + source(j) % stream, i * stream + j)
+        for i in range(span)
+        for j in range(stream)
+    ]
+    return lax.ppermute(values, ("span", "stream"), pairs)
+
+
+def ring_source(stream):
+    def source(j):
+        if j % 2 == 0:
+            return j - 2 if j >= 2 else 1
+        return j + 2 if j + 2 < stream else j - 1
+
+    return source
+
+
 def on_device(velocity, strain, row_bins, cotangent):
     span, stream = lax.axis_size("span"), lax.axis_size("stream")
     cells, rows, width = velocity.shape[1:]
@@ -347,28 +382,22 @@
         in_specs=[REMAIN],
         scratch=[pltpu.SemaphoreType.DMA((6,))],
     )
-    size_ends, sent_cot = lax.optimization_barrier((size_ends, cotangent))
     far_size = [from_ahead(size_ends, shift) for shift in range(1, span)]
-    far_cot = [from_ahead(sent_cot, shift) for shift in range(1, span)]
     (near_cot,) = call(
         fetch_kernel,
         [shaped(6, cells)],
         work,
         pltpu.with_memory_space_constraint(cotangent, pltpu.HBM),
-        in_specs=[REMAIN],
+        size_ends,
+        in_specs=[REMAIN, WHOLE],
         scratch=[pltpu.SemaphoreType.DMA((6,))],
     )
-    smooth, leonard, model, dual, message, sums = call(
+    far_cot = [from_ahead(near_cot, shift) for shift in range(1, span)]
+    table = pltpu.VMEM((8, LANES), jnp.float32)
+    smooth, leonard, model, sums = call(
         functools.partial(forward_kernel, tables),
-        [
-            shaped(3, cells),
-            shaped(6, cells),
-            shaped(6, cells),
-            shaped(3, cells),
-            shaped(18),
-            pltpu.VMEM((span * stream, 8, LANES), jnp.float32),
-        ],
-        300 * work,
+        [shaped(3, cells), shaped(6, cells), shaped(6, cells), table],
+        100000 * work,
         velocity,
         near_strain,
         near_cot,
@@ -377,8 +406,26 @@
         *far_v,
         *far_size,
     )
+    other_sums = from_source(sums, 0, lambda j: j ^ 1)
+    dual, message, pair_sums = call(
+        functools.partial(message_kernel, tables),
+        [shaped(3, cells), shaped(19), table],
+        100 * work,
+        smooth,
+        model,
+        sums,
+        other_sums,
+    )
     far_message = [from_ahead(message, shift) for shift in range(1, span)]
-    all_sums = lax.all_to_all(sums, ("span", "stream"), 0, 0, tiled=True)
+    most_rows = 2 * rows * stream // NBINS
+    reach = -(-(most_rows - 1) // rows)
+    turning = reach <= 1
+    if turning:
+        sources = [ring_source(stream)]
+    else:
+        steps = range(1, -(-reach // 2) + 1)
+        sources = [functools.partial(lambda j, away: j + away, away=2 * step * way) for step in steps for way in (1, -1)]
+    near_sums = [from_source(pair_sums, shift, source) for shift in range(span) for source in sources]
     (parts,) = call(
         functools.partial(local_kernel, tables),
         [shaped(12, cells)],
@@ -395,7 +442,7 @@
     outs = [jax.ShapeDtypeStruct((n, cells) + slab, jnp.float32) for n in (6, 3)]
     return tuple(
         call(
-            functools.partial(finish_kernel, tables),
+            functools.partial(finish_kernel, tables, len(near_sums), turning),
             outs,
             200 * work,
             velocity,
@@ -403,7 +450,8 @@
             model,
             parts,
             bins,
-            all_sums,
+            pair_sums,
+            *near_sums,
             *far_message,
             out_specs=[REMAIN] * 2,
             scratch=[pltpu.VMEM(x.shape, x.dtype) for x in outs] + [pltpu.SemaphoreType.DMA((9,))],

time: 27.3 us -> 17.5 us (0.64)
  waiting for transfers between devices: 11.9 us -> 3.02 us
  Pallas kernels: 4.28 us -> 3.65 us
    ppermute x4, waiting for transfers between devices: 11.9 us -> 1.11 us  [from_ahead(): lax.ppermute(values, 'span', [((i + shift) % peers, i) for i in range(pee...]
    all_to_all x1 -> x0, starting transfers between devices: 4.89 us -> none  [on_device(): all_sums = lax.all_to_all(sums, ('span', 'stream'), 0, 0, tiled=True)]
    ppermute x0 -> x3, starting transfers between devices: none -> 4.39 us  [from_source(): return lax.ppermute(values, ('span', 'stream'), pairs)]
    ppermute x0 -> x3, waiting for transfers between devices: none -> 1.91 us  [from_source(): return lax.ppermute(values, ('span', 'stream'), pairs)]
    pallas_call x5 -> x6, Pallas kernels: 4.28 us -> 3.65 us  [call(): pl.pallas_call(kernel, out_shape=outs, in_specs=in_specs or [WHOLE] * len...]
    ppermute x4, starting transfers between devices: 5.21 us -> 5.5 us  [from_ahead(): lax.ppermute(values, 'span', [((i + shift) % peers, i) for i in range(pee...]
  transfers between devices with their start and end apart: 5 -> 7, of which waited for: 3 -> 5; matrix products, arithmetic and copies ran while one was open for 0% -> 0% of each run, Pallas kernels for 9% -> 16%
where the time goes in v4:
time: 17.5 us; the launch traced here: 17.3 us
  starting transfers between devices  9.89 us (57%)
  Pallas kernels  3.65 us (21%)
  waiting for transfers between devices  3.02 us (17%)
  between operations  0.68 us (4%)
    ppermute x4, starting transfers between devices, from_ahead(): lax.ppermute(values, 'span', [((i + shift) % peers, i) for i in range(pee...  5.5 us
    ppermute x3, starting transfers between devices, from_source(): return lax.ppermute(values, ('span', 'stream'), pairs)  4.39 us
    pallas_call x6, Pallas kernels, call(): pl.pallas_call(kernel, out_shape=outs, in_specs=in_specs or [WHOLE] * len...  3.65 us
    ppermute x3, waiting for transfers between devices, from_source(): return lax.ppermute(values, ('span', 'stream'), pairs)  1.91 us
    ppermute x4, waiting for transfers between devices, from_ahead(): lax.ppermute(values, 'span', [((i + shift) % peers, i) for i in range(pee...  1.11 us
  transfers between devices with their start and end apart: 7, of which 5 were waited for; matrix products, arithmetic and copies ran while one was open for 0% of the time, Pallas kernels for 16%

profile of v4, /device:TPU:0, one launch (start us, length us, event | category | flops | bytes accessed | tf_op | source)
XLA Modules:
  0.0 17.3 jit_solution(6234161291484882534)
XLA Ops:
  0.6 3.0 %collective-permute-start = (f32[3,4,8,256]{3,2,1,0:T(8,128)}, f32[3,4,8,256]{3,2,1,0:T(8,128)S(1)}, u32[]{:S(2)}, u32[]{:S(2)}) collective-permute-start(f32[3,4,8,256]{3,2,1,0:T(8,128)} %refs_0_.5), channel_id=1, source_target_pairs={{16,0},{0,16},{17,1},{1,17},{18,2},{2,18},{19,3},{3,19},{20,4},{4,... | collective-permute-start | bytes 294920 | tf_op jit(solution)/shard_map/ppermute | solution.py:343
  3.7 0.9 %shard_map.59 = (f32[6,4,8,256]{3,2,1,0:T(8,128)S(1)}, f32[4,8,256]{2,1,0:T(8,128)S(1)}, f32[2,8,256]{2,1,0:T(8,128)S(1)}) custom-call(f32[6,4,8,256]{3,2,1,0:T(8,128)} %strain_hbm.1), custom_call_target="tpu_custom_call" | custom-call | flops 327680 | bytes 442368 | tf_op jit(solution)/shard_map/pallas_call | solution.py:330
  4.6 0.0 copy-start.1
  4.6 0.0 copy-start
  4.6 0.1 collective-permute-start.1
  4.7 0.9 %shard_map.60.refs_2_.refs_1_ = f32[6,4,8,256]{3,2,1,0:T(8,128)S(1)} custom-call(f32[6,4,8,256]{3,2,1,0:T(8,128)} %cot_hbm.1, f32[2,8,256]{2,1,0:T(8,128)S(1)} %get-tuple-element.13.size_ends_ref), custom_call_target="tpu_custom_call" | custom-call | flops 8192 | bytes 409600 | tf_op jit(solution)/shard_map/pallas_call | solution.py:330
  5.6 2.1 %collective-permute-start.3 = (f32[6,4,8,256]{3,2,1,0:T(8,128)S(1)}, f32[6,4,8,256]{3,2,1,0:T(8,128)S(1)}, u32[]{:S(2)}, u32[]{:S(2)}) collective-permute-start(f32[6,4,8,256]{3,2,1,0:T(8,128)S(1)} %shard_map.60.refs_2_.refs_1_), channel_id=1, source_target_pairs={{16,0},{0,16},{17,1},{1,17},{18,2},{2,18},{19,3},{3,19},{20,4},{4,... | collective-permute-start | bytes 589832 | tf_op jit(solution)/shard_map/ppermute | solution.py:343
  7.7 0.8 %collective-permute-done.1.refs_6_ = f32[2,8,256]{2,1,0:T(8,128)S(1)} collective-permute-done((f32[2,8,256]{2,1,0:T(8,128)S(1)}, f32[2,8,256]{2,1,0:T(8,128)S(1)}, u32[]{:S(2)}, u32[]{:S(2)}) %collective-permute-start.1) | collective-permute-done | bytes 16416 | tf_op jit(solution)/shard_map/ppermute | solution.py:343
  8.5 0.0 collective-permute-done.refs_5_.refs_6_
  8.5 0.0 copy-done.1
  8.5 0.1 broadcast_in_dim.2.refs_4_
  8.6 0.0 copy-done
  8.6 0.3 %shard_map.61 = (f32[3,4,8,256]{3,2,1,0:T(8,128)S(1)}, f32[6,4,8,256]{3,2,1,0:T(8,128)S(1)}, f32[6,4,8,256]{3,2,1,0:T(8,128)S(1)}, f32[8,128]{1,0:T(8,128)S(1)}) custom-call(f32[3,4,8,256]{3,2,1,0:T(8,128)S(1)} %copy-done, f32[6,4,8,256]{3,2,1,0:T(8,128)S(1)} %get-tuple-element.12.refs_1_, f32[6,4,8,256]{3,2,1,0:T(8,128)S(1)} %shard_map.60.refs_2_.refs_1_, ...), custom_call_target="tpu_custom_call" | custom-call | flops 819200000 | bytes 1138688 | tf_op jit(solution)/shard_map/pallas_call | solution.py:330
  8.9 0.0 collective-permute-start.2
  9.0 1.2 %collective-permute-done.2.other_sums_ref = f32[8,128]{1,0:T(8,128)S(1)} collective-permute-done((f32[8,128]{1,0:T(8,128)S(1)}, f32[8,128]{1,0:T(8,128)S(1)}, u32[]{:S(2)}, u32[]{:S(2)}) %collective-permute-start.2) | collective-permute-done | bytes 4128 | tf_op jit(solution)/shard_map/ppermute | solution.py:353
  10.2 0.3 %collective-permute-start.6 = (f32[19,8,256]{2,1,0:T(8,128)S(1)}, f32[19,8,256]{2,1,0:T(8,128)S(1)}, u32[]{:S(2)}, u32[]{:S(2)}) collective-permute-start(f32[19,8,256]{2,1,0:T(8,128)S(1)} %get-tuple-element.21), channel_id=1, source_target_pairs={{16,0},{0,16},{17,1},{1,17},{18,2},{2,18},{19,3},{3,19},{20,4},{4,... | collective-permute-start | bytes 466952 | tf_op jit(solution)/shard_map/ppermute | solution.py:343
  10.5 2.8 %collective-permute-start.5 = (f32[8,128]{1,0:T(8,128)S(1)}, f32[8,128]{1,0:T(8,128)S(1)}, u32[]{:S(2)}, u32[]{:S(2)}) collective-permute-start(f32[8,128]{1,0:T(8,128)S(1)} %get-tuple-element.20.refs_5_), channel_id=1, source_target_pairs={{17,0},{19,1},{16,2},{21,3},{18,4},{23,5},{20,6},{25,7},{22,8},{27... | collective-permute-start | bytes 12296 | tf_op jit(solution)/shard_map/ppermute | solution.py:353
  13.3 1.5 %collective-permute-start.4 = (f32[8,128]{1,0:T(8,128)S(1)}, f32[8,128]{1,0:T(8,128)S(1)}, u32[]{:S(2)}, u32[]{:S(2)}) collective-permute-start(f32[8,128]{1,0:T(8,128)S(1)} %get-tuple-element.20.refs_5_), channel_id=1, source_target_pairs={{1,0},{3,1},{0,2},{5,3},{2,4},{7,5},{4,6},{9,7},{6,8},{11,9},{8,10... | collective-permute-start | bytes 12296 | tf_op jit(solution)/shard_map/ppermute | solution.py:353
  14.8 0.0 collective-permute-done.3.refs_7_
  14.8 0.6 %shard_map.63.refs_3_ = f32[12,4,8,256]{3,2,1,0:T(8,128)S(1)} custom-call(f32[3,4,8,256]{3,2,1,0:T(8,128)S(1)} %copy-done, f32[6,4,8,256]{3,2,1,0:T(8,128)S(1)} %shard_map.60.refs_2_.refs_1_, f32[3,4,8,256]{3,2,1,0:T(8,128)S(1)} %get-tuple-element.17.smooth_ref.refs_2_, f32[6,4,8,256]{3,2,1,0:T(8,128)S(1)} %get-tuple-element.15.refs_3_.refs_1_, ...), custom_call_target="tpu_custom_call" | custom-call | flops 4096000 | bytes 1572864 | tf_op jit(solution)/shard_map/pallas_call | solution.py:330
  15.4 0.3 %collective-permute-done.5.refs_7_ = f32[8,128]{1,0:T(8,128)S(1)} collective-permute-done((f32[8,128]{1,0:T(8,128)S(1)}, f32[8,128]{1,0:T(8,128)S(1)}, u32[]{:S(2)}, u32[]{:S(2)}) %collective-permute-start.5) | collective-permute-done | bytes 4128 | tf_op jit(solution)/shard_map/ppermute | solution.py:353
  15.7 0.5 %collective-permute-done.4.refs_6_ = f32[8,128]{1,0:T(8,128)S(1)} collective-permute-done((f32[8,128]{1,0:T(8,128)S(1)}, f32[8,128]{1,0:T(8,128)S(1)}, u32[]{:S(2)}, u32[]{:S(2)}) %collective-permute-start.4) | collective-permute-done | bytes 4128 | tf_op jit(solution)/shard_map/ppermute | solution.py:353
  16.2 0.3 %collective-permute-done.6.refs_8_ = f32[19,8,256]{2,1,0:T(8,128)S(1)} collective-permute-done((f32[19,8,256]{2,1,0:T(8,128)S(1)}, f32[19,8,256]{2,1,0:T(8,128)S(1)}, u32[]{:S(2)}, u32[]{:S(2)}) %collective-permute-start.6) | collective-permute-done | bytes 155680 | tf_op jit(solution)/shard_map/ppermute | solution.py:343
  16.4 0.9 %shard_map.64 = (f32[6,4,8,256]{3,2,1,0:T(8,128)}, f32[3,4,8,256]{3,2,1,0:T(8,128)}) custom-call(f32[3,4,8,256]{3,2,1,0:T(8,128)S(1)} %copy-done, f32[6,4,8,256]{3,2,1,0:T(8,128)S(1)} %get-tuple-element.15.refs_3_.refs_1_, f32[6,4,8,256]{3,2,1,0:T(8,128)S(1)} %get-tuple-element.16.model_ref.refs_4_.refs_2_, f32[12,4,8,256]{3,2,1,0:T(8,128)S(1)} %shard_map.63.refs_3_, ...), custom_call_target="tpu_custom_call" | custom-call | flops 1638400 | bytes 1351680 | tf_op jit(solution)/shard_map/pallas_call | solution.py:330
  (1 shorter events, 0.0 us)
Async XLA Ops:
  0.6 7.9 %collective-permute-start = (f32[3,4,8,256]{3,2,1,0:T(8,128)}, f32[3,4,8,256]{3,2,1,0:T(8,128)S(1)}, u32[]{:S(2)}, u32[]{:S(2)}) collective-permute-start(f32[3,4,8,256]{3,2,1,0:T(8,128)} %refs_0_.5), channel_id=1, source_target_pairs={{16,0},{0,16},{17,1},{1,17},{18,2},{2,18},{19,3},{3,19},{20,4},{4,... | collective-permute-start | bytes 294920 | tf_op jit(solution)/shard_map/ppermute | solution.py:343
  4.6 3.9 %copy-start.1 = (s32[8]{0:T(128)S(1)}, s32[8]{0:T(128)}, u32[]{:S(2)}) copy-start(s32[8]{0:T(128)} %param.6) | copy-start | bytes 100
  4.6 4.0 %copy-start = (f32[3,4,8,256]{3,2,1,0:T(8,128)S(1)}, f32[3,4,8,256]{3,2,1,0:T(8,128)}, u32[]{:S(2)}) copy-start(f32[3,4,8,256]{3,2,1,0:T(8,128)} %refs_0_.5) | copy-start | bytes 294916
  4.6 3.9 %collective-permute-start.1 = (f32[2,8,256]{2,1,0:T(8,128)S(1)}, f32[2,8,256]{2,1,0:T(8,128)S(1)}, u32[]{:S(2)}, u32[]{:S(2)}) collective-permute-start(f32[2,8,256]{2,1,0:T(8,128)S(1)} %get-tuple-element.13.size_ends_ref), channel_id=1, source_target_pairs={{16,0},{0,16},{17,1},{1,17},{18,2},{2,18},{19,3},{3,19},{20,4},{4,... | collective-permute-start | bytes 49160 | tf_op jit(solution)/shard_map/ppermute | solution.py:343
  5.6 9.2 %collective-permute-start.3 = (f32[6,4,8,256]{3,2,1,0:T(8,128)S(1)}, f32[6,4,8,256]{3,2,1,0:T(8,128)S(1)}, u32[]{:S(2)}, u32[]{:S(2)}) collective-permute-start(f32[6,4,8,256]{3,2,1,0:T(8,128)S(1)} %shard_map.60.refs_2_.refs_1_), channel_id=1, source_target_pairs={{16,0},{0,16},{17,1},{1,17},{18,2},{2,18},{19,3},{3,19},{20,4},{4,... | collective-permute-start | bytes 589832 | tf_op jit(solution)/shard_map/ppermute | solution.py:343
  8.9 1.2 %collective-permute-start.2 = (f32[8,128]{1,0:T(8,128)S(1)}, f32[8,128]{1,0:T(8,128)S(1)}, u32[]{:S(2)}, u32[]{:S(2)}) collective-permute-start(f32[8,128]{1,0:T(8,128)S(1)} %get-tuple-element.18.sums_ref), channel_id=1, source_target_pairs={{1,0},{0,1},{3,2},{2,3},{5,4},{4,5},{7,6},{6,7},{9,8},{8,9},{11,10... | collective-permute-start | bytes 12296 | tf_op jit(solution)/shard_map/ppermute | solution.py:353
  10.2 6.2 %collective-permute-start.6 = (f32[19,8,256]{2,1,0:T(8,128)S(1)}, f32[19,8,256]{2,1,0:T(8,128)S(1)}, u32[]{:S(2)}, u32[]{:S(2)}) collective-permute-start(f32[19,8,256]{2,1,0:T(8,128)S(1)} %get-tuple-element.21), channel_id=1, source_target_pairs={{16,0},{0,16},{17,1},{1,17},{18,2},{2,18},{19,3},{3,19},{20,4},{4,... | collective-permute-start | bytes 466952 | tf_op jit(solution)/shard_map/ppermute | solution.py:343
  10.5 5.2 %collective-permute-start.5 = (f32[8,128]{1,0:T(8,128)S(1)}, f32[8,128]{1,0:T(8,128)S(1)}, u32[]{:S(2)}, u32[]{:S(2)}) collective-permute-start(f32[8,128]{1,0:T(8,128)S(1)} %get-tuple-element.20.refs_5_), channel_id=1, source_target_pairs={{17,0},{19,1},{16,2},{21,3},{18,4},{23,5},{20,6},{25,7},{22,8},{27... | collective-permute-start | bytes 12296 | tf_op jit(solution)/shard_map/ppermute | solution.py:353
  13.3 2.9 %collective-permute-start.4 = (f32[8,128]{1,0:T(8,128)S(1)}, f32[8,128]{1,0:T(8,128)S(1)}, u32[]{:S(2)}, u32[]{:S(2)}) collective-permute-start(f32[8,128]{1,0:T(8,128)S(1)} %get-tuple-element.20.refs_5_), channel_id=1, source_target_pairs={{1,0},{3,1},{0,2},{5,3},{2,4},{7,5},{4,6},{9,7},{6,8},{11,9},{8,10... | collective-permute-start | bytes 12296 | tf_op jit(solution)/shard_map/ppermute | solution.py:353

commit v5 on v4

--- a/solution.py
+++ b/solution.py
@@ -18,6 +18,7 @@
 PAIR_WEIGHTS = (1.0, 2.0, 2.0, 1.0, 2.0, 1.0)
 PAIR_OF = ((0, 1, 2), (1, 3, 4), (2, 4, 5))
 LANES = 128
+LONG = 10000000
 
 
 def filter_row(extent):
@@ -90,17 +91,12 @@
     return total
 
 
-def fetch(source, target, arrived):
-    copies = [pltpu.make_async_copy(source.at[k], target.at[k], arrived.at[k]) for k in range(source.shape[0])]
-    for copy in copies:
-        copy.start()
-    return copies
-
-
-def prepare_kernel(tables, strain_hbm, strain_ref, size_ref, size_ends_ref, arrived):
+def lanes_kernel(lane_ref):
+    lane_ref[...] = lax.broadcasted_iota(jnp.int32, lane_ref.shape, 1)
+
+
+def prepare_kernel(tables, lane_ref, strain_ref, size_ref, size_ends_ref):
     cells = tables.cells
-    for copy in fetch(strain_hbm, strain_ref, arrived):
-        copy.wait()
     for lanes in halves(strain_ref.shape[-1]):
         size = []
         for z in range(cells):
@@ -110,11 +106,6 @@
             size_ref[z, :, lanes] = size[z]
         for end, value in enumerate(tables.project(size)):
             size_ends_ref[end, :, lanes] = value
-
-
-def fetch_kernel(cot_hbm, size_ends_ref, cot_ref, arrived):
-    for copy in fetch(cot_hbm, cot_ref, arrived):
-        copy.wait()
 
 
 def products_of(v):
@@ -185,11 +176,8 @@
     sums_ref[...] = table
 
 
-def message_kernel(tables, smooth_ref, model_ref, sums_ref, other_sums_ref, dual_ref, message_ref, pair_ref):
+def message_kernel(tables, smooth_ref, model_ref, dual_ref, message_ref):
     cells = tables.cells
-    pair_sums = sums_ref[...] + other_sums_ref[...]
-    pair_ref[...] = pair_sums
-    message_ref[18, 0:8, 0:LANES] = pair_sums
     for lanes in halves(model_ref.shape[-1]):
         model = [[model_ref[k, z, :, lanes] for z in range(cells)] for k in range(6)]
         smooth_v = [[smooth_ref[a, z, :, lanes] for z in range(cells)] for a in range(3)]
@@ -262,11 +250,11 @@
     peers = tables.devices - 1
     cells = tables.cells
     v_ref, leonard_ref, model_ref, parts_ref, bins_ref = refs[:5]
-    pair_ref = refs[5]
-    near_refs = refs[6 : 6 + count]
-    far_message_refs = refs[6 + count : 6 + count + peers]
-    residual_hbm, grad_hbm, residual_ref, grad_ref, left = refs[6 + count + peers :]
-    total = sum_up([pair_ref[...]] + [ref[18, 0:8, 0:LANES] for ref in far_message_refs])
+    pair_refs = refs[5 : 6 + peers]
+    near_refs = refs[6 + peers : 6 + peers + count]
+    far_message_refs = refs[6 + peers + count : 6 + 2 * peers + count]
+    residual_hbm, grad_hbm, residual_ref, grad_ref, left = refs[6 + 2 * peers + count :]
+    total = sum_up([ref[...] for ref in pair_refs])
     near = sum_up([ref[...] for ref in near_refs])
     if turning:
         place = lax.axis_index("stream")
@@ -374,48 +362,31 @@
     bins = jnp.broadcast_to(row_bins[:, None], (rows, LANES))
     far_v = [from_ahead(velocity, shift) for shift in range(1, span)]
     work = cells * rows * width
-    near_strain, size, size_ends = call(
-        functools.partial(prepare_kernel, tables),
-        [shaped(6, cells), shaped(cells), shaped(2)],
-        40 * work,
-        pltpu.with_memory_space_constraint(strain, pltpu.HBM),
-        in_specs=[REMAIN],
-        scratch=[pltpu.SemaphoreType.DMA((6,))],
-    )
+    (lane,) = call(lanes_kernel, [pltpu.VMEM((rows, LANES), jnp.int32)], LONG * work)
+    size, size_ends = call(
+        functools.partial(prepare_kernel, tables), [shaped(cells), shaped(2)], LONG * work, lane, strain
+    )
+    size_ends, sent_cot = lax.optimization_barrier((size_ends, cotangent))
     far_size = [from_ahead(size_ends, shift) for shift in range(1, span)]
-    (near_cot,) = call(
-        fetch_kernel,
-        [shaped(6, cells)],
-        work,
-        pltpu.with_memory_space_constraint(cotangent, pltpu.HBM),
-        size_ends,
-        in_specs=[REMAIN, WHOLE],
-        scratch=[pltpu.SemaphoreType.DMA((6,))],
-    )
-    far_cot = [from_ahead(near_cot, shift) for shift in range(1, span)]
+    far_cot = [from_ahead(sent_cot, shift) for shift in range(1, span)]
     table = pltpu.VMEM((8, LANES), jnp.float32)
     smooth, leonard, model, sums = call(
         functools.partial(forward_kernel, tables),
         [shaped(3, cells), shaped(6, cells), shaped(6, cells), table],
-        100000 * work,
+        LONG * work,
         velocity,
-        near_strain,
-        near_cot,
+        strain,
+        cotangent,
         size,
         bins,
         *far_v,
         *far_size,
     )
     other_sums = from_source(sums, 0, lambda j: j ^ 1)
-    dual, message, pair_sums = call(
-        functools.partial(message_kernel, tables),
-        [shaped(3, cells), shaped(19), table],
-        100 * work,
-        smooth,
-        model,
-        sums,
-        other_sums,
-    )
+    dual, message = call(
+        functools.partial(message_kernel, tables), [shaped(3, cells), shaped(18)], 100 * work, smooth, model
+    )
+    pair_sums = sums + other_sums
     far_message = [from_ahead(message, shift) for shift in range(1, span)]
     most_rows = 2 * rows * stream // NBINS
     reach = -(-(most_rows - 1) // rows)
@@ -425,13 +396,14 @@
     else:
         steps = range(1, -(-reach // 2) + 1)
         sources = [functools.partial(lambda j, away: j + away, away=2 * step * way) for step in steps for way in (1, -1)]
+    far_pairs = [from_ahead(pair_sums, shift) for shift in range(1, span)]
     near_sums = [from_source(pair_sums, shift, source) for shift in range(span) for source in sources]
     (parts,) = call(
         functools.partial(local_kernel, tables),
         [shaped(12, cells)],
-        500 * work,
+        LONG * work,
         velocity,
-        near_cot,
+        cotangent,
         smooth,
         leonard,
         model,
@@ -451,6 +423,7 @@
             parts,
             bins,
             pair_sums,
+            *far_pairs,
             *near_sums,
             *far_message,
             out_specs=[REMAIN] * 2,

time: 17.5 us -> 18.7 us (1.069)
  the two profiles are of different devices: /device:TPU:0 before, /device:TPU:8 now
where the time goes in v5:
time: 18.7 us; the launch traced here: 18.5 us
  starting transfers between devices  10.1 us (54%)
  waiting for transfers between devices  3.97 us (21%)
  Pallas kernels  3.67 us (20%)
  between operations  0.7 us (4%)
    ppermute x5, starting transfers between devices, from_ahead(): lax.ppermute(values, 'span', [((i + shift) % peers, i) for i in range(pee...  6.57 us
    pallas_call x6, Pallas kernels, call(): pl.pallas_call(kernel, out_shape=outs, in_specs=in_specs or [WHOLE] * len...  3.67 us
    ppermute x3, starting transfers between devices, from_source(): return lax.ppermute(values, ('span', 'stream'), pairs)  3.52 us
    ppermute x5, waiting for transfers between devices, from_ahead(): lax.ppermute(values, 'span', [((i + shift) % peers, i) for i in range(pee...  2.02 us
    ppermute x3, waiting for transfers between devices, from_source(): return lax.ppermute(values, ('span', 'stream'), pairs)  1.95 us
  transfers between devices with their start and end apart: 8, of which 2 were waited for; matrix products, arithmetic and copies ran while one was open for 0% of the time, Pallas kernels for 15%

profile of v5, /device:TPU:8, one launch (start us, length us, event | category | flops | bytes accessed | tf_op | source)
XLA Modules:
  0.0 18.5 jit_solution(11873865369334633644)
XLA Ops:
  0.6 0.0 copy-start.1
  0.6 1.6 %collective-permute-start = (f32[3,4,8,256]{3,2,1,0:T(8,128)}, f32[3,4,8,256]{3,2,1,0:T(8,128)}, u32[]{:S(2)}, u32[]{:S(2)}) collective-permute-start(f32[3,4,8,256]{3,2,1,0:T(8,128)} %refs_0_.5), channel_id=1, source_target_pairs={{16,0},{0,16},{17,1},{1,17},{18,2},{2,18},{19,3},{3,19},{20,4},{4,... | collective-permute-start | bytes 294920 | tf_op jit(solution)/shard_map/ppermute | solution.py:331
  2.2 0.0 copy-done.1
  2.2 0.0 copy-start.2
  2.2 0.0 copy-start
  2.3 0.0 copy-start.3
  2.3 0.9 %collective-permute-start.1 = (f32[2,8,256]{2,1,0:T(8,128)S(1)}, f32[2,8,256]{2,1,0:T(8,128)S(1)}, u32[]{:S(2)}, u32[]{:S(2)}) collective-permute-start(f32[2,8,256]{2,1,0:T(8,128)S(1)} %get-tuple-element.14), channel_id=1, source_target_pairs={{16,0},{0,16},{17,1},{1,17},{18,2},{2,18},{19,3},{3,19},{20,4},{4,... | collective-permute-start | bytes 49160 | tf_op jit(solution)/shard_map/ppermute | solution.py:331
  3.2 0.0 copy-done.2
  3.2 1.2 %collective-permute-start.2 = (f32[6,4,8,256]{3,2,1,0:T(8,128)S(1)}, f32[6,4,8,256]{3,2,1,0:T(8,128)S(1)}, u32[]{:S(2)}, u32[]{:S(2)}) collective-permute-start(f32[6,4,8,256]{3,2,1,0:T(8,128)S(1)} %copy-done.2), channel_id=1, source_target_pairs={{16,0},{0,16},{17,1},{1,17},{18,2},{2,18},{19,3},{3,19},{20,4},{4,... | collective-permute-start | bytes 589832 | tf_op jit(solution)/shard_map/ppermute | solution.py:331
  4.4 2.0 %collective-permute-done.1.refs_6_ = f32[2,8,256]{2,1,0:T(8,128)S(1)} collective-permute-done((f32[2,8,256]{2,1,0:T(8,128)S(1)}, f32[2,8,256]{2,1,0:T(8,128)S(1)}, u32[]{:S(2)}, u32[]{:S(2)}) %collective-permute-start.1) | collective-permute-done | bytes 16416 | tf_op jit(solution)/shard_map/ppermute | solution.py:331
  6.4 0.0 collective-permute-done.refs_5_.refs_6_
  6.4 0.0 copy-done.3
  6.4 0.1 broadcast_in_dim.2.refs_4_
  6.5 0.0 copy-done
  6.5 1.2 %shard_map.61 = (f32[3,4,8,256]{3,2,1,0:T(8,128)S(1)}, f32[6,4,8,256]{3,2,1,0:T(8,128)S(1)}, f32[6,4,8,256]{3,2,1,0:T(8,128)S(1)}, f32[8,128]{1,0:T(8,128)S(1)}) custom-call(f32[3,4,8,256]{3,2,1,0:T(8,128)S(1)} %copy-done, f32[6,4,8,256]{3,2,1,0:T(8,128)S(1)} %copy-done.1, f32[6,4,8,256]{3,2,1,0:T(8,128)S(1)} %copy-done.2, ...), custom_call_target="tpu_custom_call" | custom-call | flops 81920000000 | bytes 1138688 | tf_op jit(solution)/shard_map/pallas_call | solution.py:318
  7.8 0.0 collective-permute-start.3
  7.9 1.8 %collective-permute-start.7 = (f32[18,8,256]{2,1,0:T(8,128)S(1)}, f32[18,8,256]{2,1,0:T(8,128)S(1)}, u32[]{:S(2)}, u32[]{:S(2)}) collective-permute-start(f32[18,8,256]{2,1,0:T(8,128)S(1)} %get-tuple-element.21), channel_id=1, source_target_pairs={{16,0},{0,16},{17,1},{1,17},{18,2},{2,18},{19,3},{3,19},{20,4},{4,... | collective-permute-start | bytes 442376 | tf_op jit(solution)/shard_map/ppermute | solution.py:331
  9.7 0.0 collective-permute-done.3
  9.7 1.0 %collective-permute-start.4 = (f32[8,128]{1,0:T(8,128)S(1)}, f32[8,128]{1,0:T(8,128)S(1)}, u32[]{:S(2)}, u32[]{:S(2)}) collective-permute-start(f32[8,128]{1,0:T(8,128)S(1)} %add.3.refs_5_), channel_id=1, source_target_pairs={{16,0},{0,16},{17,1},{1,17},{18,2},{2,18},{19,3},{3,19},{20,4},{4,... | collective-permute-start | bytes 12296 | tf_op jit(solution)/shard_map/ppermute | solution.py:331
  10.7 1.5 %collective-permute-start.5 = (f32[8,128]{1,0:T(8,128)S(1)}, f32[8,128]{1,0:T(8,128)S(1)}, u32[]{:S(2)}, u32[]{:S(2)}) collective-permute-start(f32[8,128]{1,0:T(8,128)S(1)} %add.3.refs_5_), channel_id=1, source_target_pairs={{1,0},{3,1},{0,2},{5,3},{2,4},{7,5},{4,6},{9,7},{6,8},{11,9},{8,10... | collective-permute-start | bytes 12296 | tf_op jit(solution)/shard_map/ppermute | solution.py:341
  12.2 2.0 %collective-permute-start.6 = (f32[8,128]{1,0:T(8,128)S(1)}, f32[8,128]{1,0:T(8,128)S(1)}, u32[]{:S(2)}, u32[]{:S(2)}) collective-permute-start(f32[8,128]{1,0:T(8,128)S(1)} %add.3.refs_5_), channel_id=1, source_target_pairs={{17,0},{19,1},{16,2},{21,3},{18,4},{23,5},{20,6},{25,7},{22,8},{27... | collective-permute-start | bytes 12296 | tf_op jit(solution)/shard_map/ppermute | solution.py:341
  14.2 0.0 collective-permute-done.2.refs_7_
  14.2 1.5 %shard_map.63.refs_3_ = f32[12,4,8,256]{3,2,1,0:T(8,128)S(1)} custom-call(f32[3,4,8,256]{3,2,1,0:T(8,128)S(1)} %copy-done, f32[6,4,8,256]{3,2,1,0:T(8,128)S(1)} %copy-done.2, f32[3,4,8,256]{3,2,1,0:T(8,128)S(1)} %get-tuple-element.17.smooth_ref.refs_2_, f32[6,4,8,256]{3,2,1,0:T(8,128)S(1)} %get-tuple-element.15.refs_3_.refs_1_, ...), custom_call_target="tpu_custom_call" | custom-call | flops 81920000000 | bytes 1572864 | tf_op jit(solution)/shard_map/pallas_call | solution.py:318
  15.7 0.0 collective-permute-done.4.refs_6_
  15.7 0.0 collective-permute-done.5.refs_7_
  15.7 1.9 %collective-permute-done.6.refs_8_ = f32[8,128]{1,0:T(8,128)S(1)} collective-permute-done((f32[8,128]{1,0:T(8,128)S(1)}, f32[8,128]{1,0:T(8,128)S(1)}, u32[]{:S(2)}, u32[]{:S(2)}) %collective-permute-start.6) | collective-permute-done | bytes 4128 | tf_op jit(solution)/shard_map/ppermute | solution.py:341
  17.6 0.0 collective-permute-done.7.refs_9_
  17.6 0.9 %shard_map.64 = (f32[6,4,8,256]{3,2,1,0:T(8,128)}, f32[3,4,8,256]{3,2,1,0:T(8,128)}) custom-call(f32[3,4,8,256]{3,2,1,0:T(8,128)S(1)} %copy-done, f32[6,4,8,256]{3,2,1,0:T(8,128)S(1)} %get-tuple-element.15.refs_3_.refs_1_, f32[6,4,8,256]{3,2,1,0:T(8,128)S(1)} %get-tuple-element.16.model_ref.refs_4_.refs_2_, f32[12,4,8,256]{3,2,1,0:T(8,128)S(1)} %shard_map.63.refs_3_, ...), custom_call_target="tpu_custom_call" | custom-call | flops 1638400 | bytes 1347584 | tf_op jit(solution)/shard_map/pallas_call | solution.py:318
  (4 shorter events, 0.1 us)
Async XLA Ops:
  0.6 1.6 %copy-start.1 = (f32[6,4,8,256]{3,2,1,0:T(8,128)S(1)}, f32[6,4,8,256]{3,2,1,0:T(8,128)}, u32[]{:S(2)}) copy-start(f32[6,4,8,256]{3,2,1,0:T(8,128)} %refs_1_.2) | copy-start | bytes 589828
  0.6 5.8 %collective-permute-start = (f32[3,4,8,256]{3,2,1,0:T(8,128)}, f32[3,4,8,256]{3,2,1,0:T(8,128)}, u32[]{:S(2)}, u32[]{:S(2)}) collective-permute-start(f32[3,4,8,256]{3,2,1,0:T(8,128)} %refs_0_.5), channel_id=1, source_target_pairs={{16,0},{0,16},{17,1},{1,17},{18,2},{2,18},{19,3},{3,19},{20,4},{4,... | collective-permute-start | bytes 294920 | tf_op jit(solution)/shard_map/ppermute | solution.py:331
  2.2 1.0 %copy-start.2 = (f32[6,4,8,256]{3,2,1,0:T(8,128)S(1)}, f32[6,4,8,256]{3,2,1,0:T(8,128)}, u32[]{:S(2)}) copy-start(f32[6,4,8,256]{3,2,1,0:T(8,128)} %refs_1_.3) | copy-start | bytes 589828
  2.2 4.3 %copy-start = (f32[3,4,8,256]{3,2,1,0:T(8,128)S(1)}, f32[3,4,8,256]{3,2,1,0:T(8,128)}, u32[]{:S(2)}) copy-start(f32[3,4,8,256]{3,2,1,0:T(8,128)} %refs_0_.5) | copy-start | bytes 294916
  2.3 4.2 %copy-start.3 = (s32[8]{0:T(128)S(1)}, s32[8]{0:T(128)}, u32[]{:S(2)}) copy-start(s32[8]{0:T(128)} %param.6) | copy-start | bytes 100
  2.3 4.1 %collective-permute-start.1 = (f32[2,8,256]{2,1,0:T(8,128)S(1)}, f32[2,8,256]{2,1,0:T(8,128)S(1)}, u32[]{:S(2)}, u32[]{:S(2)}) collective-permute-start(f32[2,8,256]{2,1,0:T(8,128)S(1)} %get-tuple-element.14), channel_id=1, source_target_pairs={{16,0},{0,16},{17,1},{1,17},{18,2},{2,18},{19,3},{3,19},{20,4},{4,... | collective-permute-start | bytes 49160 | tf_op jit(solution)/shard_map/ppermute | solution.py:331
  3.2 11.0 %collective-permute-start.2 = (f32[6,4,8,256]{3,2,1,0:T(8,128)S(1)}, f32[6,4,8,256]{3,2,1,0:T(8,128)S(1)}, u32[]{:S(2)}, u32[]{:S(2)}) collective-permute-start(f32[6,4,8,256]{3,2,1,0:T(8,128)S(1)} %copy-done.2), channel_id=1, source_target_pairs={{16,0},{0,16},{17,1},{1,17},{18,2},{2,18},{19,3},{3,19},{20,4},{4,... | collective-permute-start | bytes 589832 | tf_op jit(solution)/shard_map/ppermute | solution.py:331
  7.8 1.9 %collective-permute-start.3 = (f32[8,128]{1,0:T(8,128)S(1)}, f32[8,128]{1,0:T(8,128)S(1)}, u32[]{:S(2)}, u32[]{:S(2)}) collective-permute-start(f32[8,128]{1,0:T(8,128)S(1)} %get-tuple-element.20), channel_id=1, source_target_pairs={{1,0},{0,1},{3,2},{2,3},{5,4},{4,5},{7,6},{6,7},{9,8},{8,9},{11,10... | collective-permute-start | bytes 12296 | tf_op jit(solution)/shard_map/ppermute | solution.py:341
  7.9 9.8 %collective-permute-start.7 = (f32[18,8,256]{2,1,0:T(8,128)S(1)}, f32[18,8,256]{2,1,0:T(8,128)S(1)}, u32[]{:S(2)}, u32[]{:S(2)}) collective-permute-start(f32[18,8,256]{2,1,0:T(8,128)S(1)} %get-tuple-element.21), channel_id=1, source_target_pairs={{16,0},{0,16},{17,1},{1,17},{18,2},{2,18},{19,3},{3,19},{20,4},{4,... | collective-permute-start | bytes 442376 | tf_op jit(solution)/shard_map/ppermute | solution.py:331
  9.7 6.0 %collective-permute-start.4 = (f32[8,128]{1,0:T(8,128)S(1)}, f32[8,128]{1,0:T(8,128)S(1)}, u32[]{:S(2)}, u32[]{:S(2)}) collective-permute-start(f32[8,128]{1,0:T(8,128)S(1)} %add.3.refs_5_), channel_id=1, source_target_pairs={{16,0},{0,16},{17,1},{1,17},{18,2},{2,18},{19,3},{3,19},{20,4},{4,... | collective-permute-start | bytes 12296 | tf_op jit(solution)/shard_map/ppermute | solution.py:331
  10.7 4.9 %collective-permute-start.5 = (f32[8,128]{1,0:T(8,128)S(1)}, f32[8,128]{1,0:T(8,128)S(1)}, u32[]{:S(2)}, u32[]{:S(2)}) collective-permute-start(f32[8,128]{1,0:T(8,128)S(1)} %add.3.refs_5_), channel_id=1, source_target_pairs={{1,0},{3,1},{0,2},{5,3},{2,4},{7,5},{4,6},{9,7},{6,8},{11,9},{8,10... | collective-permute-start | bytes 12296 | tf_op jit(solution)/shard_map/ppermute | solution.py:341
  12.2 5.4 %collective-permute-start.6 = (f32[8,128]{1,0:T(8,128)S(1)}, f32[8,128]{1,0:T(8,128)S(1)}, u32[]{:S(2)}, u32[]{:S(2)}) collective-permute-start(f32[8,128]{1,0:T(8,128)S(1)} %add.3.refs_5_), channel_id=1, source_target_pairs={{17,0},{19,1},{16,2},{21,3},{18,4},{23,5},{20,6},{25,7},{22,8},{27... | collective-permute-start | bytes 12296 | tf_op jit(solution)/shard_map/ppermute | solution.py:341

commit v6 on v5

--- a/solution.py
+++ b/solution.py
@@ -18,7 +18,7 @@
 PAIR_WEIGHTS = (1.0, 2.0, 2.0, 1.0, 2.0, 1.0)
 PAIR_OF = ((0, 1, 2), (1, 3, 4), (2, 4, 5))
 LANES = 128
-LONG = 10000000
+LONG = 300000
 
 
 def filter_row(extent):

time: 18.7 us -> 17.8 us (0.952)
  Pallas kernels: 3.67 us -> 1.89 us
  waiting for transfers between devices: 3.97 us -> 4.87 us
    pallas_call x6, Pallas kernels: 3.67 us -> 1.89 us  [call(): pl.pallas_call(kernel, out_shape=outs, in_specs=in_specs or [WHOLE] * len...]
    ppermute x3, waiting for transfers between devices: 1.95 us -> 2.84 us  [from_source(): return lax.ppermute(values, ('span', 'stream'), pairs)]
  transfers between devices with their start and end apart: 8 -> 8, of which waited for: 2 -> 3; matrix products, arithmetic and copies ran while one was open for 0% -> 0% of each run, Pallas kernels for 15% -> 6%
where the time goes in v6:
time: 17.8 us; the launch traced here: 17.6 us
  starting transfers between devices  10.1 us (57%)
  waiting for transfers between devices  4.87 us (27%)
  Pallas kernels  1.89 us (11%)
  between operations  0.69 us (4%)
    ppermute x5, starting transfers between devices, from_ahead(): lax.ppermute(values, 'span', [((i + shift) % peers, i) for i in range(pee...  6.57 us
    ppermute x3, starting transfers between devices, from_source(): return lax.ppermute(values, ('span', 'stream'), pairs)  3.52 us
    ppermute x3, waiting for transfers between devices, from_source(): return lax.ppermute(values, ('span', 'stream'), pairs)  2.84 us
    ppermute x5, waiting for transfers between devices, from_ahead(): lax.ppermute(values, 'span', [((i + shift) % peers, i) for i in range(pee...  2.02 us
    pallas_call x6, Pallas kernels, call(): pl.pallas_call(kernel, out_shape=outs, in_specs=in_specs or [WHOLE] * len...  1.89 us
  transfers between devices with their start and end apart: 8, of which 3 were waited for; matrix products, arithmetic and copies ran while one was open for 0% of the time, Pallas kernels for 6%

profile of v6, /device:TPU:8, one launch (start us, length us, event | category | flops | bytes accessed | tf_op | source)
XLA Modules:
  0.0 17.6 jit_solution(14105400378978978795)
XLA Ops:
  0.6 0.0 copy-start.1
  0.6 1.6 %collective-permute-start = (f32[3,4,8,256]{3,2,1,0:T(8,128)}, f32[3,4,8,256]{3,2,1,0:T(8,128)S(1)}, u32[]{:S(2)}, u32[]{:S(2)}) collective-permute-start(f32[3,4,8,256]{3,2,1,0:T(8,128)} %refs_0_.5), channel_id=1, source_target_pairs={{16,0},{0,16},{17,1},{1,17},{18,2},{2,18},{19,3},{3,19},{20,4},{4,... | collective-permute-start | bytes 294920 | tf_op jit(solution)/shard_map/ppermute | solution.py:331
  2.2 0.0 copy-done.1
  2.2 0.0 copy-start.2
  2.2 0.0 copy-start
  2.3 0.0 copy-start.3
  2.3 0.9 %collective-permute-start.1 = (f32[2,8,256]{2,1,0:T(8,128)S(1)}, f32[2,8,256]{2,1,0:T(8,128)S(1)}, u32[]{:S(2)}, u32[]{:S(2)}) collective-permute-start(f32[2,8,256]{2,1,0:T(8,128)S(1)} %get-tuple-element.14), channel_id=1, source_target_pairs={{16,0},{0,16},{17,1},{1,17},{18,2},{2,18},{19,3},{3,19},{20,4},{4,... | collective-permute-start | bytes 49160 | tf_op jit(solution)/shard_map/ppermute | solution.py:331
  3.2 0.0 copy-done.2
  3.2 1.2 %collective-permute-start.2 = (f32[6,4,8,256]{3,2,1,0:T(8,128)S(1)}, f32[6,4,8,256]{3,2,1,0:T(8,128)S(1)}, u32[]{:S(2)}, u32[]{:S(2)}) collective-permute-start(f32[6,4,8,256]{3,2,1,0:T(8,128)S(1)} %copy-done.2), channel_id=1, source_target_pairs={{16,0},{0,16},{17,1},{1,17},{18,2},{2,18},{19,3},{3,19},{20,4},{4,... | collective-permute-start | bytes 589832 | tf_op jit(solution)/shard_map/ppermute | solution.py:331
  4.4 2.0 %collective-permute-done.1.refs_6_ = f32[2,8,256]{2,1,0:T(8,128)S(1)} collective-permute-done((f32[2,8,256]{2,1,0:T(8,128)S(1)}, f32[2,8,256]{2,1,0:T(8,128)S(1)}, u32[]{:S(2)}, u32[]{:S(2)}) %collective-permute-start.1) | collective-permute-done | bytes 16416 | tf_op jit(solution)/shard_map/ppermute | solution.py:331
  6.4 0.0 collective-permute-done.refs_5_.refs_6_
  6.4 0.0 copy-done.3
  6.4 0.1 broadcast_in_dim.2.refs_4_
  6.5 0.0 copy-done
  6.5 0.4 %shard_map.61 = (f32[3,4,8,256]{3,2,1,0:T(8,128)S(1)}, f32[6,4,8,256]{3,2,1,0:T(8,128)S(1)}, f32[6,4,8,256]{3,2,1,0:T(8,128)S(1)}, f32[8,128]{1,0:T(8,128)S(1)}) custom-call(f32[3,4,8,256]{3,2,1,0:T(8,128)S(1)} %copy-done, f32[6,4,8,256]{3,2,1,0:T(8,128)S(1)} %copy-done.1, f32[6,4,8,256]{3,2,1,0:T(8,128)S(1)} %copy-done.2, ...), custom_call_target="tpu_custom_call" | custom-call | flops 2457600000 | bytes 1138688 | tf_op jit(solution)/shard_map/pallas_call | solution.py:318
  6.9 0.0 collective-permute-start.3
  7.0 1.8 %collective-permute-start.7 = (f32[18,8,256]{2,1,0:T(8,128)S(1)}, f32[18,8,256]{2,1,0:T(8,128)S(1)}, u32[]{:S(2)}, u32[]{:S(2)}) collective-permute-start(f32[18,8,256]{2,1,0:T(8,128)S(1)} %get-tuple-element.21), channel_id=1, source_target_pairs={{16,0},{0,16},{17,1},{1,17},{18,2},{2,18},{19,3},{3,19},{20,4},{4,... | collective-permute-start | bytes 442376 | tf_op jit(solution)/shard_map/ppermute | solution.py:331
  8.8 0.0 collective-permute-done.3
  8.8 1.0 %collective-permute-start.4 = (f32[8,128]{1,0:T(8,128)S(1)}, f32[8,128]{1,0:T(8,128)S(1)}, u32[]{:S(2)}, u32[]{:S(2)}) collective-permute-start(f32[8,128]{1,0:T(8,128)S(1)} %add.3.refs_5_), channel_id=1, source_target_pairs={{16,0},{0,16},{17,1},{1,17},{18,2},{2,18},{19,3},{3,19},{20,4},{4,... | collective-permute-start | bytes 12296 | tf_op jit(solution)/shard_map/ppermute | solution.py:331
  9.8 1.5 %collective-permute-start.5 = (f32[8,128]{1,0:T(8,128)S(1)}, f32[8,128]{1,0:T(8,128)S(1)}, u32[]{:S(2)}, u32[]{:S(2)}) collective-permute-start(f32[8,128]{1,0:T(8,128)S(1)} %add.3.refs_5_), channel_id=1, source_target_pairs={{1,0},{3,1},{0,2},{5,3},{2,4},{7,5},{4,6},{9,7},{6,8},{11,9},{8,10... | collective-permute-start | bytes 12296 | tf_op jit(solution)/shard_map/ppermute | solution.py:341
  11.3 2.0 %collective-permute-start.6 = (f32[8,128]{1,0:T(8,128)S(1)}, f32[8,128]{1,0:T(8,128)S(1)}, u32[]{:S(2)}, u32[]{:S(2)}) collective-permute-start(f32[8,128]{1,0:T(8,128)S(1)} %add.3.refs_5_), channel_id=1, source_target_pairs={{17,0},{19,1},{16,2},{21,3},{18,4},{23,5},{20,6},{25,7},{22,8},{27... | collective-permute-start | bytes 12296 | tf_op jit(solution)/shard_map/ppermute | solution.py:341
  13.3 0.0 collective-permute-done.2.refs_7_
  13.3 0.6 %shard_map.63.refs_3_ = f32[12,4,8,256]{3,2,1,0:T(8,128)S(1)} custom-call(f32[3,4,8,256]{3,2,1,0:T(8,128)S(1)} %copy-done, f32[6,4,8,256]{3,2,1,0:T(8,128)S(1)} %copy-done.2, f32[3,4,8,256]{3,2,1,0:T(8,128)S(1)} %get-tuple-element.17.smooth_ref.refs_2_, f32[6,4,8,256]{3,2,1,0:T(8,128)S(1)} %get-tuple-element.15.refs_3_.refs_1_, ...), custom_call_target="tpu_custom_call" | custom-call | flops 2457600000 | bytes 1572864 | tf_op jit(solution)/shard_map/pallas_call | solution.py:318
  13.9 0.0 collective-permute-done.4.refs_6_
  13.9 0.4 %collective-permute-done.5.refs_7_ = f32[8,128]{1,0:T(8,128)S(1)} collective-permute-done((f32[8,128]{1,0:T(8,128)S(1)}, f32[8,128]{1,0:T(8,128)S(1)}, u32[]{:S(2)}, u32[]{:S(2)}) %collective-permute-start.5) | collective-permute-done | bytes 4128 | tf_op jit(solution)/shard_map/ppermute | solution.py:341
  14.4 2.4 %collective-permute-done.6.refs_8_ = f32[8,128]{1,0:T(8,128)S(1)} collective-permute-done((f32[8,128]{1,0:T(8,128)S(1)}, f32[8,128]{1,0:T(8,128)S(1)}, u32[]{:S(2)}, u32[]{:S(2)}) %collective-permute-start.6) | collective-permute-done | bytes 4128 | tf_op jit(solution)/shard_map/ppermute | solution.py:341
  16.7 0.0 collective-permute-done.7.refs_9_
  16.7 0.9 %shard_map.64 = (f32[6,4,8,256]{3,2,1,0:T(8,128)}, f32[3,4,8,256]{3,2,1,0:T(8,128)}) custom-call(f32[3,4,8,256]{3,2,1,0:T(8,128)S(1)} %copy-done, f32[6,4,8,256]{3,2,1,0:T(8,128)S(1)} %get-tuple-element.15.refs_3_.refs_1_, f32[6,4,8,256]{3,2,1,0:T(8,128)S(1)} %get-tuple-element.16.model_ref.refs_4_.refs_2_, f32[12,4,8,256]{3,2,1,0:T(8,128)S(1)} %shard_map.63.refs_3_, ...), custom_call_target="tpu_custom_call" | custom-call | flops 1638400 | bytes 1347584 | tf_op jit(solution)/shard_map/pallas_call | solution.py:318
  (4 shorter events, 0.1 us)
Async XLA Ops:
  0.6 1.6 %copy-start.1 = (f32[6,4,8,256]{3,2,1,0:T(8,128)S(1)}, f32[6,4,8,256]{3,2,1,0:T(8,128)}, u32[]{:S(2)}) copy-start(f32[6,4,8,256]{3,2,1,0:T(8,128)} %refs_1_.2) | copy-start | bytes 589828
  0.6 5.8 %collective-permute-start = (f32[3,4,8,256]{3,2,1,0:T(8,128)}, f32[3,4,8,256]{3,2,1,0:T(8,128)S(1)}, u32[]{:S(2)}, u32[]{:S(2)}) collective-permute-start(f32[3,4,8,256]{3,2,1,0:T(8,128)} %refs_0_.5), channel_id=1, source_target_pairs={{16,0},{0,16},{17,1},{1,17},{18,2},{2,18},{19,3},{3,19},{20,4},{4,... | collective-permute-start | bytes 294920 | tf_op jit(solution)/shard_map/ppermute | solution.py:331
  2.2 1.0 %copy-start.2 = (f32[6,4,8,256]{3,2,1,0:T(8,128)S(1)}, f32[6,4,8,256]{3,2,1,0:T(8,128)}, u32[]{:S(2)}) copy-start(f32[6,4,8,256]{3,2,1,0:T(8,128)} %refs_1_.3) | copy-start | bytes 589828
  2.2 4.3 %copy-start = (f32[3,4,8,256]{3,2,1,0:T(8,128)S(1)}, f32[3,4,8,256]{3,2,1,0:T(8,128)}, u32[]{:S(2)}) copy-start(f32[3,4,8,256]{3,2,1,0:T(8,128)} %refs_0_.5) | copy-start | bytes 294916
  2.3 4.2 %copy-start.3 = (s32[8]{0:T(128)S(1)}, s32[8]{0:T(128)}, u32[]{:S(2)}) copy-start(s32[8]{0:T(128)} %param.6) | copy-start | bytes 100
  2.3 4.1 %collective-permute-start.1 = (f32[2,8,256]{2,1,0:T(8,128)S(1)}, f32[2,8,256]{2,1,0:T(8,128)S(1)}, u32[]{:S(2)}, u32[]{:S(2)}) collective-permute-start(f32[2,8,256]{2,1,0:T(8,128)S(1)} %get-tuple-element.14), channel_id=1, source_target_pairs={{16,0},{0,16},{17,1},{1,17},{18,2},{2,18},{19,3},{3,19},{20,4},{4,... | collective-permute-start | bytes 49160 | tf_op jit(solution)/shard_map/ppermute | solution.py:331
  3.2 10.1 %collective-permute-start.2 = (f32[6,4,8,256]{3,2,1,0:T(8,128)S(1)}, f32[6,4,8,256]{3,2,1,0:T(8,128)S(1)}, u32[]{:S(2)}, u32[]{:S(2)}) collective-permute-start(f32[6,4,8,256]{3,2,1,0:T(8,128)S(1)} %copy-done.2), channel_id=1, source_target_pairs={{16,0},{0,16},{17,1},{1,17},{18,2},{2,18},{19,3},{3,19},{20,4},{4,... | collective-permute-start | bytes 589832 | tf_op jit(solution)/shard_map/ppermute | solution.py:331
  6.9 1.9 %collective-permute-start.3 = (f32[8,128]{1,0:T(8,128)S(1)}, f32[8,128]{1,0:T(8,128)S(1)}, u32[]{:S(2)}, u32[]{:S(2)}) collective-permute-start(f32[8,128]{1,0:T(8,128)S(1)} %get-tuple-element.20), channel_id=1, source_target_pairs={{1,0},{0,1},{3,2},{2,3},{5,4},{4,5},{7,6},{6,7},{9,8},{8,9},{11,10... | collective-permute-start | bytes 12296 | tf_op jit(solution)/shard_map/ppermute | solution.py:341
  7.0 9.8 %collective-permute-start.7 = (f32[18,8,256]{2,1,0:T(8,128)S(1)}, f32[18,8,256]{2,1,0:T(8,128)S(1)}, u32[]{:S(2)}, u32[]{:S(2)}) collective-permute-start(f32[18,8,256]{2,1,0:T(8,128)S(1)} %get-tuple-element.21), channel_id=1, source_target_pairs={{16,0},{0,16},{17,1},{1,17},{18,2},{2,18},{19,3},{3,19},{20,4},{4,... | collective-permute-start | bytes 442376 | tf_op jit(solution)/shard_map/ppermute | solution.py:331
  8.8 5.1 %collective-permute-start.4 = (f32[8,128]{1,0:T(8,128)S(1)}, f32[8,128]{1,0:T(8,128)S(1)}, u32[]{:S(2)}, u32[]{:S(2)}) collective-permute-start(f32[8,128]{1,0:T(8,128)S(1)} %add.3.refs_5_), channel_id=1, source_target_pairs={{16,0},{0,16},{17,1},{1,17},{18,2},{2,18},{19,3},{3,19},{20,4},{4,... | collective-permute-start | bytes 12296 | tf_op jit(solution)/shard_map/ppermute | solution.py:331
  9.8 4.5 %collective-permute-start.5 = (f32[8,128]{1,0:T(8,128)S(1)}, f32[8,128]{1,0:T(8,128)S(1)}, u32[]{:S(2)}, u32[]{:S(2)}) collective-permute-start(f32[8,128]{1,0:T(8,128)S(1)} %add.3.refs_5_), channel_id=1, source_target_pairs={{1,0},{3,1},{0,2},{5,3},{2,4},{7,5},{4,6},{9,7},{6,8},{11,9},{8,10... | collective-permute-start | bytes 12296 | tf_op jit(solution)/shard_map/ppermute | solution.py:341
  11.3 5.4 %collective-permute-start.6 = (f32[8,128]{1,0:T(8,128)S(1)}, f32[8,128]{1,0:T(8,128)S(1)}, u32[]{:S(2)}, u32[]{:S(2)}) collective-permute-start(f32[8,128]{1,0:T(8,128)S(1)} %add.3.refs_5_), channel_id=1, source_target_pairs={{17,0},{19,1},{16,2},{21,3},{18,4},{23,5},{20,6},{25,7},{22,8},{27... | collective-permute-start | bytes 12296 | tf_op jit(solution)/shard_map/ppermute | solution.py:341

commit v7 on v6

--- a/solution.py
+++ b/solution.py
@@ -250,8 +250,8 @@
     peers = tables.devices - 1
     cells = tables.cells
     v_ref, leonard_ref, model_ref, parts_ref, bins_ref = refs[:5]
-    pair_refs = refs[5 : 6 + peers]
-    near_refs = refs[6 + peers : 6 + peers + count]
+    near_refs = refs[5 : 5 + count]
+    pair_refs = refs[5 + count : 6 + peers + count]
     far_message_refs = refs[6 + peers + count : 6 + 2 * peers + count]
     residual_hbm, grad_hbm, residual_ref, grad_ref, left = refs[6 + 2 * peers + count :]
     total = sum_up([ref[...] for ref in pair_refs])
@@ -280,7 +280,7 @@
                     leonard_ref[k, z, :, lanes] - coefficient * model_ref[k, z, :, lanes]
                 )
         copies.append(pltpu.make_async_copy(residual_ref.at[k], residual_hbm.at[k], left.at[k]))
-        copies[k].start()
+        copies[k].start(priority=k % 2)
     for lanes in halves(v_ref.shape[-1]):
         v = [[v_ref[a, z, :, lanes] for z in range(cells)] for a in range(3)]
         from_model = [[] for _ in range(6)]
@@ -304,7 +304,7 @@
                 )
     for a in range(3):
         copies.append(pltpu.make_async_copy(grad_ref.at[a], grad_hbm.at[a], left.at[6 + a]))
-        copies[6 + a].start()
+        copies[6 + a].start(priority=a % 2)
     for copy in copies:
         copy.wait()
 
@@ -396,8 +396,8 @@
     else:
         steps = range(1, -(-reach // 2) + 1)
         sources = [functools.partial(lambda j, away: j + away, away=2 * step * way) for step in steps for way in (1, -1)]
+    near_sums = [from_source(pair_sums, shift, source) for shift in reversed(range(span)) for source in sources]
     far_pairs = [from_ahead(pair_sums, shift) for shift in range(1, span)]
-    near_sums = [from_source(pair_sums, shift, source) for shift in range(span) for source in sources]
     (parts,) = call(
         functools.partial(local_kernel, tables),
         [shaped(12, cells)],
@@ -422,9 +422,9 @@
             model,
             parts,
             bins,
+            *near_sums,
             pair_sums,
             *far_pairs,
-            *near_sums,
             *far_message,
             out_specs=[REMAIN] * 2,
             scratch=[pltpu.VMEM(x.shape, x.dtype) for x in outs] + [pltpu.SemaphoreType.DMA((9,))],

time: 17.8 us -> 18.4 us (1.034)
  the two profiles are of different devices: /device:TPU:8 before, /device:TPU:0 now
where the time goes in v7:
time: 18.4 us; the launch traced here: 18.3 us
  starting transfers between devices  11.7 us (64%)
  waiting for transfers between devices  3.86 us (21%)
  Pallas kernels  1.89 us (10%)
  between operations  0.7 us (4%)
    ppermute x5, starting transfers between devices, from_ahead(): lax.ppermute(values, 'span', [((i + shift) % peers, i) for i in range(pee...  8.17 us
    ppermute x5, waiting for transfers between devices, from_ahead(): lax.ppermute(values, 'span', [((i + shift) % peers, i) for i in range(pee...  3.85 us
    ppermute x3, starting transfers between devices, from_source(): return lax.ppermute(values, ('span', 'stream'), pairs)  3.55 us
    pallas_call x6, Pallas kernels, call(): pl.pallas_call(kernel, out_shape=outs, in_specs=in_specs or [WHOLE] * len...  1.89 us
  transfers between devices with their start and end apart: 8, of which 2 were waited for; matrix products, arithmetic and copies ran while one was open for 0% of the time, Pallas kernels for 6%

profile of v7, /device:TPU:0, one launch (start us, length us, event | category | flops | bytes accessed | tf_op | source)
XLA Modules:
  0.0 18.3 jit_solution(11035250372304243039)
XLA Ops:
  0.6 0.0 copy-start.1
  0.6 3.0 %collective-permute-start = (f32[3,4,8,256]{3,2,1,0:T(8,128)}, f32[3,4,8,256]{3,2,1,0:T(8,128)S(1)}, u32[]{:S(2)}, u32[]{:S(2)}) collective-permute-start(f32[3,4,8,256]{3,2,1,0:T(8,128)} %refs_0_.5), channel_id=1, source_target_pairs={{16,0},{0,16},{17,1},{1,17},{18,2},{2,18},{19,3},{3,19},{20,4},{4,... | collective-permute-start | bytes 294920 | tf_op jit(solution)/shard_map/ppermute | solution.py:331
  3.7 0.0 copy-done.1
  3.7 0.0 copy-start.2
  3.7 0.0 copy-start
  3.7 0.0 copy-start.3
  3.7 0.9 %collective-permute-start.1 = (f32[2,8,256]{2,1,0:T(8,128)S(1)}, f32[2,8,256]{2,1,0:T(8,128)S(1)}, u32[]{:S(2)}, u32[]{:S(2)}) collective-permute-start(f32[2,8,256]{2,1,0:T(8,128)S(1)} %get-tuple-element.14), channel_id=1, source_target_pairs={{16,0},{0,16},{17,1},{1,17},{18,2},{2,18},{19,3},{3,19},{20,4},{4,... | collective-permute-start | bytes 49160 | tf_op jit(solution)/shard_map/ppermute | solution.py:331
  4.6 0.0 copy-done.2
  4.6 1.2 %collective-permute-start.2 = (f32[6,4,8,256]{3,2,1,0:T(8,128)S(1)}, f32[6,4,8,256]{3,2,1,0:T(8,128)S(1)}, u32[]{:S(2)}, u32[]{:S(2)}) collective-permute-start(f32[6,4,8,256]{3,2,1,0:T(8,128)S(1)} %copy-done.2), channel_id=1, source_target_pairs={{16,0},{0,16},{17,1},{1,17},{18,2},{2,18},{19,3},{3,19},{20,4},{4,... | collective-permute-start | bytes 589832 | tf_op jit(solution)/shard_map/ppermute | solution.py:331
  5.9 1.8 %collective-permute-done.1.refs_6_ = f32[2,8,256]{2,1,0:T(8,128)S(1)} collective-permute-done((f32[2,8,256]{2,1,0:T(8,128)S(1)}, f32[2,8,256]{2,1,0:T(8,128)S(1)}, u32[]{:S(2)}, u32[]{:S(2)}) %collective-permute-start.1) | collective-permute-done | bytes 16416 | tf_op jit(solution)/shard_map/ppermute | solution.py:331
  7.7 0.0 collective-permute-done.refs_5_.refs_6_
  7.7 0.0 copy-done.3
  7.7 0.1 broadcast_in_dim.2.refs_4_
  7.8 0.0 copy-done
  7.8 0.4 %shard_map.61 = (f32[3,4,8,256]{3,2,1,0:T(8,128)S(1)}, f32[6,4,8,256]{3,2,1,0:T(8,128)S(1)}, f32[6,4,8,256]{3,2,1,0:T(8,128)S(1)}, f32[8,128]{1,0:T(8,128)S(1)}) custom-call(f32[3,4,8,256]{3,2,1,0:T(8,128)S(1)} %copy-done, f32[6,4,8,256]{3,2,1,0:T(8,128)S(1)} %copy-done.1, f32[6,4,8,256]{3,2,1,0:T(8,128)S(1)} %copy-done.2, ...), custom_call_target="tpu_custom_call" | custom-call | flops 2457600000 | bytes 1138688 | tf_op jit(solution)/shard_map/pallas_call | solution.py:318
  8.1 0.0 collective-permute-start.3
  8.2 2.0 %collective-permute-start.7 = (f32[18,8,256]{2,1,0:T(8,128)S(1)}, f32[18,8,256]{2,1,0:T(8,128)S(1)}, u32[]{:S(2)}, u32[]{:S(2)}) collective-permute-start(f32[18,8,256]{2,1,0:T(8,128)S(1)} %get-tuple-element.21), channel_id=1, source_target_pairs={{16,0},{0,16},{17,1},{1,17},{18,2},{2,18},{19,3},{3,19},{20,4},{4,... | collective-permute-start | bytes 442376 | tf_op jit(solution)/shard_map/ppermute | solution.py:331
  10.3 0.0 collective-permute-done.3
  10.3 2.0 %collective-permute-start.4 = (f32[8,128]{1,0:T(8,128)S(1)}, f32[8,128]{1,0:T(8,128)S(1)}, u32[]{:S(2)}, u32[]{:S(2)}) collective-permute-start(f32[8,128]{1,0:T(8,128)S(1)} %add.3.refs_7_), channel_id=1, source_target_pairs={{17,0},{19,1},{16,2},{21,3},{18,4},{23,5},{20,6},{25,7},{22,8},{27... | collective-permute-start | bytes 12296 | tf_op jit(solution)/shard_map/ppermute | solution.py:341
  12.2 1.5 %collective-permute-start.5 = (f32[8,128]{1,0:T(8,128)S(1)}, f32[8,128]{1,0:T(8,128)S(1)}, u32[]{:S(2)}, u32[]{:S(2)}) collective-permute-start(f32[8,128]{1,0:T(8,128)S(1)} %add.3.refs_7_), channel_id=1, source_target_pairs={{1,0},{3,1},{0,2},{5,3},{2,4},{7,5},{4,6},{9,7},{6,8},{11,9},{8,10... | collective-permute-start | bytes 12296 | tf_op jit(solution)/shard_map/ppermute | solution.py:341
  13.8 1.0 %collective-permute-start.6 = (f32[8,128]{1,0:T(8,128)S(1)}, f32[8,128]{1,0:T(8,128)S(1)}, u32[]{:S(2)}, u32[]{:S(2)}) collective-permute-start(f32[8,128]{1,0:T(8,128)S(1)} %add.3.refs_7_), channel_id=1, source_target_pairs={{16,0},{0,16},{17,1},{1,17},{18,2},{2,18},{19,3},{3,19},{20,4},{4,... | collective-permute-start | bytes 12296 | tf_op jit(solution)/shard_map/ppermute | solution.py:331
  14.8 0.0 collective-permute-done.2.refs_7_
  14.8 0.6 %shard_map.63.refs_3_ = f32[12,4,8,256]{3,2,1,0:T(8,128)S(1)} custom-call(f32[3,4,8,256]{3,2,1,0:T(8,128)S(1)} %copy-done, f32[6,4,8,256]{3,2,1,0:T(8,128)S(1)} %copy-done.2, f32[3,4,8,256]{3,2,1,0:T(8,128)S(1)} %get-tuple-element.17.smooth_ref.refs_2_, f32[6,4,8,256]{3,2,1,0:T(8,128)S(1)} %get-tuple-element.15.refs_3_.refs_1_, ...), custom_call_target="tpu_custom_call" | custom-call | flops 2457600000 | bytes 1572864 | tf_op jit(solution)/shard_map/pallas_call | solution.py:318
  15.3 0.0 collective-permute-done.4.refs_5_
  15.3 0.0 collective-permute-done.5.refs_6_
  15.4 2.0 %collective-permute-done.6.refs_8_ = f32[8,128]{1,0:T(8,128)S(1)} collective-permute-done((f32[8,128]{1,0:T(8,128)S(1)}, f32[8,128]{1,0:T(8,128)S(1)}, u32[]{:S(2)}, u32[]{:S(2)}) %collective-permute-start.6) | collective-permute-done | bytes 4128 | tf_op jit(solution)/shard_map/ppermute | solution.py:331
  17.4 0.0 collective-permute-done.7.refs_9_
  17.4 0.9 %shard_map.64 = (f32[6,4,8,256]{3,2,1,0:T(8,128)}, f32[3,4,8,256]{3,2,1,0:T(8,128)}) custom-call(f32[3,4,8,256]{3,2,1,0:T(8,128)S(1)} %copy-done, f32[6,4,8,256]{3,2,1,0:T(8,128)S(1)} %get-tuple-element.15.refs_3_.refs_1_, f32[6,4,8,256]{3,2,1,0:T(8,128)S(1)} %get-tuple-element.16.model_ref.refs_4_.refs_2_, f32[12,4,8,256]{3,2,1,0:T(8,128)S(1)} %shard_map.63.refs_3_, ...), custom_call_target="tpu_custom_call" | custom-call | flops 1638400 | bytes 1347584 | tf_op jit(solution)/shard_map/pallas_call | solution.py:318
  (4 shorter events, 0.1 us)
Async XLA Ops:
  0.6 3.0 %copy-start.1 = (f32[6,4,8,256]{3,2,1,0:T(8,128)S(1)}, f32[6,4,8,256]{3,2,1,0:T(8,128)}, u32[]{:S(2)}) copy-start(f32[6,4,8,256]{3,2,1,0:T(8,128)} %refs_1_.2) | copy-start | bytes 589828
  0.6 7.1 %collective-permute-start = (f32[3,4,8,256]{3,2,1,0:T(8,128)}, f32[3,4,8,256]{3,2,1,0:T(8,128)S(1)}, u32[]{:S(2)}, u32[]{:S(2)}) collective-permute-start(f32[3,4,8,256]{3,2,1,0:T(8,128)} %refs_0_.5), channel_id=1, source_target_pairs={{16,0},{0,16},{17,1},{1,17},{18,2},{2,18},{19,3},{3,19},{20,4},{4,... | collective-permute-start | bytes 294920 | tf_op jit(solution)/shard_map/ppermute | solution.py:331
  3.7 1.0 %copy-start.2 = (f32[6,4,8,256]{3,2,1,0:T(8,128)S(1)}, f32[6,4,8,256]{3,2,1,0:T(8,128)}, u32[]{:S(2)}) copy-start(f32[6,4,8,256]{3,2,1,0:T(8,128)} %refs_1_.3) | copy-start | bytes 589828
  3.7 4.1 %copy-start = (f32[3,4,8,256]{3,2,1,0:T(8,128)S(1)}, f32[3,4,8,256]{3,2,1,0:T(8,128)}, u32[]{:S(2)}) copy-start(f32[3,4,8,256]{3,2,1,0:T(8,128)} %refs_0_.5) | copy-start | bytes 294916
  3.7 4.0 %copy-start.3 = (s32[8]{0:T(128)S(1)}, s32[8]{0:T(128)}, u32[]{:S(2)}) copy-start(s32[8]{0:T(128)} %param.6) | copy-start | bytes 100
  3.7 4.0 %collective-permute-start.1 = (f32[2,8,256]{2,1,0:T(8,128)S(1)}, f32[2,8,256]{2,1,0:T(8,128)S(1)}, u32[]{:S(2)}, u32[]{:S(2)}) collective-permute-start(f32[2,8,256]{2,1,0:T(8,128)S(1)} %get-tuple-element.14), channel_id=1, source_target_pairs={{16,0},{0,16},{17,1},{1,17},{18,2},{2,18},{19,3},{3,19},{20,4},{4,... | collective-permute-start | bytes 49160 | tf_op jit(solution)/shard_map/ppermute | solution.py:331
  4.6 10.1 %collective-permute-start.2 = (f32[6,4,8,256]{3,2,1,0:T(8,128)S(1)}, f32[6,4,8,256]{3,2,1,0:T(8,128)S(1)}, u32[]{:S(2)}, u32[]{:S(2)}) collective-permute-start(f32[6,4,8,256]{3,2,1,0:T(8,128)S(1)} %copy-done.2), channel_id=1, source_target_pairs={{16,0},{0,16},{17,1},{1,17},{18,2},{2,18},{19,3},{3,19},{20,4},{4,... | collective-permute-start | bytes 589832 | tf_op jit(solution)/shard_map/ppermute | solution.py:331
  8.1 2.1 %collective-permute-start.3 = (f32[8,128]{1,0:T(8,128)S(1)}, f32[8,128]{1,0:T(8,128)S(1)}, u32[]{:S(2)}, u32[]{:S(2)}) collective-permute-start(f32[8,128]{1,0:T(8,128)S(1)} %get-tuple-element.20), channel_id=1, source_target_pairs={{1,0},{0,1},{3,2},{2,3},{5,4},{4,5},{7,6},{6,7},{9,8},{8,9},{11,10... | collective-permute-start | bytes 12296 | tf_op jit(solution)/shard_map/ppermute | solution.py:341
  8.2 9.1 %collective-permute-start.7 = (f32[18,8,256]{2,1,0:T(8,128)S(1)}, f32[18,8,256]{2,1,0:T(8,128)S(1)}, u32[]{:S(2)}, u32[]{:S(2)}) collective-permute-start(f32[18,8,256]{2,1,0:T(8,128)S(1)} %get-tuple-element.21), channel_id=1, source_target_pairs={{16,0},{0,16},{17,1},{1,17},{18,2},{2,18},{19,3},{3,19},{20,4},{4,... | collective-permute-start | bytes 442376 | tf_op jit(solution)/shard_map/ppermute | solution.py:331
  10.3 5.1 %collective-permute-start.4 = (f32[8,128]{1,0:T(8,128)S(1)}, f32[8,128]{1,0:T(8,128)S(1)}, u32[]{:S(2)}, u32[]{:S(2)}) collective-permute-start(f32[8,128]{1,0:T(8,128)S(1)} %add.3.refs_7_), channel_id=1, source_target_pairs={{17,0},{19,1},{16,2},{21,3},{18,4},{23,5},{20,6},{25,7},{22,8},{27... | collective-permute-start | bytes 12296 | tf_op jit(solution)/shard_map/ppermute | solution.py:341
  12.2 3.1 %collective-permute-start.5 = (f32[8,128]{1,0:T(8,128)S(1)}, f32[8,128]{1,0:T(8,128)S(1)}, u32[]{:S(2)}, u32[]{:S(2)}) collective-permute-start(f32[8,128]{1,0:T(8,128)S(1)} %add.3.refs_7_), channel_id=1, source_target_pairs={{1,0},{3,1},{0,2},{5,3},{2,4},{7,5},{4,6},{9,7},{6,8},{11,9},{8,10... | collective-permute-start | bytes 12296 | tf_op jit(solution)/shard_map/ppermute | solution.py:341
  13.8 3.6 %collective-permute-start.6 = (f32[8,128]{1,0:T(8,128)S(1)}, f32[8,128]{1,0:T(8,128)S(1)}, u32[]{:S(2)}, u32[]{:S(2)}) collective-permute-start(f32[8,128]{1,0:T(8,128)S(1)} %add.3.refs_7_), channel_id=1, source_target_pairs={{16,0},{0,16},{17,1},{1,17},{18,2},{2,18},{19,3},{3,19},{20,4},{4,... | collective-permute-start | bytes 12296 | tf_op jit(solution)/shard_map/ppermute | solution.py:331

commit v8 on v7

--- a/solution.py
+++ b/solution.py
@@ -176,8 +176,11 @@
     sums_ref[...] = table
 
 
-def message_kernel(tables, smooth_ref, model_ref, dual_ref, message_ref):
+def message_kernel(tables, smooth_ref, model_ref, sums_ref, other_sums_ref, dual_ref, message_ref, pair_ref):
     cells = tables.cells
+    pair_sums = sums_ref[...] + other_sums_ref[...]
+    pair_ref[...] = pair_sums
+    message_ref[18, 0:8, 0:LANES] = pair_sums
     for lanes in halves(model_ref.shape[-1]):
         model = [[model_ref[k, z, :, lanes] for z in range(cells)] for k in range(6)]
         smooth_v = [[smooth_ref[a, z, :, lanes] for z in range(cells)] for a in range(3)]
@@ -251,10 +254,10 @@
     cells = tables.cells
     v_ref, leonard_ref, model_ref, parts_ref, bins_ref = refs[:5]
     near_refs = refs[5 : 5 + count]
-    pair_refs = refs[5 + count : 6 + peers + count]
-    far_message_refs = refs[6 + peers + count : 6 + 2 * peers + count]
-    residual_hbm, grad_hbm, residual_ref, grad_ref, left = refs[6 + 2 * peers + count :]
-    total = sum_up([ref[...] for ref in pair_refs])
+    pair_ref = refs[5 + count]
+    far_message_refs = refs[6 + count : 6 + count + peers]
+    residual_hbm, grad_hbm, residual_ref, grad_ref, left = refs[6 + count + peers :]
+    total = sum_up([pair_ref[...]] + [ref[18, 0:8, 0:LANES] for ref in far_message_refs])
     near = sum_up([ref[...] for ref in near_refs])
     if turning:
         place = lax.axis_index("stream")
@@ -279,8 +282,10 @@
                 residual_ref[k, z, :, lanes] = (
                     leonard_ref[k, z, :, lanes] - coefficient * model_ref[k, z, :, lanes]
                 )
-        copies.append(pltpu.make_async_copy(residual_ref.at[k], residual_hbm.at[k], left.at[k]))
-        copies[k].start(priority=k % 2)
+        if k % 3 == 2:
+            some = pl.ds(k - 2, 3)
+            copies.append(pltpu.make_async_copy(residual_ref.at[some], residual_hbm.at[some], left.at[k // 3]))
+            copies[-1].start()
     for lanes in halves(v_ref.shape[-1]):
         v = [[v_ref[a, z, :, lanes] for z in range(cells)] for a in range(3)]
         from_model = [[] for _ in range(6)]
@@ -302,9 +307,8 @@
                 grad_ref[a, z, :, lanes] = (
                     parts_ref[a, z, :, lanes] + coefficient * parts_ref[3 + a, z, :, lanes] + pull * pulled
                 )
-    for a in range(3):
-        copies.append(pltpu.make_async_copy(grad_ref.at[a], grad_hbm.at[a], left.at[6 + a]))
-        copies[6 + a].start(priority=a % 2)
+    copies.append(pltpu.make_async_copy(grad_ref, grad_hbm, left.at[2]))
+    copies[-1].start()
     for copy in copies:
         copy.wait()
 
@@ -383,10 +387,15 @@
         *far_size,
     )
     other_sums = from_source(sums, 0, lambda j: j ^ 1)
-    dual, message = call(
-        functools.partial(message_kernel, tables), [shaped(3, cells), shaped(18)], 100 * work, smooth, model
-    )
-    pair_sums = sums + other_sums
+    dual, message, pair_sums = call(
+        functools.partial(message_kernel, tables),
+        [shaped(3, cells), shaped(19), table],
+        100 * work,
+        smooth,
+        model,
+        sums,
+        other_sums,
+    )
     far_message = [from_ahead(message, shift) for shift in range(1, span)]
     most_rows = 2 * rows * stream // NBINS
     reach = -(-(most_rows - 1) // rows)
@@ -396,12 +405,11 @@
     else:
         steps = range(1, -(-reach // 2) + 1)
         sources = [functools.partial(lambda j, away: j + away, away=2 * step * way) for step in steps for way in (1, -1)]
-    near_sums = [from_source(pair_sums, shift, source) for shift in reversed(range(span)) for source in sources]
-    far_pairs = [from_ahead(pair_sums, shift) for shift in range(1, span)]
+    near_sums = [from_source(pair_sums, shift, source) for shift in range(span) for source in sources]
     (parts,) = call(
         functools.partial(local_kernel, tables),
         [shaped(12, cells)],
-        LONG * work,
+        500 * work,
         velocity,
         cotangent,
         smooth,
@@ -424,10 +432,9 @@
             bins,
             *near_sums,
             pair_sums,
-            *far_pairs,
             *far_message,
             out_specs=[REMAIN] * 2,
-            scratch=[pltpu.VMEM(x.shape, x.dtype) for x in outs] + [pltpu.SemaphoreType.DMA((9,))],
+            scratch=[pltpu.VMEM(x.shape, x.dtype) for x in outs] + [pltpu.SemaphoreType.DMA((3,))],
         )
     )
 

time: 18.4 us -> 16.9 us (0.918)
  starting transfers between devices: 11.7 us -> 9.95 us
  waiting for transfers between devices: 3.86 us -> 4.12 us
    ppermute x3, waiting for transfers between devices: 0.01 us -> 1.91 us  [from_source(): return lax.ppermute(values, ('span', 'stream'), pairs)]
    ppermute x5 -> x4, waiting for transfers between devices: 3.85 us -> 2.21 us  [from_ahead(): lax.ppermute(values, 'span', [((i + shift) % peers, i) for i in range(pee...]
    ppermute x5 -> x4, starting transfers between devices: 8.17 us -> 7.17 us  [from_ahead(): lax.ppermute(values, 'span', [((i + shift) % peers, i) for i in range(pee...]
    ppermute x3, starting transfers between devices: 3.55 us -> 2.78 us  [from_source(): return lax.ppermute(values, ('span', 'stream'), pairs)]
  transfers between devices with their start and end apart: 8 -> 7, of which waited for: 2 -> 5; matrix products, arithmetic and copies ran while one was open for 0% -> 0% of each run, Pallas kernels for 6% -> 6%
where the time goes in v8:
time: 16.9 us; the launch traced here: 16.7 us
  starting transfers between devices  9.95 us (59%)
  waiting for transfers between devices  4.12 us (24%)
  Pallas kernels  1.83 us (11%)
  between operations  0.68 us (4%)
    ppermute x4, starting transfers between devices, from_ahead(): lax.ppermute(values, 'span', [((i + shift) % peers, i) for i in range(pee...  7.17 us
    ppermute x3, starting transfers between devices, from_source(): return lax.ppermute(values, ('span', 'stream'), pairs)  2.78 us
    ppermute x4, waiting for transfers between devices, from_ahead(): lax.ppermute(values, 'span', [((i + shift) % peers, i) for i in range(pee...  2.21 us
    ppermute x3, waiting for transfers between devices, from_source(): return lax.ppermute(values, ('span', 'stream'), pairs)  1.91 us
    pallas_call x6, Pallas kernels, call(): pl.pallas_call(kernel, out_shape=outs, in_specs=in_specs or [WHOLE] * len...  1.83 us
  transfers between devices with their start and end apart: 7, of which 5 were waited for; matrix products, arithmetic and copies ran while one was open for 0% of the time, Pallas kernels for 6%

profile of v8, /device:TPU:0, one launch (start us, length us, event | category | flops | bytes accessed | tf_op | source)
XLA Modules:
  0.0 16.7 jit_solution(8961364212995183068)
XLA Ops:
  0.6 0.0 copy-start.2
  0.6 3.0 %collective-permute-start = (f32[3,4,8,256]{3,2,1,0:T(8,128)}, f32[3,4,8,256]{3,2,1,0:T(8,128)S(1)}, u32[]{:S(2)}, u32[]{:S(2)}) collective-permute-start(f32[3,4,8,256]{3,2,1,0:T(8,128)} %refs_0_.5), channel_id=1, source_target_pairs={{16,0},{0,16},{17,1},{1,17},{18,2},{2,18},{19,3},{3,19},{20,4},{4,... | collective-permute-start | bytes 294920 | tf_op jit(solution)/shard_map/ppermute | solution.py:335
  3.7 0.0 copy-done.2
  3.7 0.0 copy-start.1
  3.7 0.0 copy-start
  3.7 0.0 copy-start.3
  3.7 0.9 %collective-permute-start.1 = (f32[2,8,256]{2,1,0:T(8,128)S(1)}, f32[2,8,256]{2,1,0:T(8,128)S(1)}, u32[]{:S(2)}, u32[]{:S(2)}) collective-permute-start(f32[2,8,256]{2,1,0:T(8,128)S(1)} %get-tuple-element.15), channel_id=1, source_target_pairs={{16,0},{0,16},{17,1},{1,17},{18,2},{2,18},{19,3},{3,19},{20,4},{4,... | collective-permute-start | bytes 49160 | tf_op jit(solution)/shard_map/ppermute | solution.py:335
  4.6 0.0 copy-done.1
  4.6 1.2 %collective-permute-start.3 = (f32[6,4,8,256]{3,2,1,0:T(8,128)S(1)}, f32[6,4,8,256]{3,2,1,0:T(8,128)S(1)}, u32[]{:S(2)}, u32[]{:S(2)}) collective-permute-start(f32[6,4,8,256]{3,2,1,0:T(8,128)S(1)} %copy-done.1), channel_id=1, source_target_pairs={{16,0},{0,16},{17,1},{1,17},{18,2},{2,18},{19,3},{3,19},{20,4},{4,... | collective-permute-start | bytes 589832 | tf_op jit(solution)/shard_map/ppermute | solution.py:335
  5.9 1.8 %collective-permute-done.1.refs_6_ = f32[2,8,256]{2,1,0:T(8,128)S(1)} collective-permute-done((f32[2,8,256]{2,1,0:T(8,128)S(1)}, f32[2,8,256]{2,1,0:T(8,128)S(1)}, u32[]{:S(2)}, u32[]{:S(2)}) %collective-permute-start.1) | collective-permute-done | bytes 16416 | tf_op jit(solution)/shard_map/ppermute | solution.py:335
  7.7 0.0 collective-permute-done.refs_5_.refs_6_
  7.7 0.0 copy-done.3
  7.7 0.1 broadcast_in_dim.2.refs_4_
  7.8 0.0 copy-done
  7.8 0.3 %shard_map.61 = (f32[3,4,8,256]{3,2,1,0:T(8,128)S(1)}, f32[6,4,8,256]{3,2,1,0:T(8,128)S(1)}, f32[6,4,8,256]{3,2,1,0:T(8,128)S(1)}, f32[8,128]{1,0:T(8,128)S(1)}) custom-call(f32[3,4,8,256]{3,2,1,0:T(8,128)S(1)} %copy-done, f32[6,4,8,256]{3,2,1,0:T(8,128)S(1)} %copy-done.2, f32[6,4,8,256]{3,2,1,0:T(8,128)S(1)} %copy-done.1, ...), custom_call_target="tpu_custom_call" | custom-call | flops 2457600000 | bytes 1138688 | tf_op jit(solution)/shard_map/pallas_call | solution.py:322
  8.1 0.0 collective-permute-start.2
  8.2 1.2 %collective-permute-done.2.other_sums_ref = f32[8,128]{1,0:T(8,128)S(1)} collective-permute-done((f32[8,128]{1,0:T(8,128)S(1)}, f32[8,128]{1,0:T(8,128)S(1)}, u32[]{:S(2)}, u32[]{:S(2)}) %collective-permute-start.2) | collective-permute-done | bytes 4128 | tf_op jit(solution)/shard_map/ppermute | solution.py:345
  9.4 2.0 %collective-permute-start.6 = (f32[19,8,256]{2,1,0:T(8,128)S(1)}, f32[19,8,256]{2,1,0:T(8,128)S(1)}, u32[]{:S(2)}, u32[]{:S(2)}) collective-permute-start(f32[19,8,256]{2,1,0:T(8,128)S(1)} %get-tuple-element.23), channel_id=1, source_target_pairs={{16,0},{0,16},{17,1},{1,17},{18,2},{2,18},{19,3},{3,19},{20,4},{4,... | collective-permute-start | bytes 466952 | tf_op jit(solution)/shard_map/ppermute | solution.py:335
  11.4 1.2 %collective-permute-start.5 = (f32[8,128]{1,0:T(8,128)S(1)}, f32[8,128]{1,0:T(8,128)S(1)}, u32[]{:S(2)}, u32[]{:S(2)}) collective-permute-start(f32[8,128]{1,0:T(8,128)S(1)} %get-tuple-element.22.refs_7_), channel_id=1, source_target_pairs={{17,0},{19,1},{16,2},{21,3},{18,4},{23,5},{20,6},{25,7},{22,8},{27... | collective-permute-start | bytes 12296 | tf_op jit(solution)/shard_map/ppermute | solution.py:345
  12.6 1.5 %collective-permute-start.4 = (f32[8,128]{1,0:T(8,128)S(1)}, f32[8,128]{1,0:T(8,128)S(1)}, u32[]{:S(2)}, u32[]{:S(2)}) collective-permute-start(f32[8,128]{1,0:T(8,128)S(1)} %get-tuple-element.22.refs_7_), channel_id=1, source_target_pairs={{1,0},{3,1},{0,2},{5,3},{2,4},{7,5},{4,6},{9,7},{6,8},{11,9},{8,10... | collective-permute-start | bytes 12296 | tf_op jit(solution)/shard_map/ppermute | solution.py:345
  14.1 0.0 collective-permute-done.3.refs_7_
  14.1 0.6 %shard_map.63.refs_3_ = f32[12,4,8,256]{3,2,1,0:T(8,128)S(1)} custom-call(f32[3,4,8,256]{3,2,1,0:T(8,128)S(1)} %copy-done, f32[6,4,8,256]{3,2,1,0:T(8,128)S(1)} %copy-done.1, f32[3,4,8,256]{3,2,1,0:T(8,128)S(1)} %get-tuple-element.18.smooth_ref.refs_2_, f32[6,4,8,256]{3,2,1,0:T(8,128)S(1)} %get-tuple-element.16.refs_3_.refs_1_, ...), custom_call_target="tpu_custom_call" | custom-call | flops 4096000 | bytes 1572864 | tf_op jit(solution)/shard_map/pallas_call | solution.py:322
  14.7 0.6 %collective-permute-done.5.refs_6_ = f32[8,128]{1,0:T(8,128)S(1)} collective-permute-done((f32[8,128]{1,0:T(8,128)S(1)}, f32[8,128]{1,0:T(8,128)S(1)}, u32[]{:S(2)}, u32[]{:S(2)}) %collective-permute-start.5) | collective-permute-done | bytes 4128 | tf_op jit(solution)/shard_map/ppermute | solution.py:345
  15.3 0.1 collective-permute-done.4.refs_5_
  15.5 0.4 %collective-permute-done.6.refs_8_ = f32[19,8,256]{2,1,0:T(8,128)S(1)} collective-permute-done((f32[19,8,256]{2,1,0:T(8,128)S(1)}, f32[19,8,256]{2,1,0:T(8,128)S(1)}, u32[]{:S(2)}, u32[]{:S(2)}) %collective-permute-start.6) | collective-permute-done | bytes 155680 | tf_op jit(solution)/shard_map/ppermute | solution.py:335
  15.8 0.8 %shard_map.64 = (f32[6,4,8,256]{3,2,1,0:T(8,128)}, f32[3,4,8,256]{3,2,1,0:T(8,128)}) custom-call(f32[3,4,8,256]{3,2,1,0:T(8,128)S(1)} %copy-done, f32[6,4,8,256]{3,2,1,0:T(8,128)S(1)} %get-tuple-element.16.refs_3_.refs_1_, f32[6,4,8,256]{3,2,1,0:T(8,128)S(1)} %get-tuple-element.17.model_ref.refs_4_.refs_2_, f32[12,4,8,256]{3,2,1,0:T(8,128)S(1)} %shard_map.63.refs_3_, ...), custom_call_target="tpu_custom_call" | custom-call | flops 1638400 | bytes 1351680 | tf_op jit(solution)/shard_map/pallas_call | solution.py:322
  (3 shorter events, 0.1 us)
Async XLA Ops:
  0.6 3.0 %copy-start.2 = (f32[6,4,8,256]{3,2,1,0:T(8,128)S(1)}, f32[6,4,8,256]{3,2,1,0:T(8,128)}, u32[]{:S(2)}) copy-start(f32[6,4,8,256]{3,2,1,0:T(8,128)} %refs_1_.2) | copy-start | bytes 589828
  0.6 7.1 %collective-permute-start = (f32[3,4,8,256]{3,2,1,0:T(8,128)}, f32[3,4,8,256]{3,2,1,0:T(8,128)S(1)}, u32[]{:S(2)}, u32[]{:S(2)}) collective-permute-start(f32[3,4,8,256]{3,2,1,0:T(8,128)} %refs_0_.5), channel_id=1, source_target_pairs={{16,0},{0,16},{17,1},{1,17},{18,2},{2,18},{19,3},{3,19},{20,4},{4,... | collective-permute-start | bytes 294920 | tf_op jit(solution)/shard_map/ppermute | solution.py:335
  3.7 1.0 %copy-start.1 = (f32[6,4,8,256]{3,2,1,0:T(8,128)S(1)}, f32[6,4,8,256]{3,2,1,0:T(8,128)}, u32[]{:S(2)}) copy-start(f32[6,4,8,256]{3,2,1,0:T(8,128)} %refs_1_.3) | copy-start | bytes 589828
  3.7 4.1 %copy-start = (f32[3,4,8,256]{3,2,1,0:T(8,128)S(1)}, f32[3,4,8,256]{3,2,1,0:T(8,128)}, u32[]{:S(2)}) copy-start(f32[3,4,8,256]{3,2,1,0:T(8,128)} %refs_0_.5) | copy-start | bytes 294916
  3.7 4.0 %copy-start.3 = (s32[8]{0:T(128)S(1)}, s32[8]{0:T(128)}, u32[]{:S(2)}) copy-start(s32[8]{0:T(128)} %param.6) | copy-start | bytes 100
  3.7 4.0 %collective-permute-start.1 = (f32[2,8,256]{2,1,0:T(8,128)S(1)}, f32[2,8,256]{2,1,0:T(8,128)S(1)}, u32[]{:S(2)}, u32[]{:S(2)}) collective-permute-start(f32[2,8,256]{2,1,0:T(8,128)S(1)} %get-tuple-element.15), channel_id=1, source_target_pairs={{16,0},{0,16},{17,1},{1,17},{18,2},{2,18},{19,3},{3,19},{20,4},{4,... | collective-permute-start | bytes 49160 | tf_op jit(solution)/shard_map/ppermute | solution.py:335
  4.6 9.5 %collective-permute-start.3 = (f32[6,4,8,256]{3,2,1,0:T(8,128)S(1)}, f32[6,4,8,256]{3,2,1,0:T(8,128)S(1)}, u32[]{:S(2)}, u32[]{:S(2)}) collective-permute-start(f32[6,4,8,256]{3,2,1,0:T(8,128)S(1)} %copy-done.1), channel_id=1, source_target_pairs={{16,0},{0,16},{17,1},{1,17},{18,2},{2,18},{19,3},{3,19},{20,4},{4,... | collective-permute-start | bytes 589832 | tf_op jit(solution)/shard_map/ppermute | solution.py:335
  8.1 1.2 %collective-permute-start.2 = (f32[8,128]{1,0:T(8,128)S(1)}, f32[8,128]{1,0:T(8,128)S(1)}, u32[]{:S(2)}, u32[]{:S(2)}) collective-permute-start(f32[8,128]{1,0:T(8,128)S(1)} %get-tuple-element.19.sums_ref), channel_id=1, source_target_pairs={{1,0},{0,1},{3,2},{2,3},{5,4},{4,5},{7,6},{6,7},{9,8},{8,9},{11,10... | collective-permute-start | bytes 12296 | tf_op jit(solution)/shard_map/ppermute | solution.py:345
  9.4 6.5 %collective-permute-start.6 = (f32[19,8,256]{2,1,0:T(8,128)S(1)}, f32[19,8,256]{2,1,0:T(8,128)S(1)}, u32[]{:S(2)}, u32[]{:S(2)}) collective-permute-start(f32[19,8,256]{2,1,0:T(8,128)S(1)} %get-tuple-element.23), channel_id=1, source_target_pairs={{16,0},{0,16},{17,1},{1,17},{18,2},{2,18},{19,3},{3,19},{20,4},{4,... | collective-permute-start | bytes 466952 | tf_op jit(solution)/shard_map/ppermute | solution.py:335
  11.4 4.0 %collective-permute-start.5 = (f32[8,128]{1,0:T(8,128)S(1)}, f32[8,128]{1,0:T(8,128)S(1)}, u32[]{:S(2)}, u32[]{:S(2)}) collective-permute-start(f32[8,128]{1,0:T(8,128)S(1)} %get-tuple-element.22.refs_7_), channel_id=1, source_target_pairs={{17,0},{19,1},{16,2},{21,3},{18,4},{23,5},{20,6},{25,7},{22,8},{27... | collective-permute-start | bytes 12296 | tf_op jit(solution)/shard_map/ppermute | solution.py:345
  12.6 2.9 %collective-permute-start.4 = (f32[8,128]{1,0:T(8,128)S(1)}, f32[8,128]{1,0:T(8,128)S(1)}, u32[]{:S(2)}, u32[]{:S(2)}) collective-permute-start(f32[8,128]{1,0:T(8,128)S(1)} %get-tuple-element.22.refs_7_), channel_id=1, source_target_pairs={{1,0},{3,1},{0,2},{5,3},{2,4},{7,5},{4,6},{9,7},{6,8},{11,9},{8,10... | collective-permute-start | bytes 12296 | tf_op jit(solution)/shard_map/ppermute | solution.py:345

commit v9 on v8

--- a/solution.py
+++ b/solution.py
@@ -106,6 +106,12 @@
             size_ref[z, :, lanes] = size[z]
         for end, value in enumerate(tables.project(size)):
             size_ends_ref[end, :, lanes] = value
+
+
+def fetch_kernel(cot_hbm, size_ends_ref, cot_ref, arrived):
+    copy = pltpu.make_async_copy(cot_hbm, cot_ref, arrived)
+    copy.start()
+    copy.wait()
 
 
 def products_of(v):
@@ -370,9 +376,17 @@
     size, size_ends = call(
         functools.partial(prepare_kernel, tables), [shaped(cells), shaped(2)], LONG * work, lane, strain
     )
-    size_ends, sent_cot = lax.optimization_barrier((size_ends, cotangent))
     far_size = [from_ahead(size_ends, shift) for shift in range(1, span)]
-    far_cot = [from_ahead(sent_cot, shift) for shift in range(1, span)]
+    (near_cot,) = call(
+        fetch_kernel,
+        [shaped(6, cells)],
+        work,
+        pltpu.with_memory_space_constraint(cotangent, pltpu.HBM),
+        size_ends,
+        in_specs=[REMAIN, WHOLE],
+        scratch=[pltpu.SemaphoreType.DMA(())],
+    )
+    far_cot = [from_ahead(near_cot, shift) for shift in range(1, span)]
     table = pltpu.VMEM((8, LANES), jnp.float32)
     smooth, leonard, model, sums = call(
         functools.partial(forward_kernel, tables),
@@ -380,7 +394,7 @@
         LONG * work,
         velocity,
         strain,
-        cotangent,
+        near_cot,
         size,
         bins,
         *far_v,
@@ -411,7 +425,7 @@
         [shaped(12, cells)],
         500 * work,
         velocity,
-        cotangent,
+        near_cot,
         smooth,
         leonard,
         model,

time: 16.9 us -> 16.5 us (0.976)
  waiting for transfers between devices: 4.12 us -> 2.97 us
  Pallas kernels: 1.83 us -> 2.77 us
    ppermute x4, waiting for transfers between devices: 2.21 us -> 1.06 us  [from_ahead(): lax.ppermute(values, 'span', [((i + shift) % peers, i) for i in range(pee...]
    pallas_call x6 -> x7, Pallas kernels: 1.83 us -> 2.77 us  [call(): pl.pallas_call(kernel, out_shape=outs, in_specs=in_specs or [WHOLE] * len...]
    ppermute x4, starting transfers between devices: 7.17 us -> 6.5 us  [from_ahead(): lax.ppermute(values, 'span', [((i + shift) % peers, i) for i in range(pee...]
    ppermute x3, starting transfers between devices: 2.78 us -> 3.3 us  [from_source(): return lax.ppermute(values, ('span', 'stream'), pairs)]
  transfers between devices with their start and end apart: 7 -> 7, of which waited for: 5 -> 5; matrix products, arithmetic and copies ran while one was open for 0% -> 0% of each run, Pallas kernels for 6% -> 12%
where the time goes in v9:
time: 16.5 us; the launch traced here: 16.3 us
  starting transfers between devices  9.8 us (59%)
  waiting for transfers between devices  2.97 us (18%)
  Pallas kernels  2.77 us (17%)
  between operations  0.69 us (4%)
    ppermute x4, starting transfers between devices, from_ahead(): lax.ppermute(values, 'span', [((i + shift) % peers, i) for i in range(pee...  6.5 us
    ppermute x3, starting transfers between devices, from_source(): return lax.ppermute(values, ('span', 'stream'), pairs)  3.3 us
    pallas_call x7, Pallas kernels, call(): pl.pallas_call(kernel, out_shape=outs, in_specs=in_specs or [WHOLE] * len...  2.77 us
    ppermute x3, waiting for transfers between devices, from_source(): return lax.ppermute(values, ('span', 'stream'), pairs)  1.91 us
    ppermute x4, waiting for transfers between devices, from_ahead(): lax.ppermute(values, 'span', [((i + shift) % peers, i) for i in range(pee...  1.06 us
  transfers between devices with their start and end apart: 7, of which 5 were waited for; matrix products, arithmetic and copies ran while one was open for 0% of the time, Pallas kernels for 12%

profile of v9, /device:TPU:0, one launch (start us, length us, event | category | flops | bytes accessed | tf_op | source)
XLA Modules:
  0.0 16.3 jit_solution(7260838102033355320)
XLA Ops:
  0.6 0.0 copy-start.1
  0.6 3.0 %collective-permute-start = (f32[3,4,8,256]{3,2,1,0:T(8,128)}, f32[3,4,8,256]{3,2,1,0:T(8,128)S(1)}, u32[]{:S(2)}, u32[]{:S(2)}) collective-permute-start(f32[3,4,8,256]{3,2,1,0:T(8,128)} %refs_0_.5), channel_id=1, source_target_pairs={{16,0},{0,16},{17,1},{1,17},{18,2},{2,18},{19,3},{3,19},{20,4},{4,... | collective-permute-start | bytes 294920 | tf_op jit(solution)/shard_map/ppermute | solution.py:341
  3.7 0.0 copy-done.1
  3.7 0.0 copy-start.2
  3.7 0.0 copy-start
  3.7 0.9 %collective-permute-start.1 = (f32[2,8,256]{2,1,0:T(8,128)S(1)}, f32[2,8,256]{2,1,0:T(8,128)S(1)}, u32[]{:S(2)}, u32[]{:S(2)}) collective-permute-start(f32[2,8,256]{2,1,0:T(8,128)S(1)} %get-tuple-element.11.size_ends_ref), channel_id=1, source_target_pairs={{16,0},{0,16},{17,1},{1,17},{18,2},{2,18},{19,3},{3,19},{20,4},{4,... | collective-permute-start | bytes 49160 | tf_op jit(solution)/shard_map/ppermute | solution.py:341
  4.7 0.9 %shard_map.61.refs_2_.refs_1_ = f32[6,4,8,256]{3,2,1,0:T(8,128)S(1)} custom-call(f32[6,4,8,256]{3,2,1,0:T(8,128)} %cot_hbm.1, f32[2,8,256]{2,1,0:T(8,128)S(1)} %get-tuple-element.11.size_ends_ref), custom_call_target="tpu_custom_call" | custom-call | flops 8192 | bytes 409600 | tf_op jit(solution)/shard_map/pallas_call | solution.py:328
  5.6 1.2 %collective-permute-start.3 = (f32[6,4,8,256]{3,2,1,0:T(8,128)S(1)}, f32[6,4,8,256]{3,2,1,0:T(8,128)S(1)}, u32[]{:S(2)}, u32[]{:S(2)}) collective-permute-start(f32[6,4,8,256]{3,2,1,0:T(8,128)S(1)} %shard_map.61.refs_2_.refs_1_), channel_id=1, source_target_pairs={{16,0},{0,16},{17,1},{1,17},{18,2},{2,18},{19,3},{3,19},{20,4},{4,... | collective-permute-start | bytes 589832 | tf_op jit(solution)/shard_map/ppermute | solution.py:341
  6.8 0.7 %collective-permute-done.1.refs_6_ = f32[2,8,256]{2,1,0:T(8,128)S(1)} collective-permute-done((f32[2,8,256]{2,1,0:T(8,128)S(1)}, f32[2,8,256]{2,1,0:T(8,128)S(1)}, u32[]{:S(2)}, u32[]{:S(2)}) %collective-permute-start.1) | collective-permute-done | bytes 16416 | tf_op jit(solution)/shard_map/ppermute | solution.py:341
  7.5 0.0 collective-permute-done.refs_5_.refs_6_
  7.5 0.0 copy-done.2
  7.6 0.1 broadcast_in_dim.2.refs_4_
  7.6 0.0 copy-done
  7.6 0.3 %shard_map.62 = (f32[3,4,8,256]{3,2,1,0:T(8,128)S(1)}, f32[6,4,8,256]{3,2,1,0:T(8,128)S(1)}, f32[6,4,8,256]{3,2,1,0:T(8,128)S(1)}, f32[8,128]{1,0:T(8,128)S(1)}) custom-call(f32[3,4,8,256]{3,2,1,0:T(8,128)S(1)} %copy-done, f32[6,4,8,256]{3,2,1,0:T(8,128)S(1)} %copy-done.1, f32[6,4,8,256]{3,2,1,0:T(8,128)S(1)} %shard_map.61.refs_2_.refs_1_, ...), custom_call_target="tpu_custom_call" | custom-call | flops 2457600000 | bytes 1138688 | tf_op jit(solution)/shard_map/pallas_call | solution.py:328
  8.0 0.0 collective-permute-start.2
  8.0 1.2 %collective-permute-done.2.other_sums_ref = f32[8,128]{1,0:T(8,128)S(1)} collective-permute-done((f32[8,128]{1,0:T(8,128)S(1)}, f32[8,128]{1,0:T(8,128)S(1)}, u32[]{:S(2)}, u32[]{:S(2)}) %collective-permute-start.2) | collective-permute-done | bytes 4128 | tf_op jit(solution)/shard_map/ppermute | solution.py:351
  9.2 1.3 %collective-permute-start.6 = (f32[19,8,256]{2,1,0:T(8,128)S(1)}, f32[19,8,256]{2,1,0:T(8,128)S(1)}, u32[]{:S(2)}, u32[]{:S(2)}) collective-permute-start(f32[19,8,256]{2,1,0:T(8,128)S(1)} %get-tuple-element.19), channel_id=1, source_target_pairs={{16,0},{0,16},{17,1},{1,17},{18,2},{2,18},{19,3},{3,19},{20,4},{4,... | collective-permute-start | bytes 466952 | tf_op jit(solution)/shard_map/ppermute | solution.py:341
  10.5 1.7 %collective-permute-start.5 = (f32[8,128]{1,0:T(8,128)S(1)}, f32[8,128]{1,0:T(8,128)S(1)}, u32[]{:S(2)}, u32[]{:S(2)}) collective-permute-start(f32[8,128]{1,0:T(8,128)S(1)} %get-tuple-element.18.refs_7_), channel_id=1, source_target_pairs={{17,0},{19,1},{16,2},{21,3},{18,4},{23,5},{20,6},{25,7},{22,8},{27... | collective-permute-start | bytes 12296 | tf_op jit(solution)/shard_map/ppermute | solution.py:351
  12.2 1.5 %collective-permute-start.4 = (f32[8,128]{1,0:T(8,128)S(1)}, f32[8,128]{1,0:T(8,128)S(1)}, u32[]{:S(2)}, u32[]{:S(2)}) collective-permute-start(f32[8,128]{1,0:T(8,128)S(1)} %get-tuple-element.18.refs_7_), channel_id=1, source_target_pairs={{1,0},{3,1},{0,2},{5,3},{2,4},{7,5},{4,6},{9,7},{6,8},{11,9},{8,10... | collective-permute-start | bytes 12296 | tf_op jit(solution)/shard_map/ppermute | solution.py:351
  13.8 0.0 collective-permute-done.3.refs_7_
  13.8 0.6 %shard_map.64.refs_3_ = f32[12,4,8,256]{3,2,1,0:T(8,128)S(1)} custom-call(f32[3,4,8,256]{3,2,1,0:T(8,128)S(1)} %copy-done, f32[6,4,8,256]{3,2,1,0:T(8,128)S(1)} %shard_map.61.refs_2_.refs_1_, f32[3,4,8,256]{3,2,1,0:T(8,128)S(1)} %get-tuple-element.15.smooth_ref.refs_2_, f32[6,4,8,256]{3,2,1,0:T(8,128)S(1)} %get-tuple-element.13.refs_3_.refs_1_, ...), custom_call_target="tpu_custom_call" | custom-call | flops 4096000 | bytes 1572864 | tf_op jit(solution)/shard_map/pallas_call | solution.py:328
  14.4 0.4 %collective-permute-done.5.refs_6_ = f32[8,128]{1,0:T(8,128)S(1)} collective-permute-done((f32[8,128]{1,0:T(8,128)S(1)}, f32[8,128]{1,0:T(8,128)S(1)}, u32[]{:S(2)}, u32[]{:S(2)}) %collective-permute-start.5) | collective-permute-done | bytes 4128 | tf_op jit(solution)/shard_map/ppermute | solution.py:351
  14.7 0.4 %collective-permute-done.4.refs_5_ = f32[8,128]{1,0:T(8,128)S(1)} collective-permute-done((f32[8,128]{1,0:T(8,128)S(1)}, f32[8,128]{1,0:T(8,128)S(1)}, u32[]{:S(2)}, u32[]{:S(2)}) %collective-permute-start.4) | collective-permute-done | bytes 4128 | tf_op jit(solution)/shard_map/ppermute | solution.py:351
  15.1 0.4 %collective-permute-done.6.refs_8_ = f32[19,8,256]{2,1,0:T(8,128)S(1)} collective-permute-done((f32[19,8,256]{2,1,0:T(8,128)S(1)}, f32[19,8,256]{2,1,0:T(8,128)S(1)}, u32[]{:S(2)}, u32[]{:S(2)}) %collective-permute-start.6) | collective-permute-done | bytes 155680 | tf_op jit(solution)/shard_map/ppermute | solution.py:341
  15.5 0.8 %shard_map.65 = (f32[6,4,8,256]{3,2,1,0:T(8,128)}, f32[3,4,8,256]{3,2,1,0:T(8,128)}) custom-call(f32[3,4,8,256]{3,2,1,0:T(8,128)S(1)} %copy-done, f32[6,4,8,256]{3,2,1,0:T(8,128)S(1)} %get-tuple-element.13.refs_3_.refs_1_, f32[6,4,8,256]{3,2,1,0:T(8,128)S(1)} %get-tuple-element.14.model_ref.refs_4_.refs_2_, f32[12,4,8,256]{3,2,1,0:T(8,128)S(1)} %shard_map.64.refs_3_, ...), custom_call_target="tpu_custom_call" | custom-call | flops 1638400 | bytes 1351680 | tf_op jit(solution)/shard_map/pallas_call | solution.py:328
  (3 shorter events, 0.1 us)
Async XLA Ops:
  0.6 3.0 %copy-start.1 = (f32[6,4,8,256]{3,2,1,0:T(8,128)S(1)}, f32[6,4,8,256]{3,2,1,0:T(8,128)}, u32[]{:S(2)}) copy-start(f32[6,4,8,256]{3,2,1,0:T(8,128)} %refs_1_.1) | copy-start | bytes 589828
  0.6 6.9 %collective-permute-start = (f32[3,4,8,256]{3,2,1,0:T(8,128)}, f32[3,4,8,256]{3,2,1,0:T(8,128)S(1)}, u32[]{:S(2)}, u32[]{:S(2)}) collective-permute-start(f32[3,4,8,256]{3,2,1,0:T(8,128)} %refs_0_.5), channel_id=1, source_target_pairs={{16,0},{0,16},{17,1},{1,17},{18,2},{2,18},{19,3},{3,19},{20,4},{4,... | collective-permute-start | bytes 294920 | tf_op jit(solution)/shard_map/ppermute | solution.py:341
  3.7 3.8 %copy-start.2 = (s32[8]{0:T(128)S(1)}, s32[8]{0:T(128)}, u32[]{:S(2)}) copy-start(s32[8]{0:T(128)} %param.6) | copy-start | bytes 100
  3.7 3.9 %copy-start = (f32[3,4,8,256]{3,2,1,0:T(8,128)S(1)}, f32[3,4,8,256]{3,2,1,0:T(8,128)}, u32[]{:S(2)}) copy-start(f32[3,4,8,256]{3,2,1,0:T(8,128)} %refs_0_.5) | copy-start | bytes 294916
  3.7 3.8 %collective-permute-start.1 = (f32[2,8,256]{2,1,0:T(8,128)S(1)}, f32[2,8,256]{2,1,0:T(8,128)S(1)}, u32[]{:S(2)}, u32[]{:S(2)}) collective-permute-start(f32[2,8,256]{2,1,0:T(8,128)S(1)} %get-tuple-element.11.size_ends_ref), channel_id=1, source_target_pairs={{16,0},{0,16},{17,1},{1,17},{18,2},{2,18},{19,3},{3,19},{20,4},{4,... | collective-permute-start | bytes 49160 | tf_op jit(solution)/shard_map/ppermute | solution.py:341
  5.6 8.2 %collective-permute-start.3 = (f32[6,4,8,256]{3,2,1,0:T(8,128)S(1)}, f32[6,4,8,256]{3,2,1,0:T(8,128)S(1)}, u32[]{:S(2)}, u32[]{:S(2)}) collective-permute-start(f32[6,4,8,256]{3,2,1,0:T(8,128)S(1)} %shard_map.61.refs_2_.refs_1_), channel_id=1, source_target_pairs={{16,0},{0,16},{17,1},{1,17},{18,2},{2,18},{19,3},{3,19},{20,4},{4,... | collective-permute-start | bytes 589832 | tf_op jit(solution)/shard_map/ppermute | solution.py:341
  8.0 1.2 %collective-permute-start.2 = (f32[8,128]{1,0:T(8,128)S(1)}, f32[8,128]{1,0:T(8,128)S(1)}, u32[]{:S(2)}, u32[]{:S(2)}) collective-permute-start(f32[8,128]{1,0:T(8,128)S(1)} %get-tuple-element.16.sums_ref), channel_id=1, source_target_pairs={{1,0},{0,1},{3,2},{2,3},{5,4},{4,5},{7,6},{6,7},{9,8},{8,9},{11,10... | collective-permute-start | bytes 12296 | tf_op jit(solution)/shard_map/ppermute | solution.py:351
  9.2 6.2 %collective-permute-start.6 = (f32[19,8,256]{2,1,0:T(8,128)S(1)}, f32[19,8,256]{2,1,0:T(8,128)S(1)}, u32[]{:S(2)}, u32[]{:S(2)}) collective-permute-start(f32[19,8,256]{2,1,0:T(8,128)S(1)} %get-tuple-element.19), channel_id=1, source_target_pairs={{16,0},{0,16},{17,1},{1,17},{18,2},{2,18},{19,3},{3,19},{20,4},{4,... | collective-permute-start | bytes 466952 | tf_op jit(solution)/shard_map/ppermute | solution.py:341
  10.5 4.2 %collective-permute-start.5 = (f32[8,128]{1,0:T(8,128)S(1)}, f32[8,128]{1,0:T(8,128)S(1)}, u32[]{:S(2)}, u32[]{:S(2)}) collective-permute-start(f32[8,128]{1,0:T(8,128)S(1)} %get-tuple-element.18.refs_7_), channel_id=1, source_target_pairs={{17,0},{19,1},{16,2},{21,3},{18,4},{23,5},{20,6},{25,7},{22,8},{27... | collective-permute-start | bytes 12296 | tf_op jit(solution)/shard_map/ppermute | solution.py:351
  12.2 2.9 %collective-permute-start.4 = (f32[8,128]{1,0:T(8,128)S(1)}, f32[8,128]{1,0:T(8,128)S(1)}, u32[]{:S(2)}, u32[]{:S(2)}) collective-permute-start(f32[8,128]{1,0:T(8,128)S(1)} %get-tuple-element.18.refs_7_), channel_id=1, source_target_pairs={{1,0},{3,1},{0,2},{5,3},{2,4},{7,5},{4,6},{9,7},{6,8},{11,9},{8,10... | collective-permute-start | bytes 12296 | tf_op jit(solution)/shard_map/ppermute | solution.py:351

commit v10 on v9

--- a/solution.py
+++ b/solution.py
@@ -182,11 +182,8 @@
     sums_ref[...] = table
 
 
-def message_kernel(tables, smooth_ref, model_ref, sums_ref, other_sums_ref, dual_ref, message_ref, pair_ref):
+def message_kernel(tables, smooth_ref, model_ref, dual_ref, message_ref):
     cells = tables.cells
-    pair_sums = sums_ref[...] + other_sums_ref[...]
-    pair_ref[...] = pair_sums
-    message_ref[18, 0:8, 0:LANES] = pair_sums
     for lanes in halves(model_ref.shape[-1]):
         model = [[model_ref[k, z, :, lanes] for z in range(cells)] for k in range(6)]
         smooth_v = [[smooth_ref[a, z, :, lanes] for z in range(cells)] for a in range(3)]
@@ -263,11 +260,11 @@
     pair_ref = refs[5 + count]
     far_message_refs = refs[6 + count : 6 + count + peers]
     residual_hbm, grad_hbm, residual_ref, grad_ref, left = refs[6 + count + peers :]
-    total = sum_up([pair_ref[...]] + [ref[18, 0:8, 0:LANES] for ref in far_message_refs])
+    total = pair_ref[...]
     near = sum_up([ref[...] for ref in near_refs])
     if turning:
-        place = lax.axis_index("stream")
-        inner = jnp.logical_and(place > 0, place < lax.axis_size("stream") - 1)
+        place = 2 * lax.axis_index("pair") + lax.axis_index("core")
+        inner = jnp.logical_and(place > 0, place < 2 * lax.axis_size("pair") - 1)
         near = jnp.where(inner, near, 0.0)
     total = total + near
     inverse = 1.0 / (total[1:2] + EPSILON)
@@ -341,14 +338,9 @@
     return lax.ppermute(values, "span", [((i + shift) % peers, i) for i in range(peers)])
 
 
-def from_source(values, span_shift, source):
-    span, stream = lax.axis_size("span"), lax.axis_size("stream")
-    pairs = [
-        (((i + span_shift) % span) * stream + source(j) % stream, i * stream + j)
-        for i in range(span)
-        for j in range(stream)
-    ]
-    return lax.ppermute(values, ("span", "stream"), pairs)
+def from_source(values, source):
+    stream = 2 * lax.axis_size("pair")
+    return lax.ppermute(values, ("pair", "core"), [(source(j) % stream, j) for j in range(stream)])
 
 
 def ring_source(stream):
@@ -361,7 +353,7 @@
 
 
 def on_device(velocity, strain, row_bins, cotangent):
-    span, stream = lax.axis_size("span"), lax.axis_size("stream")
+    span, stream = lax.axis_size("span"), 2 * lax.axis_size("pair")
     cells, rows, width = velocity.shape[1:]
     tables = Tables(cells, span)
     slab = (rows, width)
@@ -400,16 +392,10 @@
         *far_v,
         *far_size,
     )
-    other_sums = from_source(sums, 0, lambda j: j ^ 1)
-    dual, message, pair_sums = call(
-        functools.partial(message_kernel, tables),
-        [shaped(3, cells), shaped(19), table],
-        100 * work,
-        smooth,
-        model,
-        sums,
-        other_sums,
-    )
+    dual, message = call(
+        functools.partial(message_kernel, tables), [shaped(3, cells), shaped(18)], 100 * work, smooth, model
+    )
+    pair_sums = lax.psum(sums, ("span", "core"))
     far_message = [from_ahead(message, shift) for shift in range(1, span)]
     most_rows = 2 * rows * stream // NBINS
     reach = -(-(most_rows - 1) // rows)
@@ -419,7 +405,7 @@
     else:
         steps = range(1, -(-reach // 2) + 1)
         sources = [functools.partial(lambda j, away: j + away, away=2 * step * way) for step in steps for way in (1, -1)]
-    near_sums = [from_source(pair_sums, shift, source) for shift in range(span) for source in sources]
+    near_sums = [from_source(pair_sums, source) for source in sources]
     (parts,) = call(
         functools.partial(local_kernel, tables),
         [shaped(12, cells)],
@@ -454,11 +440,13 @@
 
 
 def solution(mesh):
-    fields = P(None, "span", "stream", None)
+    span, stream = mesh.devices.shape
+    cut = jax.sharding.Mesh(mesh.devices.reshape(span, stream // 2, 2), ("span", "pair", "core"))
+    fields = P(None, "span", ("pair", "core"), None)
     return jax.shard_map(
         on_device,
-        mesh=mesh,
-        in_specs=(fields, fields, P("stream"), fields),
+        mesh=cut,
+        in_specs=(fields, fields, P(("pair", "core")), fields),
         out_specs=(fields, fields),
         check_vma=False,
     )

time: 16.5 us -> 21.3 us (1.29)
  blocking collectives: 0 us -> 7.89 us
  starting transfers between devices: 9.8 us -> 8.05 us
  waiting for transfers between devices: 2.97 us -> 1.46 us
    psum x0 -> x1, blocking collectives: none -> 7.89 us  [on_device(): pair_sums = lax.psum(sums, ('span', 'core'))]
    ppermute x3 -> x1, starting transfers between devices: 3.3 us -> 1.54 us  [from_source(): lax.ppermute(values, ('pair', 'core'), [(source(j) % stream, j) for j in...]
    ppermute x3 -> x1, waiting for transfers between devices: 1.91 us -> 0.76 us  [from_source(): lax.ppermute(values, ('pair', 'core'), [(source(j) % stream, j) for j in...]
    ppermute x4, waiting for transfers between devices: 1.06 us -> 0.7 us  [from_ahead(): lax.ppermute(values, 'span', [((i + shift) % peers, i) for i in range(pee...]
  transfers between devices with their start and end apart: 7 -> 5, of which waited for: 5 -> 2; matrix products, arithmetic and copies ran while one was open for 0% -> 0% of each run, Pallas kernels for 12% -> 9%
where the time goes in v10:
time: 21.3 us; the launch traced here: 20.9 us
  starting transfers between devices  8.05 us (38%)
  blocking collectives  7.89 us (37%)
  Pallas kernels  2.76 us (13%)
  waiting for transfers between devices  1.46 us (7%)
  between operations  0.68 us (3%)
    psum x1, blocking collectives, on_device(): pair_sums = lax.psum(sums, ('span', 'core'))  7.89 us
    ppermute x4, starting transfers between devices, from_ahead(): lax.ppermute(values, 'span', [((i + shift) % peers, i) for i in range(pee...  6.51 us
    pallas_call x7, Pallas kernels, call(): pl.pallas_call(kernel, out_shape=outs, in_specs=in_specs or [WHOLE] * len...  2.76 us
    ppermute x1, starting transfers between devices, from_source(): lax.ppermute(values, ('pair', 'core'), [(source(j) % stream, j) for j in...  1.54 us
    ppermute x1, waiting for transfers between devices, from_source(): lax.ppermute(values, ('pair', 'core'), [(source(j) % stream, j) for j in...  0.76 us
    ppermute x4, waiting for transfers between devices, from_ahead(): lax.ppermute(values, 'span', [((i + shift) % peers, i) for i in range(pee...  0.7 us
  transfers between devices with their start and end apart: 5, of which 2 were waited for; matrix products, arithmetic and copies ran while one was open for 0% of the time, Pallas kernels for 9%

profile of v10, /device:TPU:0, one launch (start us, length us, event | category | flops | bytes accessed | tf_op | source)
XLA Modules:
  0.0 20.9 jit_solution(8875252189927275640)
XLA Ops:
  0.6 0.0 copy-start.1
  0.6 3.0 %collective-permute-start = (f32[3,4,8,256]{3,2,1,0:T(8,128)}, f32[3,4,8,256]{3,2,1,0:T(8,128)S(1)}, u32[]{:S(2)}, u32[]{:S(2)}) collective-permute-start(f32[3,4,8,256]{3,2,1,0:T(8,128)} %refs_0_.5), channel_id=1, source_target_pairs={{16,0},{0,16},{17,1},{1,17},{18,2},{2,18},{19,3},{3,19},{20,4},{4,... | collective-permute-start | bytes 294920 | tf_op jit(solution)/shard_map/ppermute | solution.py:338
  3.7 0.0 copy-done.1
  3.7 0.0 copy-start
  3.7 0.9 %collective-permute-start.1 = (f32[2,8,256]{2,1,0:T(8,128)S(1)}, f32[2,8,256]{2,1,0:T(8,128)S(1)}, u32[]{:S(2)}, u32[]{:S(2)}) collective-permute-start(f32[2,8,256]{2,1,0:T(8,128)S(1)} %get-tuple-element.10.size_ends_ref), channel_id=1, source_target_pairs={{16,0},{0,16},{17,1},{1,17},{18,2},{2,18},{19,3},{3,19},{20,4},{4,... | collective-permute-start | bytes 49160 | tf_op jit(solution)/shard_map/ppermute | solution.py:338
  4.6 0.9 %shard_map.61.refs_2_.refs_1_ = f32[6,4,8,256]{3,2,1,0:T(8,128)S(1)} custom-call(f32[6,4,8,256]{3,2,1,0:T(8,128)} %cot_hbm.1, f32[2,8,256]{2,1,0:T(8,128)S(1)} %get-tuple-element.10.size_ends_ref), custom_call_target="tpu_custom_call" | custom-call | flops 8192 | bytes 409600 | tf_op jit(solution)/shard_map/pallas_call | solution.py:325
  5.6 0.0 copy-start.2
  5.6 1.2 %collective-permute-start.2 = (f32[6,4,8,256]{3,2,1,0:T(8,128)S(1)}, f32[6,4,8,256]{3,2,1,0:T(8,128)S(1)}, u32[]{:S(2)}, u32[]{:S(2)}) collective-permute-start(f32[6,4,8,256]{3,2,1,0:T(8,128)S(1)} %shard_map.61.refs_2_.refs_1_), channel_id=1, source_target_pairs={{16,0},{0,16},{17,1},{1,17},{18,2},{2,18},{19,3},{3,19},{20,4},{4,... | collective-permute-start | bytes 589832 | tf_op jit(solution)/shard_map/ppermute | solution.py:338
  6.8 0.7 %collective-permute-done.1.refs_6_ = f32[2,8,256]{2,1,0:T(8,128)S(1)} collective-permute-done((f32[2,8,256]{2,1,0:T(8,128)S(1)}, f32[2,8,256]{2,1,0:T(8,128)S(1)}, u32[]{:S(2)}, u32[]{:S(2)}) %collective-permute-start.1) | collective-permute-done | bytes 16416 | tf_op jit(solution)/shard_map/ppermute | solution.py:338
  7.5 0.0 collective-permute-done.refs_5_.refs_6_
  7.5 0.0 copy-done.2
  7.5 0.1 broadcast_in_dim.2.refs_4_
  7.6 0.0 copy-done
  7.6 0.3 %shard_map.62 = (f32[3,4,8,256]{3,2,1,0:T(8,128)S(1)}, f32[6,4,8,256]{3,2,1,0:T(8,128)S(1)}, f32[6,4,8,256]{3,2,1,0:T(8,128)S(1)}, f32[8,128]{1,0:T(8,128)S(1)}) custom-call(f32[3,4,8,256]{3,2,1,0:T(8,128)S(1)} %copy-done, f32[6,4,8,256]{3,2,1,0:T(8,128)S(1)} %copy-done.1, f32[6,4,8,256]{3,2,1,0:T(8,128)S(1)} %shard_map.61.refs_2_.refs_1_, ...), custom_call_target="tpu_custom_call" | custom-call | flops 2457600000 | bytes 1138688 | tf_op jit(solution)/shard_map/pallas_call | solution.py:325
  8.0 1.3 %collective-permute-start.4 = (f32[18,8,256]{2,1,0:T(8,128)S(1)}, f32[18,8,256]{2,1,0:T(8,128)S(1)}, u32[]{:S(2)}, u32[]{:S(2)}) collective-permute-start(f32[18,8,256]{2,1,0:T(8,128)S(1)} %get-tuple-element.17), channel_id=1, source_target_pairs={{16,0},{0,16},{17,1},{1,17},{18,2},{2,18},{19,3},{3,19},{20,4},{4,... | collective-permute-start | bytes 442376 | tf_op jit(solution)/shard_map/ppermute | solution.py:338
  9.3 7.9 %psum.7.refs_6_ = f32[8,128]{1,0:T(8,128)S(1)} all-reduce(f32[8,128]{1,0:T(8,128)S(1)} %get-tuple-element.16), channel_id=1, replica_groups=mesh['span'=2,'pair'=8,'core'=2] {'span','core'}, use_global_device_ids=true, to_apply=%region_0.0 | all-reduce | flops 1024 | bytes 8192 | tf_op jit(solution)/shard_map/psum | solution.py:398
  17.2 1.5 %collective-permute-start.3 = (f32[8,128]{1,0:T(8,128)S(1)}, f32[8,128]{1,0:T(8,128)S(1)}, u32[]{:S(2)}, u32[]{:S(2)}) collective-permute-start(f32[8,128]{1,0:T(8,128)S(1)} %psum.7.refs_6_), channel_id=1, source_target_pairs={{1,0},{3,1},{0,2},{5,3},{2,4},{7,5},{4,6},{9,7},{6,8},{11,9},{8,10... | collective-permute-start | bytes 12296 | tf_op jit(solution)/shard_map/ppermute | solution.py:343
  18.8 0.0 collective-permute-done.2.refs_7_
  18.8 0.6 %shard_map.64.refs_3_ = f32[12,4,8,256]{3,2,1,0:T(8,128)S(1)} custom-call(f32[3,4,8,256]{3,2,1,0:T(8,128)S(1)} %copy-done, f32[6,4,8,256]{3,2,1,0:T(8,128)S(1)} %shard_map.61.refs_2_.refs_1_, f32[3,4,8,256]{3,2,1,0:T(8,128)S(1)} %get-tuple-element.14.smooth_ref.refs_2_, f32[6,4,8,256]{3,2,1,0:T(8,128)S(1)} %get-tuple-element.12.refs_3_.refs_1_, ...), custom_call_target="tpu_custom_call" | custom-call | flops 4096000 | bytes 1572864 | tf_op jit(solution)/shard_map/pallas_call | solution.py:325
  19.3 0.8 %collective-permute-done.3.refs_5_ = f32[8,128]{1,0:T(8,128)S(1)} collective-permute-done((f32[8,128]{1,0:T(8,128)S(1)}, f32[8,128]{1,0:T(8,128)S(1)}, u32[]{:S(2)}, u32[]{:S(2)}) %collective-permute-start.3) | collective-permute-done | bytes 4128 | tf_op jit(solution)/shard_map/ppermute | solution.py:343
  20.1 0.0 collective-permute-done.4.refs_7_
  20.1 0.8 %shard_map.65 = (f32[6,4,8,256]{3,2,1,0:T(8,128)}, f32[3,4,8,256]{3,2,1,0:T(8,128)}) custom-call(f32[3,4,8,256]{3,2,1,0:T(8,128)S(1)} %copy-done, f32[6,4,8,256]{3,2,1,0:T(8,128)S(1)} %get-tuple-element.12.refs_3_.refs_1_, f32[6,4,8,256]{3,2,1,0:T(8,128)S(1)} %get-tuple-element.13.model_ref.refs_4_.refs_2_, f32[12,4,8,256]{3,2,1,0:T(8,128)S(1)} %shard_map.64.refs_3_, ...), custom_call_target="tpu_custom_call" | custom-call | flops 1638400 | bytes 1339392 | tf_op jit(solution)/shard_map/pallas_call | solution.py:325
  (3 shorter events, 0.1 us)
Async XLA Ops:
  0.6 3.0 %copy-start.1 = (f32[6,4,8,256]{3,2,1,0:T(8,128)S(1)}, f32[6,4,8,256]{3,2,1,0:T(8,128)}, u32[]{:S(2)}) copy-start(f32[6,4,8,256]{3,2,1,0:T(8,128)} %refs_1_.1) | copy-start | bytes 589828
  0.6 6.9 %collective-permute-start = (f32[3,4,8,256]{3,2,1,0:T(8,128)}, f32[3,4,8,256]{3,2,1,0:T(8,128)S(1)}, u32[]{:S(2)}, u32[]{:S(2)}) collective-permute-start(f32[3,4,8,256]{3,2,1,0:T(8,128)} %refs_0_.5), channel_id=1, source_target_pairs={{16,0},{0,16},{17,1},{1,17},{18,2},{2,18},{19,3},{3,19},{20,4},{4,... | collective-permute-start | bytes 294920 | tf_op jit(solution)/shard_map/ppermute | solution.py:338
  3.7 3.9 %copy-start = (f32[3,4,8,256]{3,2,1,0:T(8,128)S(1)}, f32[3,4,8,256]{3,2,1,0:T(8,128)}, u32[]{:S(2)}) copy-start(f32[3,4,8,256]{3,2,1,0:T(8,128)} %refs_0_.5) | copy-start | bytes 294916
  3.7 3.8 %collective-permute-start.1 = (f32[2,8,256]{2,1,0:T(8,128)S(1)}, f32[2,8,256]{2,1,0:T(8,128)S(1)}, u32[]{:S(2)}, u32[]{:S(2)}) collective-permute-start(f32[2,8,256]{2,1,0:T(8,128)S(1)} %get-tuple-element.10.size_ends_ref), channel_id=1, source_target_pairs={{16,0},{0,16},{17,1},{1,17},{18,2},{2,18},{19,3},{3,19},{20,4},{4,... | collective-permute-start | bytes 49160 | tf_op jit(solution)/shard_map/ppermute | solution.py:338
  5.6 2.0 %copy-start.2 = (s32[8]{0:T(128)S(1)}, s32[8]{0:T(128)}, u32[]{:S(2)}) copy-start(s32[8]{0:T(128)} %param.6) | copy-start | bytes 100
  5.6 13.2 %collective-permute-start.2 = (f32[6,4,8,256]{3,2,1,0:T(8,128)S(1)}, f32[6,4,8,256]{3,2,1,0:T(8,128)S(1)}, u32[]{:S(2)}, u32[]{:S(2)}) collective-permute-start(f32[6,4,8,256]{3,2,1,0:T(8,128)S(1)} %shard_map.61.refs_2_.refs_1_), channel_id=1, source_target_pairs={{16,0},{0,16},{17,1},{1,17},{18,2},{2,18},{19,3},{3,19},{20,4},{4,... | collective-permute-start | bytes 589832 | tf_op jit(solution)/shard_map/ppermute | solution.py:338
  8.0 12.1 %collective-permute-start.4 = (f32[18,8,256]{2,1,0:T(8,128)S(1)}, f32[18,8,256]{2,1,0:T(8,128)S(1)}, u32[]{:S(2)}, u32[]{:S(2)}) collective-permute-start(f32[18,8,256]{2,1,0:T(8,128)S(1)} %get-tuple-element.17), channel_id=1, source_target_pairs={{16,0},{0,16},{17,1},{1,17},{18,2},{2,18},{19,3},{3,19},{20,4},{4,... | collective-permute-start | bytes 442376 | tf_op jit(solution)/shard_map/ppermute | solution.py:338
  17.2 2.9 %collective-permute-start.3 = (f32[8,128]{1,0:T(8,128)S(1)}, f32[8,128]{1,0:T(8,128)S(1)}, u32[]{:S(2)}, u32[]{:S(2)}) collective-permute-start(f32[8,128]{1,0:T(8,128)S(1)} %psum.7.refs_6_), channel_id=1, source_target_pairs={{1,0},{3,1},{0,2},{5,3},{2,4},{7,5},{4,6},{9,7},{6,8},{11,9},{8,10... | collective-permute-start | bytes 12296 | tf_op jit(solution)/shard_map/ppermute | solution.py:343

commit v11 on v9

--- a/solution.py
+++ b/solution.py
@@ -108,7 +108,7 @@
             size_ends_ref[end, :, lanes] = value
 
 
-def fetch_kernel(cot_hbm, size_ends_ref, cot_ref, arrived):
+def fetch_kernel(cot_hbm, size_ends_ref, bins_ref, cot_ref, arrived):
     copy = pltpu.make_async_copy(cot_hbm, cot_ref, arrived)
     copy.start()
     copy.wait()
@@ -255,15 +255,36 @@
                 parts_ref[9 + a, z, :, lanes] = 2.0 * dual[z] - 4.0 * fourth[z]
 
 
+def far_kernel(tables, v_ref, parts_ref, *refs):
+    message_refs, whole_ref = refs[:-1], refs[-1]
+    cells = tables.cells
+    for lanes in halves(v_ref.shape[-1]):
+        v = [[v_ref[a, z, :, lanes] for z in range(cells)] for a in range(3)]
+        pulled = [[parts_ref[6 + a, z, :, lanes] for z in range(cells)] for a in range(3)]
+        crossed = [[parts_ref[9 + a, z, :, lanes] for z in range(cells)] for a in range(3)]
+        for place, ends in enumerate(message_refs, start=1):
+            from_model = [
+                tables.outside(place, [2.0 * ends[2 * k + end, :, lanes] for end in range(2)]) for k in range(6)
+            ]
+            for a in range(3):
+                dual = tables.outside(place, [ends[12 + 2 * a + end, :, lanes] for end in range(2)])
+                through = plain_dual(from_model, v, a, cells)
+                for z in range(cells):
+                    pulled[a][z] = pulled[a][z] + (through[z] - dual[z])
+                    crossed[a][z] = crossed[a][z] + 2.0 * dual[z]
+        for a in range(3):
+            for z in range(cells):
+                whole_ref[a, z, :, lanes] = pulled[a][z]
+                whole_ref[3 + a, z, :, lanes] = crossed[a][z]
+
+
 def finish_kernel(tables, count, turning, *refs):
-    peers = tables.devices - 1
-    cells = tables.cells
-    v_ref, leonard_ref, model_ref, parts_ref, bins_ref = refs[:5]
-    near_refs = refs[5 : 5 + count]
-    pair_ref = refs[5 + count]
-    far_message_refs = refs[6 + count : 6 + count + peers]
-    residual_hbm, grad_hbm, residual_ref, grad_ref, left = refs[6 + count + peers :]
-    total = sum_up([pair_ref[...]] + [ref[18, 0:8, 0:LANES] for ref in far_message_refs])
+    cells = tables.cells
+    leonard_ref, model_ref, parts_ref, whole_ref, bins_ref, pair_ref = refs[:6]
+    near_refs = refs[6 : 6 + count]
+    table_refs = refs[6 + count : 5 + count + tables.devices]
+    residual_hbm, grad_hbm, residual_ref, grad_ref, left = refs[5 + count + tables.devices :]
+    total = sum_up([pair_ref[...]] + [ref[18, 0:8, 0:LANES] for ref in table_refs])
     near = sum_up([ref[...] for ref in near_refs])
     if turning:
         place = lax.axis_index("stream")
@@ -271,7 +292,7 @@
         near = jnp.where(inner, near, 0.0)
     total = total + near
     inverse = 1.0 / (total[1:2] + EPSILON)
-    rows = v_ref.shape[2]
+    rows = leonard_ref.shape[2]
     lane = lax.broadcasted_iota(jnp.int32, bins_ref.shape, 1)
     mine = bins_ref[...] == lane
 
@@ -283,35 +304,20 @@
     pull = of_rows(-(total[2:3] * inverse))
     copies = []
     for k in range(6):
-        for lanes in halves(v_ref.shape[-1]):
-            for z in range(cells):
-                residual_ref[k, z, :, lanes] = (
-                    leonard_ref[k, z, :, lanes] - coefficient * model_ref[k, z, :, lanes]
-                )
+        for lanes in halves(leonard_ref.shape[-1]):
+            for z in range(cells):
+                residual_ref[k, z, :, lanes] = leonard_ref[k, z, :, lanes] - coefficient * model_ref[k, z, :, lanes]
         if k % 3 == 2:
             some = pl.ds(k - 2, 3)
             copies.append(pltpu.make_async_copy(residual_ref.at[some], residual_hbm.at[some], left.at[k // 3]))
             copies[-1].start()
-    for lanes in halves(v_ref.shape[-1]):
-        v = [[v_ref[a, z, :, lanes] for z in range(cells)] for a in range(3)]
-        from_model = [[] for _ in range(6)]
-        from_dual = [[] for _ in range(3)]
-        for place, ends in enumerate(far_message_refs, start=1):
-            for k in range(6):
-                from_model[k].append(tables.outside(place, [2.0 * ends[2 * k + end, :, lanes] for end in range(2)]))
-            for a in range(3):
-                pair = [(2.0 * coefficient - 1.0) * ends[12 + 2 * a + end, :, lanes] for end in range(2)]
-                from_dual[a].append(tables.outside(place, pair))
-        from_model = [functools.reduce(add_lists, lists) if lists else None for lists in from_model]
-        from_dual = [functools.reduce(add_lists, lists) if lists else None for lists in from_dual]
-        for a in range(3):
-            for z in range(cells):
-                pulled = parts_ref[6 + a, z, :, lanes] + coefficient * parts_ref[9 + a, z, :, lanes]
-                if peers:
-                    terms = [from_model[PAIR_OF[a][b]][z] * v[b][z] for b in range(3)]
-                    pulled = pulled + from_dual[a][z] + sum_up(terms)
+    for a in range(3):
+        for lanes in halves(leonard_ref.shape[-1]):
+            for z in range(cells):
                 grad_ref[a, z, :, lanes] = (
-                    parts_ref[a, z, :, lanes] + coefficient * parts_ref[3 + a, z, :, lanes] + pull * pulled
+                    parts_ref[a, z, :, lanes]
+                    + coefficient * parts_ref[3 + a, z, :, lanes]
+                    + pull * (whole_ref[a, z, :, lanes] + coefficient * whole_ref[3 + a, z, :, lanes])
                 )
     copies.append(pltpu.make_async_copy(grad_ref, grad_hbm, left.at[2]))
     copies[-1].start()
@@ -383,7 +389,8 @@
         work,
         pltpu.with_memory_space_constraint(cotangent, pltpu.HBM),
         size_ends,
-        in_specs=[REMAIN, WHOLE],
+        bins,
+        in_specs=[REMAIN, WHOLE, WHOLE],
         scratch=[pltpu.SemaphoreType.DMA(())],
     )
     far_cot = [from_ahead(near_cot, shift) for shift in range(1, span)]
@@ -433,19 +440,22 @@
         *far_v,
         *far_cot,
     )
+    (whole,) = call(
+        functools.partial(far_kernel, tables), [shaped(6, cells)], 100 * work, velocity, parts, *far_message
+    )
     outs = [jax.ShapeDtypeStruct((n, cells) + slab, jnp.float32) for n in (6, 3)]
     return tuple(
         call(
             functools.partial(finish_kernel, tables, len(near_sums), turning),
             outs,
             200 * work,
-            velocity,
             leonard,
             model,
             parts,
+            whole,
             bins,
+            pair_sums,
             *near_sums,
-            pair_sums,
             *far_message,
             out_specs=[REMAIN] * 2,
             scratch=[pltpu.VMEM(x.shape, x.dtype) for x in outs] + [pltpu.SemaphoreType.DMA((3,))],

time: 16.5 us -> 16.6 us (level)
    ppermute x4, waiting for transfers between devices: 1.06 us -> 1.86 us  [from_ahead(): lax.ppermute(values, 'span', [((i + shift) % peers, i) for i in range(pee...]
    ppermute x3, waiting for transfers between devices: 1.91 us -> 1.16 us  [from_source(): return lax.ppermute(values, ('span', 'stream'), pairs)]
    pallas_call x7 -> x8, Pallas kernels: 2.77 us -> 2.88 us  [call(): pl.pallas_call(kernel, out_shape=outs, in_specs=in_specs or [WHOLE] * len...]
  transfers between devices with their start and end apart: 7 -> 7, of which waited for: 5 -> 3; matrix products, arithmetic and copies ran while one was open for 0% -> 0% of each run, Pallas kernels for 12% -> 12%
where the time goes in v11:
time: 16.6 us; the launch traced here: 16.5 us
  starting transfers between devices  9.8 us (59%)
  waiting for transfers between devices  3.01 us (18%)
  Pallas kernels  2.88 us (17%)
  between operations  0.7 us (4%)
    ppermute x4, starting transfers between devices, from_ahead(): lax.ppermute(values, 'span', [((i + shift) % peers, i) for i in range(pee...  6.49 us
    ppermute x3, starting transfers between devices, from_source(): return lax.ppermute(values, ('span', 'stream'), pairs)  3.31 us
    pallas_call x8, Pallas kernels, call(): pl.pallas_call(kernel, out_shape=outs, in_specs=in_specs or [WHOLE] * len...  2.88 us
    ppermute x4, waiting for transfers between devices, from_ahead(): lax.ppermute(values, 'span', [((i + shift) % peers, i) for i in range(pee...  1.86 us
    ppermute x3, waiting for transfers between devices, from_source(): return lax.ppermute(values, ('span', 'stream'), pairs)  1.16 us
  transfers between devices with their start and end apart: 7, of which 3 were waited for; matrix products, arithmetic and copies ran while one was open for 0% of the time, Pallas kernels for 12%

profile of v11, /device:TPU:0, one launch (start us, length us, event | category | flops | bytes accessed | tf_op | source)
XLA Modules:
  0.0 16.5 jit_solution(6402809305435216059)
XLA Ops:
  0.6 0.0 copy-start.1
  0.6 3.0 %collective-permute-start = (f32[3,4,8,256]{3,2,1,0:T(8,128)}, f32[3,4,8,256]{3,2,1,0:T(8,128)S(1)}, u32[]{:S(2)}, u32[]{:S(2)}) collective-permute-start(f32[3,4,8,256]{3,2,1,0:T(8,128)} %v_ref.1), channel_id=1, source_target_pairs={{16,0},{0,16},{17,1},{1,17},{18,2},{2,18},{19,3},{3,19},{20,4},{4,... | collective-permute-start | bytes 294920 | tf_op jit(solution)/shard_map/ppermute | solution.py:347
  3.7 0.0 copy-done.1
  3.7 0.0 copy-start.2
  3.7 0.9 %collective-permute-start.1 = (f32[2,8,256]{2,1,0:T(8,128)S(1)}, f32[2,8,256]{2,1,0:T(8,128)S(1)}, u32[]{:S(2)}, u32[]{:S(2)}) collective-permute-start(f32[2,8,256]{2,1,0:T(8,128)S(1)} %get-tuple-element.11.size_ends_ref), channel_id=1, source_target_pairs={{16,0},{0,16},{17,1},{1,17},{18,2},{2,18},{19,3},{3,19},{20,4},{4,... | collective-permute-start | bytes 49160 | tf_op jit(solution)/shard_map/ppermute | solution.py:347
  4.6 0.0 copy-done.2
  4.6 0.1 broadcast_in_dim.2.bins_ref.refs_4_
  4.7 0.0 copy-start
  4.7 1.0 %shard_map.61.refs_2_.refs_1_ = f32[6,4,8,256]{3,2,1,0:T(8,128)S(1)} custom-call(f32[6,4,8,256]{3,2,1,0:T(8,128)} %cot_hbm.1, f32[2,8,256]{2,1,0:T(8,128)S(1)} %get-tuple-element.11.size_ends_ref, s32[8,128]{1,0:T(8,128)S(1)} %broadcast_in_dim.2.bins_ref.refs_4_), custom_call_target="tpu_custom_call" | custom-call | flops 8192 | bytes 413696 | tf_op jit(solution)/shard_map/pallas_call | solution.py:334
  5.7 1.2 %collective-permute-start.3 = (f32[6,4,8,256]{3,2,1,0:T(8,128)S(1)}, f32[6,4,8,256]{3,2,1,0:T(8,128)S(1)}, u32[]{:S(2)}, u32[]{:S(2)}) collective-permute-start(f32[6,4,8,256]{3,2,1,0:T(8,128)S(1)} %shard_map.61.refs_2_.refs_1_), channel_id=1, source_target_pairs={{16,0},{0,16},{17,1},{1,17},{18,2},{2,18},{19,3},{3,19},{20,4},{4,... | collective-permute-start | bytes 589832 | tf_op jit(solution)/shard_map/ppermute | solution.py:347
  6.9 0.6 %collective-permute-done.1.refs_6_ = f32[2,8,256]{2,1,0:T(8,128)S(1)} collective-permute-done((f32[2,8,256]{2,1,0:T(8,128)S(1)}, f32[2,8,256]{2,1,0:T(8,128)S(1)}, u32[]{:S(2)}, u32[]{:S(2)}) %collective-permute-start.1) | collective-permute-done | bytes 16416 | tf_op jit(solution)/shard_map/ppermute | solution.py:347
  7.5 0.0 collective-permute-done.refs_5_.refs_6_
  7.5 0.0 copy-done
  7.5 0.3 %shard_map.62 = (f32[3,4,8,256]{3,2,1,0:T(8,128)S(1)}, f32[6,4,8,256]{3,2,1,0:T(8,128)S(1)}, f32[6,4,8,256]{3,2,1,0:T(8,128)S(1)}, f32[8,128]{1,0:T(8,128)S(1)}) custom-call(f32[3,4,8,256]{3,2,1,0:T(8,128)S(1)} %copy-done, f32[6,4,8,256]{3,2,1,0:T(8,128)S(1)} %copy-done.1, f32[6,4,8,256]{3,2,1,0:T(8,128)S(1)} %shard_map.61.refs_2_.refs_1_, ...), custom_call_target="tpu_custom_call" | custom-call | flops 2457600000 | bytes 1138688 | tf_op jit(solution)/shard_map/pallas_call | solution.py:334
  7.9 0.0 collective-permute-start.2
  7.9 1.2 %collective-permute-done.2.other_sums_ref = f32[8,128]{1,0:T(8,128)S(1)} collective-permute-done((f32[8,128]{1,0:T(8,128)S(1)}, f32[8,128]{1,0:T(8,128)S(1)}, u32[]{:S(2)}, u32[]{:S(2)}) %collective-permute-start.2) | collective-permute-done | bytes 4128 | tf_op jit(solution)/shard_map/ppermute | solution.py:357
  9.1 1.3 %collective-permute-start.4 = (f32[19,8,256]{2,1,0:T(8,128)S(1)}, f32[19,8,256]{2,1,0:T(8,128)S(1)}, u32[]{:S(2)}, u32[]{:S(2)}) collective-permute-start(f32[19,8,256]{2,1,0:T(8,128)S(1)} %get-tuple-element.18), channel_id=1, source_target_pairs={{16,0},{0,16},{17,1},{1,17},{18,2},{2,18},{19,3},{3,19},{20,4},{4,... | collective-permute-start | bytes 466952 | tf_op jit(solution)/shard_map/ppermute | solution.py:347
  10.4 1.7 %collective-permute-start.6 = (f32[8,128]{1,0:T(8,128)S(1)}, f32[8,128]{1,0:T(8,128)S(1)}, u32[]{:S(2)}, u32[]{:S(2)}) collective-permute-start(f32[8,128]{1,0:T(8,128)S(1)} %get-tuple-element.19.refs_5_), channel_id=1, source_target_pairs={{17,0},{19,1},{16,2},{21,3},{18,4},{23,5},{20,6},{25,7},{22,8},{27... | collective-permute-start | bytes 12296 | tf_op jit(solution)/shard_map/ppermute | solution.py:357
  12.2 1.5 %collective-permute-start.5 = (f32[8,128]{1,0:T(8,128)S(1)}, f32[8,128]{1,0:T(8,128)S(1)}, u32[]{:S(2)}, u32[]{:S(2)}) collective-permute-start(f32[8,128]{1,0:T(8,128)S(1)} %get-tuple-element.19.refs_5_), channel_id=1, source_target_pairs={{1,0},{3,1},{0,2},{5,3},{2,4},{7,5},{4,6},{9,7},{6,8},{11,9},{8,10... | collective-permute-start | bytes 12296 | tf_op jit(solution)/shard_map/ppermute | solution.py:357
  13.7 0.0 collective-permute-done.3.refs_7_
  13.7 0.6 %shard_map.64.parts_ref.refs_2_ = f32[12,4,8,256]{3,2,1,0:T(8,128)S(1)} custom-call(f32[3,4,8,256]{3,2,1,0:T(8,128)S(1)} %copy-done, f32[6,4,8,256]{3,2,1,0:T(8,128)S(1)} %shard_map.61.refs_2_.refs_1_, f32[3,4,8,256]{3,2,1,0:T(8,128)S(1)} %get-tuple-element.15.smooth_ref.refs_2_, f32[6,4,8,256]{3,2,1,0:T(8,128)S(1)} %get-tuple-element.13.refs_3_.refs_0_, ...), custom_call_target="tpu_custom_call" | custom-call | flops 4096000 | bytes 1572864 | tf_op jit(solution)/shard_map/pallas_call | solution.py:334
  14.3 1.3 %collective-permute-done.4.refs_0_.refs_8_ = f32[19,8,256]{2,1,0:T(8,128)S(1)} collective-permute-done((f32[19,8,256]{2,1,0:T(8,128)S(1)}, f32[19,8,256]{2,1,0:T(8,128)S(1)}, u32[]{:S(2)}, u32[]{:S(2)}) %collective-permute-start.4) | collective-permute-done | bytes 155680 | tf_op jit(solution)/shard_map/ppermute | solution.py:347
  15.5 0.1 shard_map.65.refs_3_
  15.6 0.0 collective-permute-done.6.refs_7_
  15.6 0.0 collective-permute-done.5.refs_6_
  15.6 0.8 %shard_map.66 = (f32[6,4,8,256]{3,2,1,0:T(8,128)}, f32[3,4,8,256]{3,2,1,0:T(8,128)}) custom-call(f32[6,4,8,256]{3,2,1,0:T(8,128)S(1)} %get-tuple-element.13.refs_3_.refs_0_, f32[6,4,8,256]{3,2,1,0:T(8,128)S(1)} %get-tuple-element.14.model_ref.refs_4_.refs_1_, f32[12,4,8,256]{3,2,1,0:T(8,128)S(1)} %shard_map.64.parts_ref.refs_2_, ...), custom_call_target="tpu_custom_call" | custom-call | flops 1638400 | bytes 1449984 | tf_op jit(solution)/shard_map/pallas_call | solution.py:334
  (3 shorter events, 0.1 us)
Async XLA Ops:
  0.6 3.0 %copy-start.1 = (f32[6,4,8,256]{3,2,1,0:T(8,128)S(1)}, f32[6,4,8,256]{3,2,1,0:T(8,128)}, u32[]{:S(2)}) copy-start(f32[6,4,8,256]{3,2,1,0:T(8,128)} %refs_1_.1) | copy-start | bytes 589828
  0.6 6.9 %collective-permute-start = (f32[3,4,8,256]{3,2,1,0:T(8,128)}, f32[3,4,8,256]{3,2,1,0:T(8,128)S(1)}, u32[]{:S(2)}, u32[]{:S(2)}) collective-permute-start(f32[3,4,8,256]{3,2,1,0:T(8,128)} %v_ref.1), channel_id=1, source_target_pairs={{16,0},{0,16},{17,1},{1,17},{18,2},{2,18},{19,3},{3,19},{20,4},{4,... | collective-permute-start | bytes 294920 | tf_op jit(solution)/shard_map/ppermute | solution.py:347
  3.7 0.9 %copy-start.2 = (s32[8]{0:T(128)S(1)}, s32[8]{0:T(128)}, u32[]{:S(2)}) copy-start(s32[8]{0:T(128)} %param.6) | copy-start | bytes 100
  3.7 3.8 %collective-permute-start.1 = (f32[2,8,256]{2,1,0:T(8,128)S(1)}, f32[2,8,256]{2,1,0:T(8,128)S(1)}, u32[]{:S(2)}, u32[]{:S(2)}) collective-permute-start(f32[2,8,256]{2,1,0:T(8,128)S(1)} %get-tuple-element.11.size_ends_ref), channel_id=1, source_target_pairs={{16,0},{0,16},{17,1},{1,17},{18,2},{2,18},{19,3},{3,19},{20,4},{4,... | collective-permute-start | bytes 49160 | tf_op jit(solution)/shard_map/ppermute | solution.py:347
  4.7 2.8 %copy-start = (f32[3,4,8,256]{3,2,1,0:T(8,128)S(1)}, f32[3,4,8,256]{3,2,1,0:T(8,128)}, u32[]{:S(2)}) copy-start(f32[3,4,8,256]{3,2,1,0:T(8,128)} %v_ref.1) | copy-start | bytes 294916
  5.7 8.0 %collective-permute-start.3 = (f32[6,4,8,256]{3,2,1,0:T(8,128)S(1)}, f32[6,4,8,256]{3,2,1,0:T(8,128)S(1)}, u32[]{:S(2)}, u32[]{:S(2)}) collective-permute-start(f32[6,4,8,256]{3,2,1,0:T(8,128)S(1)} %shard_map.61.refs_2_.refs_1_), channel_id=1, source_target_pairs={{16,0},{0,16},{17,1},{1,17},{18,2},{2,18},{19,3},{3,19},{20,4},{4,... | collective-permute-start | bytes 589832 | tf_op jit(solution)/shard_map/ppermute | solution.py:347
  7.9 1.2 %collective-permute-start.2 = (f32[8,128]{1,0:T(8,128)S(1)}, f32[8,128]{1,0:T(8,128)S(1)}, u32[]{:S(2)}, u32[]{:S(2)}) collective-permute-start(f32[8,128]{1,0:T(8,128)S(1)} %get-tuple-element.16.sums_ref), channel_id=1, source_target_pairs={{1,0},{0,1},{3,2},{2,3},{5,4},{4,5},{7,6},{6,7},{9,8},{8,9},{11,10... | collective-permute-start | bytes 12296 | tf_op jit(solution)/shard_map/ppermute | solution.py:357
  9.1 6.4 %collective-permute-start.4 = (f32[19,8,256]{2,1,0:T(8,128)S(1)}, f32[19,8,256]{2,1,0:T(8,128)S(1)}, u32[]{:S(2)}, u32[]{:S(2)}) collective-permute-start(f32[19,8,256]{2,1,0:T(8,128)S(1)} %get-tuple-element.18), channel_id=1, source_target_pairs={{16,0},{0,16},{17,1},{1,17},{18,2},{2,18},{19,3},{3,19},{20,4},{4,... | collective-permute-start | bytes 466952 | tf_op jit(solution)/shard_map/ppermute | solution.py:347
  10.4 5.2 %collective-permute-start.6 = (f32[8,128]{1,0:T(8,128)S(1)}, f32[8,128]{1,0:T(8,128)S(1)}, u32[]{:S(2)}, u32[]{:S(2)}) collective-permute-start(f32[8,128]{1,0:T(8,128)S(1)} %get-tuple-element.19.refs_5_), channel_id=1, source_target_pairs={{17,0},{19,1},{16,2},{21,3},{18,4},{23,5},{20,6},{25,7},{22,8},{27... | collective-permute-start | bytes 12296 | tf_op jit(solution)/shard_map/ppermute | solution.py:357
  12.2 3.5 %collective-permute-start.5 = (f32[8,128]{1,0:T(8,128)S(1)}, f32[8,128]{1,0:T(8,128)S(1)}, u32[]{:S(2)}, u32[]{:S(2)}) collective-permute-start(f32[8,128]{1,0:T(8,128)S(1)} %get-tuple-element.19.refs_5_), channel_id=1, source_target_pairs={{1,0},{3,1},{0,2},{5,3},{2,4},{7,5},{4,6},{9,7},{6,8},{11,9},{8,10... | collective-permute-start | bytes 12296 | tf_op jit(solution)/shard_map/ppermute | solution.py:357

commit v12 on v9

--- a/solution.py
+++ b/solution.py
@@ -108,8 +108,8 @@
             size_ends_ref[end, :, lanes] = value
 
 
-def fetch_kernel(cot_hbm, size_ends_ref, cot_ref, arrived):
-    copy = pltpu.make_async_copy(cot_hbm, cot_ref, arrived)
+def fetch_kernel(v_hbm, size_ends_ref, bins_ref, v_ref, arrived):
+    copy = pltpu.make_async_copy(v_hbm, v_ref, arrived)
     copy.start()
     copy.wait()
 
@@ -377,22 +377,24 @@
         functools.partial(prepare_kernel, tables), [shaped(cells), shaped(2)], LONG * work, lane, strain
     )
     far_size = [from_ahead(size_ends, shift) for shift in range(1, span)]
-    (near_cot,) = call(
+    (near_v,) = call(
         fetch_kernel,
-        [shaped(6, cells)],
+        [shaped(3, cells)],
         work,
-        pltpu.with_memory_space_constraint(cotangent, pltpu.HBM),
+        pltpu.with_memory_space_constraint(velocity, pltpu.HBM),
         size_ends,
-        in_specs=[REMAIN, WHOLE],
+        bins,
+        in_specs=[REMAIN, WHOLE, WHOLE],
         scratch=[pltpu.SemaphoreType.DMA(())],
     )
+    near_v, near_cot = lax.optimization_barrier((near_v, cotangent))
     far_cot = [from_ahead(near_cot, shift) for shift in range(1, span)]
     table = pltpu.VMEM((8, LANES), jnp.float32)
     smooth, leonard, model, sums = call(
         functools.partial(forward_kernel, tables),
         [shaped(3, cells), shaped(6, cells), shaped(6, cells), table],
         LONG * work,
-        velocity,
+        near_v,
         strain,
         near_cot,
         size,
@@ -424,7 +426,7 @@
         functools.partial(local_kernel, tables),
         [shaped(12, cells)],
         500 * work,
-        velocity,
+        near_v,
         near_cot,
         smooth,
         leonard,
@@ -439,7 +441,7 @@
             functools.partial(finish_kernel, tables, len(near_sums), turning),
             outs,
             200 * work,
-            velocity,
+            near_v,
             leonard,
             model,
             parts,

time: 16.5 us -> 16.5 us (level)
  no operation moved by 1% of the time
where the time goes in v12:
time: 16.5 us; the launch traced here: 16.3 us
  starting transfers between devices  9.8 us (59%)
  waiting for transfers between devices  3.02 us (18%)
  Pallas kernels  2.73 us (17%)
  between operations  0.69 us (4%)
    ppermute x4, starting transfers between devices, from_ahead(): lax.ppermute(values, 'span', [((i + shift) % peers, i) for i in range(pee...  6.49 us
    ppermute x3, starting transfers between devices, from_source(): return lax.ppermute(values, ('span', 'stream'), pairs)  3.31 us
    pallas_call x7, Pallas kernels, call(): pl.pallas_call(kernel, out_shape=outs, in_specs=in_specs or [WHOLE] * len...  2.73 us
    ppermute x3, waiting for transfers between devices, from_source(): return lax.ppermute(values, ('span', 'stream'), pairs)  1.91 us
    ppermute x4, waiting for transfers between devices, from_ahead(): lax.ppermute(values, 'span', [((i + shift) % peers, i) for i in range(pee...  1.11 us
  transfers between devices with their start and end apart: 7, of which 5 were waited for; matrix products, arithmetic and copies ran while one was open for 0% of the time, Pallas kernels for 12%

profile of v12, /device:TPU:0, one launch (start us, length us, event | category | flops | bytes accessed | tf_op | source)
XLA Modules:
  0.0 16.3 jit_solution(3794361537118126447)
XLA Ops:
  0.6 0.0 copy-start.1
  0.6 3.0 %collective-permute-start = (f32[3,4,8,256]{3,2,1,0:T(8,128)}, f32[3,4,8,256]{3,2,1,0:T(8,128)S(1)}, u32[]{:S(2)}, u32[]{:S(2)}) collective-permute-start(f32[3,4,8,256]{3,2,1,0:T(8,128)} %v_hbm.1), channel_id=1, source_target_pairs={{16,0},{0,16},{17,1},{1,17},{18,2},{2,18},{19,3},{3,19},{20,4},{4,... | collective-permute-start | bytes 294920 | tf_op jit(solution)/shard_map/ppermute | solution.py:341
  3.7 0.0 copy-done.1
  3.7 0.0 copy-start.2
  3.7 0.0 copy-start
  3.7 0.9 %collective-permute-start.1 = (f32[2,8,256]{2,1,0:T(8,128)S(1)}, f32[2,8,256]{2,1,0:T(8,128)S(1)}, u32[]{:S(2)}, u32[]{:S(2)}) collective-permute-start(f32[2,8,256]{2,1,0:T(8,128)S(1)} %get-tuple-element.13.size_ends_ref), channel_id=1, source_target_pairs={{16,0},{0,16},{17,1},{1,17},{18,2},{2,18},{19,3},{3,19},{20,4},{4,... | collective-permute-start | bytes 49160 | tf_op jit(solution)/shard_map/ppermute | solution.py:341
  4.6 0.0 copy-done.2
  4.6 0.1 broadcast_in_dim.2.bins_ref.refs_4_
  4.7 0.9 %shard_map.61.refs_0_ = f32[3,4,8,256]{3,2,1,0:T(8,128)S(1)} custom-call(f32[3,4,8,256]{3,2,1,0:T(8,128)} %v_hbm.1, f32[2,8,256]{2,1,0:T(8,128)S(1)} %get-tuple-element.13.size_ends_ref, s32[8,128]{1,0:T(8,128)S(1)} %broadcast_in_dim.2.bins_ref.refs_4_), custom_call_target="tpu_custom_call" | custom-call | flops 8192 | bytes 217088 | tf_op jit(solution)/shard_map/pallas_call | solution.py:328
  5.6 0.0 copy-done
  5.6 1.2 %collective-permute-start.3 = (f32[6,4,8,256]{3,2,1,0:T(8,128)S(1)}, f32[6,4,8,256]{3,2,1,0:T(8,128)S(1)}, u32[]{:S(2)}, u32[]{:S(2)}) collective-permute-start(f32[6,4,8,256]{3,2,1,0:T(8,128)S(1)} %copy-done), channel_id=1, source_target_pairs={{16,0},{0,16},{17,1},{1,17},{18,2},{2,18},{19,3},{3,19},{20,4},{4,... | collective-permute-start | bytes 589832 | tf_op jit(solution)/shard_map/ppermute | solution.py:341
  6.9 0.7 %collective-permute-done.1.refs_6_ = f32[2,8,256]{2,1,0:T(8,128)S(1)} collective-permute-done((f32[2,8,256]{2,1,0:T(8,128)S(1)}, f32[2,8,256]{2,1,0:T(8,128)S(1)}, u32[]{:S(2)}, u32[]{:S(2)}) %collective-permute-start.1) | collective-permute-done | bytes 16416 | tf_op jit(solution)/shard_map/ppermute | solution.py:341
  7.5 0.0 collective-permute-done.refs_5_.refs_6_
  7.5 0.3 %shard_map.62 = (f32[3,4,8,256]{3,2,1,0:T(8,128)S(1)}, f32[6,4,8,256]{3,2,1,0:T(8,128)S(1)}, f32[6,4,8,256]{3,2,1,0:T(8,128)S(1)}, f32[8,128]{1,0:T(8,128)S(1)}) custom-call(f32[3,4,8,256]{3,2,1,0:T(8,128)S(1)} %shard_map.61.refs_0_, f32[6,4,8,256]{3,2,1,0:T(8,128)S(1)} %copy-done.1, f32[6,4,8,256]{3,2,1,0:T(8,128)S(1)} %copy-done, ...), custom_call_target="tpu_custom_call" | custom-call | flops 2457600000 | bytes 1138688 | tf_op jit(solution)/shard_map/pallas_call | solution.py:328
  7.9 0.0 collective-permute-start.2
  7.9 1.2 %collective-permute-done.2.other_sums_ref = f32[8,128]{1,0:T(8,128)S(1)} collective-permute-done((f32[8,128]{1,0:T(8,128)S(1)}, f32[8,128]{1,0:T(8,128)S(1)}, u32[]{:S(2)}, u32[]{:S(2)}) %collective-permute-start.2) | collective-permute-done | bytes 4128 | tf_op jit(solution)/shard_map/ppermute | solution.py:351
  9.1 1.3 %collective-permute-start.6 = (f32[19,8,256]{2,1,0:T(8,128)S(1)}, f32[19,8,256]{2,1,0:T(8,128)S(1)}, u32[]{:S(2)}, u32[]{:S(2)}) collective-permute-start(f32[19,8,256]{2,1,0:T(8,128)S(1)} %get-tuple-element.23), channel_id=1, source_target_pairs={{16,0},{0,16},{17,1},{1,17},{18,2},{2,18},{19,3},{3,19},{20,4},{4,... | collective-permute-start | bytes 466952 | tf_op jit(solution)/shard_map/ppermute | solution.py:341
  10.4 1.7 %collective-permute-start.5 = (f32[8,128]{1,0:T(8,128)S(1)}, f32[8,128]{1,0:T(8,128)S(1)}, u32[]{:S(2)}, u32[]{:S(2)}) collective-permute-start(f32[8,128]{1,0:T(8,128)S(1)} %get-tuple-element.22.refs_7_), channel_id=1, source_target_pairs={{17,0},{19,1},{16,2},{21,3},{18,4},{23,5},{20,6},{25,7},{22,8},{27... | collective-permute-start | bytes 12296 | tf_op jit(solution)/shard_map/ppermute | solution.py:351
  12.2 1.5 %collective-permute-start.4 = (f32[8,128]{1,0:T(8,128)S(1)}, f32[8,128]{1,0:T(8,128)S(1)}, u32[]{:S(2)}, u32[]{:S(2)}) collective-permute-start(f32[8,128]{1,0:T(8,128)S(1)} %get-tuple-element.22.refs_7_), channel_id=1, source_target_pairs={{1,0},{3,1},{0,2},{5,3},{2,4},{7,5},{4,6},{9,7},{6,8},{11,9},{8,10... | collective-permute-start | bytes 12296 | tf_op jit(solution)/shard_map/ppermute | solution.py:351
  13.7 0.0 collective-permute-done.3.refs_7_
  13.7 0.6 %shard_map.64.refs_3_ = f32[12,4,8,256]{3,2,1,0:T(8,128)S(1)} custom-call(f32[3,4,8,256]{3,2,1,0:T(8,128)S(1)} %shard_map.61.refs_0_, f32[6,4,8,256]{3,2,1,0:T(8,128)S(1)} %copy-done, f32[3,4,8,256]{3,2,1,0:T(8,128)S(1)} %get-tuple-element.19.smooth_ref.refs_2_, f32[6,4,8,256]{3,2,1,0:T(8,128)S(1)} %get-tuple-element.17.refs_3_.refs_1_, ...), custom_call_target="tpu_custom_call" | custom-call | flops 4096000 | bytes 1572864 | tf_op jit(solution)/shard_map/pallas_call | solution.py:328
  14.3 0.6 %collective-permute-done.5.refs_6_ = f32[8,128]{1,0:T(8,128)S(1)} collective-permute-done((f32[8,128]{1,0:T(8,128)S(1)}, f32[8,128]{1,0:T(8,128)S(1)}, u32[]{:S(2)}, u32[]{:S(2)}) %collective-permute-start.5) | collective-permute-done | bytes 4128 | tf_op jit(solution)/shard_map/ppermute | solution.py:351
  14.8 0.2 %collective-permute-done.4.refs_5_ = f32[8,128]{1,0:T(8,128)S(1)} collective-permute-done((f32[8,128]{1,0:T(8,128)S(1)}, f32[8,128]{1,0:T(8,128)S(1)}, u32[]{:S(2)}, u32[]{:S(2)}) %collective-permute-start.4) | collective-permute-done | bytes 4128 | tf_op jit(solution)/shard_map/ppermute | solution.py:351
  15.0 0.4 %collective-permute-done.6.refs_8_ = f32[19,8,256]{2,1,0:T(8,128)S(1)} collective-permute-done((f32[19,8,256]{2,1,0:T(8,128)S(1)}, f32[19,8,256]{2,1,0:T(8,128)S(1)}, u32[]{:S(2)}, u32[]{:S(2)}) %collective-permute-start.6) | collective-permute-done | bytes 155680 | tf_op jit(solution)/shard_map/ppermute | solution.py:341
  15.5 0.8 %shard_map.65 = (f32[6,4,8,256]{3,2,1,0:T(8,128)}, f32[3,4,8,256]{3,2,1,0:T(8,128)}) custom-call(f32[3,4,8,256]{3,2,1,0:T(8,128)S(1)} %shard_map.61.refs_0_, f32[6,4,8,256]{3,2,1,0:T(8,128)S(1)} %get-tuple-element.17.refs_3_.refs_1_, f32[6,4,8,256]{3,2,1,0:T(8,128)S(1)} %get-tuple-element.18.model_ref.refs_4_.refs_2_, ...), custom_call_target="tpu_custom_call" | custom-call | flops 1638400 | bytes 1351680 | tf_op jit(solution)/shard_map/pallas_call | solution.py:328
  (3 shorter events, 0.1 us)
Async XLA Ops:
  0.6 3.0 %copy-start.1 = (f32[6,4,8,256]{3,2,1,0:T(8,128)S(1)}, f32[6,4,8,256]{3,2,1,0:T(8,128)}, u32[]{:S(2)}) copy-start(f32[6,4,8,256]{3,2,1,0:T(8,128)} %refs_1_.1) | copy-start | bytes 589828
  0.6 6.9 %collective-permute-start = (f32[3,4,8,256]{3,2,1,0:T(8,128)}, f32[3,4,8,256]{3,2,1,0:T(8,128)S(1)}, u32[]{:S(2)}, u32[]{:S(2)}) collective-permute-start(f32[3,4,8,256]{3,2,1,0:T(8,128)} %v_hbm.1), channel_id=1, source_target_pairs={{16,0},{0,16},{17,1},{1,17},{18,2},{2,18},{19,3},{3,19},{20,4},{4,... | collective-permute-start | bytes 294920 | tf_op jit(solution)/shard_map/ppermute | solution.py:341
  3.7 1.0 %copy-start.2 = (s32[8]{0:T(128)S(1)}, s32[8]{0:T(128)}, u32[]{:S(2)}) copy-start(s32[8]{0:T(128)} %param.6) | copy-start | bytes 100
  3.7 1.9 %copy-start = (f32[6,4,8,256]{3,2,1,0:T(8,128)S(1)}, f32[6,4,8,256]{3,2,1,0:T(8,128)}, u32[]{:S(2)}) copy-start(f32[6,4,8,256]{3,2,1,0:T(8,128)} %refs_1_.2) | copy-start | bytes 589828
  3.7 3.8 %collective-permute-start.1 = (f32[2,8,256]{2,1,0:T(8,128)S(1)}, f32[2,8,256]{2,1,0:T(8,128)S(1)}, u32[]{:S(2)}, u32[]{:S(2)}) collective-permute-start(f32[2,8,256]{2,1,0:T(8,128)S(1)} %get-tuple-element.13.size_ends_ref), channel_id=1, source_target_pairs={{16,0},{0,16},{17,1},{1,17},{18,2},{2,18},{19,3},{3,19},{20,4},{4,... | collective-permute-start | bytes 49160 | tf_op jit(solution)/shard_map/ppermute | solution.py:341
  5.6 8.1 %collective-permute-start.3 = (f32[6,4,8,256]{3,2,1,0:T(8,128)S(1)}, f32[6,4,8,256]{3,2,1,0:T(8,128)S(1)}, u32[]{:S(2)}, u32[]{:S(2)}) collective-permute-start(f32[6,4,8,256]{3,2,1,0:T(8,128)S(1)} %copy-done), channel_id=1, source_target_pairs={{16,0},{0,16},{17,1},{1,17},{18,2},{2,18},{19,3},{3,19},{20,4},{4,... | collective-permute-start | bytes 589832 | tf_op jit(solution)/shard_map/ppermute | solution.py:341
  7.9 1.2 %collective-permute-start.2 = (f32[8,128]{1,0:T(8,128)S(1)}, f32[8,128]{1,0:T(8,128)S(1)}, u32[]{:S(2)}, u32[]{:S(2)}) collective-permute-start(f32[8,128]{1,0:T(8,128)S(1)} %get-tuple-element.20.sums_ref), channel_id=1, source_target_pairs={{1,0},{0,1},{3,2},{2,3},{5,4},{4,5},{7,6},{6,7},{9,8},{8,9},{11,10... | collective-permute-start | bytes 12296 | tf_op jit(solution)/shard_map/ppermute | solution.py:351
  9.1 6.3 %collective-permute-start.6 = (f32[19,8,256]{2,1,0:T(8,128)S(1)}, f32[19,8,256]{2,1,0:T(8,128)S(1)}, u32[]{:S(2)}, u32[]{:S(2)}) collective-permute-start(f32[19,8,256]{2,1,0:T(8,128)S(1)} %get-tuple-element.23), channel_id=1, source_target_pairs={{16,0},{0,16},{17,1},{1,17},{18,2},{2,18},{19,3},{3,19},{20,4},{4,... | collective-permute-start | bytes 466952 | tf_op jit(solution)/shard_map/ppermute | solution.py:341
  10.4 4.4 %collective-permute-start.5 = (f32[8,128]{1,0:T(8,128)S(1)}, f32[8,128]{1,0:T(8,128)S(1)}, u32[]{:S(2)}, u32[]{:S(2)}) collective-permute-start(f32[8,128]{1,0:T(8,128)S(1)} %get-tuple-element.22.refs_7_), channel_id=1, source_target_pairs={{17,0},{19,1},{16,2},{21,3},{18,4},{23,5},{20,6},{25,7},{22,8},{27... | collective-permute-start | bytes 12296 | tf_op jit(solution)/shard_map/ppermute | solution.py:351
  12.2 2.9 %collective-permute-start.4 = (f32[8,128]{1,0:T(8,128)S(1)}, f32[8,128]{1,0:T(8,128)S(1)}, u32[]{:S(2)}, u32[]{:S(2)}) collective-permute-start(f32[8,128]{1,0:T(8,128)S(1)} %get-tuple-element.22.refs_7_), channel_id=1, source_target_pairs={{1,0},{3,1},{0,2},{5,3},{2,4},{7,5},{4,6},{9,7},{6,8},{11,9},{8,10... | collective-permute-start | bytes 12296 | tf_op jit(solution)/shard_map/ppermute | solution.py:351

commit v13 on v9

--- a/solution.py
+++ b/solution.py
@@ -182,11 +182,8 @@
     sums_ref[...] = table
 
 
-def message_kernel(tables, smooth_ref, model_ref, sums_ref, other_sums_ref, dual_ref, message_ref, pair_ref):
+def message_kernel(tables, smooth_ref, model_ref, dual_ref, message_ref):
     cells = tables.cells
-    pair_sums = sums_ref[...] + other_sums_ref[...]
-    pair_ref[...] = pair_sums
-    message_ref[18, 0:8, 0:LANES] = pair_sums
     for lanes in halves(model_ref.shape[-1]):
         model = [[model_ref[k, z, :, lanes] for z in range(cells)] for k in range(6)]
         smooth_v = [[smooth_ref[a, z, :, lanes] for z in range(cells)] for a in range(3)]
@@ -259,11 +256,12 @@
     peers = tables.devices - 1
     cells = tables.cells
     v_ref, leonard_ref, model_ref, parts_ref, bins_ref = refs[:5]
-    near_refs = refs[5 : 5 + count]
-    pair_ref = refs[5 + count]
-    far_message_refs = refs[6 + count : 6 + count + peers]
-    residual_hbm, grad_hbm, residual_ref, grad_ref, left = refs[6 + count + peers :]
-    total = sum_up([pair_ref[...]] + [ref[18, 0:8, 0:LANES] for ref in far_message_refs])
+    split = count - count // tables.devices
+    near_refs = refs[5 : 5 + split] + refs[6 + split + peers : 6 + count + peers]
+    pair_refs = refs[5 + split : 6 + split + peers]
+    far_message_refs = refs[6 + count + peers : 6 + count + 2 * peers]
+    residual_hbm, grad_hbm, residual_ref, grad_ref, left = refs[6 + count + 2 * peers :]
+    total = sum_up([ref[...] for ref in pair_refs])
     near = sum_up([ref[...] for ref in near_refs])
     if turning:
         place = lax.axis_index("stream")
@@ -401,15 +399,10 @@
         *far_size,
     )
     other_sums = from_source(sums, 0, lambda j: j ^ 1)
-    dual, message, pair_sums = call(
-        functools.partial(message_kernel, tables),
-        [shaped(3, cells), shaped(19), table],
-        100 * work,
-        smooth,
-        model,
-        sums,
-        other_sums,
-    )
+    dual, message = call(
+        functools.partial(message_kernel, tables), [shaped(3, cells), shaped(18)], 100 * work, smooth, model
+    )
+    pair_sums = sums + other_sums
     far_message = [from_ahead(message, shift) for shift in range(1, span)]
     most_rows = 2 * rows * stream // NBINS
     reach = -(-(most_rows - 1) // rows)
@@ -419,11 +412,13 @@
     else:
         steps = range(1, -(-reach // 2) + 1)
         sources = [functools.partial(lambda j, away: j + away, away=2 * step * way) for step in steps for way in (1, -1)]
-    near_sums = [from_source(pair_sums, shift, source) for shift in range(span) for source in sources]
+    across_sums = [from_source(pair_sums, shift, source) for shift in range(1, span) for source in sources]
+    far_pairs = [from_ahead(pair_sums, shift) for shift in range(1, span)]
+    near_sums = [from_source(pair_sums, 0, source) for source in sources]
     (parts,) = call(
         functools.partial(local_kernel, tables),
         [shaped(12, cells)],
-        500 * work,
+        LONG * work,
         velocity,
         near_cot,
         smooth,
@@ -436,7 +431,7 @@
     outs = [jax.ShapeDtypeStruct((n, cells) + slab, jnp.float32) for n in (6, 3)]
     return tuple(
         call(
-            functools.partial(finish_kernel, tables, len(near_sums), turning),
+            functools.partial(finish_kernel, tables, len(across_sums) + len(near_sums), turning),
             outs,
             200 * work,
             velocity,
@@ -444,8 +439,10 @@
             model,
             parts,
             bins,
+            *across_sums,
+            *far_pairs,
+            pair_sums,
             *near_sums,
-            pair_sums,
             *far_message,
             out_specs=[REMAIN] * 2,
             scratch=[pltpu.VMEM(x.shape, x.dtype) for x in outs] + [pltpu.SemaphoreType.DMA((3,))],

time: 16.5 us -> 16.4 us (level)
  waiting for transfers between devices: 2.97 us -> 1.59 us
  starting transfers between devices: 9.8 us -> 11.1 us
    ppermute x3, waiting for transfers between devices: 1.91 us -> 0.1 us  [from_source(): return lax.ppermute(values, ('span', 'stream'), pairs)]
    ppermute x4 -> x5, starting transfers between devices: 6.5 us -> 7.51 us  [from_ahead(): lax.ppermute(values, 'span', [((i + shift) % peers, i) for i in range(pee...]
    ppermute x4 -> x5, waiting for transfers between devices: 1.06 us -> 1.49 us  [from_ahead(): lax.ppermute(values, 'span', [((i + shift) % peers, i) for i in range(pee...]
    ppermute x3, starting transfers between devices: 3.3 us -> 3.55 us  [from_source(): return lax.ppermute(values, ('span', 'stream'), pairs)]
  transfers between devices with their start and end apart: 7 -> 8, of which waited for: 5 -> 3; matrix products, arithmetic and copies ran while one was open for 0% -> 0% of each run, Pallas kernels for 12% -> 12%
where the time goes in v13:
time: 16.4 us; the launch traced here: 16.2 us
  starting transfers between devices  11.1 us (68%)
  Pallas kernels  2.77 us (17%)
  waiting for transfers between devices  1.59 us (10%)
  between operations  0.69 us (4%)
    ppermute x5, starting transfers between devices, from_ahead(): lax.ppermute(values, 'span', [((i + shift) % peers, i) for i in range(pee...  7.51 us
    ppermute x3, starting transfers between devices, from_source(): return lax.ppermute(values, ('span', 'stream'), pairs)  3.55 us
    pallas_call x7, Pallas kernels, call(): pl.pallas_call(kernel, out_shape=outs, in_specs=in_specs or [WHOLE] * len...  2.77 us
    ppermute x5, waiting for transfers between devices, from_ahead(): lax.ppermute(values, 'span', [((i + shift) % peers, i) for i in range(pee...  1.49 us
  transfers between devices with their start and end apart: 8, of which 3 were waited for; matrix products, arithmetic and copies ran while one was open for 0% of the time, Pallas kernels for 12%

profile of v13, /device:TPU:0, one launch (start us, length us, event | category | flops | bytes accessed | tf_op | source)
XLA Modules:
  0.0 16.2 jit_solution(6190157984159447646)
XLA Ops:
  0.6 0.0 copy-start.1
  0.6 3.0 %collective-permute-start = (f32[3,4,8,256]{3,2,1,0:T(8,128)}, f32[3,4,8,256]{3,2,1,0:T(8,128)S(1)}, u32[]{:S(2)}, u32[]{:S(2)}) collective-permute-start(f32[3,4,8,256]{3,2,1,0:T(8,128)} %refs_0_.5), channel_id=1, source_target_pairs={{16,0},{0,16},{17,1},{1,17},{18,2},{2,18},{19,3},{3,19},{20,4},{4,... | collective-permute-start | bytes 294920 | tf_op jit(solution)/shard_map/ppermute | solution.py:339
  3.7 0.0 copy-done.1
  3.7 0.0 copy-start
  3.7 0.9 %collective-permute-start.1 = (f32[2,8,256]{2,1,0:T(8,128)S(1)}, f32[2,8,256]{2,1,0:T(8,128)S(1)}, u32[]{:S(2)}, u32[]{:S(2)}) collective-permute-start(f32[2,8,256]{2,1,0:T(8,128)S(1)} %get-tuple-element.10.size_ends_ref), channel_id=1, source_target_pairs={{16,0},{0,16},{17,1},{1,17},{18,2},{2,18},{19,3},{3,19},{20,4},{4,... | collective-permute-start | bytes 49160 | tf_op jit(solution)/shard_map/ppermute | solution.py:339
  4.6 0.9 %shard_map.61.refs_2_.refs_1_ = f32[6,4,8,256]{3,2,1,0:T(8,128)S(1)} custom-call(f32[6,4,8,256]{3,2,1,0:T(8,128)} %cot_hbm.1, f32[2,8,256]{2,1,0:T(8,128)S(1)} %get-tuple-element.10.size_ends_ref), custom_call_target="tpu_custom_call" | custom-call | flops 8192 | bytes 409600 | tf_op jit(solution)/shard_map/pallas_call | solution.py:326
  5.6 0.0 copy-start.2
  5.6 1.2 %collective-permute-start.2 = (f32[6,4,8,256]{3,2,1,0:T(8,128)S(1)}, f32[6,4,8,256]{3,2,1,0:T(8,128)S(1)}, u32[]{:S(2)}, u32[]{:S(2)}) collective-permute-start(f32[6,4,8,256]{3,2,1,0:T(8,128)S(1)} %shard_map.61.refs_2_.refs_1_), channel_id=1, source_target_pairs={{16,0},{0,16},{17,1},{1,17},{18,2},{2,18},{19,3},{3,19},{20,4},{4,... | collective-permute-start | bytes 589832 | tf_op jit(solution)/shard_map/ppermute | solution.py:339
  6.8 0.7 %collective-permute-done.1.refs_6_ = f32[2,8,256]{2,1,0:T(8,128)S(1)} collective-permute-done((f32[2,8,256]{2,1,0:T(8,128)S(1)}, f32[2,8,256]{2,1,0:T(8,128)S(1)}, u32[]{:S(2)}, u32[]{:S(2)}) %collective-permute-start.1) | collective-permute-done | bytes 16416 | tf_op jit(solution)/shard_map/ppermute | solution.py:339
  7.5 0.0 collective-permute-done.refs_5_.refs_6_
  7.5 0.0 copy-done.2
  7.5 0.1 broadcast_in_dim.2.refs_4_
  7.6 0.0 copy-done
  7.6 0.3 %shard_map.62 = (f32[3,4,8,256]{3,2,1,0:T(8,128)S(1)}, f32[6,4,8,256]{3,2,1,0:T(8,128)S(1)}, f32[6,4,8,256]{3,2,1,0:T(8,128)S(1)}, f32[8,128]{1,0:T(8,128)S(1)}) custom-call(f32[3,4,8,256]{3,2,1,0:T(8,128)S(1)} %copy-done, f32[6,4,8,256]{3,2,1,0:T(8,128)S(1)} %copy-done.1, f32[6,4,8,256]{3,2,1,0:T(8,128)S(1)} %shard_map.61.refs_2_.refs_1_, ...), custom_call_target="tpu_custom_call" | custom-call | flops 2457600000 | bytes 1138688 | tf_op jit(solution)/shard_map/pallas_call | solution.py:326
  8.0 0.0 collective-permute-start.3
  8.1 1.3 %collective-permute-start.7 = (f32[18,8,256]{2,1,0:T(8,128)S(1)}, f32[18,8,256]{2,1,0:T(8,128)S(1)}, u32[]{:S(2)}, u32[]{:S(2)}) collective-permute-start(f32[18,8,256]{2,1,0:T(8,128)S(1)} %get-tuple-element.17), channel_id=1, source_target_pairs={{16,0},{0,16},{17,1},{1,17},{18,2},{2,18},{19,3},{3,19},{20,4},{4,... | collective-permute-start | bytes 442376 | tf_op jit(solution)/shard_map/ppermute | solution.py:339
  9.4 0.0 collective-permute-done.3
  9.4 2.0 %collective-permute-start.4 = (f32[8,128]{1,0:T(8,128)S(1)}, f32[8,128]{1,0:T(8,128)S(1)}, u32[]{:S(2)}, u32[]{:S(2)}) collective-permute-start(f32[8,128]{1,0:T(8,128)S(1)} %add.3.refs_7_), channel_id=1, source_target_pairs={{17,0},{19,1},{16,2},{21,3},{18,4},{23,5},{20,6},{25,7},{22,8},{27... | collective-permute-start | bytes 12296 | tf_op jit(solution)/shard_map/ppermute | solution.py:349
  11.3 1.0 %collective-permute-start.5 = (f32[8,128]{1,0:T(8,128)S(1)}, f32[8,128]{1,0:T(8,128)S(1)}, u32[]{:S(2)}, u32[]{:S(2)}) collective-permute-start(f32[8,128]{1,0:T(8,128)S(1)} %add.3.refs_7_), channel_id=1, source_target_pairs={{16,0},{0,16},{17,1},{1,17},{18,2},{2,18},{19,3},{3,19},{20,4},{4,... | collective-permute-start | bytes 12296 | tf_op jit(solution)/shard_map/ppermute | solution.py:339
  12.3 1.5 %collective-permute-start.6 = (f32[8,128]{1,0:T(8,128)S(1)}, f32[8,128]{1,0:T(8,128)S(1)}, u32[]{:S(2)}, u32[]{:S(2)}) collective-permute-start(f32[8,128]{1,0:T(8,128)S(1)} %add.3.refs_7_), channel_id=1, source_target_pairs={{1,0},{3,1},{0,2},{5,3},{2,4},{7,5},{4,6},{9,7},{6,8},{11,9},{8,10... | collective-permute-start | bytes 12296 | tf_op jit(solution)/shard_map/ppermute | solution.py:349
  13.9 0.0 collective-permute-done.2.refs_7_
  13.9 0.6 %shard_map.64.refs_3_ = f32[12,4,8,256]{3,2,1,0:T(8,128)S(1)} custom-call(f32[3,4,8,256]{3,2,1,0:T(8,128)S(1)} %copy-done, f32[6,4,8,256]{3,2,1,0:T(8,128)S(1)} %shard_map.61.refs_2_.refs_1_, f32[3,4,8,256]{3,2,1,0:T(8,128)S(1)} %get-tuple-element.14.smooth_ref.refs_2_, f32[6,4,8,256]{3,2,1,0:T(8,128)S(1)} %get-tuple-element.12.refs_3_.refs_1_, ...), custom_call_target="tpu_custom_call" | custom-call | flops 2457600000 | bytes 1572864 | tf_op jit(solution)/shard_map/pallas_call | solution.py:326
  14.5 0.1 collective-permute-done.4.refs_5_
  14.6 0.8 %collective-permute-done.5.refs_6_ = f32[8,128]{1,0:T(8,128)S(1)} collective-permute-done((f32[8,128]{1,0:T(8,128)S(1)}, f32[8,128]{1,0:T(8,128)S(1)}, u32[]{:S(2)}, u32[]{:S(2)}) %collective-permute-start.5) | collective-permute-done | bytes 4128 | tf_op jit(solution)/shard_map/ppermute | solution.py:339
  15.4 0.0 collective-permute-done.6.refs_8_
  15.4 0.0 collective-permute-done.7.refs_9_
  15.4 0.8 %shard_map.65 = (f32[6,4,8,256]{3,2,1,0:T(8,128)}, f32[3,4,8,256]{3,2,1,0:T(8,128)}) custom-call(f32[3,4,8,256]{3,2,1,0:T(8,128)S(1)} %copy-done, f32[6,4,8,256]{3,2,1,0:T(8,128)S(1)} %get-tuple-element.12.refs_3_.refs_1_, f32[6,4,8,256]{3,2,1,0:T(8,128)S(1)} %get-tuple-element.13.model_ref.refs_4_.refs_2_, f32[12,4,8,256]{3,2,1,0:T(8,128)S(1)} %shard_map.64.refs_3_, ...), custom_call_target="tpu_custom_call" | custom-call | flops 1638400 | bytes 1347584 | tf_op jit(solution)/shard_map/pallas_call | solution.py:326
  (4 shorter events, 0.1 us)
Async XLA Ops:
  0.6 3.0 %copy-start.1 = (f32[6,4,8,256]{3,2,1,0:T(8,128)S(1)}, f32[6,4,8,256]{3,2,1,0:T(8,128)}, u32[]{:S(2)}) copy-start(f32[6,4,8,256]{3,2,1,0:T(8,128)} %refs_1_.1) | copy-start | bytes 589828
  0.6 6.9 %collective-permute-start = (f32[3,4,8,256]{3,2,1,0:T(8,128)}, f32[3,4,8,256]{3,2,1,0:T(8,128)S(1)}, u32[]{:S(2)}, u32[]{:S(2)}) collective-permute-start(f32[3,4,8,256]{3,2,1,0:T(8,128)} %refs_0_.5), channel_id=1, source_target_pairs={{16,0},{0,16},{17,1},{1,17},{18,2},{2,18},{19,3},{3,19},{20,4},{4,... | collective-permute-start | bytes 294920 | tf_op jit(solution)/shard_map/ppermute | solution.py:339
  3.7 3.9 %copy-start = (f32[3,4,8,256]{3,2,1,0:T(8,128)S(1)}, f32[3,4,8,256]{3,2,1,0:T(8,128)}, u32[]{:S(2)}) copy-start(f32[3,4,8,256]{3,2,1,0:T(8,128)} %refs_0_.5) | copy-start | bytes 294916
  3.7 3.8 %collective-permute-start.1 = (f32[2,8,256]{2,1,0:T(8,128)S(1)}, f32[2,8,256]{2,1,0:T(8,128)S(1)}, u32[]{:S(2)}, u32[]{:S(2)}) collective-permute-start(f32[2,8,256]{2,1,0:T(8,128)S(1)} %get-tuple-element.10.size_ends_ref), channel_id=1, source_target_pairs={{16,0},{0,16},{17,1},{1,17},{18,2},{2,18},{19,3},{3,19},{20,4},{4,... | collective-permute-start | bytes 49160 | tf_op jit(solution)/shard_map/ppermute | solution.py:339
  5.6 2.0 %copy-start.2 = (s32[8]{0:T(128)S(1)}, s32[8]{0:T(128)}, u32[]{:S(2)}) copy-start(s32[8]{0:T(128)} %param.6) | copy-start | bytes 100
  5.6 8.3 %collective-permute-start.2 = (f32[6,4,8,256]{3,2,1,0:T(8,128)S(1)}, f32[6,4,8,256]{3,2,1,0:T(8,128)S(1)}, u32[]{:S(2)}, u32[]{:S(2)}) collective-permute-start(f32[6,4,8,256]{3,2,1,0:T(8,128)S(1)} %shard_map.61.refs_2_.refs_1_), channel_id=1, source_target_pairs={{16,0},{0,16},{17,1},{1,17},{18,2},{2,18},{19,3},{3,19},{20,4},{4,... | collective-permute-start | bytes 589832 | tf_op jit(solution)/shard_map/ppermute | solution.py:339
  8.0 1.4 %collective-permute-start.3 = (f32[8,128]{1,0:T(8,128)S(1)}, f32[8,128]{1,0:T(8,128)S(1)}, u32[]{:S(2)}, u32[]{:S(2)}) collective-permute-start(f32[8,128]{1,0:T(8,128)S(1)} %get-tuple-element.16), channel_id=1, source_target_pairs={{1,0},{0,1},{3,2},{2,3},{5,4},{4,5},{7,6},{6,7},{9,8},{8,9},{11,10... | collective-permute-start | bytes 12296 | tf_op jit(solution)/shard_map/ppermute | solution.py:349
  8.1 7.3 %collective-permute-start.7 = (f32[18,8,256]{2,1,0:T(8,128)S(1)}, f32[18,8,256]{2,1,0:T(8,128)S(1)}, u32[]{:S(2)}, u32[]{:S(2)}) collective-permute-start(f32[18,8,256]{2,1,0:T(8,128)S(1)} %get-tuple-element.17), channel_id=1, source_target_pairs={{16,0},{0,16},{17,1},{1,17},{18,2},{2,18},{19,3},{3,19},{20,4},{4,... | collective-permute-start | bytes 442376 | tf_op jit(solution)/shard_map/ppermute | solution.py:339
  9.4 5.2 %collective-permute-start.4 = (f32[8,128]{1,0:T(8,128)S(1)}, f32[8,128]{1,0:T(8,128)S(1)}, u32[]{:S(2)}, u32[]{:S(2)}) collective-permute-start(f32[8,128]{1,0:T(8,128)S(1)} %add.3.refs_7_), channel_id=1, source_target_pairs={{17,0},{19,1},{16,2},{21,3},{18,4},{23,5},{20,6},{25,7},{22,8},{27... | collective-permute-start | bytes 12296 | tf_op jit(solution)/shard_map/ppermute | solution.py:349
  11.3 4.0 %collective-permute-start.5 = (f32[8,128]{1,0:T(8,128)S(1)}, f32[8,128]{1,0:T(8,128)S(1)}, u32[]{:S(2)}, u32[]{:S(2)}) collective-permute-start(f32[8,128]{1,0:T(8,128)S(1)} %add.3.refs_7_), channel_id=1, source_target_pairs={{16,0},{0,16},{17,1},{1,17},{18,2},{2,18},{19,3},{3,19},{20,4},{4,... | collective-permute-start | bytes 12296 | tf_op jit(solution)/shard_map/ppermute | solution.py:339
  12.3 3.0 %collective-permute-start.6 = (f32[8,128]{1,0:T(8,128)S(1)}, f32[8,128]{1,0:T(8,128)S(1)}, u32[]{:S(2)}, u32[]{:S(2)}) collective-permute-start(f32[8,128]{1,0:T(8,128)S(1)} %add.3.refs_7_), channel_id=1, source_target_pairs={{1,0},{3,1},{0,2},{5,3},{2,4},{7,5},{4,6},{9,7},{6,8},{11,9},{8,10... | collective-permute-start | bytes 12296 | tf_op jit(solution)/shard_map/ppermute | solution.py:349

commit v14 on v9

--- a/solution.py
+++ b/solution.py
@@ -136,43 +136,51 @@
     return [plain[z] + tensor[PAIR_OF[a][a]][z] * vector[a][z] for z in range(cells)]
 
 
-def forward_kernel(tables, *refs):
-    peers = tables.devices - 1
-    cells = tables.cells
-    v_ref, strain_ref, cot_ref, size_ref, bins_ref = refs[:5]
-    far_v_refs = refs[5 : 5 + peers]
-    far_size_refs = refs[5 + peers : 5 + 2 * peers]
-    smooth_ref, leonard_ref, model_ref, sums_ref = refs[5 + 2 * peers :]
-    cross, square, blame = [], [], []
+def velocity_kernel(tables, v_ref, bins_ref, *refs):
+    far_v_refs = refs[:-4]
+    smooth_ref, leonard_ref, rest_ref, mask_ref = refs[-4:]
+    cells = tables.cells
     for lanes in halves(v_ref.shape[-1]):
         v = [[v_ref[a, z, :, lanes] for z in range(cells)] for a in range(3)]
-        size = [size_ref[z, :, lanes] for z in range(cells)]
         products = products_of(v)
         ends = [None]
-        for far_v_ref, far_size_ref in zip(far_v_refs, far_size_refs):
+        for far_v_ref in far_v_refs:
             far = [[far_v_ref[a, z, :, lanes] for z in range(cells)] for a in range(3)]
             ends.append([tables.project(field) for field in far + products_of(far)])
-            ends[-1].append([far_size_ref[end, :, lanes] for end in range(2)])
-        filtered = filtered_block(tables, 0, v + products + [size], ends)
-        smooth_v = filtered[:3]
-        factor = [2.0 * (4.0 * filtered[9][z] - size[z]) for z in range(cells)]
+        filtered = filtered_block(tables, 0, v + products, ends)
+        for a in range(3):
+            for z in range(cells):
+                smooth_ref[a, z, :, lanes] = filtered[a][z]
         for k, (a, b) in enumerate(INDEX_PAIRS):
             for z in range(cells):
-                coarse = smooth_v[a][z] * smooth_v[b][z]
-                leonard = filtered[3 + k][z] - coarse
-                term = products[k][z] - coarse + factor[z] * strain_ref[k, z, :, lanes]
-                leonard_ref[k, z, :, lanes] = leonard
+                coarse = filtered[a][z] * filtered[b][z]
+                leonard_ref[k, z, :, lanes] = filtered[3 + k][z] - coarse
+                rest_ref[k, z, :, lanes] = products[k][z] - coarse
+    lane = lax.broadcasted_iota(jnp.int32, bins_ref.shape, 1)
+    mask_ref[...] = jnp.where(bins_ref[...] == lane, 1.0, 0.0)
+
+
+def model_kernel(tables, strain_ref, cot_ref, size_ref, leonard_ref, rest_ref, mask_ref, *refs):
+    far_size_refs = refs[:-2]
+    model_ref, sums_ref = refs[-2:]
+    cells = tables.cells
+    cross, square, blame = [], [], []
+    for lanes in halves(strain_ref.shape[-1]):
+        size = [size_ref[z, :, lanes] for z in range(cells)]
+        ends = [None] + [[[far[end, :, lanes] for end in range(2)]] for far in far_size_refs]
+        smooth_size = filtered_block(tables, 0, [size], ends)[0]
+        factor = [2.0 * (4.0 * smooth_size[z] - size[z]) for z in range(cells)]
+        for k in range(6):
+            for z in range(cells):
+                leonard = leonard_ref[k, z, :, lanes]
+                term = rest_ref[k, z, :, lanes] + factor[z] * strain_ref[k, z, :, lanes]
                 model_ref[k, z, :, lanes] = term
                 scaled = PAIR_WEIGHTS[k] * term
                 cross.append(scaled * leonard)
                 square.append(scaled * term)
                 blame.append(term * cot_ref[k, z, :, lanes])
             cross, square, blame = [sum_up(cross)], [sum_up(square)], [sum_up(blame)]
-        for a in range(3):
-            for z in range(cells):
-                smooth_ref[a, z, :, lanes] = smooth_v[a][z]
-    lane = lax.broadcasted_iota(jnp.int32, bins_ref.shape, 1)
-    mine = bins_ref[...] == lane
+    mine = mask_ref[...] > 0.5
     place = lax.broadcasted_iota(jnp.int32, (8, LANES), 0)
     table = jnp.zeros((8, LANES), jnp.float32)
     for index, sums in enumerate((cross, square, blame)):
@@ -258,7 +266,7 @@
 def finish_kernel(tables, count, turning, *refs):
     peers = tables.devices - 1
     cells = tables.cells
-    v_ref, leonard_ref, model_ref, parts_ref, bins_ref = refs[:5]
+    v_ref, leonard_ref, model_ref, parts_ref, mask_ref = refs[:5]
     near_refs = refs[5 : 5 + count]
     pair_ref = refs[5 + count]
     far_message_refs = refs[6 + count : 6 + count + peers]
@@ -272,8 +280,7 @@
     total = total + near
     inverse = 1.0 / (total[1:2] + EPSILON)
     rows = v_ref.shape[2]
-    lane = lax.broadcasted_iota(jnp.int32, bins_ref.shape, 1)
-    mine = bins_ref[...] == lane
+    mine = mask_ref[...] > 0.5
 
     def of_rows(per_bin):
         column = jnp.sum(jnp.where(mine, per_bin, 0.0), axis=1, keepdims=True)
@@ -388,16 +395,24 @@
     )
     far_cot = [from_ahead(near_cot, shift) for shift in range(1, span)]
     table = pltpu.VMEM((8, LANES), jnp.float32)
-    smooth, leonard, model, sums = call(
-        functools.partial(forward_kernel, tables),
-        [shaped(3, cells), shaped(6, cells), shaped(6, cells), table],
+    smooth, leonard, rest, mask = call(
+        functools.partial(velocity_kernel, tables),
+        [shaped(3, cells), shaped(6, cells), shaped(6, cells), pltpu.VMEM((rows, LANES), jnp.float32)],
         LONG * work,
         velocity,
+        bins,
+        *far_v,
+    )
+    model, sums = call(
+        functools.partial(model_kernel, tables),
+        [shaped(6, cells), table],
+        LONG * work,
         strain,
         near_cot,
         size,
-        bins,
-        *far_v,
+        leonard,
+        rest,
+        mask,
         *far_size,
     )
     other_sums = from_source(sums, 0, lambda j: j ^ 1)
@@ -443,7 +458,7 @@
             leonard,
             model,
             parts,
-            bins,
+            mask,
             *near_sums,
             pair_sums,
             *far_message,

time: 16.5 us -> 16.4 us (level)
    pallas_call x7 -> x8, Pallas kernels: 2.77 us -> 2.78 us  [call(): pl.pallas_call(kernel, out_shape=outs, in_specs=in_specs or [WHOLE] * len...]
  transfers between devices with their start and end apart: 7 -> 7, of which waited for: 5 -> 4; matrix products, arithmetic and copies ran while one was open for 0% -> 0% of each run, Pallas kernels for 12% -> 12%
where the time goes in v14:
time: 16.4 us; the launch traced here: 16.3 us
  starting transfers between devices  9.82 us (60%)
  waiting for transfers between devices  2.91 us (18%)
  Pallas kernels  2.78 us (17%)
  between operations  0.69 us (4%)
    ppermute x4, starting transfers between devices, from_ahead(): lax.ppermute(values, 'span', [((i + shift) % peers, i) for i in range(pee...  6.55 us
    ppermute x3, starting transfers between devices, from_source(): return lax.ppermute(values, ('span', 'stream'), pairs)  3.27 us
    pallas_call x8, Pallas kernels, call(): pl.pallas_call(kernel, out_shape=outs, in_specs=in_specs or [WHOLE] * len...  2.78 us
    ppermute x3, waiting for transfers between devices, from_source(): return lax.ppermute(values, ('span', 'stream'), pairs)  1.9 us
    ppermute x4, waiting for transfers between devices, from_ahead(): lax.ppermute(values, 'span', [((i + shift) % peers, i) for i in range(pee...  1.01 us
  transfers between devices with their start and end apart: 7, of which 4 were waited for; matrix products, arithmetic and copies ran while one was open for 0% of the time, Pallas kernels for 12%

profile of v14, /device:TPU:0, one launch (start us, length us, event | category | flops | bytes accessed | tf_op | source)
XLA Modules:
  0.0 16.3 jit_solution(12232939903626979381)
XLA Ops:
  0.6 0.0 copy-start.1
  0.6 3.0 %collective-permute-start = (f32[3,4,8,256]{3,2,1,0:T(8,128)}, f32[3,4,8,256]{3,2,1,0:T(8,128)S(1)}, u32[]{:S(2)}, u32[]{:S(2)}) collective-permute-start(f32[3,4,8,256]{3,2,1,0:T(8,128)} %refs_0_.3), channel_id=1, source_target_pairs={{16,0},{0,16},{17,1},{1,17},{18,2},{2,18},{19,3},{3,19},{20,4},{4,... | collective-permute-start | bytes 294920 | tf_op jit(solution)/shard_map/ppermute | solution.py:348
  3.7 0.0 copy-done.1
  3.7 0.0 copy-start.2
  3.7 0.0 copy-start
  3.7 0.9 %collective-permute-start.1 = (f32[2,8,256]{2,1,0:T(8,128)S(1)}, f32[2,8,256]{2,1,0:T(8,128)S(1)}, u32[]{:S(2)}, u32[]{:S(2)}) collective-permute-start(f32[2,8,256]{2,1,0:T(8,128)S(1)} %get-tuple-element.14.size_ends_ref), channel_id=1, source_target_pairs={{16,0},{0,16},{17,1},{1,17},{18,2},{2,18},{19,3},{3,19},{20,4},{4,... | collective-permute-start | bytes 49160 | tf_op jit(solution)/shard_map/ppermute | solution.py:348
  4.7 0.9 %shard_map.62.cot_ref.refs_1_ = f32[6,4,8,256]{3,2,1,0:T(8,128)S(1)} custom-call(f32[6,4,8,256]{3,2,1,0:T(8,128)} %cot_hbm.1, f32[2,8,256]{2,1,0:T(8,128)S(1)} %get-tuple-element.14.size_ends_ref), custom_call_target="tpu_custom_call" | custom-call | flops 8192 | bytes 409600 | tf_op jit(solution)/shard_map/pallas_call | solution.py:335
  5.6 1.2 %collective-permute-start.3 = (f32[6,4,8,256]{3,2,1,0:T(8,128)S(1)}, f32[6,4,8,256]{3,2,1,0:T(8,128)S(1)}, u32[]{:S(2)}, u32[]{:S(2)}) collective-permute-start(f32[6,4,8,256]{3,2,1,0:T(8,128)S(1)} %shard_map.62.cot_ref.refs_1_), channel_id=1, source_target_pairs={{16,0},{0,16},{17,1},{1,17},{18,2},{2,18},{19,3},{3,19},{20,4},{4,... | collective-permute-start | bytes 589832 | tf_op jit(solution)/shard_map/ppermute | solution.py:348
  6.8 0.0 collective-permute-done.refs_0_.refs_6_
  6.9 0.0 copy-done.2
  6.9 0.1 broadcast_in_dim.2.bins_ref
  6.9 0.0 copy-done
  6.9 0.2 shard_map.59
  7.1 0.5 %collective-permute-done.1.refs_0_ = f32[2,8,256]{2,1,0:T(8,128)S(1)} collective-permute-done((f32[2,8,256]{2,1,0:T(8,128)S(1)}, f32[2,8,256]{2,1,0:T(8,128)S(1)}, u32[]{:S(2)}, u32[]{:S(2)}) %collective-permute-start.1) | collective-permute-done | bytes 16416 | tf_op jit(solution)/shard_map/ppermute | solution.py:348
  7.5 0.2 %shard_map.63 = (f32[6,4,8,256]{3,2,1,0:T(8,128)S(1)}, f32[8,128]{1,0:T(8,128)S(1)}) custom-call(f32[6,4,8,256]{3,2,1,0:T(8,128)S(1)} %copy-done.1, f32[6,4,8,256]{3,2,1,0:T(8,128)S(1)} %shard_map.62.cot_ref.refs_1_, f32[4,8,256]{2,1,0:T(8,128)S(1)} %get-tuple-element.15.size_ref, f32[6,4,8,256]{3,2,1,0:T(8,128)S(1)} %get-tuple-element.13.leonard_ref.refs_3_.refs_1_, ...), custom_call_target="tpu_custom_call" | custom-call | flops 2457600000 | bytes 1040384 | tf_op jit(solution)/shard_map/pallas_call | solution.py:335
  7.7 0.1 collective-permute-start.2
  7.8 1.2 %collective-permute-done.2.other_sums_ref = f32[8,128]{1,0:T(8,128)S(1)} collective-permute-done((f32[8,128]{1,0:T(8,128)S(1)}, f32[8,128]{1,0:T(8,128)S(1)}, u32[]{:S(2)}, u32[]{:S(2)}) %collective-permute-start.2) | collective-permute-done | bytes 4128 | tf_op jit(solution)/shard_map/ppermute | solution.py:358
  9.0 1.4 %collective-permute-start.6 = (f32[19,8,256]{2,1,0:T(8,128)S(1)}, f32[19,8,256]{2,1,0:T(8,128)S(1)}, u32[]{:S(2)}, u32[]{:S(2)}) collective-permute-start(f32[19,8,256]{2,1,0:T(8,128)S(1)} %get-tuple-element.23), channel_id=1, source_target_pairs={{16,0},{0,16},{17,1},{1,17},{18,2},{2,18},{19,3},{3,19},{20,4},{4,... | collective-permute-start | bytes 466952 | tf_op jit(solution)/shard_map/ppermute | solution.py:348
  10.4 1.7 %collective-permute-start.5 = (f32[8,128]{1,0:T(8,128)S(1)}, f32[8,128]{1,0:T(8,128)S(1)}, u32[]{:S(2)}, u32[]{:S(2)}) collective-permute-start(f32[8,128]{1,0:T(8,128)S(1)} %get-tuple-element.22.refs_7_), channel_id=1, source_target_pairs={{17,0},{19,1},{16,2},{21,3},{18,4},{23,5},{20,6},{25,7},{22,8},{27... | collective-permute-start | bytes 12296 | tf_op jit(solution)/shard_map/ppermute | solution.py:358
  12.0 1.5 %collective-permute-start.4 = (f32[8,128]{1,0:T(8,128)S(1)}, f32[8,128]{1,0:T(8,128)S(1)}, u32[]{:S(2)}, u32[]{:S(2)}) collective-permute-start(f32[8,128]{1,0:T(8,128)S(1)} %get-tuple-element.22.refs_7_), channel_id=1, source_target_pairs={{1,0},{3,1},{0,2},{5,3},{2,4},{7,5},{4,6},{9,7},{6,8},{11,9},{8,10... | collective-permute-start | bytes 12296 | tf_op jit(solution)/shard_map/ppermute | solution.py:358
  13.6 0.0 collective-permute-done.3.refs_7_
  13.6 0.6 %shard_map.65.refs_3_ = f32[12,4,8,256]{3,2,1,0:T(8,128)S(1)} custom-call(f32[3,4,8,256]{3,2,1,0:T(8,128)S(1)} %copy-done, f32[6,4,8,256]{3,2,1,0:T(8,128)S(1)} %shard_map.62.cot_ref.refs_1_, f32[3,4,8,256]{3,2,1,0:T(8,128)S(1)} %get-tuple-element.19.smooth_ref.refs_2_, f32[6,4,8,256]{3,2,1,0:T(8,128)S(1)} %get-tuple-element.13.leonard_ref.refs_3_.refs_1_, ...), custom_call_target="tpu_custom_call" | custom-call | flops 4096000 | bytes 1572864 | tf_op jit(solution)/shard_map/pallas_call | solution.py:335
  14.2 0.7 %collective-permute-done.5.refs_6_ = f32[8,128]{1,0:T(8,128)S(1)} collective-permute-done((f32[8,128]{1,0:T(8,128)S(1)}, f32[8,128]{1,0:T(8,128)S(1)}, u32[]{:S(2)}, u32[]{:S(2)}) %collective-permute-start.5) | collective-permute-done | bytes 4128 | tf_op jit(solution)/shard_map/ppermute | solution.py:358
  14.9 0.0 collective-permute-done.4.refs_5_
  14.9 0.5 %collective-permute-done.6.refs_8_ = f32[19,8,256]{2,1,0:T(8,128)S(1)} collective-permute-done((f32[19,8,256]{2,1,0:T(8,128)S(1)}, f32[19,8,256]{2,1,0:T(8,128)S(1)}, u32[]{:S(2)}, u32[]{:S(2)}) %collective-permute-start.6) | collective-permute-done | bytes 155680 | tf_op jit(solution)/shard_map/ppermute | solution.py:348
  15.4 0.8 %shard_map.66 = (f32[6,4,8,256]{3,2,1,0:T(8,128)}, f32[3,4,8,256]{3,2,1,0:T(8,128)}) custom-call(f32[3,4,8,256]{3,2,1,0:T(8,128)S(1)} %copy-done, f32[6,4,8,256]{3,2,1,0:T(8,128)S(1)} %get-tuple-element.13.leonard_ref.refs_3_.refs_1_, f32[6,4,8,256]{3,2,1,0:T(8,128)S(1)} %get-tuple-element.18.model_ref.refs_4_.refs_2_, ...), custom_call_target="tpu_custom_call" | custom-call | flops 1638400 | bytes 1351680 | tf_op jit(solution)/shard_map/pallas_call | solution.py:335
  (3 shorter events, 0.1 us)
Async XLA Ops:
  0.6 3.0 %copy-start.1 = (f32[6,4,8,256]{3,2,1,0:T(8,128)S(1)}, f32[6,4,8,256]{3,2,1,0:T(8,128)}, u32[]{:S(2)}) copy-start(f32[6,4,8,256]{3,2,1,0:T(8,128)} %strain_ref.3) | copy-start | bytes 589828
  0.6 6.2 %collective-permute-start = (f32[3,4,8,256]{3,2,1,0:T(8,128)}, f32[3,4,8,256]{3,2,1,0:T(8,128)S(1)}, u32[]{:S(2)}, u32[]{:S(2)}) collective-permute-start(f32[3,4,8,256]{3,2,1,0:T(8,128)} %refs_0_.3), channel_id=1, source_target_pairs={{16,0},{0,16},{17,1},{1,17},{18,2},{2,18},{19,3},{3,19},{20,4},{4,... | collective-permute-start | bytes 294920 | tf_op jit(solution)/shard_map/ppermute | solution.py:348
  3.7 3.1 %copy-start.2 = (s32[8]{0:T(128)S(1)}, s32[8]{0:T(128)}, u32[]{:S(2)}) copy-start(s32[8]{0:T(128)} %param.6) | copy-start | bytes 100
  3.7 3.2 %copy-start = (f32[3,4,8,256]{3,2,1,0:T(8,128)S(1)}, f32[3,4,8,256]{3,2,1,0:T(8,128)}, u32[]{:S(2)}) copy-start(f32[3,4,8,256]{3,2,1,0:T(8,128)} %refs_0_.3) | copy-start | bytes 294916
  3.7 3.8 %collective-permute-start.1 = (f32[2,8,256]{2,1,0:T(8,128)S(1)}, f32[2,8,256]{2,1,0:T(8,128)S(1)}, u32[]{:S(2)}, u32[]{:S(2)}) collective-permute-start(f32[2,8,256]{2,1,0:T(8,128)S(1)} %get-tuple-element.14.size_ends_ref), channel_id=1, source_target_pairs={{16,0},{0,16},{17,1},{1,17},{18,2},{2,18},{19,3},{3,19},{20,4},{4,... | collective-permute-start | bytes 49160 | tf_op jit(solution)/shard_map/ppermute | solution.py:348
  5.6 8.0 %collective-permute-start.3 = (f32[6,4,8,256]{3,2,1,0:T(8,128)S(1)}, f32[6,4,8,256]{3,2,1,0:T(8,128)S(1)}, u32[]{:S(2)}, u32[]{:S(2)}) collective-permute-start(f32[6,4,8,256]{3,2,1,0:T(8,128)S(1)} %shard_map.62.cot_ref.refs_1_), channel_id=1, source_target_pairs={{16,0},{0,16},{17,1},{1,17},{18,2},{2,18},{19,3},{3,19},{20,4},{4,... | collective-permute-start | bytes 589832 | tf_op jit(solution)/shard_map/ppermute | solution.py:348
  7.7 1.2 %collective-permute-start.2 = (f32[8,128]{1,0:T(8,128)S(1)}, f32[8,128]{1,0:T(8,128)S(1)}, u32[]{:S(2)}, u32[]{:S(2)}) collective-permute-start(f32[8,128]{1,0:T(8,128)S(1)} %get-tuple-element.20.sums_ref), channel_id=1, source_target_pairs={{1,0},{0,1},{3,2},{2,3},{5,4},{4,5},{7,6},{6,7},{9,8},{8,9},{11,10... | collective-permute-start | bytes 12296 | tf_op jit(solution)/shard_map/ppermute | solution.py:358
  9.0 6.4 %collective-permute-start.6 = (f32[19,8,256]{2,1,0:T(8,128)S(1)}, f32[19,8,256]{2,1,0:T(8,128)S(1)}, u32[]{:S(2)}, u32[]{:S(2)}) collective-permute-start(f32[19,8,256]{2,1,0:T(8,128)S(1)} %get-tuple-element.23), channel_id=1, source_target_pairs={{16,0},{0,16},{17,1},{1,17},{18,2},{2,18},{19,3},{3,19},{20,4},{4,... | collective-permute-start | bytes 466952 | tf_op jit(solution)/shard_map/ppermute | solution.py:348
  10.4 4.5 %collective-permute-start.5 = (f32[8,128]{1,0:T(8,128)S(1)}, f32[8,128]{1,0:T(8,128)S(1)}, u32[]{:S(2)}, u32[]{:S(2)}) collective-permute-start(f32[8,128]{1,0:T(8,128)S(1)} %get-tuple-element.22.refs_7_), channel_id=1, source_target_pairs={{17,0},{19,1},{16,2},{21,3},{18,4},{23,5},{20,6},{25,7},{22,8},{27... | collective-permute-start | bytes 12296 | tf_op jit(solution)/shard_map/ppermute | solution.py:358
  12.0 2.9 %collective-permute-start.4 = (f32[8,128]{1,0:T(8,128)S(1)}, f32[8,128]{1,0:T(8,128)S(1)}, u32[]{:S(2)}, u32[]{:S(2)}) collective-permute-start(f32[8,128]{1,0:T(8,128)S(1)} %get-tuple-element.22.refs_7_), channel_id=1, source_target_pairs={{1,0},{3,1},{0,2},{5,3},{2,4},{7,5},{4,6},{9,7},{6,8},{11,9},{8,10... | collective-permute-start | bytes 12296 | tf_op jit(solution)/shard_map/ppermute | solution.py:358

commit v15 on v14

--- a/solution.py
+++ b/solution.py
@@ -190,7 +190,58 @@
     sums_ref[...] = table
 
 
-def message_kernel(tables, smooth_ref, model_ref, sums_ref, other_sums_ref, dual_ref, message_ref, pair_ref):
+def on_second_core():
+    return lax.rem(lax.axis_index("stream"), 2) == 1
+
+
+def velocity_fields(tables, refs, lanes):
+    fields, ends = [], []
+    for ref in refs:
+        v = [[ref[a, z, :, lanes] for z in range(tables.cells)] for a in range(3)]
+        fields.append(v + products_of(v))
+        ends.append([tables.project(field) for field in fields[-1]])
+    return fields, ends
+
+
+def own_parts(tables, v_ref, cot_ref, smooth_ref, leonard_ref, model_ref, dual_ref, far_v_refs, parts_ref):
+    cells = tables.cells
+    for lanes in halves(v_ref.shape[-1]):
+
+        def load(ref, count):
+            return [[ref[f, z, :, lanes] for z in range(cells)] for f in range(count)]
+
+        fields, ends = velocity_fields(tables, (v_ref, *far_v_refs), lanes)
+        v = fields[0][:3]
+        cot, model, leonard, smooth_v = load(cot_ref, 6), load(model_ref, 6), load(leonard_ref, 6), load(smooth_ref, 3)
+        smooth_cot = [tables.inside(field) for field in cot]
+        smooth_duals = [tables.inside(weighted_dual(cot, smooth_v, a, cells)) for a in range(3)]
+        smooth_others = [tables.inside(plain_dual(leonard, smooth_v, a, cells)) for a in range(3)]
+        for place in range(1, tables.devices):
+            filtered = filtered_block(tables, place, fields[place], ends)
+            far_leonard = [
+                [filtered[3 + k][z] - filtered[a][z] * filtered[b][z] for z in range(cells)]
+                for k, (a, b) in enumerate(INDEX_PAIRS)
+            ]
+            for a in range(3):
+                far = tables.outside(place, tables.project(plain_dual(far_leonard, filtered, a, cells)))
+                smooth_others[a] = add_lists(smooth_others[a], far)
+        inner = [add_lists(tables.inside(model[k]), leonard[k]) for k in range(6)]
+        for a in range(3):
+            first = weighted_dual(smooth_cot, v, a, cells)
+            second = weighted_dual(cot, v, a, cells)
+            dual = tables.inside([dual_ref[a, z, :, lanes] for z in range(cells)])
+            third = plain_dual(inner, v, a, cells)
+            fourth = plain_dual(model, v, a, cells)
+            for z in range(cells):
+                parts_ref[a, z, :, lanes] = first[z] - smooth_duals[a][z]
+                parts_ref[3 + a, z, :, lanes] = smooth_duals[a][z] - second[z]
+                parts_ref[6 + a, z, :, lanes] = 2.0 * (third[z] - smooth_others[a][z]) - dual[z]
+                parts_ref[9 + a, z, :, lanes] = 2.0 * dual[z] - 4.0 * fourth[z]
+
+
+def message_kernel(tables, v_ref, cot_ref, smooth_ref, leonard_ref, model_ref, sums_ref, other_sums_ref, *refs):
+    far_v_refs = refs[:-4]
+    dual_ref, message_ref, pair_ref, early_ref = refs[-4:]
     cells = tables.cells
     pair_sums = sums_ref[...] + other_sums_ref[...]
     pair_ref[...] = pair_sums
@@ -208,59 +259,46 @@
             for end, value in enumerate(tables.project(dual)):
                 message_ref[12 + 2 * a + end, :, lanes] = value
 
-
-def local_kernel(tables, *refs):
+    @pl.when(on_second_core())
+    def _():
+        own_parts(tables, v_ref, cot_ref, smooth_ref, leonard_ref, model_ref, dual_ref, far_v_refs, early_ref)
+
+
+def local_kernel(tables, early_ref, v_ref, cot_ref, smooth_ref, leonard_ref, model_ref, dual_ref, *refs):
     peers = tables.devices - 1
     cells = tables.cells
-    v_ref, cot_ref, smooth_ref, leonard_ref, model_ref, dual_ref = refs[:6]
-    far_v_refs = refs[6 : 6 + peers]
-    far_cot_refs = refs[6 + peers : 6 + 2 * peers]
-    parts_ref = refs[-1]
+    far_v_refs, far_cot_refs, parts_ref = refs[:peers], refs[peers : 2 * peers], refs[-1]
+
+    @pl.when(on_second_core())
+    def _():
+        parts_ref[...] = early_ref[...]
+
+    @pl.when(jnp.logical_not(on_second_core()))
+    def _():
+        own_parts(tables, v_ref, cot_ref, smooth_ref, leonard_ref, model_ref, dual_ref, far_v_refs, parts_ref)
+
     for lanes in halves(v_ref.shape[-1]):
-
-        def load(ref, count):
-            return [[ref[f, z, :, lanes] for z in range(cells)] for f in range(count)]
-
-        fields, ends = [], []
-        for ref in (v_ref, *far_v_refs):
-            v = load(ref, 3)
-            fields.append(v + products_of(v))
-            ends.append([tables.project(field) for field in fields[-1]])
+        fields, ends = velocity_fields(tables, (v_ref, *far_v_refs), lanes)
         v = fields[0][:3]
-        cot, model, leonard, smooth_v = load(cot_ref, 6), load(model_ref, 6), load(leonard_ref, 6), load(smooth_ref, 3)
-        smooth_cot = [tables.inside(field) for field in cot]
-        duals = [weighted_dual(cot, smooth_v, a, cells) for a in range(3)]
-        others = [plain_dual(leonard, smooth_v, a, cells) for a in range(3)]
-        smooth_duals = [tables.inside(field) for field in duals]
-        smooth_others = [tables.inside(field) for field in others]
+        smooth_cot, smooth_duals = [[] for _ in range(6)], [[] for _ in range(3)]
         for place in range(1, tables.devices):
-            far_cot = load(far_cot_refs[place - 1], 6)
-            filtered = filtered_block(tables, place, fields[place], ends)
-            far_smooth = filtered[:3]
-            far_leonard = [
-                [filtered[3 + k][z] - far_smooth[a][z] * far_smooth[b][z] for z in range(cells)]
-                for k, (a, b) in enumerate(INDEX_PAIRS)
-            ]
+            far_cot_ref = far_cot_refs[place - 1]
+            far_cot = [[far_cot_ref[k, z, :, lanes] for z in range(cells)] for k in range(6)]
+            far_smooth = filtered_block(tables, place, fields[place][:3], [x[:3] for x in ends])
             for k in range(6):
-                far = tables.outside(place, tables.project(far_cot[k]))
-                smooth_cot[k] = add_lists(smooth_cot[k], far)
+                smooth_cot[k].append(tables.outside(place, tables.project(far_cot[k])))
             for a in range(3):
-                far = tables.outside(place, tables.project(weighted_dual(far_cot, far_smooth, a, cells)))
-                smooth_duals[a] = add_lists(smooth_duals[a], far)
-                far = tables.outside(place, tables.project(plain_dual(far_leonard, far_smooth, a, cells)))
-                smooth_others[a] = add_lists(smooth_others[a], far)
-        inner = [add_lists(tables.inside(model[k]), leonard[k]) for k in range(6)]
+                dual = weighted_dual(far_cot, far_smooth, a, cells)
+                smooth_duals[a].append(tables.outside(place, tables.project(dual)))
+        if not peers:
+            continue
+        smooth_cot = [functools.reduce(add_lists, lists) for lists in smooth_cot]
+        smooth_duals = [functools.reduce(add_lists, lists) for lists in smooth_duals]
         for a in range(3):
             first = weighted_dual(smooth_cot, v, a, cells)
-            second = weighted_dual(cot, v, a, cells)
-            dual = tables.inside([dual_ref[a, z, :, lanes] for z in range(cells)])
-            third = plain_dual(inner, v, a, cells)
-            fourth = plain_dual(model, v, a, cells)
-            for z in range(cells):
-                parts_ref[a, z, :, lanes] = first[z] - smooth_duals[a][z]
-                parts_ref[3 + a, z, :, lanes] = smooth_duals[a][z] - second[z]
-                parts_ref[6 + a, z, :, lanes] = 2.0 * (third[z] - smooth_others[a][z]) - dual[z]
-                parts_ref[9 + a, z, :, lanes] = 2.0 * dual[z] - 4.0 * fourth[z]
+            for z in range(cells):
+                parts_ref[a, z, :, lanes] = parts_ref[a, z, :, lanes] + (first[z] - smooth_duals[a][z])
+                parts_ref[3 + a, z, :, lanes] = parts_ref[3 + a, z, :, lanes] + smooth_duals[a][z]
 
 
 def finish_kernel(tables, count, turning, *refs):
@@ -416,14 +454,18 @@
         *far_size,
     )
     other_sums = from_source(sums, 0, lambda j: j ^ 1)
-    dual, message, pair_sums = call(
+    dual, message, pair_sums, early = call(
         functools.partial(message_kernel, tables),
-        [shaped(3, cells), shaped(19), table],
+        [shaped(3, cells), shaped(19), table, shaped(12, cells)],
         100 * work,
+        velocity,
+        near_cot,
         smooth,
+        leonard,
         model,
         sums,
         other_sums,
+        *far_v,
     )
     far_message = [from_ahead(message, shift) for shift in range(1, span)]
     most_rows = 2 * rows * stream // NBINS
@@ -439,6 +481,7 @@
         functools.partial(local_kernel, tables),
         [shaped(12, cells)],
         500 * work,
+        early,
         velocity,
         near_cot,
         smooth,

time: 16.4 us -> 16.7 us (1.018)
  waiting for transfers between devices: 2.91 us -> 3.15 us
    ppermute x3, waiting for transfers between devices: 1.9 us -> 2.41 us  [from_source(): return lax.ppermute(values, ('span', 'stream'), pairs)]
    ppermute x4, waiting for transfers between devices: 1.01 us -> 0.74 us  [from_ahead(): lax.ppermute(values, 'span', [((i + shift) % peers, i) for i in range(pee...]
where the time goes in v15:
time: 16.7 us; the launch traced here: 16.6 us
  starting transfers between devices  9.82 us (59%)
  waiting for transfers between devices  3.15 us (19%)
  Pallas kernels  2.84 us (17%)
  between operations  0.69 us (4%)
    ppermute x4, starting transfers between devices, from_ahead(): lax.ppermute(values, 'span', [((i + shift) % peers, i) for i in range(pee...  6.55 us
    ppermute x3, starting transfers between devices, from_source(): return lax.ppermute(values, ('span', 'stream'), pairs)  3.27 us
    pallas_call x8, Pallas kernels, call(): pl.pallas_call(kernel, out_shape=outs, in_specs=in_specs or [WHOLE] * len...  2.84 us
    ppermute x3, waiting for transfers between devices, from_source(): return lax.ppermute(values, ('span', 'stream'), pairs)  2.41 us
    ppermute x4, waiting for transfers between devices, from_ahead(): lax.ppermute(values, 'span', [((i + shift) % peers, i) for i in range(pee...  0.74 us
  transfers between devices with their start and end apart: 7, of which 4 were waited for; matrix products, arithmetic and copies ran while one was open for 0% of the time, Pallas kernels for 12%

profile of v15, /device:TPU:0, one launch (start us, length us, event | category | flops | bytes accessed | tf_op | source)
XLA Modules:
  0.0 16.6 jit_solution(17455278697407954726)
XLA Ops:
  0.6 0.0 copy-start.1
  0.6 3.0 %collective-permute-start = (f32[3,4,8,256]{3,2,1,0:T(8,128)}, f32[3,4,8,256]{3,2,1,0:T(8,128)S(1)}, u32[]{:S(2)}, u32[]{:S(2)}) collective-permute-start(f32[3,4,8,256]{3,2,1,0:T(8,128)} %refs_0_.1), channel_id=1, source_target_pairs={{16,0},{0,16},{17,1},{1,17},{18,2},{2,18},{19,3},{3,19},{20,4},{4,... | collective-permute-start | bytes 294920 | tf_op jit(solution)/shard_map/ppermute | solution.py:386
  3.7 0.0 copy-done.1
  3.7 0.0 copy-start.2
  3.7 0.0 copy-start
  3.7 0.9 %collective-permute-start.1 = (f32[2,8,256]{2,1,0:T(8,128)S(1)}, f32[2,8,256]{2,1,0:T(8,128)S(1)}, u32[]{:S(2)}, u32[]{:S(2)}) collective-permute-start(f32[2,8,256]{2,1,0:T(8,128)S(1)} %get-tuple-element.15.size_ends_ref), channel_id=1, source_target_pairs={{16,0},{0,16},{17,1},{1,17},{18,2},{2,18},{19,3},{3,19},{20,4},{4,... | collective-permute-start | bytes 49160 | tf_op jit(solution)/shard_map/ppermute | solution.py:386
  4.7 0.9 %shard_map.62.cot_ref = f32[6,4,8,256]{3,2,1,0:T(8,128)S(1)} custom-call(f32[6,4,8,256]{3,2,1,0:T(8,128)} %cot_hbm.1, f32[2,8,256]{2,1,0:T(8,128)S(1)} %get-tuple-element.15.size_ends_ref), custom_call_target="tpu_custom_call" | custom-call | flops 8192 | bytes 409600 | tf_op jit(solution)/shard_map/pallas_call | solution.py:373
  5.6 1.2 %collective-permute-start.3 = (f32[6,4,8,256]{3,2,1,0:T(8,128)S(1)}, f32[6,4,8,256]{3,2,1,0:T(8,128)S(1)}, u32[]{:S(2)}, u32[]{:S(2)}) collective-permute-start(f32[6,4,8,256]{3,2,1,0:T(8,128)S(1)} %shard_map.62.cot_ref), channel_id=1, source_target_pairs={{16,0},{0,16},{17,1},{1,17},{18,2},{2,18},{19,3},{3,19},{20,4},{4,... | collective-permute-start | bytes 589832 | tf_op jit(solution)/shard_map/ppermute | solution.py:386
  6.8 0.0 collective-permute-done.refs_0_
  6.9 0.0 copy-done.2
  6.9 0.1 broadcast_in_dim.2.bins_ref
  6.9 0.0 copy-done
  6.9 0.2 shard_map.59
  7.1 0.5 %collective-permute-done.1.refs_0_ = f32[2,8,256]{2,1,0:T(8,128)S(1)} collective-permute-done((f32[2,8,256]{2,1,0:T(8,128)S(1)}, f32[2,8,256]{2,1,0:T(8,128)S(1)}, u32[]{:S(2)}, u32[]{:S(2)}) %collective-permute-start.1) | collective-permute-done | bytes 16416 | tf_op jit(solution)/shard_map/ppermute | solution.py:386
  7.5 0.2 %shard_map.63 = (f32[6,4,8,256]{3,2,1,0:T(8,128)S(1)}, f32[8,128]{1,0:T(8,128)S(1)}) custom-call(f32[6,4,8,256]{3,2,1,0:T(8,128)S(1)} %copy-done.1, f32[6,4,8,256]{3,2,1,0:T(8,128)S(1)} %shard_map.62.cot_ref, f32[4,8,256]{2,1,0:T(8,128)S(1)} %get-tuple-element.16.size_ref, f32[6,4,8,256]{3,2,1,0:T(8,128)S(1)} %get-tuple-element.14.leonard_ref.refs_1_, ...), custom_call_target="tpu_custom_call" | custom-call | flops 2457600000 | bytes 1040384 | tf_op jit(solution)/shard_map/pallas_call | solution.py:373
  7.7 0.1 collective-permute-start.2
  7.8 1.2 %collective-permute-done.2.other_sums_ref = f32[8,128]{1,0:T(8,128)S(1)} collective-permute-done((f32[8,128]{1,0:T(8,128)S(1)}, f32[8,128]{1,0:T(8,128)S(1)}, u32[]{:S(2)}, u32[]{:S(2)}) %collective-permute-start.2) | collective-permute-done | bytes 4128 | tf_op jit(solution)/shard_map/ppermute | solution.py:396
  9.0 1.4 %collective-permute-start.6 = (f32[19,8,256]{2,1,0:T(8,128)S(1)}, f32[19,8,256]{2,1,0:T(8,128)S(1)}, u32[]{:S(2)}, u32[]{:S(2)}) collective-permute-start(f32[19,8,256]{2,1,0:T(8,128)S(1)} %get-tuple-element.25), channel_id=1, source_target_pairs={{16,0},{0,16},{17,1},{1,17},{18,2},{2,18},{19,3},{3,19},{20,4},{4,... | collective-permute-start | bytes 466952 | tf_op jit(solution)/shard_map/ppermute | solution.py:386
  10.4 1.7 %collective-permute-start.5 = (f32[8,128]{1,0:T(8,128)S(1)}, f32[8,128]{1,0:T(8,128)S(1)}, u32[]{:S(2)}, u32[]{:S(2)}) collective-permute-start(f32[8,128]{1,0:T(8,128)S(1)} %get-tuple-element.24.refs_7_), channel_id=1, source_target_pairs={{17,0},{19,1},{16,2},{21,3},{18,4},{23,5},{20,6},{25,7},{22,8},{27... | collective-permute-start | bytes 12296 | tf_op jit(solution)/shard_map/ppermute | solution.py:396
  12.0 1.5 %collective-permute-start.4 = (f32[8,128]{1,0:T(8,128)S(1)}, f32[8,128]{1,0:T(8,128)S(1)}, u32[]{:S(2)}, u32[]{:S(2)}) collective-permute-start(f32[8,128]{1,0:T(8,128)S(1)} %get-tuple-element.24.refs_7_), channel_id=1, source_target_pairs={{1,0},{3,1},{0,2},{5,3},{2,4},{7,5},{4,6},{9,7},{6,8},{11,9},{8,10... | collective-permute-start | bytes 12296 | tf_op jit(solution)/shard_map/ppermute | solution.py:396
  13.6 0.0 collective-permute-done.3.refs_1_
  13.6 0.6 %shard_map.65.refs_3_ = f32[12,4,8,256]{3,2,1,0:T(8,128)S(1)} custom-call(f32[12,4,8,256]{3,2,1,0:T(8,128)S(1)} %get-tuple-element.22.early_ref, f32[3,4,8,256]{3,2,1,0:T(8,128)S(1)} %copy-done, f32[6,4,8,256]{3,2,1,0:T(8,128)S(1)} %shard_map.62.cot_ref, f32[3,4,8,256]{3,2,1,0:T(8,128)S(1)} %get-tuple-element.20.smooth_ref, ...), custom_call_target="tpu_custom_call" | custom-call | flops 4096000 | bytes 1966080 | tf_op jit(solution)/shard_map/pallas_call | solution.py:373
  14.2 1.3 %collective-permute-done.5.refs_6_ = f32[8,128]{1,0:T(8,128)S(1)} collective-permute-done((f32[8,128]{1,0:T(8,128)S(1)}, f32[8,128]{1,0:T(8,128)S(1)}, u32[]{:S(2)}, u32[]{:S(2)}) %collective-permute-start.5) | collective-permute-done | bytes 4128 | tf_op jit(solution)/shard_map/ppermute | solution.py:396
  15.5 0.0 collective-permute-done.4.refs_5_
  15.5 0.3 %collective-permute-done.6.refs_8_ = f32[19,8,256]{2,1,0:T(8,128)S(1)} collective-permute-done((f32[19,8,256]{2,1,0:T(8,128)S(1)}, f32[19,8,256]{2,1,0:T(8,128)S(1)}, u32[]{:S(2)}, u32[]{:S(2)}) %collective-permute-start.6) | collective-permute-done | bytes 155680 | tf_op jit(solution)/shard_map/ppermute | solution.py:386
  15.8 0.8 %shard_map.66 = (f32[6,4,8,256]{3,2,1,0:T(8,128)}, f32[3,4,8,256]{3,2,1,0:T(8,128)}) custom-call(f32[3,4,8,256]{3,2,1,0:T(8,128)S(1)} %copy-done, f32[6,4,8,256]{3,2,1,0:T(8,128)S(1)} %get-tuple-element.14.leonard_ref.refs_1_, f32[6,4,8,256]{3,2,1,0:T(8,128)S(1)} %get-tuple-element.19.model_ref.refs_2_, f32[12,4,8,256]{3,2,1,0:T(8,128)S(1)} %shard_map.65.refs_3_, ...), custom_call_target="tpu_custom_call" | custom-call | flops 1638400 | bytes 1351680 | tf_op jit(solution)/shard_map/pallas_call | solution.py:373
  (3 shorter events, 0.1 us)
Async XLA Ops:
  0.6 3.0 %copy-start.1 = (f32[6,4,8,256]{3,2,1,0:T(8,128)S(1)}, f32[6,4,8,256]{3,2,1,0:T(8,128)}, u32[]{:S(2)}) copy-start(f32[6,4,8,256]{3,2,1,0:T(8,128)} %strain_ref.3) | copy-start | bytes 589828
  0.6 6.2 %collective-permute-start = (f32[3,4,8,256]{3,2,1,0:T(8,128)}, f32[3,4,8,256]{3,2,1,0:T(8,128)S(1)}, u32[]{:S(2)}, u32[]{:S(2)}) collective-permute-start(f32[3,4,8,256]{3,2,1,0:T(8,128)} %refs_0_.1), channel_id=1, source_target_pairs={{16,0},{0,16},{17,1},{1,17},{18,2},{2,18},{19,3},{3,19},{20,4},{4,... | collective-permute-start | bytes 294920 | tf_op jit(solution)/shard_map/ppermute | solution.py:386
  3.7 3.1 %copy-start.2 = (s32[8]{0:T(128)S(1)}, s32[8]{0:T(128)}, u32[]{:S(2)}) copy-start(s32[8]{0:T(128)} %param.6) | copy-start | bytes 100
  3.7 3.2 %copy-start = (f32[3,4,8,256]{3,2,1,0:T(8,128)S(1)}, f32[3,4,8,256]{3,2,1,0:T(8,128)}, u32[]{:S(2)}) copy-start(f32[3,4,8,256]{3,2,1,0:T(8,128)} %refs_0_.1) | copy-start | bytes 294916
  3.7 3.8 %collective-permute-start.1 = (f32[2,8,256]{2,1,0:T(8,128)S(1)}, f32[2,8,256]{2,1,0:T(8,128)S(1)}, u32[]{:S(2)}, u32[]{:S(2)}) collective-permute-start(f32[2,8,256]{2,1,0:T(8,128)S(1)} %get-tuple-element.15.size_ends_ref), channel_id=1, source_target_pairs={{16,0},{0,16},{17,1},{1,17},{18,2},{2,18},{19,3},{3,19},{20,4},{4,... | collective-permute-start | bytes 49160 | tf_op jit(solution)/shard_map/ppermute | solution.py:386
  5.6 8.0 %collective-permute-start.3 = (f32[6,4,8,256]{3,2,1,0:T(8,128)S(1)}, f32[6,4,8,256]{3,2,1,0:T(8,128)S(1)}, u32[]{:S(2)}, u32[]{:S(2)}) collective-permute-start(f32[6,4,8,256]{3,2,1,0:T(8,128)S(1)} %shard_map.62.cot_ref), channel_id=1, source_target_pairs={{16,0},{0,16},{17,1},{1,17},{18,2},{2,18},{19,3},{3,19},{20,4},{4,... | collective-permute-start | bytes 589832 | tf_op jit(solution)/shard_map/ppermute | solution.py:386
  7.7 1.2 %collective-permute-start.2 = (f32[8,128]{1,0:T(8,128)S(1)}, f32[8,128]{1,0:T(8,128)S(1)}, u32[]{:S(2)}, u32[]{:S(2)}) collective-permute-start(f32[8,128]{1,0:T(8,128)S(1)} %get-tuple-element.21.sums_ref), channel_id=1, source_target_pairs={{1,0},{0,1},{3,2},{2,3},{5,4},{4,5},{7,6},{6,7},{9,8},{8,9},{11,10... | collective-permute-start | bytes 12296 | tf_op jit(solution)/shard_map/ppermute | solution.py:396
  9.0 6.7 %collective-permute-start.6 = (f32[19,8,256]{2,1,0:T(8,128)S(1)}, f32[19,8,256]{2,1,0:T(8,128)S(1)}, u32[]{:S(2)}, u32[]{:S(2)}) collective-permute-start(f32[19,8,256]{2,1,0:T(8,128)S(1)} %get-tuple-element.25), channel_id=1, source_target_pairs={{16,0},{0,16},{17,1},{1,17},{18,2},{2,18},{19,3},{3,19},{20,4},{4,... | collective-permute-start | bytes 466952 | tf_op jit(solution)/shard_map/ppermute | solution.py:386
  10.4 5.1 %collective-permute-start.5 = (f32[8,128]{1,0:T(8,128)S(1)}, f32[8,128]{1,0:T(8,128)S(1)}, u32[]{:S(2)}, u32[]{:S(2)}) collective-permute-start(f32[8,128]{1,0:T(8,128)S(1)} %get-tuple-element.24.refs_7_), channel_id=1, source_target_pairs={{17,0},{19,1},{16,2},{21,3},{18,4},{23,5},{20,6},{25,7},{22,8},{27... | collective-permute-start | bytes 12296 | tf_op jit(solution)/shard_map/ppermute | solution.py:396
  12.0 3.4 %collective-permute-start.4 = (f32[8,128]{1,0:T(8,128)S(1)}, f32[8,128]{1,0:T(8,128)S(1)}, u32[]{:S(2)}, u32[]{:S(2)}) collective-permute-start(f32[8,128]{1,0:T(8,128)S(1)} %get-tuple-element.24.refs_7_), channel_id=1, source_target_pairs={{1,0},{3,1},{0,2},{5,3},{2,4},{7,5},{4,6},{9,7},{6,8},{11,9},{8,10... | collective-permute-start | bytes 12296 | tf_op jit(solution)/shard_map/ppermute | solution.py:396

commit v16 on v14

--- a/solution.py
+++ b/solution.py
@@ -108,9 +108,15 @@
             size_ends_ref[end, :, lanes] = value
 
 
-def fetch_kernel(cot_hbm, size_ends_ref, cot_ref, arrived):
+def fetch_kernel(cot_hbm, bins_ref, size_ends_ref, cot_ref, mask_ref, arrived):
     copy = pltpu.make_async_copy(cot_hbm, cot_ref, arrived)
     copy.start()
+    rows = bins_ref.shape[1]
+    along = jnp.broadcast_to(bins_ref[...].astype(jnp.float32), (rows, rows))
+    diagonal = lax.broadcasted_iota(jnp.int32, (rows, rows), 0) == lax.broadcasted_iota(jnp.int32, (rows, rows), 1)
+    column = jnp.sum(jnp.where(diagonal, along, 0.0), axis=1, keepdims=True)
+    lane = lax.broadcasted_iota(jnp.int32, (rows, LANES), 1).astype(jnp.float32)
+    mask_ref[...] = jnp.where(jnp.broadcast_to(column, (rows, LANES)) == lane, 1.0, 0.0)
     copy.wait()
 
 
@@ -136,9 +142,9 @@
     return [plain[z] + tensor[PAIR_OF[a][a]][z] * vector[a][z] for z in range(cells)]
 
 
-def velocity_kernel(tables, v_ref, bins_ref, *refs):
-    far_v_refs = refs[:-4]
-    smooth_ref, leonard_ref, rest_ref, mask_ref = refs[-4:]
+def velocity_kernel(tables, v_ref, *refs):
+    far_v_refs = refs[:-3]
+    smooth_ref, leonard_ref, rest_ref = refs[-3:]
     cells = tables.cells
     for lanes in halves(v_ref.shape[-1]):
         v = [[v_ref[a, z, :, lanes] for z in range(cells)] for a in range(3)]
@@ -156,8 +162,6 @@
                 coarse = filtered[a][z] * filtered[b][z]
                 leonard_ref[k, z, :, lanes] = filtered[3 + k][z] - coarse
                 rest_ref[k, z, :, lanes] = products[k][z] - coarse
-    lane = lax.broadcasted_iota(jnp.int32, bins_ref.shape, 1)
-    mask_ref[...] = jnp.where(bins_ref[...] == lane, 1.0, 0.0)
 
 
 def model_kernel(tables, strain_ref, cot_ref, size_ref, leonard_ref, rest_ref, mask_ref, *refs):
@@ -194,19 +198,19 @@
     cells = tables.cells
     pair_sums = sums_ref[...] + other_sums_ref[...]
     pair_ref[...] = pair_sums
-    message_ref[18, 0:8, 0:LANES] = pair_sums
-    for lanes in halves(model_ref.shape[-1]):
+    message_ref[message_ref.shape[0] - 1] = pair_sums
+    for half, lanes in enumerate(halves(model_ref.shape[-1])):
         model = [[model_ref[k, z, :, lanes] for z in range(cells)] for k in range(6)]
         smooth_v = [[smooth_ref[a, z, :, lanes] for z in range(cells)] for a in range(3)]
         for k in range(6):
             for end, value in enumerate(tables.project(model[k])):
-                message_ref[2 * k + end, :, lanes] = value
+                message_ref[18 * half + 2 * k + end] = value
         for a in range(3):
             dual = [2.0 * x for x in plain_dual(model, smooth_v, a, cells)]
             for z in range(cells):
                 dual_ref[a, z, :, lanes] = dual[z]
             for end, value in enumerate(tables.project(dual)):
-                message_ref[12 + 2 * a + end, :, lanes] = value
+                message_ref[18 * half + 12 + 2 * a + end] = value
 
 
 def local_kernel(tables, *refs):
@@ -271,7 +275,7 @@
     pair_ref = refs[5 + count]
     far_message_refs = refs[6 + count : 6 + count + peers]
     residual_hbm, grad_hbm, residual_ref, grad_ref, left = refs[6 + count + peers :]
-    total = sum_up([pair_ref[...]] + [ref[18, 0:8, 0:LANES] for ref in far_message_refs])
+    total = sum_up([pair_ref[...]] + [ref[ref.shape[0] - 1] for ref in far_message_refs])
     near = sum_up([ref[...] for ref in near_refs])
     if turning:
         place = lax.axis_index("stream")
@@ -299,15 +303,15 @@
             some = pl.ds(k - 2, 3)
             copies.append(pltpu.make_async_copy(residual_ref.at[some], residual_hbm.at[some], left.at[k // 3]))
             copies[-1].start()
-    for lanes in halves(v_ref.shape[-1]):
+    for half, lanes in enumerate(halves(v_ref.shape[-1])):
         v = [[v_ref[a, z, :, lanes] for z in range(cells)] for a in range(3)]
         from_model = [[] for _ in range(6)]
         from_dual = [[] for _ in range(3)]
         for place, ends in enumerate(far_message_refs, start=1):
             for k in range(6):
-                from_model[k].append(tables.outside(place, [2.0 * ends[2 * k + end, :, lanes] for end in range(2)]))
+                from_model[k].append(tables.outside(place, [2.0 * ends[18 * half + 2 * k + end] for end in range(2)]))
             for a in range(3):
-                pair = [(2.0 * coefficient - 1.0) * ends[12 + 2 * a + end, :, lanes] for end in range(2)]
+                pair = [(2.0 * coefficient - 1.0) * ends[18 * half + 12 + 2 * a + end] for end in range(2)]
                 from_dual[a].append(tables.outside(place, pair))
         from_model = [functools.reduce(add_lists, lists) if lists else None for lists in from_model]
         from_dual = [functools.reduce(add_lists, lists) if lists else None for lists in from_dual]
@@ -376,7 +380,6 @@
     def shaped(*leading):
         return pltpu.VMEM(leading + slab, jnp.float32)
 
-    bins = jnp.broadcast_to(row_bins[:, None], (rows, LANES))
     far_v = [from_ahead(velocity, shift) for shift in range(1, span)]
     work = cells * rows * width
     (lane,) = call(lanes_kernel, [pltpu.VMEM((rows, LANES), jnp.int32)], LONG * work)
@@ -384,23 +387,23 @@
         functools.partial(prepare_kernel, tables), [shaped(cells), shaped(2)], LONG * work, lane, strain
     )
     far_size = [from_ahead(size_ends, shift) for shift in range(1, span)]
-    (near_cot,) = call(
+    near_cot, mask = call(
         fetch_kernel,
-        [shaped(6, cells)],
+        [shaped(6, cells), pltpu.VMEM((rows, LANES), jnp.float32)],
         work,
         pltpu.with_memory_space_constraint(cotangent, pltpu.HBM),
+        row_bins.reshape(1, rows),
         size_ends,
-        in_specs=[REMAIN, WHOLE],
+        in_specs=[REMAIN, WHOLE, WHOLE],
         scratch=[pltpu.SemaphoreType.DMA(())],
     )
     far_cot = [from_ahead(near_cot, shift) for shift in range(1, span)]
     table = pltpu.VMEM((8, LANES), jnp.float32)
-    smooth, leonard, rest, mask = call(
+    smooth, leonard, rest = call(
         functools.partial(velocity_kernel, tables),
-        [shaped(3, cells), shaped(6, cells), shaped(6, cells), pltpu.VMEM((rows, LANES), jnp.float32)],
+        [shaped(3, cells), shaped(6, cells), shaped(6, cells)],
         LONG * work,
         velocity,
-        bins,
         *far_v,
     )
     model, sums = call(
@@ -418,7 +421,7 @@
     other_sums = from_source(sums, 0, lambda j: j ^ 1)
     dual, message, pair_sums = call(
         functools.partial(message_kernel, tables),
-        [shaped(3, cells), shaped(19), table],
+        [shaped(3, cells), pltpu.VMEM((18 * (width // LANES) + 1, rows, LANES), jnp.float32), table],
         100 * work,
         smooth,
         model,

time: 16.4 us -> 16.4 us (level)
  no operation moved by 1% of the time
where the time goes in v16:
time: 16.4 us; the launch traced here: 16.2 us
  starting transfers between devices  9.82 us (60%)
  waiting for transfers between devices  2.91 us (18%)
  Pallas kernels  2.8 us (17%)
  between operations  0.68 us (4%)
    ppermute x4, starting transfers between devices, from_ahead(): lax.ppermute(values, 'span', [((i + shift) % peers, i) for i in range(pee...  6.49 us
    ppermute x3, starting transfers between devices, from_source(): return lax.ppermute(values, ('span', 'stream'), pairs)  3.33 us
    pallas_call x8, Pallas kernels, call(): pl.pallas_call(kernel, out_shape=outs, in_specs=in_specs or [WHOLE] * len...  2.8 us
    ppermute x3, waiting for transfers between devices, from_source(): return lax.ppermute(values, ('span', 'stream'), pairs)  1.92 us
    ppermute x4, waiting for transfers between devices, from_ahead(): lax.ppermute(values, 'span', [((i + shift) % peers, i) for i in range(pee...  0.99 us
  transfers between devices with their start and end apart: 7, of which 4 were waited for; matrix products, arithmetic and copies ran while one was open for 0% of the time, Pallas kernels for 12%

profile of v16, /device:TPU:0, one launch (start us, length us, event | category | flops | bytes accessed | tf_op | source)
XLA Modules:
  0.0 16.2 jit_solution(2249119899975554764)
XLA Ops:
  0.6 0.0 copy-start.2
  0.6 3.0 %collective-permute-start = (f32[3,4,8,256]{3,2,1,0:T(8,128)}, f32[3,4,8,256]{3,2,1,0:T(8,128)S(1)}, u32[]{:S(2)}, u32[]{:S(2)}) collective-permute-start(f32[3,4,8,256]{3,2,1,0:T(8,128)} %refs_0_.3), channel_id=1, source_target_pairs={{16,0},{0,16},{17,1},{1,17},{18,2},{2,18},{19,3},{3,19},{20,4},{4,... | collective-permute-start | bytes 294920 | tf_op jit(solution)/shard_map/ppermute | solution.py:352
  3.7 0.0 copy-done.2
  3.7 0.0 copy-start.1
  3.7 0.9 %collective-permute-start.1 = (f32[2,8,256]{2,1,0:T(8,128)S(1)}, f32[2,8,256]{2,1,0:T(8,128)S(1)}, u32[]{:S(2)}, u32[]{:S(2)}) collective-permute-start(f32[2,8,256]{2,1,0:T(8,128)S(1)} %get-tuple-element.15.size_ends_ref), channel_id=1, source_target_pairs={{16,0},{0,16},{17,1},{1,17},{18,2},{2,18},{19,3},{3,19},{20,4},{4,... | collective-permute-start | bytes 49160 | tf_op jit(solution)/shard_map/ppermute | solution.py:352
  4.6 0.0 copy-done.1
  4.6 0.0 copy-start
  4.6 1.0 %shard_map.62 = (f32[6,4,8,256]{3,2,1,0:T(8,128)S(1)}, f32[8,128]{1,0:T(8,128)S(1)}) custom-call(f32[6,4,8,256]{3,2,1,0:T(8,128)} %cot_hbm.1, s32[1,8]{1,0:T(1,128)S(1)} %bitcast.1, f32[2,8,256]{2,1,0:T(8,128)S(1)} %get-tuple-element.15.size_ends_ref), custom_call_target="tpu_custom_call" | custom-call | flops 8192 | bytes 413728 | tf_op jit(solution)/shard_map/pallas_call | solution.py:339
  5.6 1.2 %collective-permute-start.3 = (f32[6,4,8,256]{3,2,1,0:T(8,128)S(1)}, f32[6,4,8,256]{3,2,1,0:T(8,128)S(1)}, u32[]{:S(2)}, u32[]{:S(2)}) collective-permute-start(f32[6,4,8,256]{3,2,1,0:T(8,128)S(1)} %get-tuple-element.16.cot_ref.refs_1_), channel_id=1, source_target_pairs={{16,0},{0,16},{17,1},{1,17},{18,2},{2,18},{19,3},{3,19},{20,4},{4,... | collective-permute-start | bytes 589832 | tf_op jit(solution)/shard_map/ppermute | solution.py:352
  6.9 0.0 collective-permute-done.refs_0_.refs_6_
  6.9 0.0 copy-done
  6.9 0.2 shard_map.59
  7.0 0.5 %collective-permute-done.1.refs_0_ = f32[2,8,256]{2,1,0:T(8,128)S(1)} collective-permute-done((f32[2,8,256]{2,1,0:T(8,128)S(1)}, f32[2,8,256]{2,1,0:T(8,128)S(1)}, u32[]{:S(2)}, u32[]{:S(2)}) %collective-permute-start.1) | collective-permute-done | bytes 16416 | tf_op jit(solution)/shard_map/ppermute | solution.py:352
  7.5 0.2 %shard_map.63 = (f32[6,4,8,256]{3,2,1,0:T(8,128)S(1)}, f32[8,128]{1,0:T(8,128)S(1)}) custom-call(f32[6,4,8,256]{3,2,1,0:T(8,128)S(1)} %copy-done.2, f32[6,4,8,256]{3,2,1,0:T(8,128)S(1)} %get-tuple-element.16.cot_ref.refs_1_, f32[4,8,256]{2,1,0:T(8,128)S(1)} %get-tuple-element.17.size_ref, f32[6,4,8,256]{3,2,1,0:T(8,128)S(1)} %get-tuple-element.14.leonard_ref.refs_3_.refs_1_, ...), custom_call_target="tpu_custom_call" | custom-call | flops 2457600000 | bytes 1040384 | tf_op jit(solution)/shard_map/pallas_call | solution.py:339
  7.7 0.1 collective-permute-start.2
  7.8 1.2 %collective-permute-done.2.other_sums_ref = f32[8,128]{1,0:T(8,128)S(1)} collective-permute-done((f32[8,128]{1,0:T(8,128)S(1)}, f32[8,128]{1,0:T(8,128)S(1)}, u32[]{:S(2)}, u32[]{:S(2)}) %collective-permute-start.2) | collective-permute-done | bytes 4128 | tf_op jit(solution)/shard_map/ppermute | solution.py:362
  9.0 1.3 %collective-permute-start.6 = (f32[37,8,128]{2,1,0:T(8,128)S(1)}, f32[37,8,128]{2,1,0:T(8,128)S(1)}, u32[]{:S(2)}, u32[]{:S(2)}) collective-permute-start(f32[37,8,128]{2,1,0:T(8,128)S(1)} %get-tuple-element.25), channel_id=1, source_target_pairs={{16,0},{0,16},{17,1},{1,17},{18,2},{2,18},{19,3},{3,19},{20,4},{4,... | collective-permute-start | bytes 454664 | tf_op jit(solution)/shard_map/ppermute | solution.py:352
  10.3 1.7 %collective-permute-start.5 = (f32[8,128]{1,0:T(8,128)S(1)}, f32[8,128]{1,0:T(8,128)S(1)}, u32[]{:S(2)}, u32[]{:S(2)}) collective-permute-start(f32[8,128]{1,0:T(8,128)S(1)} %get-tuple-element.24.refs_7_), channel_id=1, source_target_pairs={{17,0},{19,1},{16,2},{21,3},{18,4},{23,5},{20,6},{25,7},{22,8},{27... | collective-permute-start | bytes 12296 | tf_op jit(solution)/shard_map/ppermute | solution.py:362
  12.0 1.5 %collective-permute-start.4 = (f32[8,128]{1,0:T(8,128)S(1)}, f32[8,128]{1,0:T(8,128)S(1)}, u32[]{:S(2)}, u32[]{:S(2)}) collective-permute-start(f32[8,128]{1,0:T(8,128)S(1)} %get-tuple-element.24.refs_7_), channel_id=1, source_target_pairs={{1,0},{3,1},{0,2},{5,3},{2,4},{7,5},{4,6},{9,7},{6,8},{11,9},{8,10... | collective-permute-start | bytes 12296 | tf_op jit(solution)/shard_map/ppermute | solution.py:362
  13.6 0.0 collective-permute-done.3.refs_7_
  13.6 0.6 %shard_map.65.refs_3_ = f32[12,4,8,256]{3,2,1,0:T(8,128)S(1)} custom-call(f32[3,4,8,256]{3,2,1,0:T(8,128)S(1)} %copy-done, f32[6,4,8,256]{3,2,1,0:T(8,128)S(1)} %get-tuple-element.16.cot_ref.refs_1_, f32[3,4,8,256]{3,2,1,0:T(8,128)S(1)} %get-tuple-element.21.smooth_ref.refs_2_, f32[6,4,8,256]{3,2,1,0:T(8,128)S(1)} %get-tuple-element.14.leonard_ref.refs_3_.refs_1_, ...), custom_call_target="tpu_custom_call" | custom-call | flops 4096000 | bytes 1572864 | tf_op jit(solution)/shard_map/pallas_call | solution.py:339
  14.1 0.7 %collective-permute-done.5.refs_6_ = f32[8,128]{1,0:T(8,128)S(1)} collective-permute-done((f32[8,128]{1,0:T(8,128)S(1)}, f32[8,128]{1,0:T(8,128)S(1)}, u32[]{:S(2)}, u32[]{:S(2)}) %collective-permute-start.5) | collective-permute-done | bytes 4128 | tf_op jit(solution)/shard_map/ppermute | solution.py:362
  14.9 0.0 collective-permute-done.4.refs_5_
  14.9 0.5 %collective-permute-done.6.refs_8_ = f32[37,8,128]{2,1,0:T(8,128)S(1)} collective-permute-done((f32[37,8,128]{2,1,0:T(8,128)S(1)}, f32[37,8,128]{2,1,0:T(8,128)S(1)}, u32[]{:S(2)}, u32[]{:S(2)}) %collective-permute-start.6) | collective-permute-done | bytes 151584 | tf_op jit(solution)/shard_map/ppermute | solution.py:352
  15.4 0.8 %shard_map.66 = (f32[6,4,8,256]{3,2,1,0:T(8,128)}, f32[3,4,8,256]{3,2,1,0:T(8,128)}) custom-call(f32[3,4,8,256]{3,2,1,0:T(8,128)S(1)} %copy-done, f32[6,4,8,256]{3,2,1,0:T(8,128)S(1)} %get-tuple-element.14.leonard_ref.refs_3_.refs_1_, f32[6,4,8,256]{3,2,1,0:T(8,128)S(1)} %get-tuple-element.20.model_ref.refs_4_.refs_2_, ...), custom_call_target="tpu_custom_call" | custom-call | flops 1638400 | bytes 1347584 | tf_op jit(solution)/shard_map/pallas_call | solution.py:339
  (3 shorter events, 0.1 us)
Async XLA Ops:
  0.6 3.0 %copy-start.2 = (f32[6,4,8,256]{3,2,1,0:T(8,128)S(1)}, f32[6,4,8,256]{3,2,1,0:T(8,128)}, u32[]{:S(2)}) copy-start(f32[6,4,8,256]{3,2,1,0:T(8,128)} %strain_ref.3) | copy-start | bytes 589828
  0.6 6.2 %collective-permute-start = (f32[3,4,8,256]{3,2,1,0:T(8,128)}, f32[3,4,8,256]{3,2,1,0:T(8,128)S(1)}, u32[]{:S(2)}, u32[]{:S(2)}) collective-permute-start(f32[3,4,8,256]{3,2,1,0:T(8,128)} %refs_0_.3), channel_id=1, source_target_pairs={{16,0},{0,16},{17,1},{1,17},{18,2},{2,18},{19,3},{3,19},{20,4},{4,... | collective-permute-start | bytes 294920 | tf_op jit(solution)/shard_map/ppermute | solution.py:352
  3.7 0.9 %copy-start.1 = (s32[8]{0:T(128)S(1)}, s32[8]{0:T(128)}, u32[]{:S(2)}) copy-start(s32[8]{0:T(128)} %param.6) | copy-start | bytes 100
  3.7 3.8 %collective-permute-start.1 = (f32[2,8,256]{2,1,0:T(8,128)S(1)}, f32[2,8,256]{2,1,0:T(8,128)S(1)}, u32[]{:S(2)}, u32[]{:S(2)}) collective-permute-start(f32[2,8,256]{2,1,0:T(8,128)S(1)} %get-tuple-element.15.size_ends_ref), channel_id=1, source_target_pairs={{16,0},{0,16},{17,1},{1,17},{18,2},{2,18},{19,3},{3,19},{20,4},{4,... | collective-permute-start | bytes 49160 | tf_op jit(solution)/shard_map/ppermute | solution.py:352
  4.6 2.2 %copy-start = (f32[3,4,8,256]{3,2,1,0:T(8,128)S(1)}, f32[3,4,8,256]{3,2,1,0:T(8,128)}, u32[]{:S(2)}) copy-start(f32[3,4,8,256]{3,2,1,0:T(8,128)} %refs_0_.3) | copy-start | bytes 294916
  5.6 7.9 %collective-permute-start.3 = (f32[6,4,8,256]{3,2,1,0:T(8,128)S(1)}, f32[6,4,8,256]{3,2,1,0:T(8,128)S(1)}, u32[]{:S(2)}, u32[]{:S(2)}) collective-permute-start(f32[6,4,8,256]{3,2,1,0:T(8,128)S(1)} %get-tuple-element.16.cot_ref.refs_1_), channel_id=1, source_target_pairs={{16,0},{0,16},{17,1},{1,17},{18,2},{2,18},{19,3},{3,19},{20,4},{4,... | collective-permute-start | bytes 589832 | tf_op jit(solution)/shard_map/ppermute | solution.py:352
  7.7 1.2 %collective-permute-start.2 = (f32[8,128]{1,0:T(8,128)S(1)}, f32[8,128]{1,0:T(8,128)S(1)}, u32[]{:S(2)}, u32[]{:S(2)}) collective-permute-start(f32[8,128]{1,0:T(8,128)S(1)} %get-tuple-element.22.sums_ref), channel_id=1, source_target_pairs={{1,0},{0,1},{3,2},{2,3},{5,4},{4,5},{7,6},{6,7},{9,8},{8,9},{11,10... | collective-permute-start | bytes 12296 | tf_op jit(solution)/shard_map/ppermute | solution.py:362
  9.0 6.4 %collective-permute-start.6 = (f32[37,8,128]{2,1,0:T(8,128)S(1)}, f32[37,8,128]{2,1,0:T(8,128)S(1)}, u32[]{:S(2)}, u32[]{:S(2)}) collective-permute-start(f32[37,8,128]{2,1,0:T(8,128)S(1)} %get-tuple-element.25), channel_id=1, source_target_pairs={{16,0},{0,16},{17,1},{1,17},{18,2},{2,18},{19,3},{3,19},{20,4},{4,... | collective-permute-start | bytes 454664 | tf_op jit(solution)/shard_map/ppermute | solution.py:352
  10.3 4.6 %collective-permute-start.5 = (f32[8,128]{1,0:T(8,128)S(1)}, f32[8,128]{1,0:T(8,128)S(1)}, u32[]{:S(2)}, u32[]{:S(2)}) collective-permute-start(f32[8,128]{1,0:T(8,128)S(1)} %get-tuple-element.24.refs_7_), channel_id=1, source_target_pairs={{17,0},{19,1},{16,2},{21,3},{18,4},{23,5},{20,6},{25,7},{22,8},{27... | collective-permute-start | bytes 12296 | tf_op jit(solution)/shard_map/ppermute | solution.py:362
  12.0 2.9 %collective-permute-start.4 = (f32[8,128]{1,0:T(8,128)S(1)}, f32[8,128]{1,0:T(8,128)S(1)}, u32[]{:S(2)}, u32[]{:S(2)}) collective-permute-start(f32[8,128]{1,0:T(8,128)S(1)} %get-tuple-element.24.refs_7_), channel_id=1, source_target_pairs={{1,0},{3,1},{0,2},{5,3},{2,4},{7,5},{4,6},{9,7},{6,8},{11,9},{8,10... | collective-permute-start | bytes 12296 | tf_op jit(solution)/shard_map/ppermute | solution.py:362

commit v17 on v16

--- a/solution.py
+++ b/solution.py
@@ -194,11 +194,9 @@
     sums_ref[...] = table
 
 
-def message_kernel(tables, smooth_ref, model_ref, sums_ref, other_sums_ref, dual_ref, message_ref, pair_ref):
-    cells = tables.cells
-    pair_sums = sums_ref[...] + other_sums_ref[...]
-    pair_ref[...] = pair_sums
-    message_ref[message_ref.shape[0] - 1] = pair_sums
+def message_kernel(tables, smooth_ref, model_ref, sums_ref, dual_ref, message_ref):
+    cells = tables.cells
+    message_ref[message_ref.shape[0] - 1] = sums_ref[...]
     for half, lanes in enumerate(halves(model_ref.shape[-1])):
         model = [[model_ref[k, z, :, lanes] for z in range(cells)] for k in range(6)]
         smooth_v = [[smooth_ref[a, z, :, lanes] for z in range(cells)] for a in range(3)]
@@ -272,10 +270,10 @@
     cells = tables.cells
     v_ref, leonard_ref, model_ref, parts_ref, mask_ref = refs[:5]
     near_refs = refs[5 : 5 + count]
-    pair_ref = refs[5 + count]
-    far_message_refs = refs[6 + count : 6 + count + peers]
-    residual_hbm, grad_hbm, residual_ref, grad_ref, left = refs[6 + count + peers :]
-    total = sum_up([pair_ref[...]] + [ref[ref.shape[0] - 1] for ref in far_message_refs])
+    pair_refs = refs[5 + count : 6 + count + peers]
+    far_message_refs = refs[6 + count + peers : 6 + count + 2 * peers]
+    residual_hbm, grad_hbm, residual_ref, grad_ref, left = refs[6 + count + 2 * peers :]
+    total = sum_up([ref[...] for ref in pair_refs] + [ref[ref.shape[0] - 1] for ref in far_message_refs])
     near = sum_up([ref[...] for ref in near_refs])
     if turning:
         place = lax.axis_index("stream")
@@ -419,15 +417,16 @@
         *far_size,
     )
     other_sums = from_source(sums, 0, lambda j: j ^ 1)
-    dual, message, pair_sums = call(
+    across_sums = [from_source(sums, shift, lambda j: j ^ 1) for shift in range(1, span)]
+    dual, message = call(
         functools.partial(message_kernel, tables),
-        [shaped(3, cells), pltpu.VMEM((18 * (width // LANES) + 1, rows, LANES), jnp.float32), table],
+        [shaped(3, cells), pltpu.VMEM((18 * (width // LANES) + 1, rows, LANES), jnp.float32)],
         100 * work,
         smooth,
         model,
         sums,
-        other_sums,
-    )
+    )
+    pair_sums = sums + other_sums
     far_message = [from_ahead(message, shift) for shift in range(1, span)]
     most_rows = 2 * rows * stream // NBINS
     reach = -(-(most_rows - 1) // rows)
@@ -437,11 +436,11 @@
     else:
         steps = range(1, -(-reach // 2) + 1)
         sources = [functools.partial(lambda j, away: j + away, away=2 * step * way) for step in steps for way in (1, -1)]
-    near_sums = [from_source(pair_sums, shift, source) for shift in range(span) for source in sources]
+    near_sums = [from_source(pair_sums, shift, source) for shift in reversed(range(span)) for source in sources]
     (parts,) = call(
         functools.partial(local_kernel, tables),
         [shaped(12, cells)],
-        500 * work,
+        LONG * work,
         velocity,
         near_cot,
         smooth,
@@ -464,6 +463,7 @@
             mask,
             *near_sums,
             pair_sums,
+            *across_sums,
             *far_message,
             out_specs=[REMAIN] * 2,
             scratch=[pltpu.VMEM(x.shape, x.dtype) for x in outs] + [pltpu.SemaphoreType.DMA((3,))],

time: 16.4 us -> 16.5 us (level)
  starting transfers between devices: 9.82 us -> 11.2 us
  waiting for transfers between devices: 2.91 us -> 1.63 us
    ppermute x3 -> x4, starting transfers between devices: 3.33 us -> 5.13 us  [from_source(): return lax.ppermute(values, ('span', 'stream'), pairs)]
    ppermute x3 -> x4, waiting for transfers between devices: 1.92 us -> 0.75 us  [from_source(): return lax.ppermute(values, ('span', 'stream'), pairs)]
    ppermute x4, starting transfers between devices: 6.49 us -> 6.04 us  [from_ahead(): lax.ppermute(values, 'span', [((i + shift) % peers, i) for i in range(pee...]
  transfers between devices with their start and end apart: 7 -> 8, of which waited for: 4 -> 4; matrix products, arithmetic and copies ran while one was open for 0% -> 0% of each run, Pallas kernels for 12% -> 12%
where the time goes in v17:
time: 16.5 us; the launch traced here: 16.3 us
  starting transfers between devices  11.2 us (68%)
  Pallas kernels  2.81 us (17%)
  waiting for transfers between devices  1.63 us (10%)
  between operations  0.69 us (4%)
    ppermute x4, starting transfers between devices, from_ahead(): lax.ppermute(values, 'span', [((i + shift) % peers, i) for i in range(pee...  6.04 us
    ppermute x4, starting transfers between devices, from_source(): return lax.ppermute(values, ('span', 'stream'), pairs)  5.13 us
    pallas_call x8, Pallas kernels, call(): pl.pallas_call(kernel, out_shape=outs, in_specs=in_specs or [WHOLE] * len...  2.81 us
    ppermute x4, waiting for transfers between devices, from_ahead(): lax.ppermute(values, 'span', [((i + shift) % peers, i) for i in range(pee...  0.87 us
    ppermute x4, waiting for transfers between devices, from_source(): return lax.ppermute(values, ('span', 'stream'), pairs)  0.75 us
  transfers between devices with their start and end apart: 8, of which 4 were waited for; matrix products, arithmetic and copies ran while one was open for 0% of the time, Pallas kernels for 12%

profile of v17, /device:TPU:0, one launch (start us, length us, event | category | flops | bytes accessed | tf_op | source)
XLA Modules:
  0.0 16.3 jit_solution(1244326930908891661)
XLA Ops:
  0.6 0.0 copy-start.2
  0.6 3.0 %collective-permute-start = (f32[3,4,8,256]{3,2,1,0:T(8,128)}, f32[3,4,8,256]{3,2,1,0:T(8,128)S(1)}, u32[]{:S(2)}, u32[]{:S(2)}) collective-permute-start(f32[3,4,8,256]{3,2,1,0:T(8,128)} %refs_0_.3), channel_id=1, source_target_pairs={{16,0},{0,16},{17,1},{1,17},{18,2},{2,18},{19,3},{3,19},{20,4},{4,... | collective-permute-start | bytes 294920 | tf_op jit(solution)/shard_map/ppermute | solution.py:350
  3.7 0.0 copy-done.2
  3.7 0.0 copy-start.1
  3.7 0.9 %collective-permute-start.1 = (f32[2,8,256]{2,1,0:T(8,128)S(1)}, f32[2,8,256]{2,1,0:T(8,128)S(1)}, u32[]{:S(2)}, u32[]{:S(2)}) collective-permute-start(f32[2,8,256]{2,1,0:T(8,128)S(1)} %get-tuple-element.14.size_ends_ref), channel_id=1, source_target_pairs={{16,0},{0,16},{17,1},{1,17},{18,2},{2,18},{19,3},{3,19},{20,4},{4,... | collective-permute-start | bytes 49160 | tf_op jit(solution)/shard_map/ppermute | solution.py:350
  4.6 0.0 copy-done.1
  4.6 0.0 copy-start
  4.6 1.0 %shard_map.62 = (f32[6,4,8,256]{3,2,1,0:T(8,128)S(1)}, f32[8,128]{1,0:T(8,128)S(1)}) custom-call(f32[6,4,8,256]{3,2,1,0:T(8,128)} %cot_hbm.1, s32[1,8]{1,0:T(1,128)S(1)} %bitcast.1, f32[2,8,256]{2,1,0:T(8,128)S(1)} %get-tuple-element.14.size_ends_ref), custom_call_target="tpu_custom_call" | custom-call | flops 8192 | bytes 413728 | tf_op jit(solution)/shard_map/pallas_call | solution.py:337
  5.6 1.2 %collective-permute-start.2 = (f32[6,4,8,256]{3,2,1,0:T(8,128)S(1)}, f32[6,4,8,256]{3,2,1,0:T(8,128)S(1)}, u32[]{:S(2)}, u32[]{:S(2)}) collective-permute-start(f32[6,4,8,256]{3,2,1,0:T(8,128)S(1)} %get-tuple-element.15.cot_ref.refs_1_), channel_id=1, source_target_pairs={{16,0},{0,16},{17,1},{1,17},{18,2},{2,18},{19,3},{3,19},{20,4},{4,... | collective-permute-start | bytes 589832 | tf_op jit(solution)/shard_map/ppermute | solution.py:350
  6.9 0.0 collective-permute-done.refs_0_.refs_6_
  6.9 0.0 copy-done
  6.9 0.2 shard_map.59
  7.0 0.5 %collective-permute-done.1.refs_0_ = f32[2,8,256]{2,1,0:T(8,128)S(1)} collective-permute-done((f32[2,8,256]{2,1,0:T(8,128)S(1)}, f32[2,8,256]{2,1,0:T(8,128)S(1)}, u32[]{:S(2)}, u32[]{:S(2)}) %collective-permute-start.1) | collective-permute-done | bytes 16416 | tf_op jit(solution)/shard_map/ppermute | solution.py:350
  7.5 0.2 %shard_map.63 = (f32[6,4,8,256]{3,2,1,0:T(8,128)S(1)}, f32[8,128]{1,0:T(8,128)S(1)}) custom-call(f32[6,4,8,256]{3,2,1,0:T(8,128)S(1)} %copy-done.2, f32[6,4,8,256]{3,2,1,0:T(8,128)S(1)} %get-tuple-element.15.cot_ref.refs_1_, f32[4,8,256]{2,1,0:T(8,128)S(1)} %get-tuple-element.16.size_ref, f32[6,4,8,256]{3,2,1,0:T(8,128)S(1)} %get-tuple-element.13.leonard_ref.refs_3_.refs_1_, ...), custom_call_target="tpu_custom_call" | custom-call | flops 2457600000 | bytes 1040384 | tf_op jit(solution)/shard_map/pallas_call | solution.py:337
  7.7 0.1 collective-permute-start.3
  7.8 1.4 %collective-permute-start.6 = (f32[8,128]{1,0:T(8,128)S(1)}, f32[8,128]{1,0:T(8,128)S(1)}, u32[]{:S(2)}, u32[]{:S(2)}) collective-permute-start(f32[8,128]{1,0:T(8,128)S(1)} %get-tuple-element.21.sums_ref), channel_id=1, source_target_pairs={{17,0},{16,1},{19,2},{18,3},{21,4},{20,5},{23,6},{22,7},{25,8},{24... | collective-permute-start | bytes 12296 | tf_op jit(solution)/shard_map/ppermute | solution.py:360
  9.2 0.9 %collective-permute-start.7 = (f32[37,8,128]{2,1,0:T(8,128)S(1)}, f32[37,8,128]{2,1,0:T(8,128)S(1)}, u32[]{:S(2)}, u32[]{:S(2)}) collective-permute-start(f32[37,8,128]{2,1,0:T(8,128)S(1)} %get-tuple-element.23), channel_id=1, source_target_pairs={{16,0},{0,16},{17,1},{1,17},{18,2},{2,18},{19,3},{3,19},{20,4},{4,... | collective-permute-start | bytes 454664 | tf_op jit(solution)/shard_map/ppermute | solution.py:350
  10.1 0.0 collective-permute-done.3
  10.1 2.2 %collective-permute-start.4 = (f32[8,128]{1,0:T(8,128)S(1)}, f32[8,128]{1,0:T(8,128)S(1)}, u32[]{:S(2)}, u32[]{:S(2)}) collective-permute-start(f32[8,128]{1,0:T(8,128)S(1)} %add.3.refs_7_), channel_id=1, source_target_pairs={{17,0},{19,1},{16,2},{21,3},{18,4},{23,5},{20,6},{25,7},{22,8},{27... | collective-permute-start | bytes 12296 | tf_op jit(solution)/shard_map/ppermute | solution.py:360
  12.2 1.5 %collective-permute-start.5 = (f32[8,128]{1,0:T(8,128)S(1)}, f32[8,128]{1,0:T(8,128)S(1)}, u32[]{:S(2)}, u32[]{:S(2)}) collective-permute-start(f32[8,128]{1,0:T(8,128)S(1)} %add.3.refs_7_), channel_id=1, source_target_pairs={{1,0},{3,1},{0,2},{5,3},{2,4},{7,5},{4,6},{9,7},{6,8},{11,9},{8,10... | collective-permute-start | bytes 12296 | tf_op jit(solution)/shard_map/ppermute | solution.py:360
  13.8 0.0 collective-permute-done.2.refs_7_
  13.8 0.6 %shard_map.65.refs_3_ = f32[12,4,8,256]{3,2,1,0:T(8,128)S(1)} custom-call(f32[3,4,8,256]{3,2,1,0:T(8,128)S(1)} %copy-done, f32[6,4,8,256]{3,2,1,0:T(8,128)S(1)} %get-tuple-element.15.cot_ref.refs_1_, f32[3,4,8,256]{3,2,1,0:T(8,128)S(1)} %get-tuple-element.20.smooth_ref.refs_2_, f32[6,4,8,256]{3,2,1,0:T(8,128)S(1)} %get-tuple-element.13.leonard_ref.refs_3_.refs_1_, ...), custom_call_target="tpu_custom_call" | custom-call | flops 2457600000 | bytes 1572864 | tf_op jit(solution)/shard_map/pallas_call | solution.py:337
  14.3 0.0 collective-permute-done.6.refs_8_
  14.4 0.5 %collective-permute-done.4.refs_5_ = f32[8,128]{1,0:T(8,128)S(1)} collective-permute-done((f32[8,128]{1,0:T(8,128)S(1)}, f32[8,128]{1,0:T(8,128)S(1)}, u32[]{:S(2)}, u32[]{:S(2)}) %collective-permute-start.4) | collective-permute-done | bytes 4128 | tf_op jit(solution)/shard_map/ppermute | solution.py:360
  14.8 0.3 %collective-permute-done.5.refs_6_ = f32[8,128]{1,0:T(8,128)S(1)} collective-permute-done((f32[8,128]{1,0:T(8,128)S(1)}, f32[8,128]{1,0:T(8,128)S(1)}, u32[]{:S(2)}, u32[]{:S(2)}) %collective-permute-start.5) | collective-permute-done | bytes 4128 | tf_op jit(solution)/shard_map/ppermute | solution.py:360
  15.1 0.4 %collective-permute-done.7.refs_9_ = f32[37,8,128]{2,1,0:T(8,128)S(1)} collective-permute-done((f32[37,8,128]{2,1,0:T(8,128)S(1)}, f32[37,8,128]{2,1,0:T(8,128)S(1)}, u32[]{:S(2)}, u32[]{:S(2)}) %collective-permute-start.7) | collective-permute-done | bytes 151584 | tf_op jit(solution)/shard_map/ppermute | solution.py:350
  15.5 0.8 %shard_map.66 = (f32[6,4,8,256]{3,2,1,0:T(8,128)}, f32[3,4,8,256]{3,2,1,0:T(8,128)}) custom-call(f32[3,4,8,256]{3,2,1,0:T(8,128)S(1)} %copy-done, f32[6,4,8,256]{3,2,1,0:T(8,128)S(1)} %get-tuple-element.13.leonard_ref.refs_3_.refs_1_, f32[6,4,8,256]{3,2,1,0:T(8,128)S(1)} %get-tuple-element.19.model_ref.refs_4_.refs_2_, ...), custom_call_target="tpu_custom_call" | custom-call | flops 1638400 | bytes 1351680 | tf_op jit(solution)/shard_map/pallas_call | solution.py:337
  (4 shorter events, 0.1 us)
Async XLA Ops:
  0.6 3.0 %copy-start.2 = (f32[6,4,8,256]{3,2,1,0:T(8,128)S(1)}, f32[6,4,8,256]{3,2,1,0:T(8,128)}, u32[]{:S(2)}) copy-start(f32[6,4,8,256]{3,2,1,0:T(8,128)} %strain_ref.3) | copy-start | bytes 589828
  0.6 6.2 %collective-permute-start = (f32[3,4,8,256]{3,2,1,0:T(8,128)}, f32[3,4,8,256]{3,2,1,0:T(8,128)S(1)}, u32[]{:S(2)}, u32[]{:S(2)}) collective-permute-start(f32[3,4,8,256]{3,2,1,0:T(8,128)} %refs_0_.3), channel_id=1, source_target_pairs={{16,0},{0,16},{17,1},{1,17},{18,2},{2,18},{19,3},{3,19},{20,4},{4,... | collective-permute-start | bytes 294920 | tf_op jit(solution)/shard_map/ppermute | solution.py:350
  3.7 0.9 %copy-start.1 = (s32[8]{0:T(128)S(1)}, s32[8]{0:T(128)}, u32[]{:S(2)}) copy-start(s32[8]{0:T(128)} %param.6) | copy-start | bytes 100
  3.7 3.8 %collective-permute-start.1 = (f32[2,8,256]{2,1,0:T(8,128)S(1)}, f32[2,8,256]{2,1,0:T(8,128)S(1)}, u32[]{:S(2)}, u32[]{:S(2)}) collective-permute-start(f32[2,8,256]{2,1,0:T(8,128)S(1)} %get-tuple-element.14.size_ends_ref), channel_id=1, source_target_pairs={{16,0},{0,16},{17,1},{1,17},{18,2},{2,18},{19,3},{3,19},{20,4},{4,... | collective-permute-start | bytes 49160 | tf_op jit(solution)/shard_map/ppermute | solution.py:350
  4.6 2.2 %copy-start = (f32[3,4,8,256]{3,2,1,0:T(8,128)S(1)}, f32[3,4,8,256]{3,2,1,0:T(8,128)}, u32[]{:S(2)}) copy-start(f32[3,4,8,256]{3,2,1,0:T(8,128)} %refs_0_.3) | copy-start | bytes 294916
  5.6 8.2 %collective-permute-start.2 = (f32[6,4,8,256]{3,2,1,0:T(8,128)S(1)}, f32[6,4,8,256]{3,2,1,0:T(8,128)S(1)}, u32[]{:S(2)}, u32[]{:S(2)}) collective-permute-start(f32[6,4,8,256]{3,2,1,0:T(8,128)S(1)} %get-tuple-element.15.cot_ref.refs_1_), channel_id=1, source_target_pairs={{16,0},{0,16},{17,1},{1,17},{18,2},{2,18},{19,3},{3,19},{20,4},{4,... | collective-permute-start | bytes 589832 | tf_op jit(solution)/shard_map/ppermute | solution.py:350
  7.7 2.3 %collective-permute-start.3 = (f32[8,128]{1,0:T(8,128)S(1)}, f32[8,128]{1,0:T(8,128)S(1)}, u32[]{:S(2)}, u32[]{:S(2)}) collective-permute-start(f32[8,128]{1,0:T(8,128)S(1)} %get-tuple-element.21.sums_ref), channel_id=1, source_target_pairs={{1,0},{0,1},{3,2},{2,3},{5,4},{4,5},{7,6},{6,7},{9,8},{8,9},{11,10... | collective-permute-start | bytes 12296 | tf_op jit(solution)/shard_map/ppermute | solution.py:360
  7.8 6.5 %collective-permute-start.6 = (f32[8,128]{1,0:T(8,128)S(1)}, f32[8,128]{1,0:T(8,128)S(1)}, u32[]{:S(2)}, u32[]{:S(2)}) collective-permute-start(f32[8,128]{1,0:T(8,128)S(1)} %get-tuple-element.21.sums_ref), channel_id=1, source_target_pairs={{17,0},{16,1},{19,2},{18,3},{21,4},{20,5},{23,6},{22,7},{25,8},{24... | collective-permute-start | bytes 12296 | tf_op jit(solution)/shard_map/ppermute | solution.py:360
  9.2 6.3 %collective-permute-start.7 = (f32[37,8,128]{2,1,0:T(8,128)S(1)}, f32[37,8,128]{2,1,0:T(8,128)S(1)}, u32[]{:S(2)}, u32[]{:S(2)}) collective-permute-start(f32[37,8,128]{2,1,0:T(8,128)S(1)} %get-tuple-element.23), channel_id=1, source_target_pairs={{16,0},{0,16},{17,1},{1,17},{18,2},{2,18},{19,3},{3,19},{20,4},{4,... | collective-permute-start | bytes 454664 | tf_op jit(solution)/shard_map/ppermute | solution.py:350
  10.1 4.8 %collective-permute-start.4 = (f32[8,128]{1,0:T(8,128)S(1)}, f32[8,128]{1,0:T(8,128)S(1)}, u32[]{:S(2)}, u32[]{:S(2)}) collective-permute-start(f32[8,128]{1,0:T(8,128)S(1)} %add.3.refs_7_), channel_id=1, source_target_pairs={{17,0},{19,1},{16,2},{21,3},{18,4},{23,5},{20,6},{25,7},{22,8},{27... | collective-permute-start | bytes 12296 | tf_op jit(solution)/shard_map/ppermute | solution.py:360
  12.2 2.9 %collective-permute-start.5 = (f32[8,128]{1,0:T(8,128)S(1)}, f32[8,128]{1,0:T(8,128)S(1)}, u32[]{:S(2)}, u32[]{:S(2)}) collective-permute-start(f32[8,128]{1,0:T(8,128)S(1)} %add.3.refs_7_), channel_id=1, source_target_pairs={{1,0},{3,1},{0,2},{5,3},{2,4},{7,5},{4,6},{9,7},{6,8},{11,9},{8,10... | collective-permute-start | bytes 12296 | tf_op jit(solution)/shard_map/ppermute | solution.py:360

commit v18 on v16

--- a/solution.py
+++ b/solution.py
@@ -108,16 +108,16 @@
             size_ends_ref[end, :, lanes] = value
 
 
-def fetch_kernel(cot_hbm, bins_ref, size_ends_ref, cot_ref, mask_ref, arrived):
-    copy = pltpu.make_async_copy(cot_hbm, cot_ref, arrived)
+def mask_kernel(bins_hbm, size_ends_ref, mask_ref, bins_ref, arrived):
+    copy = pltpu.make_async_copy(bins_hbm, bins_ref, arrived)
     copy.start()
+    copy.wait()
     rows = bins_ref.shape[1]
     along = jnp.broadcast_to(bins_ref[...].astype(jnp.float32), (rows, rows))
     diagonal = lax.broadcasted_iota(jnp.int32, (rows, rows), 0) == lax.broadcasted_iota(jnp.int32, (rows, rows), 1)
     column = jnp.sum(jnp.where(diagonal, along, 0.0), axis=1, keepdims=True)
     lane = lax.broadcasted_iota(jnp.int32, (rows, LANES), 1).astype(jnp.float32)
     mask_ref[...] = jnp.where(jnp.broadcast_to(column, (rows, LANES)) == lane, 1.0, 0.0)
-    copy.wait()
 
 
 def products_of(v):
@@ -387,16 +387,16 @@
         functools.partial(prepare_kernel, tables), [shaped(cells), shaped(2)], LONG * work, lane, strain
     )
     far_size = [from_ahead(size_ends, shift) for shift in range(1, span)]
-    near_cot, mask = call(
-        fetch_kernel,
-        [shaped(6, cells), pltpu.VMEM((rows, LANES), jnp.float32)],
+    (mask,) = call(
+        mask_kernel,
+        [pltpu.VMEM((rows, LANES), jnp.float32)],
         work,
-        pltpu.with_memory_space_constraint(cotangent, pltpu.HBM),
-        row_bins.reshape(1, rows),
+        pltpu.with_memory_space_constraint(row_bins.reshape(1, rows), pltpu.HBM),
         size_ends,
-        in_specs=[REMAIN, WHOLE, WHOLE],
-        scratch=[pltpu.SemaphoreType.DMA(())],
-    )
+        in_specs=[REMAIN, WHOLE],
+        scratch=[pltpu.VMEM((1, rows), jnp.int32), pltpu.SemaphoreType.DMA(())],
+    )
+    mask, near_cot = lax.optimization_barrier((mask, cotangent))
     far_cot = [from_ahead(near_cot, shift) for shift in range(1, span)]
     table = pltpu.VMEM((8, LANES), jnp.float32)
     smooth, leonard, rest = call(

time: 16.4 us -> 16.2 us (0.988)
  Pallas kernels: 2.8 us -> 2.57 us
    ppermute x3, starting transfers between devices: 3.33 us -> 3.09 us  [from_source(): return lax.ppermute(values, ('span', 'stream'), pairs)]
    ppermute x4, starting transfers between devices: 6.49 us -> 6.73 us  [from_ahead(): lax.ppermute(values, 'span', [((i + shift) % peers, i) for i in range(pee...]
    pallas_call x8, Pallas kernels: 2.8 us -> 2.57 us  [call(): pl.pallas_call(kernel, out_shape=outs, in_specs=in_specs or [WHOLE] * len...]
  transfers between devices with their start and end apart: 7 -> 7, of which waited for: 4 -> 6; matrix products, arithmetic and copies ran while one was open for 0% -> 0% of each run, Pallas kernels for 12% -> 11%
where the time goes in v18:
time: 16.2 us; the launch traced here: 16 us
  starting transfers between devices  9.82 us (61%)
  waiting for transfers between devices  2.91 us (18%)
  Pallas kernels  2.57 us (16%)
  between operations  0.69 us (4%)
    ppermute x4, starting transfers between devices, from_ahead(): lax.ppermute(values, 'span', [((i + shift) % peers, i) for i in range(pee...  6.73 us
    ppermute x3, starting transfers between devices, from_source(): return lax.ppermute(values, ('span', 'stream'), pairs)  3.09 us
    pallas_call x8, Pallas kernels, call(): pl.pallas_call(kernel, out_shape=outs, in_specs=in_specs or [WHOLE] * len...  2.57 us
    ppermute x3, waiting for transfers between devices, from_source(): return lax.ppermute(values, ('span', 'stream'), pairs)  1.92 us
    ppermute x4, waiting for transfers between devices, from_ahead(): lax.ppermute(values, 'span', [((i + shift) % peers, i) for i in range(pee...  0.99 us
  transfers between devices with their start and end apart: 7, of which 6 were waited for; matrix products, arithmetic and copies ran while one was open for 0% of the time, Pallas kernels for 11%

profile of v18, /device:TPU:0, one launch (start us, length us, event | category | flops | bytes accessed | tf_op | source)
XLA Modules:
  0.0 16.0 jit_solution(9989304737721163277)
XLA Ops:
  0.6 0.0 copy-start.2
  0.6 3.0 %collective-permute-start = (f32[3,4,8,256]{3,2,1,0:T(8,128)}, f32[3,4,8,256]{3,2,1,0:T(8,128)S(1)}, u32[]{:S(2)}, u32[]{:S(2)}) collective-permute-start(f32[3,4,8,256]{3,2,1,0:T(8,128)} %refs_0_.3), channel_id=1, source_target_pairs={{16,0},{0,16},{17,1},{1,17},{18,2},{2,18},{19,3},{3,19},{20,4},{4,... | collective-permute-start | bytes 294920 | tf_op jit(solution)/shard_map/ppermute | solution.py:352
  3.7 0.0 copy-done.2
  3.7 0.0 copy-start.1
  3.7 0.0 copy-start
  3.7 0.9 %collective-permute-start.1 = (f32[2,8,256]{2,1,0:T(8,128)S(1)}, f32[2,8,256]{2,1,0:T(8,128)S(1)}, u32[]{:S(2)}, u32[]{:S(2)}) collective-permute-start(f32[2,8,256]{2,1,0:T(8,128)S(1)} %get-tuple-element.15.size_ends_ref), channel_id=1, source_target_pairs={{16,0},{0,16},{17,1},{1,17},{18,2},{2,18},{19,3},{3,19},{20,4},{4,... | collective-permute-start | bytes 49160 | tf_op jit(solution)/shard_map/ppermute | solution.py:352
  4.6 0.7 %shard_map.62.mask_ref.refs_4_ = f32[8,128]{1,0:T(8,128)S(1)} custom-call(s32[1,8]{1,0:T(1,128)} %bitcast.1, f32[2,8,256]{2,1,0:T(8,128)S(1)} %get-tuple-element.15.size_ends_ref), custom_call_target="tpu_custom_call" | custom-call | flops 8192 | bytes 20512 | tf_op jit(solution)/shard_map/pallas_call | solution.py:339
  5.4 0.0 copy-done.1
  5.4 1.3 %collective-permute-start.3 = (f32[6,4,8,256]{3,2,1,0:T(8,128)S(1)}, f32[6,4,8,256]{3,2,1,0:T(8,128)S(1)}, u32[]{:S(2)}, u32[]{:S(2)}) collective-permute-start(f32[6,4,8,256]{3,2,1,0:T(8,128)S(1)} %copy-done.1), channel_id=1, source_target_pairs={{16,0},{0,16},{17,1},{1,17},{18,2},{2,18},{19,3},{3,19},{20,4},{4,... | collective-permute-start | bytes 589832 | tf_op jit(solution)/shard_map/ppermute | solution.py:352
  6.6 0.2 %collective-permute-done.refs_0_.refs_6_ = f32[3,4,8,256]{3,2,1,0:T(8,128)S(1)} collective-permute-done((f32[3,4,8,256]{3,2,1,0:T(8,128)}, f32[3,4,8,256]{3,2,1,0:T(8,128)S(1)}, u32[]{:S(2)}, u32[]{:S(2)}) %collective-permute-start) | collective-permute-done | bytes 98336 | tf_op jit(solution)/shard_map/ppermute | solution.py:352
  6.9 0.0 copy-done
  6.9 0.2 shard_map.59
  7.0 0.5 %collective-permute-done.1.refs_0_ = f32[2,8,256]{2,1,0:T(8,128)S(1)} collective-permute-done((f32[2,8,256]{2,1,0:T(8,128)S(1)}, f32[2,8,256]{2,1,0:T(8,128)S(1)}, u32[]{:S(2)}, u32[]{:S(2)}) %collective-permute-start.1) | collective-permute-done | bytes 16416 | tf_op jit(solution)/shard_map/ppermute | solution.py:352
  7.5 0.2 %shard_map.63 = (f32[6,4,8,256]{3,2,1,0:T(8,128)S(1)}, f32[8,128]{1,0:T(8,128)S(1)}) custom-call(f32[6,4,8,256]{3,2,1,0:T(8,128)S(1)} %copy-done.2, f32[6,4,8,256]{3,2,1,0:T(8,128)S(1)} %copy-done.1, f32[4,8,256]{2,1,0:T(8,128)S(1)} %get-tuple-element.17.size_ref, f32[6,4,8,256]{3,2,1,0:T(8,128)S(1)} %get-tuple-element.14.leonard_ref.refs_3_.refs_1_, ...), custom_call_target="tpu_custom_call" | custom-call | flops 2457600000 | bytes 1040384 | tf_op jit(solution)/shard_map/pallas_call | solution.py:339
  7.7 0.1 collective-permute-start.2
  7.8 1.2 %collective-permute-done.2.other_sums_ref = f32[8,128]{1,0:T(8,128)S(1)} collective-permute-done((f32[8,128]{1,0:T(8,128)S(1)}, f32[8,128]{1,0:T(8,128)S(1)}, u32[]{:S(2)}, u32[]{:S(2)}) %collective-permute-start.2) | collective-permute-done | bytes 4128 | tf_op jit(solution)/shard_map/ppermute | solution.py:362
  9.0 1.5 %collective-permute-start.6 = (f32[37,8,128]{2,1,0:T(8,128)S(1)}, f32[37,8,128]{2,1,0:T(8,128)S(1)}, u32[]{:S(2)}, u32[]{:S(2)}) collective-permute-start(f32[37,8,128]{2,1,0:T(8,128)S(1)} %get-tuple-element.25), channel_id=1, source_target_pairs={{16,0},{0,16},{17,1},{1,17},{18,2},{2,18},{19,3},{3,19},{20,4},{4,... | collective-permute-start | bytes 454664 | tf_op jit(solution)/shard_map/ppermute | solution.py:352
  10.5 1.5 %collective-permute-start.5 = (f32[8,128]{1,0:T(8,128)S(1)}, f32[8,128]{1,0:T(8,128)S(1)}, u32[]{:S(2)}, u32[]{:S(2)}) collective-permute-start(f32[8,128]{1,0:T(8,128)S(1)} %get-tuple-element.24.refs_7_), channel_id=1, source_target_pairs={{17,0},{19,1},{16,2},{21,3},{18,4},{23,5},{20,6},{25,7},{22,8},{27... | collective-permute-start | bytes 12296 | tf_op jit(solution)/shard_map/ppermute | solution.py:362
  12.0 1.5 %collective-permute-start.4 = (f32[8,128]{1,0:T(8,128)S(1)}, f32[8,128]{1,0:T(8,128)S(1)}, u32[]{:S(2)}, u32[]{:S(2)}) collective-permute-start(f32[8,128]{1,0:T(8,128)S(1)} %get-tuple-element.24.refs_7_), channel_id=1, source_target_pairs={{1,0},{3,1},{0,2},{5,3},{2,4},{7,5},{4,6},{9,7},{6,8},{11,9},{8,10... | collective-permute-start | bytes 12296 | tf_op jit(solution)/shard_map/ppermute | solution.py:362
  13.6 0.0 collective-permute-done.3.refs_7_
  13.6 0.6 %shard_map.65.refs_3_ = f32[12,4,8,256]{3,2,1,0:T(8,128)S(1)} custom-call(f32[3,4,8,256]{3,2,1,0:T(8,128)S(1)} %copy-done, f32[6,4,8,256]{3,2,1,0:T(8,128)S(1)} %copy-done.1, f32[3,4,8,256]{3,2,1,0:T(8,128)S(1)} %get-tuple-element.21.smooth_ref.refs_2_, f32[6,4,8,256]{3,2,1,0:T(8,128)S(1)} %get-tuple-element.14.leonard_ref.refs_3_.refs_1_, ...), custom_call_target="tpu_custom_call" | custom-call | flops 4096000 | bytes 1572864 | tf_op jit(solution)/shard_map/pallas_call | solution.py:339
  14.1 0.3 %collective-permute-done.5.refs_6_ = f32[8,128]{1,0:T(8,128)S(1)} collective-permute-done((f32[8,128]{1,0:T(8,128)S(1)}, f32[8,128]{1,0:T(8,128)S(1)}, u32[]{:S(2)}, u32[]{:S(2)}) %collective-permute-start.5) | collective-permute-done | bytes 4128 | tf_op jit(solution)/shard_map/ppermute | solution.py:362
  14.4 0.5 %collective-permute-done.4.refs_5_ = f32[8,128]{1,0:T(8,128)S(1)} collective-permute-done((f32[8,128]{1,0:T(8,128)S(1)}, f32[8,128]{1,0:T(8,128)S(1)}, u32[]{:S(2)}, u32[]{:S(2)}) %collective-permute-start.4) | collective-permute-done | bytes 4128 | tf_op jit(solution)/shard_map/ppermute | solution.py:362
  14.9 0.3 %collective-permute-done.6.refs_8_ = f32[37,8,128]{2,1,0:T(8,128)S(1)} collective-permute-done((f32[37,8,128]{2,1,0:T(8,128)S(1)}, f32[37,8,128]{2,1,0:T(8,128)S(1)}, u32[]{:S(2)}, u32[]{:S(2)}) %collective-permute-start.6) | collective-permute-done | bytes 151584 | tf_op jit(solution)/shard_map/ppermute | solution.py:352
  15.2 0.8 %shard_map.66 = (f32[6,4,8,256]{3,2,1,0:T(8,128)}, f32[3,4,8,256]{3,2,1,0:T(8,128)}) custom-call(f32[3,4,8,256]{3,2,1,0:T(8,128)S(1)} %copy-done, f32[6,4,8,256]{3,2,1,0:T(8,128)S(1)} %get-tuple-element.14.leonard_ref.refs_3_.refs_1_, f32[6,4,8,256]{3,2,1,0:T(8,128)S(1)} %get-tuple-element.20.model_ref.refs_4_.refs_2_, ...), custom_call_target="tpu_custom_call" | custom-call | flops 1638400 | bytes 1347584 | tf_op jit(solution)/shard_map/pallas_call | solution.py:339
  (3 shorter events, 0.1 us)
Async XLA Ops:
  0.6 3.0 %copy-start.2 = (f32[6,4,8,256]{3,2,1,0:T(8,128)S(1)}, f32[6,4,8,256]{3,2,1,0:T(8,128)}, u32[]{:S(2)}) copy-start(f32[6,4,8,256]{3,2,1,0:T(8,128)} %strain_ref.3) | copy-start | bytes 589828
  0.6 6.2 %collective-permute-start = (f32[3,4,8,256]{3,2,1,0:T(8,128)}, f32[3,4,8,256]{3,2,1,0:T(8,128)S(1)}, u32[]{:S(2)}, u32[]{:S(2)}) collective-permute-start(f32[3,4,8,256]{3,2,1,0:T(8,128)} %refs_0_.3), channel_id=1, source_target_pairs={{16,0},{0,16},{17,1},{1,17},{18,2},{2,18},{19,3},{3,19},{20,4},{4,... | collective-permute-start | bytes 294920 | tf_op jit(solution)/shard_map/ppermute | solution.py:352
  3.7 1.7 %copy-start.1 = (f32[6,4,8,256]{3,2,1,0:T(8,128)S(1)}, f32[6,4,8,256]{3,2,1,0:T(8,128)}, u32[]{:S(2)}) copy-start(f32[6,4,8,256]{3,2,1,0:T(8,128)} %refs_1_) | copy-start | bytes 589828
  3.7 3.2 %copy-start = (f32[3,4,8,256]{3,2,1,0:T(8,128)S(1)}, f32[3,4,8,256]{3,2,1,0:T(8,128)}, u32[]{:S(2)}) copy-start(f32[3,4,8,256]{3,2,1,0:T(8,128)} %refs_0_.3) | copy-start | bytes 294916
  3.7 3.8 %collective-permute-start.1 = (f32[2,8,256]{2,1,0:T(8,128)S(1)}, f32[2,8,256]{2,1,0:T(8,128)S(1)}, u32[]{:S(2)}, u32[]{:S(2)}) collective-permute-start(f32[2,8,256]{2,1,0:T(8,128)S(1)} %get-tuple-element.15.size_ends_ref), channel_id=1, source_target_pairs={{16,0},{0,16},{17,1},{1,17},{18,2},{2,18},{19,3},{3,19},{20,4},{4,... | collective-permute-start | bytes 49160 | tf_op jit(solution)/shard_map/ppermute | solution.py:352
  5.4 8.2 %collective-permute-start.3 = (f32[6,4,8,256]{3,2,1,0:T(8,128)S(1)}, f32[6,4,8,256]{3,2,1,0:T(8,128)S(1)}, u32[]{:S(2)}, u32[]{:S(2)}) collective-permute-start(f32[6,4,8,256]{3,2,1,0:T(8,128)S(1)} %copy-done.1), channel_id=1, source_target_pairs={{16,0},{0,16},{17,1},{1,17},{18,2},{2,18},{19,3},{3,19},{20,4},{4,... | collective-permute-start | bytes 589832 | tf_op jit(solution)/shard_map/ppermute | solution.py:352
  7.7 1.2 %collective-permute-start.2 = (f32[8,128]{1,0:T(8,128)S(1)}, f32[8,128]{1,0:T(8,128)S(1)}, u32[]{:S(2)}, u32[]{:S(2)}) collective-permute-start(f32[8,128]{1,0:T(8,128)S(1)} %get-tuple-element.22.sums_ref), channel_id=1, source_target_pairs={{1,0},{0,1},{3,2},{2,3},{5,4},{4,5},{7,6},{6,7},{9,8},{8,9},{11,10... | collective-permute-start | bytes 12296 | tf_op jit(solution)/shard_map/ppermute | solution.py:362
  9.0 6.2 %collective-permute-start.6 = (f32[37,8,128]{2,1,0:T(8,128)S(1)}, f32[37,8,128]{2,1,0:T(8,128)S(1)}, u32[]{:S(2)}, u32[]{:S(2)}) collective-permute-start(f32[37,8,128]{2,1,0:T(8,128)S(1)} %get-tuple-element.25), channel_id=1, source_target_pairs={{16,0},{0,16},{17,1},{1,17},{18,2},{2,18},{19,3},{3,19},{20,4},{4,... | collective-permute-start | bytes 454664 | tf_op jit(solution)/shard_map/ppermute | solution.py:352
  10.5 3.9 %collective-permute-start.5 = (f32[8,128]{1,0:T(8,128)S(1)}, f32[8,128]{1,0:T(8,128)S(1)}, u32[]{:S(2)}, u32[]{:S(2)}) collective-permute-start(f32[8,128]{1,0:T(8,128)S(1)} %get-tuple-element.24.refs_7_), channel_id=1, source_target_pairs={{17,0},{19,1},{16,2},{21,3},{18,4},{23,5},{20,6},{25,7},{22,8},{27... | collective-permute-start | bytes 12296 | tf_op jit(solution)/shard_map/ppermute | solution.py:362
  12.0 2.9 %collective-permute-start.4 = (f32[8,128]{1,0:T(8,128)S(1)}, f32[8,128]{1,0:T(8,128)S(1)}, u32[]{:S(2)}, u32[]{:S(2)}) collective-permute-start(f32[8,128]{1,0:T(8,128)S(1)} %get-tuple-element.24.refs_7_), channel_id=1, source_target_pairs={{1,0},{3,1},{0,2},{5,3},{2,4},{7,5},{4,6},{9,7},{6,8},{11,9},{8,10... | collective-permute-start | bytes 12296 | tf_op jit(solution)/shard_map/ppermute | solution.py:362

commit v19 on v18

--- a/solution.py
+++ b/solution.py
@@ -292,17 +292,6 @@
 
     coefficient = of_rows(total[0:1] * inverse)
     pull = of_rows(-(total[2:3] * inverse))
-    copies = []
-    for k in range(6):
-        for lanes in halves(v_ref.shape[-1]):
-            for z in range(cells):
-                residual_ref[k, z, :, lanes] = (
-                    leonard_ref[k, z, :, lanes] - coefficient * model_ref[k, z, :, lanes]
-                )
-        if k % 3 == 2:
-            some = pl.ds(k - 2, 3)
-            copies.append(pltpu.make_async_copy(residual_ref.at[some], residual_hbm.at[some], left.at[k // 3]))
-            copies[-1].start()
     for half, lanes in enumerate(halves(v_ref.shape[-1])):
         v = [[v_ref[a, z, :, lanes] for z in range(cells)] for a in range(3)]
         from_model = [[] for _ in range(6)]
@@ -324,8 +313,18 @@
                 grad_ref[a, z, :, lanes] = (
                     parts_ref[a, z, :, lanes] + coefficient * parts_ref[3 + a, z, :, lanes] + pull * pulled
                 )
-    copies.append(pltpu.make_async_copy(grad_ref, grad_hbm, left.at[2]))
-    copies[-1].start()
+    copies = [pltpu.make_async_copy(grad_ref, grad_hbm, left.at[0])]
+    copies[0].start()
+    for k in range(6):
+        for lanes in halves(v_ref.shape[-1]):
+            for z in range(cells):
+                residual_ref[k, z, :, lanes] = (
+                    leonard_ref[k, z, :, lanes] - coefficient * model_ref[k, z, :, lanes]
+                )
+        if k % 3 == 2:
+            some = pl.ds(k - 2, 3)
+            copies.append(pltpu.make_async_copy(residual_ref.at[some], residual_hbm.at[some], left.at[1 + k // 3]))
+            copies[-1].start()
     for copy in copies:
         copy.wait()
 

time: 16.2 us -> 16.2 us (level)
  no operation moved by 1% of the time
where the time goes in v19:
time: 16.2 us; the launch traced here: 16 us
  starting transfers between devices  9.82 us (61%)
  waiting for transfers between devices  2.91 us (18%)
  Pallas kernels  2.61 us (16%)
  between operations  0.69 us (4%)
    ppermute x4, starting transfers between devices, from_ahead(): lax.ppermute(values, 'span', [((i + shift) % peers, i) for i in range(pee...  6.73 us
    ppermute x3, starting transfers between devices, from_source(): return lax.ppermute(values, ('span', 'stream'), pairs)  3.09 us
    pallas_call x8, Pallas kernels, call(): pl.pallas_call(kernel, out_shape=outs, in_specs=in_specs or [WHOLE] * len...  2.61 us
    ppermute x3, waiting for transfers between devices, from_source(): return lax.ppermute(values, ('span', 'stream'), pairs)  1.92 us
    ppermute x4, waiting for transfers between devices, from_ahead(): lax.ppermute(values, 'span', [((i + shift) % peers, i) for i in range(pee...  0.99 us
  transfers between devices with their start and end apart: 7, of which 6 were waited for; matrix products, arithmetic and copies ran while one was open for 0% of the time, Pallas kernels for 11%

profile of v19, /device:TPU:0, one launch (start us, length us, event | category | flops | bytes accessed | tf_op | source)
XLA Modules:
  0.0 16.0 jit_solution(7333836900475676842)
XLA Ops:
  0.6 0.0 copy-start.2
  0.6 3.0 %collective-permute-start = (f32[3,4,8,256]{3,2,1,0:T(8,128)}, f32[3,4,8,256]{3,2,1,0:T(8,128)S(1)}, u32[]{:S(2)}, u32[]{:S(2)}) collective-permute-start(f32[3,4,8,256]{3,2,1,0:T(8,128)} %refs_0_.3), channel_id=1, source_target_pairs={{16,0},{0,16},{17,1},{1,17},{18,2},{2,18},{19,3},{3,19},{20,4},{4,... | collective-permute-start | bytes 294920 | tf_op jit(solution)/shard_map/ppermute | solution.py:351
  3.7 0.0 copy-done.2
  3.7 0.0 copy-start.1
  3.7 0.0 copy-start
  3.7 0.9 %collective-permute-start.1 = (f32[2,8,256]{2,1,0:T(8,128)S(1)}, f32[2,8,256]{2,1,0:T(8,128)S(1)}, u32[]{:S(2)}, u32[]{:S(2)}) collective-permute-start(f32[2,8,256]{2,1,0:T(8,128)S(1)} %get-tuple-element.15.size_ends_ref), channel_id=1, source_target_pairs={{16,0},{0,16},{17,1},{1,17},{18,2},{2,18},{19,3},{3,19},{20,4},{4,... | collective-permute-start | bytes 49160 | tf_op jit(solution)/shard_map/ppermute | solution.py:351
  4.6 0.7 %shard_map.62.mask_ref.refs_4_ = f32[8,128]{1,0:T(8,128)S(1)} custom-call(s32[1,8]{1,0:T(1,128)} %bitcast.1, f32[2,8,256]{2,1,0:T(8,128)S(1)} %get-tuple-element.15.size_ends_ref), custom_call_target="tpu_custom_call" | custom-call | flops 8192 | bytes 20512 | tf_op jit(solution)/shard_map/pallas_call | solution.py:338
  5.4 0.0 copy-done.1
  5.4 1.3 %collective-permute-start.3 = (f32[6,4,8,256]{3,2,1,0:T(8,128)S(1)}, f32[6,4,8,256]{3,2,1,0:T(8,128)S(1)}, u32[]{:S(2)}, u32[]{:S(2)}) collective-permute-start(f32[6,4,8,256]{3,2,1,0:T(8,128)S(1)} %copy-done.1), channel_id=1, source_target_pairs={{16,0},{0,16},{17,1},{1,17},{18,2},{2,18},{19,3},{3,19},{20,4},{4,... | collective-permute-start | bytes 589832 | tf_op jit(solution)/shard_map/ppermute | solution.py:351
  6.6 0.2 %collective-permute-done.refs_0_.refs_6_ = f32[3,4,8,256]{3,2,1,0:T(8,128)S(1)} collective-permute-done((f32[3,4,8,256]{3,2,1,0:T(8,128)}, f32[3,4,8,256]{3,2,1,0:T(8,128)S(1)}, u32[]{:S(2)}, u32[]{:S(2)}) %collective-permute-start) | collective-permute-done | bytes 98336 | tf_op jit(solution)/shard_map/ppermute | solution.py:351
  6.9 0.0 copy-done
  6.9 0.2 shard_map.59
  7.0 0.5 %collective-permute-done.1.refs_0_ = f32[2,8,256]{2,1,0:T(8,128)S(1)} collective-permute-done((f32[2,8,256]{2,1,0:T(8,128)S(1)}, f32[2,8,256]{2,1,0:T(8,128)S(1)}, u32[]{:S(2)}, u32[]{:S(2)}) %collective-permute-start.1) | collective-permute-done | bytes 16416 | tf_op jit(solution)/shard_map/ppermute | solution.py:351
  7.5 0.2 %shard_map.63 = (f32[6,4,8,256]{3,2,1,0:T(8,128)S(1)}, f32[8,128]{1,0:T(8,128)S(1)}) custom-call(f32[6,4,8,256]{3,2,1,0:T(8,128)S(1)} %copy-done.2, f32[6,4,8,256]{3,2,1,0:T(8,128)S(1)} %copy-done.1, f32[4,8,256]{2,1,0:T(8,128)S(1)} %get-tuple-element.17.size_ref, f32[6,4,8,256]{3,2,1,0:T(8,128)S(1)} %get-tuple-element.14.leonard_ref.refs_3_.refs_1_, ...), custom_call_target="tpu_custom_call" | custom-call | flops 2457600000 | bytes 1040384 | tf_op jit(solution)/shard_map/pallas_call | solution.py:338
  7.7 0.1 collective-permute-start.2
  7.8 1.2 %collective-permute-done.2.other_sums_ref = f32[8,128]{1,0:T(8,128)S(1)} collective-permute-done((f32[8,128]{1,0:T(8,128)S(1)}, f32[8,128]{1,0:T(8,128)S(1)}, u32[]{:S(2)}, u32[]{:S(2)}) %collective-permute-start.2) | collective-permute-done | bytes 4128 | tf_op jit(solution)/shard_map/ppermute | solution.py:361
  9.0 1.5 %collective-permute-start.6 = (f32[37,8,128]{2,1,0:T(8,128)S(1)}, f32[37,8,128]{2,1,0:T(8,128)S(1)}, u32[]{:S(2)}, u32[]{:S(2)}) collective-permute-start(f32[37,8,128]{2,1,0:T(8,128)S(1)} %get-tuple-element.25), channel_id=1, source_target_pairs={{16,0},{0,16},{17,1},{1,17},{18,2},{2,18},{19,3},{3,19},{20,4},{4,... | collective-permute-start | bytes 454664 | tf_op jit(solution)/shard_map/ppermute | solution.py:351
  10.5 1.5 %collective-permute-start.5 = (f32[8,128]{1,0:T(8,128)S(1)}, f32[8,128]{1,0:T(8,128)S(1)}, u32[]{:S(2)}, u32[]{:S(2)}) collective-permute-start(f32[8,128]{1,0:T(8,128)S(1)} %get-tuple-element.24.refs_7_), channel_id=1, source_target_pairs={{17,0},{19,1},{16,2},{21,3},{18,4},{23,5},{20,6},{25,7},{22,8},{27... | collective-permute-start | bytes 12296 | tf_op jit(solution)/shard_map/ppermute | solution.py:361
  12.0 1.5 %collective-permute-start.4 = (f32[8,128]{1,0:T(8,128)S(1)}, f32[8,128]{1,0:T(8,128)S(1)}, u32[]{:S(2)}, u32[]{:S(2)}) collective-permute-start(f32[8,128]{1,0:T(8,128)S(1)} %get-tuple-element.24.refs_7_), channel_id=1, source_target_pairs={{1,0},{3,1},{0,2},{5,3},{2,4},{7,5},{4,6},{9,7},{6,8},{11,9},{8,10... | collective-permute-start | bytes 12296 | tf_op jit(solution)/shard_map/ppermute | solution.py:361
  13.6 0.0 collective-permute-done.3.refs_7_
  13.6 0.6 %shard_map.65.refs_3_ = f32[12,4,8,256]{3,2,1,0:T(8,128)S(1)} custom-call(f32[3,4,8,256]{3,2,1,0:T(8,128)S(1)} %copy-done, f32[6,4,8,256]{3,2,1,0:T(8,128)S(1)} %copy-done.1, f32[3,4,8,256]{3,2,1,0:T(8,128)S(1)} %get-tuple-element.21.smooth_ref.refs_2_, f32[6,4,8,256]{3,2,1,0:T(8,128)S(1)} %get-tuple-element.14.leonard_ref.refs_3_.refs_1_, ...), custom_call_target="tpu_custom_call" | custom-call | flops 4096000 | bytes 1572864 | tf_op jit(solution)/shard_map/pallas_call | solution.py:338
  14.1 0.3 %collective-permute-done.5.refs_6_ = f32[8,128]{1,0:T(8,128)S(1)} collective-permute-done((f32[8,128]{1,0:T(8,128)S(1)}, f32[8,128]{1,0:T(8,128)S(1)}, u32[]{:S(2)}, u32[]{:S(2)}) %collective-permute-start.5) | collective-permute-done | bytes 4128 | tf_op jit(solution)/shard_map/ppermute | solution.py:361
  14.4 0.5 %collective-permute-done.4.refs_5_ = f32[8,128]{1,0:T(8,128)S(1)} collective-permute-done((f32[8,128]{1,0:T(8,128)S(1)}, f32[8,128]{1,0:T(8,128)S(1)}, u32[]{:S(2)}, u32[]{:S(2)}) %collective-permute-start.4) | collective-permute-done | bytes 4128 | tf_op jit(solution)/shard_map/ppermute | solution.py:361
  14.9 0.3 %collective-permute-done.6.refs_8_ = f32[37,8,128]{2,1,0:T(8,128)S(1)} collective-permute-done((f32[37,8,128]{2,1,0:T(8,128)S(1)}, f32[37,8,128]{2,1,0:T(8,128)S(1)}, u32[]{:S(2)}, u32[]{:S(2)}) %collective-permute-start.6) | collective-permute-done | bytes 151584 | tf_op jit(solution)/shard_map/ppermute | solution.py:351
  15.2 0.9 %shard_map.66 = (f32[6,4,8,256]{3,2,1,0:T(8,128)}, f32[3,4,8,256]{3,2,1,0:T(8,128)}) custom-call(f32[3,4,8,256]{3,2,1,0:T(8,128)S(1)} %copy-done, f32[6,4,8,256]{3,2,1,0:T(8,128)S(1)} %get-tuple-element.14.leonard_ref.refs_3_.refs_1_, f32[6,4,8,256]{3,2,1,0:T(8,128)S(1)} %get-tuple-element.20.model_ref.refs_4_.refs_2_, ...), custom_call_target="tpu_custom_call" | custom-call | flops 1638400 | bytes 1347584 | tf_op jit(solution)/shard_map/pallas_call | solution.py:338
  (3 shorter events, 0.1 us)
Async XLA Ops:
  0.6 3.0 %copy-start.2 = (f32[6,4,8,256]{3,2,1,0:T(8,128)S(1)}, f32[6,4,8,256]{3,2,1,0:T(8,128)}, u32[]{:S(2)}) copy-start(f32[6,4,8,256]{3,2,1,0:T(8,128)} %strain_ref.3) | copy-start | bytes 589828
  0.6 6.2 %collective-permute-start = (f32[3,4,8,256]{3,2,1,0:T(8,128)}, f32[3,4,8,256]{3,2,1,0:T(8,128)S(1)}, u32[]{:S(2)}, u32[]{:S(2)}) collective-permute-start(f32[3,4,8,256]{3,2,1,0:T(8,128)} %refs_0_.3), channel_id=1, source_target_pairs={{16,0},{0,16},{17,1},{1,17},{18,2},{2,18},{19,3},{3,19},{20,4},{4,... | collective-permute-start | bytes 294920 | tf_op jit(solution)/shard_map/ppermute | solution.py:351
  3.7 1.7 %copy-start.1 = (f32[6,4,8,256]{3,2,1,0:T(8,128)S(1)}, f32[6,4,8,256]{3,2,1,0:T(8,128)}, u32[]{:S(2)}) copy-start(f32[6,4,8,256]{3,2,1,0:T(8,128)} %refs_1_) | copy-start | bytes 589828
  3.7 3.2 %copy-start = (f32[3,4,8,256]{3,2,1,0:T(8,128)S(1)}, f32[3,4,8,256]{3,2,1,0:T(8,128)}, u32[]{:S(2)}) copy-start(f32[3,4,8,256]{3,2,1,0:T(8,128)} %refs_0_.3) | copy-start | bytes 294916
  3.7 3.8 %collective-permute-start.1 = (f32[2,8,256]{2,1,0:T(8,128)S(1)}, f32[2,8,256]{2,1,0:T(8,128)S(1)}, u32[]{:S(2)}, u32[]{:S(2)}) collective-permute-start(f32[2,8,256]{2,1,0:T(8,128)S(1)} %get-tuple-element.15.size_ends_ref), channel_id=1, source_target_pairs={{16,0},{0,16},{17,1},{1,17},{18,2},{2,18},{19,3},{3,19},{20,4},{4,... | collective-permute-start | bytes 49160 | tf_op jit(solution)/shard_map/ppermute | solution.py:351
  5.4 8.2 %collective-permute-start.3 = (f32[6,4,8,256]{3,2,1,0:T(8,128)S(1)}, f32[6,4,8,256]{3,2,1,0:T(8,128)S(1)}, u32[]{:S(2)}, u32[]{:S(2)}) collective-permute-start(f32[6,4,8,256]{3,2,1,0:T(8,128)S(1)} %copy-done.1), channel_id=1, source_target_pairs={{16,0},{0,16},{17,1},{1,17},{18,2},{2,18},{19,3},{3,19},{20,4},{4,... | collective-permute-start | bytes 589832 | tf_op jit(solution)/shard_map/ppermute | solution.py:351
  7.7 1.2 %collective-permute-start.2 = (f32[8,128]{1,0:T(8,128)S(1)}, f32[8,128]{1,0:T(8,128)S(1)}, u32[]{:S(2)}, u32[]{:S(2)}) collective-permute-start(f32[8,128]{1,0:T(8,128)S(1)} %get-tuple-element.22.sums_ref), channel_id=1, source_target_pairs={{1,0},{0,1},{3,2},{2,3},{5,4},{4,5},{7,6},{6,7},{9,8},{8,9},{11,10... | collective-permute-start | bytes 12296 | tf_op jit(solution)/shard_map/ppermute | solution.py:361
  9.0 6.2 %collective-permute-start.6 = (f32[37,8,128]{2,1,0:T(8,128)S(1)}, f32[37,8,128]{2,1,0:T(8,128)S(1)}, u32[]{:S(2)}, u32[]{:S(2)}) collective-permute-start(f32[37,8,128]{2,1,0:T(8,128)S(1)} %get-tuple-element.25), channel_id=1, source_target_pairs={{16,0},{0,16},{17,1},{1,17},{18,2},{2,18},{19,3},{3,19},{20,4},{4,... | collective-permute-start | bytes 454664 | tf_op jit(solution)/shard_map/ppermute | solution.py:351
  10.5 3.9 %collective-permute-start.5 = (f32[8,128]{1,0:T(8,128)S(1)}, f32[8,128]{1,0:T(8,128)S(1)}, u32[]{:S(2)}, u32[]{:S(2)}) collective-permute-start(f32[8,128]{1,0:T(8,128)S(1)} %get-tuple-element.24.refs_7_), channel_id=1, source_target_pairs={{17,0},{19,1},{16,2},{21,3},{18,4},{23,5},{20,6},{25,7},{22,8},{27... | collective-permute-start | bytes 12296 | tf_op jit(solution)/shard_map/ppermute | solution.py:361
  12.0 2.9 %collective-permute-start.4 = (f32[8,128]{1,0:T(8,128)S(1)}, f32[8,128]{1,0:T(8,128)S(1)}, u32[]{:S(2)}, u32[]{:S(2)}) collective-permute-start(f32[8,128]{1,0:T(8,128)S(1)} %get-tuple-element.24.refs_7_), channel_id=1, source_target_pairs={{1,0},{3,1},{0,2},{5,3},{2,4},{7,5},{4,6},{9,7},{6,8},{11,9},{8,10... | collective-permute-start | bytes 12296 | tf_op jit(solution)/shard_map/ppermute | solution.py:361

commit v20 on v18

--- a/solution.py
+++ b/solution.py
@@ -142,9 +142,9 @@
     return [plain[z] + tensor[PAIR_OF[a][a]][z] * vector[a][z] for z in range(cells)]
 
 
-def velocity_kernel(tables, v_ref, *refs):
-    far_v_refs = refs[:-3]
-    smooth_ref, leonard_ref, rest_ref = refs[-3:]
+def velocity_kernel(tables, v_ref, strain_ref, cot_ref, *refs):
+    far_v_refs = refs[:-4]
+    smooth_ref, leonard_ref, rest_ref, powers_ref = refs[-4:]
     cells = tables.cells
     for lanes in halves(v_ref.shape[-1]):
         v = [[v_ref[a, z, :, lanes] for z in range(cells)] for a in range(3)]
@@ -157,33 +157,48 @@
         for a in range(3):
             for z in range(cells):
                 smooth_ref[a, z, :, lanes] = filtered[a][z]
-        for k, (a, b) in enumerate(INDEX_PAIRS):
-            for z in range(cells):
+        for z in range(cells):
+            powers = [[] for _ in range(7)]
+            for k, (a, b) in enumerate(INDEX_PAIRS):
                 coarse = filtered[a][z] * filtered[b][z]
-                leonard_ref[k, z, :, lanes] = filtered[3 + k][z] - coarse
-                rest_ref[k, z, :, lanes] = products[k][z] - coarse
-
-
-def model_kernel(tables, strain_ref, cot_ref, size_ref, leonard_ref, rest_ref, mask_ref, *refs):
+                leonard = filtered[3 + k][z] - coarse
+                rest = products[k][z] - coarse
+                leonard_ref[k, z, :, lanes] = leonard
+                rest_ref[k, z, :, lanes] = rest
+                strain, cot = strain_ref[k, z, :, lanes], cot_ref[k, z, :, lanes]
+                scaled_rest, scaled_strain = PAIR_WEIGHTS[k] * rest, PAIR_WEIGHTS[k] * strain
+                terms = (
+                    scaled_rest * leonard,
+                    scaled_strain * leonard,
+                    scaled_rest * rest,
+                    scaled_strain * rest,
+                    scaled_strain * strain,
+                    cot * rest,
+                    cot * strain,
+                )
+                for power, term in zip(powers, terms):
+                    power.append(term)
+            for index, power in enumerate(powers):
+                powers_ref[index, z, :, lanes] = sum_up(power)
+
+
+def sums_kernel(tables, size_ref, powers_ref, mask_ref, *refs):
     far_size_refs = refs[:-2]
-    model_ref, sums_ref = refs[-2:]
+    factor_ref, sums_ref = refs[-2:]
     cells = tables.cells
     cross, square, blame = [], [], []
-    for lanes in halves(strain_ref.shape[-1]):
+    for lanes in halves(size_ref.shape[-1]):
         size = [size_ref[z, :, lanes] for z in range(cells)]
         ends = [None] + [[[far[end, :, lanes] for end in range(2)]] for far in far_size_refs]
         smooth_size = filtered_block(tables, 0, [size], ends)[0]
-        factor = [2.0 * (4.0 * smooth_size[z] - size[z]) for z in range(cells)]
-        for k in range(6):
-            for z in range(cells):
-                leonard = leonard_ref[k, z, :, lanes]
-                term = rest_ref[k, z, :, lanes] + factor[z] * strain_ref[k, z, :, lanes]
-                model_ref[k, z, :, lanes] = term
-                scaled = PAIR_WEIGHTS[k] * term
-                cross.append(scaled * leonard)
-                square.append(scaled * term)
-                blame.append(term * cot_ref[k, z, :, lanes])
-            cross, square, blame = [sum_up(cross)], [sum_up(square)], [sum_up(blame)]
+        for z in range(cells):
+            factor = 2.0 * (4.0 * smooth_size[z] - size[z])
+            factor_ref[z, :, lanes] = factor
+            power = [powers_ref[index, z, :, lanes] for index in range(7)]
+            cross.append(power[0] + factor * power[1])
+            square.append(power[2] + factor * (2.0 * power[3] + factor * power[4]))
+            blame.append(power[5] + factor * power[6])
+    cross, square, blame = [sum_up(cross)], [sum_up(square)], [sum_up(blame)]
     mine = mask_ref[...] > 0.5
     place = lax.broadcasted_iota(jnp.int32, (8, LANES), 0)
     table = jnp.zeros((8, LANES), jnp.float32)
@@ -192,6 +207,14 @@
         per_bin = jnp.sum(jnp.where(mine, per_row, 0.0), axis=0, keepdims=True)
         table = jnp.where(place == index, per_bin, table)
     sums_ref[...] = table
+
+
+def model_kernel(tables, strain_ref, rest_ref, factor_ref, model_ref):
+    for lanes in halves(strain_ref.shape[-1]):
+        for z in range(tables.cells):
+            factor = factor_ref[z, :, lanes]
+            for k in range(6):
+                model_ref[k, z, :, lanes] = rest_ref[k, z, :, lanes] + factor * strain_ref[k, z, :, lanes]
 
 
 def message_kernel(tables, smooth_ref, model_ref, sums_ref, other_sums_ref, dual_ref, message_ref, pair_ref):
@@ -399,24 +422,20 @@
     mask, near_cot = lax.optimization_barrier((mask, cotangent))
     far_cot = [from_ahead(near_cot, shift) for shift in range(1, span)]
     table = pltpu.VMEM((8, LANES), jnp.float32)
-    smooth, leonard, rest = call(
+    smooth, leonard, rest, powers = call(
         functools.partial(velocity_kernel, tables),
-        [shaped(3, cells), shaped(6, cells), shaped(6, cells)],
+        [shaped(3, cells), shaped(6, cells), shaped(6, cells), shaped(7, cells)],
         LONG * work,
         velocity,
-        *far_v,
-    )
-    model, sums = call(
-        functools.partial(model_kernel, tables),
-        [shaped(6, cells), table],
-        LONG * work,
         strain,
         near_cot,
-        size,
-        leonard,
-        rest,
-        mask,
-        *far_size,
+        *far_v,
+    )
+    factor, sums = call(
+        functools.partial(sums_kernel, tables), [shaped(cells), table], LONG * work, size, powers, mask, *far_size
+    )
+    (model,) = call(
+        functools.partial(model_kernel, tables), [shaped(6, cells)], LONG * work, strain, rest, factor
     )
     other_sums = from_source(sums, 0, lambda j: j ^ 1)
     dual, message, pair_sums = call(

time: 16.2 us -> 16.1 us (level)
    pallas_call x8 -> x9, Pallas kernels: 2.57 us -> 2.63 us  [call(): pl.pallas_call(kernel, out_shape=outs, in_specs=in_specs or [WHOLE] * len...]
where the time goes in v20:
time: 16.1 us; the launch traced here: 16 us
  starting transfers between devices  9.82 us (61%)
  waiting for transfers between devices  2.83 us (18%)
  Pallas kernels  2.63 us (16%)
  between operations  0.7 us (4%)
    ppermute x4, starting transfers between devices, from_ahead(): lax.ppermute(values, 'span', [((i + shift) % peers, i) for i in range(pee...  6.73 us
    ppermute x3, starting transfers between devices, from_source(): return lax.ppermute(values, ('span', 'stream'), pairs)  3.1 us
    pallas_call x9, Pallas kernels, call(): pl.pallas_call(kernel, out_shape=outs, in_specs=in_specs or [WHOLE] * len...  2.63 us
    ppermute x3, waiting for transfers between devices, from_source(): return lax.ppermute(values, ('span', 'stream'), pairs)  1.87 us
    ppermute x4, waiting for transfers between devices, from_ahead(): lax.ppermute(values, 'span', [((i + shift) % peers, i) for i in range(pee...  0.96 us
  transfers between devices with their start and end apart: 7, of which 6 were waited for; matrix products, arithmetic and copies ran while one was open for 0% of the time, Pallas kernels for 11%

profile of v20, /device:TPU:0, one launch (start us, length us, event | category | flops | bytes accessed | tf_op | source)
XLA Modules:
  0.0 16.0 jit_solution(15999229847269519915)
XLA Ops:
  0.6 0.0 copy-start.2
  0.6 3.0 %collective-permute-start = (f32[3,4,8,256]{3,2,1,0:T(8,128)}, f32[3,4,8,256]{3,2,1,0:T(8,128)S(1)}, u32[]{:S(2)}, u32[]{:S(2)}) collective-permute-start(f32[3,4,8,256]{3,2,1,0:T(8,128)} %refs_0_.3), channel_id=1, source_target_pairs={{16,0},{0,16},{17,1},{1,17},{18,2},{2,18},{19,3},{3,19},{20,4},{4,... | collective-permute-start | bytes 294920 | tf_op jit(solution)/shard_map/ppermute | solution.py:375
  3.7 0.0 copy-done.2
  3.7 0.0 copy-start.1
  3.7 0.0 copy-start
  3.7 0.9 %collective-permute-start.1 = (f32[2,8,256]{2,1,0:T(8,128)S(1)}, f32[2,8,256]{2,1,0:T(8,128)S(1)}, u32[]{:S(2)}, u32[]{:S(2)}) collective-permute-start(f32[2,8,256]{2,1,0:T(8,128)S(1)} %get-tuple-element.15.size_ends_ref), channel_id=1, source_target_pairs={{16,0},{0,16},{17,1},{1,17},{18,2},{2,18},{19,3},{3,19},{20,4},{4,... | collective-permute-start | bytes 49160 | tf_op jit(solution)/shard_map/ppermute | solution.py:375
  4.6 0.7 %shard_map.61.mask_ref.refs_4_ = f32[8,128]{1,0:T(8,128)S(1)} custom-call(s32[1,8]{1,0:T(1,128)} %bitcast.1, f32[2,8,256]{2,1,0:T(8,128)S(1)} %get-tuple-element.15.size_ends_ref), custom_call_target="tpu_custom_call" | custom-call | flops 8192 | bytes 20512 | tf_op jit(solution)/shard_map/pallas_call | solution.py:362
  5.4 0.0 copy-done.1
  5.4 1.3 %collective-permute-start.3 = (f32[6,4,8,256]{3,2,1,0:T(8,128)S(1)}, f32[6,4,8,256]{3,2,1,0:T(8,128)S(1)}, u32[]{:S(2)}, u32[]{:S(2)}) collective-permute-start(f32[6,4,8,256]{3,2,1,0:T(8,128)S(1)} %copy-done.1), channel_id=1, source_target_pairs={{16,0},{0,16},{17,1},{1,17},{18,2},{2,18},{19,3},{3,19},{20,4},{4,... | collective-permute-start | bytes 589832 | tf_op jit(solution)/shard_map/ppermute | solution.py:375
  6.6 0.2 %collective-permute-done.refs_0_.refs_6_ = f32[3,4,8,256]{3,2,1,0:T(8,128)S(1)} collective-permute-done((f32[3,4,8,256]{3,2,1,0:T(8,128)}, f32[3,4,8,256]{3,2,1,0:T(8,128)S(1)}, u32[]{:S(2)}, u32[]{:S(2)}) %collective-permute-start) | collective-permute-done | bytes 98336 | tf_op jit(solution)/shard_map/ppermute | solution.py:375
  6.9 0.0 copy-done
  6.9 0.3 %shard_map.62 = (f32[3,4,8,256]{3,2,1,0:T(8,128)S(1)}, f32[6,4,8,256]{3,2,1,0:T(8,128)S(1)}, f32[6,4,8,256]{3,2,1,0:T(8,128)S(1)}, f32[7,4,8,256]{3,2,1,0:T(8,128)S(1)}) custom-call(f32[3,4,8,256]{3,2,1,0:T(8,128)S(1)} %copy-done, f32[6,4,8,256]{3,2,1,0:T(8,128)S(1)} %copy-done.2, f32[6,4,8,256]{3,2,1,0:T(8,128)S(1)} %copy-done.1, ...), custom_call_target="tpu_custom_call" | custom-call | flops 2457600000 | bytes 1310720 | tf_op jit(solution)/shard_map/pallas_call | solution.py:362
  7.1 0.4 %collective-permute-done.1.refs_0_ = f32[2,8,256]{2,1,0:T(8,128)S(1)} collective-permute-done((f32[2,8,256]{2,1,0:T(8,128)S(1)}, f32[2,8,256]{2,1,0:T(8,128)S(1)}, u32[]{:S(2)}, u32[]{:S(2)}) %collective-permute-start.1) | collective-permute-done | bytes 16416 | tf_op jit(solution)/shard_map/ppermute | solution.py:375
  7.5 0.1 shard_map.63
  7.7 0.1 collective-permute-start.2
  7.8 1.1 %collective-permute-done.2.other_sums_ref = f32[8,128]{1,0:T(8,128)S(1)} collective-permute-done((f32[8,128]{1,0:T(8,128)S(1)}, f32[8,128]{1,0:T(8,128)S(1)}, u32[]{:S(2)}, u32[]{:S(2)}) %collective-permute-start.2) | collective-permute-done | bytes 4128 | tf_op jit(solution)/shard_map/ppermute | solution.py:385
  8.9 1.5 %collective-permute-start.6 = (f32[37,8,128]{2,1,0:T(8,128)S(1)}, f32[37,8,128]{2,1,0:T(8,128)S(1)}, u32[]{:S(2)}, u32[]{:S(2)}) collective-permute-start(f32[37,8,128]{2,1,0:T(8,128)S(1)} %get-tuple-element.27), channel_id=1, source_target_pairs={{16,0},{0,16},{17,1},{1,17},{18,2},{2,18},{19,3},{3,19},{20,4},{4,... | collective-permute-start | bytes 454664 | tf_op jit(solution)/shard_map/ppermute | solution.py:375
  10.5 1.5 %collective-permute-start.5 = (f32[8,128]{1,0:T(8,128)S(1)}, f32[8,128]{1,0:T(8,128)S(1)}, u32[]{:S(2)}, u32[]{:S(2)}) collective-permute-start(f32[8,128]{1,0:T(8,128)S(1)} %get-tuple-element.26.refs_7_), channel_id=1, source_target_pairs={{17,0},{19,1},{16,2},{21,3},{18,4},{23,5},{20,6},{25,7},{22,8},{27... | collective-permute-start | bytes 12296 | tf_op jit(solution)/shard_map/ppermute | solution.py:385
  12.0 1.5 %collective-permute-start.4 = (f32[8,128]{1,0:T(8,128)S(1)}, f32[8,128]{1,0:T(8,128)S(1)}, u32[]{:S(2)}, u32[]{:S(2)}) collective-permute-start(f32[8,128]{1,0:T(8,128)S(1)} %get-tuple-element.26.refs_7_), channel_id=1, source_target_pairs={{1,0},{3,1},{0,2},{5,3},{2,4},{7,5},{4,6},{9,7},{6,8},{11,9},{8,10... | collective-permute-start | bytes 12296 | tf_op jit(solution)/shard_map/ppermute | solution.py:385
  13.5 0.0 collective-permute-done.3.refs_7_
  13.5 0.6 %shard_map.66.refs_3_ = f32[12,4,8,256]{3,2,1,0:T(8,128)S(1)} custom-call(f32[3,4,8,256]{3,2,1,0:T(8,128)S(1)} %copy-done, f32[6,4,8,256]{3,2,1,0:T(8,128)S(1)} %copy-done.1, f32[3,4,8,256]{3,2,1,0:T(8,128)S(1)} %get-tuple-element.23.smooth_ref.refs_2_, f32[6,4,8,256]{3,2,1,0:T(8,128)S(1)} %get-tuple-element.17.refs_3_.refs_1_, ...), custom_call_target="tpu_custom_call" | custom-call | flops 4096000 | bytes 1572864 | tf_op jit(solution)/shard_map/pallas_call | solution.py:362
  14.1 0.4 %collective-permute-done.5.refs_6_ = f32[8,128]{1,0:T(8,128)S(1)} collective-permute-done((f32[8,128]{1,0:T(8,128)S(1)}, f32[8,128]{1,0:T(8,128)S(1)}, u32[]{:S(2)}, u32[]{:S(2)}) %collective-permute-start.5) | collective-permute-done | bytes 4128 | tf_op jit(solution)/shard_map/ppermute | solution.py:385
  14.5 0.3 %collective-permute-done.4.refs_5_ = f32[8,128]{1,0:T(8,128)S(1)} collective-permute-done((f32[8,128]{1,0:T(8,128)S(1)}, f32[8,128]{1,0:T(8,128)S(1)}, u32[]{:S(2)}, u32[]{:S(2)}) %collective-permute-start.4) | collective-permute-done | bytes 4128 | tf_op jit(solution)/shard_map/ppermute | solution.py:385
  14.8 0.3 %collective-permute-done.6.refs_8_ = f32[37,8,128]{2,1,0:T(8,128)S(1)} collective-permute-done((f32[37,8,128]{2,1,0:T(8,128)S(1)}, f32[37,8,128]{2,1,0:T(8,128)S(1)}, u32[]{:S(2)}, u32[]{:S(2)}) %collective-permute-start.6) | collective-permute-done | bytes 151584 | tf_op jit(solution)/shard_map/ppermute | solution.py:375
  15.2 0.8 %shard_map.67 = (f32[6,4,8,256]{3,2,1,0:T(8,128)}, f32[3,4,8,256]{3,2,1,0:T(8,128)}) custom-call(f32[3,4,8,256]{3,2,1,0:T(8,128)S(1)} %copy-done, f32[6,4,8,256]{3,2,1,0:T(8,128)S(1)} %get-tuple-element.17.refs_3_.refs_1_, f32[6,4,8,256]{3,2,1,0:T(8,128)S(1)} %shard_map.64.model_ref.refs_4_.refs_2_, f32[12,4,8,256]{3,2,1,0:T(8,128)S(1)} %shard_map.66.refs_3_, ...), custom_call_target="tpu_custom_call" | custom-call | flops 1638400 | bytes 1347584 | tf_op jit(solution)/shard_map/pallas_call | solution.py:362
  (4 shorter events, 0.1 us)
Async XLA Ops:
  0.6 3.0 %copy-start.2 = (f32[6,4,8,256]{3,2,1,0:T(8,128)S(1)}, f32[6,4,8,256]{3,2,1,0:T(8,128)}, u32[]{:S(2)}) copy-start(f32[6,4,8,256]{3,2,1,0:T(8,128)} %strain_ref.5) | copy-start | bytes 589828
  0.6 6.2 %collective-permute-start = (f32[3,4,8,256]{3,2,1,0:T(8,128)}, f32[3,4,8,256]{3,2,1,0:T(8,128)S(1)}, u32[]{:S(2)}, u32[]{:S(2)}) collective-permute-start(f32[3,4,8,256]{3,2,1,0:T(8,128)} %refs_0_.3), channel_id=1, source_target_pairs={{16,0},{0,16},{17,1},{1,17},{18,2},{2,18},{19,3},{3,19},{20,4},{4,... | collective-permute-start | bytes 294920 | tf_op jit(solution)/shard_map/ppermute | solution.py:375
  3.7 1.7 %copy-start.1 = (f32[6,4,8,256]{3,2,1,0:T(8,128)S(1)}, f32[6,4,8,256]{3,2,1,0:T(8,128)}, u32[]{:S(2)}) copy-start(f32[6,4,8,256]{3,2,1,0:T(8,128)} %refs_1_) | copy-start | bytes 589828
  3.7 3.2 %copy-start = (f32[3,4,8,256]{3,2,1,0:T(8,128)S(1)}, f32[3,4,8,256]{3,2,1,0:T(8,128)}, u32[]{:S(2)}) copy-start(f32[3,4,8,256]{3,2,1,0:T(8,128)} %refs_0_.3) | copy-start | bytes 294916
  3.7 3.8 %collective-permute-start.1 = (f32[2,8,256]{2,1,0:T(8,128)S(1)}, f32[2,8,256]{2,1,0:T(8,128)S(1)}, u32[]{:S(2)}, u32[]{:S(2)}) collective-permute-start(f32[2,8,256]{2,1,0:T(8,128)S(1)} %get-tuple-element.15.size_ends_ref), channel_id=1, source_target_pairs={{16,0},{0,16},{17,1},{1,17},{18,2},{2,18},{19,3},{3,19},{20,4},{4,... | collective-permute-start | bytes 49160 | tf_op jit(solution)/shard_map/ppermute | solution.py:375
  5.4 8.1 %collective-permute-start.3 = (f32[6,4,8,256]{3,2,1,0:T(8,128)S(1)}, f32[6,4,8,256]{3,2,1,0:T(8,128)S(1)}, u32[]{:S(2)}, u32[]{:S(2)}) collective-permute-start(f32[6,4,8,256]{3,2,1,0:T(8,128)S(1)} %copy-done.1), channel_id=1, source_target_pairs={{16,0},{0,16},{17,1},{1,17},{18,2},{2,18},{19,3},{3,19},{20,4},{4,... | collective-permute-start | bytes 589832 | tf_op jit(solution)/shard_map/ppermute | solution.py:375
  7.7 1.2 %collective-permute-start.2 = (f32[8,128]{1,0:T(8,128)S(1)}, f32[8,128]{1,0:T(8,128)S(1)}, u32[]{:S(2)}, u32[]{:S(2)}) collective-permute-start(f32[8,128]{1,0:T(8,128)S(1)} %get-tuple-element.24.sums_ref), channel_id=1, source_target_pairs={{1,0},{0,1},{3,2},{2,3},{5,4},{4,5},{7,6},{6,7},{9,8},{8,9},{11,10... | collective-permute-start | bytes 12296 | tf_op jit(solution)/shard_map/ppermute | solution.py:385
  8.9 6.2 %collective-permute-start.6 = (f32[37,8,128]{2,1,0:T(8,128)S(1)}, f32[37,8,128]{2,1,0:T(8,128)S(1)}, u32[]{:S(2)}, u32[]{:S(2)}) collective-permute-start(f32[37,8,128]{2,1,0:T(8,128)S(1)} %get-tuple-element.27), channel_id=1, source_target_pairs={{16,0},{0,16},{17,1},{1,17},{18,2},{2,18},{19,3},{3,19},{20,4},{4,... | collective-permute-start | bytes 454664 | tf_op jit(solution)/shard_map/ppermute | solution.py:375
  10.5 4.0 %collective-permute-start.5 = (f32[8,128]{1,0:T(8,128)S(1)}, f32[8,128]{1,0:T(8,128)S(1)}, u32[]{:S(2)}, u32[]{:S(2)}) collective-permute-start(f32[8,128]{1,0:T(8,128)S(1)} %get-tuple-element.26.refs_7_), channel_id=1, source_target_pairs={{17,0},{19,1},{16,2},{21,3},{18,4},{23,5},{20,6},{25,7},{22,8},{27... | collective-permute-start | bytes 12296 | tf_op jit(solution)/shard_map/ppermute | solution.py:385
  12.0 2.9 %collective-permute-start.4 = (f32[8,128]{1,0:T(8,128)S(1)}, f32[8,128]{1,0:T(8,128)S(1)}, u32[]{:S(2)}, u32[]{:S(2)}) collective-permute-start(f32[8,128]{1,0:T(8,128)S(1)} %get-tuple-element.26.refs_7_), channel_id=1, source_target_pairs={{1,0},{3,1},{0,2},{5,3},{2,4},{7,5},{4,6},{9,7},{6,8},{11,9},{8,10... | collective-permute-start | bytes 12296 | tf_op jit(solution)/shard_map/ppermute | solution.py:385

commit v21 on v20

--- a/solution.py
+++ b/solution.py
@@ -108,9 +108,14 @@
             size_ends_ref[end, :, lanes] = value
 
 
-def mask_kernel(bins_hbm, size_ends_ref, mask_ref, bins_ref, arrived):
+def mask_kernel(tables, bins_hbm, v_ref, size_ends_ref, mask_ref, own_ref, bins_ref, arrived):
     copy = pltpu.make_async_copy(bins_hbm, bins_ref, arrived)
     copy.start()
+    for lanes in halves(v_ref.shape[-1]):
+        v = [[v_ref[a, z, :, lanes] for z in range(tables.cells)] for a in range(3)]
+        for f, field in enumerate(v + products_of(v)):
+            for z, value in enumerate(tables.inside(field)):
+                own_ref[f, z, :, lanes] = value
     copy.wait()
     rows = bins_ref.shape[1]
     along = jnp.broadcast_to(bins_ref[...].astype(jnp.float32), (rows, rows))
@@ -142,7 +147,7 @@
     return [plain[z] + tensor[PAIR_OF[a][a]][z] * vector[a][z] for z in range(cells)]
 
 
-def velocity_kernel(tables, v_ref, strain_ref, cot_ref, *refs):
+def velocity_kernel(tables, v_ref, strain_ref, cot_ref, own_ref, *refs):
     far_v_refs = refs[:-4]
     smooth_ref, leonard_ref, rest_ref, powers_ref = refs[-4:]
     cells = tables.cells
@@ -153,7 +158,9 @@
         for far_v_ref in far_v_refs:
             far = [[far_v_ref[a, z, :, lanes] for z in range(cells)] for a in range(3)]
             ends.append([tables.project(field) for field in far + products_of(far)])
-        filtered = filtered_block(tables, 0, v + products, ends)
+        filtered = [[own_ref[f, z, :, lanes] for z in range(cells)] for f in range(9)]
+        for place in range(1, tables.devices):
+            filtered = [add_lists(near, tables.outside(place, far)) for near, far in zip(filtered, ends[place])]
         for a in range(3):
             for z in range(cells):
                 smooth_ref[a, z, :, lanes] = filtered[a][z]
@@ -410,13 +417,14 @@
         functools.partial(prepare_kernel, tables), [shaped(cells), shaped(2)], LONG * work, lane, strain
     )
     far_size = [from_ahead(size_ends, shift) for shift in range(1, span)]
-    (mask,) = call(
-        mask_kernel,
-        [pltpu.VMEM((rows, LANES), jnp.float32)],
+    mask, own = call(
+        functools.partial(mask_kernel, tables),
+        [pltpu.VMEM((rows, LANES), jnp.float32), shaped(9, cells)],
         work,
         pltpu.with_memory_space_constraint(row_bins.reshape(1, rows), pltpu.HBM),
+        velocity,
         size_ends,
-        in_specs=[REMAIN, WHOLE],
+        in_specs=[REMAIN, WHOLE, WHOLE],
         scratch=[pltpu.VMEM((1, rows), jnp.int32), pltpu.SemaphoreType.DMA(())],
     )
     mask, near_cot = lax.optimization_barrier((mask, cotangent))
@@ -429,6 +437,7 @@
         velocity,
         strain,
         near_cot,
+        own,
         *far_v,
     )
     factor, sums = call(

time: 16.1 us -> 16.2 us (level)
    ppermute x3, starting transfers between devices: 3.1 us -> 3.27 us  [from_source(): return lax.ppermute(values, ('span', 'stream'), pairs)]
    ppermute x4, starting transfers between devices: 6.73 us -> 6.55 us  [from_ahead(): lax.ppermute(values, 'span', [((i + shift) % peers, i) for i in range(pee...]
where the time goes in v21:
time: 16.2 us; the launch traced here: 16 us
  starting transfers between devices  9.82 us (61%)
  waiting for transfers between devices  2.91 us (18%)
  Pallas kernels  2.56 us (16%)
  between operations  0.7 us (4%)
    ppermute x4, starting transfers between devices, from_ahead(): lax.ppermute(values, 'span', [((i + shift) % peers, i) for i in range(pee...  6.55 us
    ppermute x3, starting transfers between devices, from_source(): return lax.ppermute(values, ('span', 'stream'), pairs)  3.27 us
    pallas_call x9, Pallas kernels, call(): pl.pallas_call(kernel, out_shape=outs, in_specs=in_specs or [WHOLE] * len...  2.56 us
    ppermute x3, waiting for transfers between devices, from_source(): return lax.ppermute(values, ('span', 'stream'), pairs)  1.88 us
    ppermute x4, waiting for transfers between devices, from_ahead(): lax.ppermute(values, 'span', [((i + shift) % peers, i) for i in range(pee...  1.03 us
  transfers between devices with their start and end apart: 7, of which 6 were waited for; matrix products, arithmetic and copies ran while one was open for 0% of the time, Pallas kernels for 11%

profile of v21, /device:TPU:0, one launch (start us, length us, event | category | flops | bytes accessed | tf_op | source)
XLA Modules:
  0.0 16.0 jit_solution(8753925327498606272)
XLA Ops:
  0.6 0.0 copy-start.2
  0.6 3.0 %collective-permute-start = (f32[3,4,8,256]{3,2,1,0:T(8,128)}, f32[3,4,8,256]{3,2,1,0:T(8,128)S(1)}, u32[]{:S(2)}, u32[]{:S(2)}) collective-permute-start(f32[3,4,8,256]{3,2,1,0:T(8,128)} %refs_0_.3), channel_id=1, source_target_pairs={{16,0},{0,16},{17,1},{1,17},{18,2},{2,18},{19,3},{3,19},{20,4},{4,... | collective-permute-start | bytes 294920 | tf_op jit(solution)/shard_map/ppermute | solution.py:382
  3.7 0.0 copy-done.2
  3.7 0.0 copy-start
  3.7 0.0 copy-start.1
  3.7 0.9 %collective-permute-start.1 = (f32[2,8,256]{2,1,0:T(8,128)S(1)}, f32[2,8,256]{2,1,0:T(8,128)S(1)}, u32[]{:S(2)}, u32[]{:S(2)}) collective-permute-start(f32[2,8,256]{2,1,0:T(8,128)S(1)} %get-tuple-element.17.size_ends_ref), channel_id=1, source_target_pairs={{16,0},{0,16},{17,1},{1,17},{18,2},{2,18},{19,3},{3,19},{20,4},{4,... | collective-permute-start | bytes 49160 | tf_op jit(solution)/shard_map/ppermute | solution.py:382
  4.6 0.0 copy-done
  4.6 0.7 %shard_map.61 = (f32[8,128]{1,0:T(8,128)S(1)}, f32[9,4,8,256]{3,2,1,0:T(8,128)S(1)}) custom-call(s32[1,8]{1,0:T(1,128)} %bitcast.1, f32[3,4,8,256]{3,2,1,0:T(8,128)S(1)} %copy-done, f32[2,8,256]{2,1,0:T(8,128)S(1)} %get-tuple-element.17.size_ends_ref), custom_call_target="tpu_custom_call" | custom-call | flops 8192 | bytes 413728 | tf_op jit(solution)/shard_map/pallas_call | solution.py:369
  5.4 0.0 copy-done.1
  5.4 1.3 %collective-permute-start.3 = (f32[6,4,8,256]{3,2,1,0:T(8,128)S(1)}, f32[6,4,8,256]{3,2,1,0:T(8,128)S(1)}, u32[]{:S(2)}, u32[]{:S(2)}) collective-permute-start(f32[6,4,8,256]{3,2,1,0:T(8,128)S(1)} %copy-done.1), channel_id=1, source_target_pairs={{16,0},{0,16},{17,1},{1,17},{18,2},{2,18},{19,3},{3,19},{20,4},{4,... | collective-permute-start | bytes 589832 | tf_op jit(solution)/shard_map/ppermute | solution.py:382
  6.7 0.2 %collective-permute-done.refs_0_.refs_6_ = f32[3,4,8,256]{3,2,1,0:T(8,128)S(1)} collective-permute-done((f32[3,4,8,256]{3,2,1,0:T(8,128)}, f32[3,4,8,256]{3,2,1,0:T(8,128)S(1)}, u32[]{:S(2)}, u32[]{:S(2)}) %collective-permute-start) | collective-permute-done | bytes 98336 | tf_op jit(solution)/shard_map/ppermute | solution.py:382
  6.9 0.2 %shard_map.62 = (f32[3,4,8,256]{3,2,1,0:T(8,128)S(1)}, f32[6,4,8,256]{3,2,1,0:T(8,128)S(1)}, f32[6,4,8,256]{3,2,1,0:T(8,128)S(1)}, f32[7,4,8,256]{3,2,1,0:T(8,128)S(1)}) custom-call(f32[3,4,8,256]{3,2,1,0:T(8,128)S(1)} %copy-done, f32[6,4,8,256]{3,2,1,0:T(8,128)S(1)} %copy-done.2, f32[6,4,8,256]{3,2,1,0:T(8,128)S(1)} %copy-done.1, ...), custom_call_target="tpu_custom_call" | custom-call | flops 2457600000 | bytes 1605632 | tf_op jit(solution)/shard_map/pallas_call | solution.py:369
  7.0 0.5 %collective-permute-done.1.refs_0_ = f32[2,8,256]{2,1,0:T(8,128)S(1)} collective-permute-done((f32[2,8,256]{2,1,0:T(8,128)S(1)}, f32[2,8,256]{2,1,0:T(8,128)S(1)}, u32[]{:S(2)}, u32[]{:S(2)}) %collective-permute-start.1) | collective-permute-done | bytes 16416 | tf_op jit(solution)/shard_map/ppermute | solution.py:382
  7.5 0.1 shard_map.63
  7.7 0.1 collective-permute-start.2
  7.8 1.1 %collective-permute-done.2.other_sums_ref = f32[8,128]{1,0:T(8,128)S(1)} collective-permute-done((f32[8,128]{1,0:T(8,128)S(1)}, f32[8,128]{1,0:T(8,128)S(1)}, u32[]{:S(2)}, u32[]{:S(2)}) %collective-permute-start.2) | collective-permute-done | bytes 4128 | tf_op jit(solution)/shard_map/ppermute | solution.py:392
  8.9 1.4 %collective-permute-start.6 = (f32[37,8,128]{2,1,0:T(8,128)S(1)}, f32[37,8,128]{2,1,0:T(8,128)S(1)}, u32[]{:S(2)}, u32[]{:S(2)}) collective-permute-start(f32[37,8,128]{2,1,0:T(8,128)S(1)} %get-tuple-element.31), channel_id=1, source_target_pairs={{16,0},{0,16},{17,1},{1,17},{18,2},{2,18},{19,3},{3,19},{20,4},{4,... | collective-permute-start | bytes 454664 | tf_op jit(solution)/shard_map/ppermute | solution.py:382
  10.3 1.7 %collective-permute-start.5 = (f32[8,128]{1,0:T(8,128)S(1)}, f32[8,128]{1,0:T(8,128)S(1)}, u32[]{:S(2)}, u32[]{:S(2)}) collective-permute-start(f32[8,128]{1,0:T(8,128)S(1)} %get-tuple-element.30.refs_7_), channel_id=1, source_target_pairs={{17,0},{19,1},{16,2},{21,3},{18,4},{23,5},{20,6},{25,7},{22,8},{27... | collective-permute-start | bytes 12296 | tf_op jit(solution)/shard_map/ppermute | solution.py:392
  12.0 1.5 %collective-permute-start.4 = (f32[8,128]{1,0:T(8,128)S(1)}, f32[8,128]{1,0:T(8,128)S(1)}, u32[]{:S(2)}, u32[]{:S(2)}) collective-permute-start(f32[8,128]{1,0:T(8,128)S(1)} %get-tuple-element.30.refs_7_), channel_id=1, source_target_pairs={{1,0},{3,1},{0,2},{5,3},{2,4},{7,5},{4,6},{9,7},{6,8},{11,9},{8,10... | collective-permute-start | bytes 12296 | tf_op jit(solution)/shard_map/ppermute | solution.py:392
  13.5 0.0 collective-permute-done.3.refs_7_
  13.5 0.6 %shard_map.66.refs_3_ = f32[12,4,8,256]{3,2,1,0:T(8,128)S(1)} custom-call(f32[3,4,8,256]{3,2,1,0:T(8,128)S(1)} %copy-done, f32[6,4,8,256]{3,2,1,0:T(8,128)S(1)} %copy-done.1, f32[3,4,8,256]{3,2,1,0:T(8,128)S(1)} %get-tuple-element.27.smooth_ref.refs_2_, f32[6,4,8,256]{3,2,1,0:T(8,128)S(1)} %get-tuple-element.21.refs_3_.refs_1_, ...), custom_call_target="tpu_custom_call" | custom-call | flops 4096000 | bytes 1572864 | tf_op jit(solution)/shard_map/pallas_call | solution.py:369
  14.1 0.4 %collective-permute-done.5.refs_6_ = f32[8,128]{1,0:T(8,128)S(1)} collective-permute-done((f32[8,128]{1,0:T(8,128)S(1)}, f32[8,128]{1,0:T(8,128)S(1)}, u32[]{:S(2)}, u32[]{:S(2)}) %collective-permute-start.5) | collective-permute-done | bytes 4128 | tf_op jit(solution)/shard_map/ppermute | solution.py:392
  14.5 0.3 %collective-permute-done.4.refs_5_ = f32[8,128]{1,0:T(8,128)S(1)} collective-permute-done((f32[8,128]{1,0:T(8,128)S(1)}, f32[8,128]{1,0:T(8,128)S(1)}, u32[]{:S(2)}, u32[]{:S(2)}) %collective-permute-start.4) | collective-permute-done | bytes 4128 | tf_op jit(solution)/shard_map/ppermute | solution.py:392
  14.8 0.3 %collective-permute-done.6.refs_8_ = f32[37,8,128]{2,1,0:T(8,128)S(1)} collective-permute-done((f32[37,8,128]{2,1,0:T(8,128)S(1)}, f32[37,8,128]{2,1,0:T(8,128)S(1)}, u32[]{:S(2)}, u32[]{:S(2)}) %collective-permute-start.6) | collective-permute-done | bytes 151584 | tf_op jit(solution)/shard_map/ppermute | solution.py:382
  15.2 0.8 %shard_map.67 = (f32[6,4,8,256]{3,2,1,0:T(8,128)}, f32[3,4,8,256]{3,2,1,0:T(8,128)}) custom-call(f32[3,4,8,256]{3,2,1,0:T(8,128)S(1)} %copy-done, f32[6,4,8,256]{3,2,1,0:T(8,128)S(1)} %get-tuple-element.21.refs_3_.refs_1_, f32[6,4,8,256]{3,2,1,0:T(8,128)S(1)} %shard_map.64.model_ref.refs_4_.refs_2_, f32[12,4,8,256]{3,2,1,0:T(8,128)S(1)} %shard_map.66.refs_3_, ...), custom_call_target="tpu_custom_call" | custom-call | flops 1638400 | bytes 1347584 | tf_op jit(solution)/shard_map/pallas_call | solution.py:369
  (4 shorter events, 0.1 us)
Async XLA Ops:
  0.6 3.0 %copy-start.2 = (f32[6,4,8,256]{3,2,1,0:T(8,128)S(1)}, f32[6,4,8,256]{3,2,1,0:T(8,128)}, u32[]{:S(2)}) copy-start(f32[6,4,8,256]{3,2,1,0:T(8,128)} %strain_ref.5) | copy-start | bytes 589828
  0.6 6.2 %collective-permute-start = (f32[3,4,8,256]{3,2,1,0:T(8,128)}, f32[3,4,8,256]{3,2,1,0:T(8,128)S(1)}, u32[]{:S(2)}, u32[]{:S(2)}) collective-permute-start(f32[3,4,8,256]{3,2,1,0:T(8,128)} %refs_0_.3), channel_id=1, source_target_pairs={{16,0},{0,16},{17,1},{1,17},{18,2},{2,18},{19,3},{3,19},{20,4},{4,... | collective-permute-start | bytes 294920 | tf_op jit(solution)/shard_map/ppermute | solution.py:382
  3.7 1.0 %copy-start = (f32[3,4,8,256]{3,2,1,0:T(8,128)S(1)}, f32[3,4,8,256]{3,2,1,0:T(8,128)}, u32[]{:S(2)}) copy-start(f32[3,4,8,256]{3,2,1,0:T(8,128)} %refs_0_.3) | copy-start | bytes 294916
  3.7 1.7 %copy-start.1 = (f32[6,4,8,256]{3,2,1,0:T(8,128)S(1)}, f32[6,4,8,256]{3,2,1,0:T(8,128)}, u32[]{:S(2)}) copy-start(f32[6,4,8,256]{3,2,1,0:T(8,128)} %refs_1_) | copy-start | bytes 589828
  3.7 3.8 %collective-permute-start.1 = (f32[2,8,256]{2,1,0:T(8,128)S(1)}, f32[2,8,256]{2,1,0:T(8,128)S(1)}, u32[]{:S(2)}, u32[]{:S(2)}) collective-permute-start(f32[2,8,256]{2,1,0:T(8,128)S(1)} %get-tuple-element.17.size_ends_ref), channel_id=1, source_target_pairs={{16,0},{0,16},{17,1},{1,17},{18,2},{2,18},{19,3},{3,19},{20,4},{4,... | collective-permute-start | bytes 49160 | tf_op jit(solution)/shard_map/ppermute | solution.py:382
  5.4 8.1 %collective-permute-start.3 = (f32[6,4,8,256]{3,2,1,0:T(8,128)S(1)}, f32[6,4,8,256]{3,2,1,0:T(8,128)S(1)}, u32[]{:S(2)}, u32[]{:S(2)}) collective-permute-start(f32[6,4,8,256]{3,2,1,0:T(8,128)S(1)} %copy-done.1), channel_id=1, source_target_pairs={{16,0},{0,16},{17,1},{1,17},{18,2},{2,18},{19,3},{3,19},{20,4},{4,... | collective-permute-start | bytes 589832 | tf_op jit(solution)/shard_map/ppermute | solution.py:382
  7.7 1.2 %collective-permute-start.2 = (f32[8,128]{1,0:T(8,128)S(1)}, f32[8,128]{1,0:T(8,128)S(1)}, u32[]{:S(2)}, u32[]{:S(2)}) collective-permute-start(f32[8,128]{1,0:T(8,128)S(1)} %get-tuple-element.28.sums_ref), channel_id=1, source_target_pairs={{1,0},{0,1},{3,2},{2,3},{5,4},{4,5},{7,6},{6,7},{9,8},{8,9},{11,10... | collective-permute-start | bytes 12296 | tf_op jit(solution)/shard_map/ppermute | solution.py:392
  8.9 6.2 %collective-permute-start.6 = (f32[37,8,128]{2,1,0:T(8,128)S(1)}, f32[37,8,128]{2,1,0:T(8,128)S(1)}, u32[]{:S(2)}, u32[]{:S(2)}) collective-permute-start(f32[37,8,128]{2,1,0:T(8,128)S(1)} %get-tuple-element.31), channel_id=1, source_target_pairs={{16,0},{0,16},{17,1},{1,17},{18,2},{2,18},{19,3},{3,19},{20,4},{4,... | collective-permute-start | bytes 454664 | tf_op jit(solution)/shard_map/ppermute | solution.py:382
  10.3 4.2 %collective-permute-start.5 = (f32[8,128]{1,0:T(8,128)S(1)}, f32[8,128]{1,0:T(8,128)S(1)}, u32[]{:S(2)}, u32[]{:S(2)}) collective-permute-start(f32[8,128]{1,0:T(8,128)S(1)} %get-tuple-element.30.refs_7_), channel_id=1, source_target_pairs={{17,0},{19,1},{16,2},{21,3},{18,4},{23,5},{20,6},{25,7},{22,8},{27... | collective-permute-start | bytes 12296 | tf_op jit(solution)/shard_map/ppermute | solution.py:392
  12.0 2.9 %collective-permute-start.4 = (f32[8,128]{1,0:T(8,128)S(1)}, f32[8,128]{1,0:T(8,128)S(1)}, u32[]{:S(2)}, u32[]{:S(2)}) collective-permute-start(f32[8,128]{1,0:T(8,128)S(1)} %get-tuple-element.30.refs_7_), channel_id=1, source_target_pairs={{1,0},{3,1},{0,2},{5,3},{2,4},{7,5},{4,6},{9,7},{6,8},{11,9},{8,10... | collective-permute-start | bytes 12296 | tf_op jit(solution)/shard_map/ppermute | solution.py:392

commit v22 on v20

--- a/solution.py
+++ b/solution.py
@@ -322,10 +322,8 @@
                 residual_ref[k, z, :, lanes] = (
                     leonard_ref[k, z, :, lanes] - coefficient * model_ref[k, z, :, lanes]
                 )
-        if k % 3 == 2:
-            some = pl.ds(k - 2, 3)
-            copies.append(pltpu.make_async_copy(residual_ref.at[some], residual_hbm.at[some], left.at[k // 3]))
-            copies[-1].start()
+    copies.append(pltpu.make_async_copy(residual_ref, residual_hbm, left.at[0]))
+    copies[-1].start()
     for half, lanes in enumerate(halves(v_ref.shape[-1])):
         v = [[v_ref[a, z, :, lanes] for z in range(cells)] for a in range(3)]
         from_model = [[] for _ in range(6)]
@@ -347,7 +345,7 @@
                 grad_ref[a, z, :, lanes] = (
                     parts_ref[a, z, :, lanes] + coefficient * parts_ref[3 + a, z, :, lanes] + pull * pulled
                 )
-    copies.append(pltpu.make_async_copy(grad_ref, grad_hbm, left.at[2]))
+    copies.append(pltpu.make_async_copy(grad_ref, grad_hbm, left.at[1]))
     copies[-1].start()
     for copy in copies:
         copy.wait()
@@ -485,7 +483,7 @@
             pair_sums,
             *far_message,
             out_specs=[REMAIN] * 2,
-            scratch=[pltpu.VMEM(x.shape, x.dtype) for x in outs] + [pltpu.SemaphoreType.DMA((3,))],
+            scratch=[pltpu.VMEM(x.shape, x.dtype) for x in outs] + [pltpu.SemaphoreType.DMA((2,))],
         )
     )
 

time: 16.1 us -> 16.1 us (level)
  no operation moved by 1% of the time
where the time goes in v22:
time: 16.1 us; the launch traced here: 16 us
  starting transfers between devices  9.82 us (61%)
  waiting for transfers between devices  2.83 us (18%)
  Pallas kernels  2.63 us (16%)
  between operations  0.7 us (4%)
    ppermute x4, starting transfers between devices, from_ahead(): lax.ppermute(values, 'span', [((i + shift) % peers, i) for i in range(pee...  6.73 us
    ppermute x3, starting transfers between devices, from_source(): return lax.ppermute(values, ('span', 'stream'), pairs)  3.1 us
    pallas_call x9, Pallas kernels, call(): pl.pallas_call(kernel, out_shape=outs, in_specs=in_specs or [WHOLE] * len...  2.63 us
    ppermute x3, waiting for transfers between devices, from_source(): return lax.ppermute(values, ('span', 'stream'), pairs)  1.87 us
    ppermute x4, waiting for transfers between devices, from_ahead(): lax.ppermute(values, 'span', [((i + shift) % peers, i) for i in range(pee...  0.96 us
  transfers between devices with their start and end apart: 7, of which 6 were waited for; matrix products, arithmetic and copies ran while one was open for 0% of the time, Pallas kernels for 11%

profile of v22, /device:TPU:0, one launch (start us, length us, event | category | flops | bytes accessed | tf_op | source)
XLA Modules:
  0.0 16.0 jit_solution(10630524388255861736)
XLA Ops:
  0.6 0.0 copy-start.2
  0.6 3.0 %collective-permute-start = (f32[3,4,8,256]{3,2,1,0:T(8,128)}, f32[3,4,8,256]{3,2,1,0:T(8,128)S(1)}, u32[]{:S(2)}, u32[]{:S(2)}) collective-permute-start(f32[3,4,8,256]{3,2,1,0:T(8,128)} %refs_0_.3), channel_id=1, source_target_pairs={{16,0},{0,16},{17,1},{1,17},{18,2},{2,18},{19,3},{3,19},{20,4},{4,... | collective-permute-start | bytes 294920 | tf_op jit(solution)/shard_map/ppermute | solution.py:373
  3.7 0.0 copy-done.2
  3.7 0.0 copy-start.1
  3.7 0.0 copy-start
  3.7 0.9 %collective-permute-start.1 = (f32[2,8,256]{2,1,0:T(8,128)S(1)}, f32[2,8,256]{2,1,0:T(8,128)S(1)}, u32[]{:S(2)}, u32[]{:S(2)}) collective-permute-start(f32[2,8,256]{2,1,0:T(8,128)S(1)} %get-tuple-element.15.size_ends_ref), channel_id=1, source_target_pairs={{16,0},{0,16},{17,1},{1,17},{18,2},{2,18},{19,3},{3,19},{20,4},{4,... | collective-permute-start | bytes 49160 | tf_op jit(solution)/shard_map/ppermute | solution.py:373
  4.6 0.7 %shard_map.61.mask_ref.refs_4_ = f32[8,128]{1,0:T(8,128)S(1)} custom-call(s32[1,8]{1,0:T(1,128)} %bitcast.1, f32[2,8,256]{2,1,0:T(8,128)S(1)} %get-tuple-element.15.size_ends_ref), custom_call_target="tpu_custom_call" | custom-call | flops 8192 | bytes 20512 | tf_op jit(solution)/shard_map/pallas_call | solution.py:360
  5.4 0.0 copy-done.1
  5.4 1.3 %collective-permute-start.3 = (f32[6,4,8,256]{3,2,1,0:T(8,128)S(1)}, f32[6,4,8,256]{3,2,1,0:T(8,128)S(1)}, u32[]{:S(2)}, u32[]{:S(2)}) collective-permute-start(f32[6,4,8,256]{3,2,1,0:T(8,128)S(1)} %copy-done.1), channel_id=1, source_target_pairs={{16,0},{0,16},{17,1},{1,17},{18,2},{2,18},{19,3},{3,19},{20,4},{4,... | collective-permute-start | bytes 589832 | tf_op jit(solution)/shard_map/ppermute | solution.py:373
  6.6 0.2 %collective-permute-done.refs_0_.refs_6_ = f32[3,4,8,256]{3,2,1,0:T(8,128)S(1)} collective-permute-done((f32[3,4,8,256]{3,2,1,0:T(8,128)}, f32[3,4,8,256]{3,2,1,0:T(8,128)S(1)}, u32[]{:S(2)}, u32[]{:S(2)}) %collective-permute-start) | collective-permute-done | bytes 98336 | tf_op jit(solution)/shard_map/ppermute | solution.py:373
  6.9 0.0 copy-done
  6.9 0.3 %shard_map.62 = (f32[3,4,8,256]{3,2,1,0:T(8,128)S(1)}, f32[6,4,8,256]{3,2,1,0:T(8,128)S(1)}, f32[6,4,8,256]{3,2,1,0:T(8,128)S(1)}, f32[7,4,8,256]{3,2,1,0:T(8,128)S(1)}) custom-call(f32[3,4,8,256]{3,2,1,0:T(8,128)S(1)} %copy-done, f32[6,4,8,256]{3,2,1,0:T(8,128)S(1)} %copy-done.2, f32[6,4,8,256]{3,2,1,0:T(8,128)S(1)} %copy-done.1, ...), custom_call_target="tpu_custom_call" | custom-call | flops 2457600000 | bytes 1310720 | tf_op jit(solution)/shard_map/pallas_call | solution.py:360
  7.1 0.4 %collective-permute-done.1.refs_0_ = f32[2,8,256]{2,1,0:T(8,128)S(1)} collective-permute-done((f32[2,8,256]{2,1,0:T(8,128)S(1)}, f32[2,8,256]{2,1,0:T(8,128)S(1)}, u32[]{:S(2)}, u32[]{:S(2)}) %collective-permute-start.1) | collective-permute-done | bytes 16416 | tf_op jit(solution)/shard_map/ppermute | solution.py:373
  7.5 0.1 shard_map.63
  7.7 0.1 collective-permute-start.2
  7.8 1.1 %collective-permute-done.2.other_sums_ref = f32[8,128]{1,0:T(8,128)S(1)} collective-permute-done((f32[8,128]{1,0:T(8,128)S(1)}, f32[8,128]{1,0:T(8,128)S(1)}, u32[]{:S(2)}, u32[]{:S(2)}) %collective-permute-start.2) | collective-permute-done | bytes 4128 | tf_op jit(solution)/shard_map/ppermute | solution.py:383
  8.9 1.5 %collective-permute-start.6 = (f32[37,8,128]{2,1,0:T(8,128)S(1)}, f32[37,8,128]{2,1,0:T(8,128)S(1)}, u32[]{:S(2)}, u32[]{:S(2)}) collective-permute-start(f32[37,8,128]{2,1,0:T(8,128)S(1)} %get-tuple-element.27), channel_id=1, source_target_pairs={{16,0},{0,16},{17,1},{1,17},{18,2},{2,18},{19,3},{3,19},{20,4},{4,... | collective-permute-start | bytes 454664 | tf_op jit(solution)/shard_map/ppermute | solution.py:373
  10.5 1.5 %collective-permute-start.5 = (f32[8,128]{1,0:T(8,128)S(1)}, f32[8,128]{1,0:T(8,128)S(1)}, u32[]{:S(2)}, u32[]{:S(2)}) collective-permute-start(f32[8,128]{1,0:T(8,128)S(1)} %get-tuple-element.26.refs_7_), channel_id=1, source_target_pairs={{17,0},{19,1},{16,2},{21,3},{18,4},{23,5},{20,6},{25,7},{22,8},{27... | collective-permute-start | bytes 12296 | tf_op jit(solution)/shard_map/ppermute | solution.py:383
  12.0 1.5 %collective-permute-start.4 = (f32[8,128]{1,0:T(8,128)S(1)}, f32[8,128]{1,0:T(8,128)S(1)}, u32[]{:S(2)}, u32[]{:S(2)}) collective-permute-start(f32[8,128]{1,0:T(8,128)S(1)} %get-tuple-element.26.refs_7_), channel_id=1, source_target_pairs={{1,0},{3,1},{0,2},{5,3},{2,4},{7,5},{4,6},{9,7},{6,8},{11,9},{8,10... | collective-permute-start | bytes 12296 | tf_op jit(solution)/shard_map/ppermute | solution.py:383
  13.5 0.0 collective-permute-done.3.refs_7_
  13.5 0.6 %shard_map.66.refs_3_ = f32[12,4,8,256]{3,2,1,0:T(8,128)S(1)} custom-call(f32[3,4,8,256]{3,2,1,0:T(8,128)S(1)} %copy-done, f32[6,4,8,256]{3,2,1,0:T(8,128)S(1)} %copy-done.1, f32[3,4,8,256]{3,2,1,0:T(8,128)S(1)} %get-tuple-element.23.smooth_ref.refs_2_, f32[6,4,8,256]{3,2,1,0:T(8,128)S(1)} %get-tuple-element.17.refs_3_.refs_1_, ...), custom_call_target="tpu_custom_call" | custom-call | flops 4096000 | bytes 1572864 | tf_op jit(solution)/shard_map/pallas_call | solution.py:360
  14.1 0.4 %collective-permute-done.5.refs_6_ = f32[8,128]{1,0:T(8,128)S(1)} collective-permute-done((f32[8,128]{1,0:T(8,128)S(1)}, f32[8,128]{1,0:T(8,128)S(1)}, u32[]{:S(2)}, u32[]{:S(2)}) %collective-permute-start.5) | collective-permute-done | bytes 4128 | tf_op jit(solution)/shard_map/ppermute | solution.py:383
  14.5 0.3 %collective-permute-done.4.refs_5_ = f32[8,128]{1,0:T(8,128)S(1)} collective-permute-done((f32[8,128]{1,0:T(8,128)S(1)}, f32[8,128]{1,0:T(8,128)S(1)}, u32[]{:S(2)}, u32[]{:S(2)}) %collective-permute-start.4) | collective-permute-done | bytes 4128 | tf_op jit(solution)/shard_map/ppermute | solution.py:383
  14.8 0.3 %collective-permute-done.6.refs_8_ = f32[37,8,128]{2,1,0:T(8,128)S(1)} collective-permute-done((f32[37,8,128]{2,1,0:T(8,128)S(1)}, f32[37,8,128]{2,1,0:T(8,128)S(1)}, u32[]{:S(2)}, u32[]{:S(2)}) %collective-permute-start.6) | collective-permute-done | bytes 151584 | tf_op jit(solution)/shard_map/ppermute | solution.py:373
  15.2 0.8 %shard_map.67 = (f32[6,4,8,256]{3,2,1,0:T(8,128)}, f32[3,4,8,256]{3,2,1,0:T(8,128)}) custom-call(f32[3,4,8,256]{3,2,1,0:T(8,128)S(1)} %copy-done, f32[6,4,8,256]{3,2,1,0:T(8,128)S(1)} %get-tuple-element.17.refs_3_.refs_1_, f32[6,4,8,256]{3,2,1,0:T(8,128)S(1)} %shard_map.64.model_ref.refs_4_.refs_2_, f32[12,4,8,256]{3,2,1,0:T(8,128)S(1)} %shard_map.66.refs_3_, ...), custom_call_target="tpu_custom_call" | custom-call | flops 1638400 | bytes 1347584 | tf_op jit(solution)/shard_map/pallas_call | solution.py:360
  (4 shorter events, 0.1 us)
Async XLA Ops:
  0.6 3.0 %copy-start.2 = (f32[6,4,8,256]{3,2,1,0:T(8,128)S(1)}, f32[6,4,8,256]{3,2,1,0:T(8,128)}, u32[]{:S(2)}) copy-start(f32[6,4,8,256]{3,2,1,0:T(8,128)} %strain_ref.5) | copy-start | bytes 589828
  0.6 6.2 %collective-permute-start = (f32[3,4,8,256]{3,2,1,0:T(8,128)}, f32[3,4,8,256]{3,2,1,0:T(8,128)S(1)}, u32[]{:S(2)}, u32[]{:S(2)}) collective-permute-start(f32[3,4,8,256]{3,2,1,0:T(8,128)} %refs_0_.3), channel_id=1, source_target_pairs={{16,0},{0,16},{17,1},{1,17},{18,2},{2,18},{19,3},{3,19},{20,4},{4,... | collective-permute-start | bytes 294920 | tf_op jit(solution)/shard_map/ppermute | solution.py:373
  3.7 1.7 %copy-start.1 = (f32[6,4,8,256]{3,2,1,0:T(8,128)S(1)}, f32[6,4,8,256]{3,2,1,0:T(8,128)}, u32[]{:S(2)}) copy-start(f32[6,4,8,256]{3,2,1,0:T(8,128)} %refs_1_) | copy-start | bytes 589828
  3.7 3.2 %copy-start = (f32[3,4,8,256]{3,2,1,0:T(8,128)S(1)}, f32[3,4,8,256]{3,2,1,0:T(8,128)}, u32[]{:S(2)}) copy-start(f32[3,4,8,256]{3,2,1,0:T(8,128)} %refs_0_.3) | copy-start | bytes 294916
  3.7 3.8 %collective-permute-start.1 = (f32[2,8,256]{2,1,0:T(8,128)S(1)}, f32[2,8,256]{2,1,0:T(8,128)S(1)}, u32[]{:S(2)}, u32[]{:S(2)}) collective-permute-start(f32[2,8,256]{2,1,0:T(8,128)S(1)} %get-tuple-element.15.size_ends_ref), channel_id=1, source_target_pairs={{16,0},{0,16},{17,1},{1,17},{18,2},{2,18},{19,3},{3,19},{20,4},{4,... | collective-permute-start | bytes 49160 | tf_op jit(solution)/shard_map/ppermute | solution.py:373
  5.4 8.1 %collective-permute-start.3 = (f32[6,4,8,256]{3,2,1,0:T(8,128)S(1)}, f32[6,4,8,256]{3,2,1,0:T(8,128)S(1)}, u32[]{:S(2)}, u32[]{:S(2)}) collective-permute-start(f32[6,4,8,256]{3,2,1,0:T(8,128)S(1)} %copy-done.1), channel_id=1, source_target_pairs={{16,0},{0,16},{17,1},{1,17},{18,2},{2,18},{19,3},{3,19},{20,4},{4,... | collective-permute-start | bytes 589832 | tf_op jit(solution)/shard_map/ppermute | solution.py:373
  7.7 1.2 %collective-permute-start.2 = (f32[8,128]{1,0:T(8,128)S(1)}, f32[8,128]{1,0:T(8,128)S(1)}, u32[]{:S(2)}, u32[]{:S(2)}) collective-permute-start(f32[8,128]{1,0:T(8,128)S(1)} %get-tuple-element.24.sums_ref), channel_id=1, source_target_pairs={{1,0},{0,1},{3,2},{2,3},{5,4},{4,5},{7,6},{6,7},{9,8},{8,9},{11,10... | collective-permute-start | bytes 12296 | tf_op jit(solution)/shard_map/ppermute | solution.py:383
  8.9 6.2 %collective-permute-start.6 = (f32[37,8,128]{2,1,0:T(8,128)S(1)}, f32[37,8,128]{2,1,0:T(8,128)S(1)}, u32[]{:S(2)}, u32[]{:S(2)}) collective-permute-start(f32[37,8,128]{2,1,0:T(8,128)S(1)} %get-tuple-element.27), channel_id=1, source_target_pairs={{16,0},{0,16},{17,1},{1,17},{18,2},{2,18},{19,3},{3,19},{20,4},{4,... | collective-permute-start | bytes 454664 | tf_op jit(solution)/shard_map/ppermute | solution.py:373
  10.5 4.0 %collective-permute-start.5 = (f32[8,128]{1,0:T(8,128)S(1)}, f32[8,128]{1,0:T(8,128)S(1)}, u32[]{:S(2)}, u32[]{:S(2)}) collective-permute-start(f32[8,128]{1,0:T(8,128)S(1)} %get-tuple-element.26.refs_7_), channel_id=1, source_target_pairs={{17,0},{19,1},{16,2},{21,3},{18,4},{23,5},{20,6},{25,7},{22,8},{27... | collective-permute-start | bytes 12296 | tf_op jit(solution)/shard_map/ppermute | solution.py:383
  12.0 2.9 %collective-permute-start.4 = (f32[8,128]{1,0:T(8,128)S(1)}, f32[8,128]{1,0:T(8,128)S(1)}, u32[]{:S(2)}, u32[]{:S(2)}) collective-permute-start(f32[8,128]{1,0:T(8,128)S(1)} %get-tuple-element.26.refs_7_), channel_id=1, source_target_pairs={{1,0},{3,1},{0,2},{5,3},{2,4},{7,5},{4,6},{9,7},{6,8},{11,9},{8,10... | collective-permute-start | bytes 12296 | tf_op jit(solution)/shard_map/ppermute | solution.py:383
